TPU v7x, 128 devices: a whole 4x4x4 slice. The times are simulated.
128 devices in a mesh: grid: 8 (over x_lo, z), band: 16 (over y, x_hi, core).
Axes of the slice: x: 4 (x_hi: 2, x_lo: 2; x = x_hi * 2 + x_lo), y: 4, z: 4, core: 2. Of those that a mesh axis runs over, the one named last changes fastest.
Arguments:
- virtual_field: bfloat16 [2048, 64, 4096], P('band', 'grid'), may hold values from -6 to 6
- occupied_field: bfloat16 [256, 64, 4096], P('band', 'grid'), may hold values from -6 to 6
- amplitudes: bfloat16 [1, 2048, 2048], P(None, 'band', 'grid'), may hold values from -0.1875 to 0.1875
- ablock: int32 [1], replicated, may hold values from 0 to 31
- pairs: int32 [1, 2], replicated, may hold values from 0 to 255
- kept_cells: int32 [128, 512], P(('grid', 'band')), may hold values from 0 to 1023, as said below
Outputs:
- ladder: float32 [1, 2048, 64], P(None, ('grid', 'band'))
Inputs may be any that keep to these rules, and one draw needn't show every extreme that they name: `kept_cells`: each row holds 512 distinct cells in rising order, and always holds 0 and 1023.
All inputs are finite; a program needn't handle non-finite values.
Results may differ from a plain program's by a relative error of at most 0.018.
Values may be sent and summed in bfloat16 or wider, within the bound.
No kernel may reach another device: no remote copies, remote signals or barrier semaphores. Data moves between devices by JAX's collectives and lax.ppermute only.
A program may use at most 256 MiB of HBM per device.

v0:
```python
import math

import jax
import jax.numpy as jnp
from jax import lax
from jax.sharding import PartitionSpec as P

NY = 64
NZ = 64
ABLK = 64


def spread(value, axis, root):
    mine = lax.axis_index(axis) == root
    return lax.psum(jnp.where(mine, value, jnp.zeros_like(value)), axis)


def twiddle_tables(length):
    wave_index = jnp.arange(length, dtype=jnp.int32)
    phase_index = wave_index[:, None] * wave_index[None, :] % length
    phase_angle = 2.0 * math.pi / length * phase_index.astype(jnp.float32)
    return (jnp.cos(phase_angle).astype(jnp.bfloat16), jnp.sin(phase_angle).astype(jnp.bfloat16))


def z_section(density):
    z_count = density.shape[-1]
    half_z = z_count // 2
    cosine_table, sine_table = twiddle_tables(z_count)
    z_table = jnp.concatenate([cosine_table[:half_z].T, -sine_table[:half_z].T], axis=1)
    return jnp.dot(density, z_table, preferred_element_type=jnp.float32).astype(jnp.bfloat16)


def y_section(zfreq):
    batch, x_local, y_count, z_count = zfreq.shape
    half_z = z_count // 2
    cosine_table, sine_table = twiddle_tables(y_count)
    with_cosine = jnp.einsum(
        "bxyq,ky->bkqx", zfreq, cosine_table, preferred_element_type=jnp.float32
    )
    with_sine = jnp.einsum("bxyq,ky->bkqx", zfreq, sine_table, preferred_element_type=jnp.float32)
    real_part = with_cosine[:, :, :half_z] + with_sine[:, :, half_z:]
    imag_part = with_cosine[:, :, half_z:] - with_sine[:, :, :half_z]
    stacked = jnp.stack([real_part, imag_part], axis=3)
    return stacked.astype(jnp.bfloat16)


def signed_freq(index, length):
    return (index + length // 2) % length - length // 2


def pair_density(fields, orbital):
    return (fields.astype(jnp.float32) * orbital.astype(jnp.float32)[None]).astype(jnp.bfloat16)


def per_device(virtual_field, occupied_field, amplitudes, ablock, pairs, kept_cells):
    band_count = lax.axis_size("band")
    grid_count = lax.axis_size("grid")
    band_rank = lax.axis_index("band")
    grid_rank = lax.axis_index("grid")
    local_bands, x_local, plane_cells = virtual_field.shape
    y_count = NY
    z_count = NZ
    half_z = z_count // 2
    occ_local = occupied_field.shape[0]
    x_count = x_local * grid_count
    all_bands = local_bands * band_count
    shard_count = grid_count * band_count
    cells_dev = y_count * half_z // shard_count
    kept_local = kept_cells[0]
    keep_count = kept_local.shape[0]
    shard_rank = grid_rank * band_count + band_rank
    band_grid = virtual_field.reshape(local_bands, x_local, y_count, z_count)
    freq_x = kept_local // cells_dev
    cell_flat = shard_rank * cells_dev + kept_local % cells_dev
    freq_y = cell_flat // half_z
    freq_z = cell_flat % half_z
    squared = signed_freq(freq_x, x_count) ** 2 + signed_freq(freq_y, y_count) ** 2 + freq_z**2
    weights = 1.0 / jnp.sqrt(
        float(x_count * y_count * z_count) * (squared.astype(jnp.float32) + 1.0)
    )
    x_cosine, x_sine = twiddle_tables(x_count)
    x_cosine = x_cosine.reshape(x_count, grid_count, x_local)
    x_sine = x_sine.reshape(x_count, grid_count, x_local)
    block_start = ablock[0] * ABLK
    block_share = ABLK // band_count
    owner_band = block_start // local_bands
    own_rows = lax.dynamic_slice_in_dim(virtual_field, block_start % local_bands, ABLK, 0)
    block_fields = spread(own_rows, "band", owner_band)
    my_block = lax.dynamic_slice_in_dim(block_fields, band_rank * block_share, block_share, 0)
    my_block = my_block.reshape(block_share, x_local, y_count, z_count)
    pick_rows = pairs[0] - band_rank * occ_local
    selector = (pick_rows[:, None] == jnp.arange(occ_local, dtype=jnp.int32)[None, :]).astype(
        jnp.bfloat16
    )
    chosen = jnp.dot(
        selector, occupied_field.reshape(occ_local, -1), preferred_element_type=jnp.float32
    )
    orbitals = lax.psum(chosen.astype(jnp.bfloat16), "band")
    orbitals = orbitals.reshape(2, x_local, y_count, z_count)
    first_orbital = orbitals[0]
    second_orbital = orbitals[1]
    products = jnp.concatenate(
        [pair_density(band_grid, second_orbital), pair_density(my_block, first_orbital)], axis=0
    )
    yfreq = y_section(z_section(products))
    item_total = yfreq.shape[0]
    outgoing = yfreq.reshape(item_total, shard_count, cells_dev * 2 * x_local)[None, None]
    received = lax.all_to_all(outgoing, ("grid", "band"), split_axis=3, concat_axis=0, tiled=True)
    item_count = received.shape[2]
    arranged = received.reshape(grid_count, band_count, item_count, cells_dev, 2, x_local)
    with_cosine = jnp.einsum(
        "gnictx,kgx->nitkc", arranged, x_cosine, preferred_element_type=jnp.float32
    )
    with_sine = jnp.einsum(
        "gnictx,kgx->nitkc", arranged, x_sine, preferred_element_type=jnp.float32
    )
    real_part = with_cosine[:, :, 0] + with_sine[:, :, 1]
    imag_part = with_cosine[:, :, 1] - with_sine[:, :, 0]
    real_kept = (
        jnp.take(real_part.reshape(band_count, item_count, -1), kept_local, axis=2) * weights
    )
    imag_kept = (
        jnp.take(imag_part.reshape(band_count, item_count, -1), kept_local, axis=2) * weights
    )
    vertex_all = jnp.stack([real_kept, imag_kept], axis=2).astype(jnp.bfloat16)
    bands_vertex = vertex_all[:, :local_bands].reshape(all_bands, 2 * keep_count)
    block_vertex = vertex_all[:, local_bands:].reshape(ABLK, 2 * keep_count)
    partial_slab = lax.dot_general(
        block_vertex, bands_vertex, (((1,), (1,)), ((), ())), preferred_element_type=jnp.float32
    )
    slab_whole = lax.psum(partial_slab, ("grid", "band"))
    slab_mine = lax.dynamic_slice_in_dim(slab_whole, band_rank * local_bands, local_bands, 1)
    slab_rounded = slab_mine.astype(jnp.bfloat16)
    local_amp = amplitudes[0]
    ladder_rows = lax.psum_scatter(
        lax.dot_general(
            local_amp, slab_rounded, (((0,), (1,)), ((), ())), preferred_element_type=jnp.float32
        ).astype(jnp.bfloat16),
        "band",
        scatter_dimension=0,
        tiled=True,
    ).astype(jnp.float32)
    outputs = [ladder_rows]
    return jnp.stack(outputs)


def solution(mesh):
    in_specs = (
        P("band", "grid", None),
        P("band", "grid", None),
        P(None, "band", "grid"),
        P(),
        P(),
        P(("grid", "band"), None),
    )
    out_specs = P(None, ("grid", "band"), None)
    return jax.shard_map(
        per_device, mesh=mesh, in_specs=in_specs, out_specs=out_specs, check_vma=False
    )
```

profile of v0, /device:TPU:1, one launch (start us, length us, event | category | flops | bytes accessed | tf_op | source)
XLA Modules:
  0.0 812.9 jit_solution(15566013997403620574)
XLA Ops:
  10.7 4.4 dynamic-slice_select_fusion
  15.2 14.1 %copy.25 = f32[128,8,4096]{0,2,1:T(8,128)} copy(bf16[128,8,4096]{2,1,0:T(8,128)(2,1)} %param.8) | data formatting | bytes 25165824 | tf_op jit(solution)/shard_map/convert_element_type | solution.py:52
  29.6 144.9 %all-reduce.4.cloned.1.call-done = (bf16[64,8,4096]{2,1,0:T(8,128)(2,1)}, bf16[2,32768]{1,0:T(2,128)(2,1)}) async-done(((bf16[64,8,4096]{2,1,0:T(8,128)(2,1)}, bf16[2,32768]{1,0:T(2,128)(2,1)}), (bf16[64,8,4096]{2,1,0:T(8,128)(2,1)}, bf16[2,32768]{1,0:T(2,128)(2,1)})) %all-reduce.4.cloned.1.call-update) | async-done | bytes 4325392 | tf_op jit(solution)/shard_map/psum | solution.py:15
  175.5 8.7 %copy.26 = f32[4,8,4096]{0,2,1:T(8,128)} copy(f32[4,8,4096]{2,1,0:T(8,128)S(1)} %dynamic-slice_convert_fusion) | data formatting | bytes 1048576 | tf_op jit(solution)/shard_map/convert_element_type | solution.py:52
  185.1 11.8 %multiply_convert_fusion = bf16[4,8,64,64]{0,3,2,1:T(8,128)(2,1)} fusion(f32[4,8,64,64]{0,3,2,1:T(8,128)} %bitcast.117, f32[8,64,64]{2,1,0:T(8,128)S(1)} %reshape.281), kind=kLoop, calls=%fused_computation.14 | loop fusion | flops 262144 | bytes 917504 | tf_op jit(solution)/shard_map/convert_element_type | solution.py:52
  196.9 11.8 %multiply_convert_fusion.1 = bf16[128,8,64,64]{0,3,2,1:T(8,128)(2,1)} fusion(f32[128,8,64,64]{0,3,2,1:T(8,128)} %bitcast.116, f32[8,64,64]{2,1,0:T(8,128)S(1)} %reshape.279), kind=kLoop, calls=%fused_computation.15 | loop fusion | flops 8388608 | bytes 25296896 | tf_op jit(solution)/shard_map/convert_element_type | solution.py:52
  208.7 11.6 %fusion.16 = bf16[132,8,64,64]{0,3,2,1:T(8,128)(2,1)} fusion(bf16[4,8,64,64]{0,3,2,1:T(8,128)(2,1)} %multiply_convert_fusion, bf16[128,8,64,64]{0,3,2,1:T(8,128)(2,1)} %multiply_convert_fusion.1, bf16[64,32]{0,1:T(8,128)(2,1)S(1)} %get-tuple-element.16, bf16[64,32]{0,1:T(8,128)(2,1)S(1)} %get-tuple-element.17), kind=kOutput, calls=%fused_computation.24 | convolution fusion | flops 575291392 | bytes 17309696 | tf_op jit(solution)/shard_map/dot_general | solution.py:30
  220.3 25.7 %fusion.10 = f32[132,64,64,8]{0,1,2,3:T(8,128)} fusion(bf16[132,8,64,64]{0,3,2,1:T(8,128)(2,1)} %fusion.16), kind=kOutput, calls=%fused_computation.22 | convolution fusion | flops 553709568 | bytes 25952256 | tf_op jit(solution)/shard_map/bxyq,ky->bkqx/dot_general | solution.py:37
  246.0 26.0 %fusion.13 = f32[132,64,64,8]{0,1,2,3:T(8,128)} fusion(bf16[132,8,64,64]{0,3,2,1:T(8,128)(2,1)} %fusion.16), kind=kOutput, calls=%fused_computation.23 | convolution fusion | flops 553709568 | bytes 25952256 | tf_op jit(solution)/shard_map/bxyq,ky->bkqx/dot_general | solution.py:40
  272.0 25.6 %fusion.19 = (bf16[132,64,32,1,8]{0,1,2,4,3:T(8,128)(2,1)S(1)}, bf16[132,64,32,1,8]{0,1,2,4,3:T(8,128)(2,1)}) fusion(f32[132,64,64,8]{0,1,2,3:T(8,128)} %fusion.13, f32[132,64,64,8]{0,1,2,3:T(8,128)} %fusion.10), kind=kLoop, calls=%fused_computation.25 | loop fusion | flops 8650752 | bytes 43253760 | tf_op jit(solution)/shard_map/stack | solution.py:43
  297.6 7.2 pad_maximum_fusion
  304.8 21.1 %copy.29 = bf16[132,64,32,2,8]{0,4,3,2,1:T(8,128)(2,1)} copy(bf16[132,64,32,2,8]{0,1,2,4,3:T(8,128)(2,1)S(1)} %pad_maximum_fusion) | data formatting | bytes 17301504 | tf_op jit(solution)/shard_map/stack | solution.py:43
  325.9 17.5 %copy.30 = bf16[1,1,132,128,256]{4,2,1,0,3:T(8,128)(2,1)} copy(bf16[1,1,132,128,256]{2,4,3,1,0:T(8,128)(2,1)} %bitcast.118) | data formatting | bytes 17301504 | tf_op jit(solution)/shard_map/convert_element_type | solution.py:44
  343.4 10.2 %all-to-all-start = ((bf16[1,1,132,128,256]{4,2,1,0,3:T(8,128)(2,1)}), bf16[1,1,132,128,256]{4,2,1,0,3:T(8,128)(2,1)}, u32[]{:S(2)}, u32[]{:S(2)}) async-start(bf16[1,1,132,128,256]{4,2,1,0,3:T(8,128)(2,1)} %copy.30), calls=%async_computation | async-start | bytes 17825792 | tf_op jit(solution)/shard_map/all_to_all | solution.py:108
  353.7 108.6 %all-to-all-done = bf16[1,1,132,128,256]{4,2,1,0,3:T(8,128)(2,1)} async-done(((bf16[1,1,132,128,256]{4,2,1,0,3:T(8,128)(2,1)}), bf16[1,1,132,128,256]{4,2,1,0,3:T(8,128)(2,1)}, u32[]{:S(2)}, u32[]{:S(2)}) %all-to-all-start) | async-done | bytes 8650784 | tf_op jit(solution)/shard_map/all_to_all | solution.py:108
  462.4 17.0 %copy.31 = bf16[1,1,132,128,256]{2,4,3,1,0:T(8,128)(2,1)} copy(bf16[1,1,132,128,256]{4,2,1,0,3:T(8,128)(2,1)} %all-to-all-done) | data formatting | bytes 17301504 | tf_op jit(solution)/shard_map/all_to_all | solution.py:108
  479.4 16.8 %convolution_bitcast_fusion = f32[16,132,2,64,16]{1,3,2,4,0:T(8,128)} fusion(bf16[8,16,132,16,2,8]{2,5,4,3,1,0:T(8,128)(2,1)} %bitcast.114, s32[8,8]{1,0:T(8,128)S(1)} %multiply_add_fusion), kind=kOutput, calls=%fused_computation.20 | convolution fusion | flops 553709568 | bytes 25952512 | tf_op jit(solution)/shard_map/gnictx,kgx->nitkc/dot_general | solution.py:114
  496.2 16.8 %convolution_bitcast_fusion.1 = f32[16,132,2,64,16]{1,3,2,4,0:T(8,128)} fusion(bf16[8,16,132,16,2,8]{2,5,4,3,1,0:T(8,128)(2,1)} %bitcast.115, s32[8,8]{1,0:T(8,128)S(1)} %multiply_add_fusion), kind=kOutput, calls=%fused_computation.21 | convolution fusion | flops 553709568 | bytes 25952512 | tf_op jit(solution)/shard_map/gnictx,kgx->nitkc/dot_general | solution.py:111
  513.0 34.3 %slice_subtract_fusion = (f32[16,132,1,64,16]{1,3,2,4,0:T(8,128)}, f32[16,132,1,64,16]{1,3,2,4,0:T(8,128)}) fusion(f32[16,132,2,64,16]{1,3,2,4,0:T(8,128)} %convolution_bitcast_fusion, f32[16,132,2,64,16]{1,3,2,4,0:T(8,128)} %convolution_bitcast_fusion.1), kind=kLoop, calls=%fused_computation.3 | loop fusion | flops 4325376 | bytes 51904512 | tf_op jit(solution)/shard_map/sub | solution.py:118
  547.4 15.6 %copy.34 = f32[16,132,1,64,16]{1,4,3,0,2:T(8,128)S(1)} copy(f32[16,132,1,64,16]{1,3,2,4,0:T(8,128)} %get-tuple-element.11) | data formatting | bytes 17301504 | tf_op jit(solution)/shard_map/add | solution.py:117
  563.1 23.1 %copy.35 = f32[16,132,1024]{1,0,2:T(8,128)} copy(f32[16,132,1024]{1,2,0:T(8,128)S(1)} %bitcast.119) | data formatting | bytes 17301504 | tf_op jit(solution)/shard_map/add | solution.py:117
  586.2 20.4 %copy.36 = f32[16,132,1,64,16]{1,4,3,0,2:T(8,128)S(1)} copy(f32[16,132,1,64,16]{1,3,2,4,0:T(8,128)S(1)} %bitcast.122) | data formatting | bytes 17301504 | tf_op jit(solution)/shard_map/sub | solution.py:118
  606.5 23.1 %copy.37 = f32[16,132,1024]{1,0,2:T(8,128)} copy(f32[16,132,1024]{1,2,0:T(8,128)S(1)} %bitcast.120) | data formatting | bytes 17301504 | tf_op jit(solution)/shard_map/sub | solution.py:118
  629.6 10.1 %gather_fusion = f32[512,16,132]{2,1,0:T(8,128)} fusion(f32[16,132,1024]{1,0,2:T(8,128)} %copy.35, s32[1024]{0:T(1024)S(1)} %pad_clamp_fusion), kind=kCustom, calls=%fused_computation.clone | custom fusion | bytes 8652800 | tf_op jit(solution)/shard_map/jit(_take)/gather | solution.py:120
  639.7 10.1 %gather_fusion.1 = f32[512,16,132]{2,1,0:T(8,128)} fusion(f32[16,132,1024]{1,0,2:T(8,128)} %copy.37, s32[1024]{0:T(1024)S(1)} %pad_clamp_fusion), kind=kCustom, calls=%fused_computation.1.clone | custom fusion | bytes 8652800 | tf_op jit(solution)/shard_map/jit(_take)/gather | solution.py:123
  649.8 7.0 fusion.24
  656.8 2.7 pad_maximum_fusion.1
  659.5 2.5 fusion.25
  662.0 4.8 copy.38
  666.9 3.1 fusion.26
  669.9 74.9 %all-reduce.5 = bf16[64,2048]{1,0:T(8,128)(2,1)S(1)} all-reduce(f32[64,2048]{1,0:T(8,128)S(1)} %fusion.26), channel_id=1, replica_groups=mesh['grid'=8,'band'=16] {'grid','band'}, use_global_device_ids=true, to_apply=%region_2.4 | all-reduce | flops 131072 | bytes 786432 | tf_op jit(solution)/shard_map/psum | solution.py:131
  745.7 58.4 %reduce-scatter.4.cloned.1.call-done = bf16[16,64]{1,0:T(8,128)(2,1)} async-done(((bf16[256,64]{1,0:T(8,128)(2,1)}), bf16[16,64]{1,0:T(8,128)(2,1)}) %reduce-scatter.4.cloned.1.call-update) | async-done | bytes 2064
  (40 shorter events, 8.2 us)
Async XLA Ops:
  6.5 738.3 %copy-start = (bf16[1,128,256]{2,1,0:T(8,128)(2,1)S(1)}, bf16[1,128,256]{2,1,0:T(8,128)(2,1)}, u32[]{:S(2)}) copy-start(bf16[1,128,256]{2,1,0:T(8,128)(2,1)} %param.10) | copy-start | bytes 196612
  6.5 167.9 %all-reduce.4.cloned.1.call-start = ((), (), s32[]{:S(2)}) async-start(), calls=%async_computation.3 | async-start | bytes 8650752 | tf_op jit(solution)/shard_map/psum | solution.py:15
  174.5 9.7 %copy-start.1 = (bf16[2,32768]{1,0:T(2,128)(2,1)S(1)}, bf16[2,32768]{1,0:T(2,128)(2,1)}, u32[]{:S(2)}) copy-start(bf16[2,32768]{1,0:T(2,128)(2,1)} %get-tuple-element.9) | copy-start | bytes 393220
  325.9 27.7 %copy-start.2 = (s32[1,512]{1,0:T(1,128)S(1)}, s32[1,512]{1,0:T(1,128)}, u32[]{:S(2)}) copy-start(s32[1,512]{1,0:T(1,128)} %param.13) | copy-start | bytes 6148
  343.4 119.0 %all-to-all-start = ((bf16[1,1,132,128,256]{4,2,1,0,3:T(8,128)(2,1)}), bf16[1,1,132,128,256]{4,2,1,0,3:T(8,128)(2,1)}, u32[]{:S(2)}, u32[]{:S(2)}) async-start(bf16[1,1,132,128,256]{4,2,1,0,3:T(8,128)(2,1)} %copy.30), calls=%async_computation | async-start | bytes 17825792 | tf_op jit(solution)/shard_map/all_to_all | solution.py:108
  353.6 450.6 %reduce-scatter.4.cloned.1.call-start = ((), (), s32[]{:S(2)}) async-start(), calls=%async_computation.2 | async-start | bytes 69632
  547.4 38.7 %slice-start = ((s8[16777216]{0:T(1024)(128)(4,1)}), s8[4194304]{0:T(1024)(128)(4,1)S(1)}, s32[]{:S(2)}) async-start(s8[16777216]{0:T(1024)(128)(4,1)} %bitcast.121), calls=%async_computation.4 | async-start | bytes 8388608
  547.4 38.7 %slice-start.1 = ((s8[16777216]{0:T(1024)(128)(4,1)}), s8[4194304]{0:T(1024)(128)(4,1)S(1)}, s32[]{:S(2)}) async-start(s8[16777216]{0:T(1024)(128)(4,1)} %bitcast.121), calls=%async_computation.5 | async-start | bytes 8388608
  563.0 23.1 %slice-start.2 = ((s8[16777216]{0:T(1024)(128)(4,1)}), s8[4194304]{0:T(1024)(128)(4,1)S(1)}, s32[]{:S(2)}) async-start(s8[16777216]{0:T(1024)(128)(4,1)} %bitcast.121), calls=%async_computation.6 | async-start | bytes 8388608
  563.0 23.1 %slice-start.3 = ((s8[16777216]{0:T(1024)(128)(4,1)}), s8[4194304]{0:T(1024)(128)(4,1)S(1)}, s32[]{:S(2)}) async-start(s8[16777216]{0:T(1024)(128)(4,1)} %bitcast.121), calls=%async_computation.7 | async-start | bytes 8388608
Sparse Core Ops, SparseCore 0:
  15.3 159.1 all-reduce.3
  745.9 58.2 reduce-scatter.3
where the time goes:
time: 822 us; the launch traced here: 813 us
  waiting for transfers between devices  312 us (38%)
  local copies, waits for them, and re-layouts  190 us (23%)
  other arithmetic  110 us (13%)
  matrix products  101 us (12%)
  blocking collectives  74.9 us (9%)
  between operations  14.8 us (2%)
  starting transfers between devices  10.2 us (1%)
    psum x1, waiting for transfers between devices, spread(): return lax.psum(jnp.where(mine, value, jnp.zeros_like(value)), axis)  145 us
    all_to_all x1, waiting for transfers between devices, per_device(): lax.all_to_all(outgoing, ('grid', 'band'), split_axis=3, concat_axis=0, t...  109 us
    psum x1, blocking collectives, per_device(): slab_whole = lax.psum(partial_slab, ('grid', 'band'))  74.9 us
    unnamed x3, waiting for transfers between devices  58.5 us
    sub x2, local copies, waits for them, and re-layouts, per_device(): imag_part = with_cosine[:, :, 1] - with_sine[:, :, 0]  43.4 us
    add x2, local copies, waits for them, and re-layouts, per_device(): real_part = with_cosine[:, :, 0] + with_sine[:, :, 1]  38.7 us
    sub x1, other arithmetic, per_device(): imag_part = with_cosine[:, :, 1] - with_sine[:, :, 0]  34.3 us
    another operation x2, other arithmetic, y_section(): stacked = jnp.stack([real_part, imag_part], axis=3)  32.8 us
  transfers between devices with their start and end apart: 3, of which 3 were waited for; matrix products, arithmetic and copies ran while one was open for 2% of the time, Pallas kernels for 0%

commit v1 on v0

v1 whole, which is shorter than its diff:
```python
import functools
import math

import jax
import jax.numpy as jnp
import numpy as np
from jax import lax
from jax.experimental import pallas as pl
from jax.experimental.pallas import tpu as pltpu
from jax.sharding import PartitionSpec as P


N = 64
HALF = 32
ABLK = 64
GRID = 8
BAND = 16
XL = 8
SHARE = ABLK // BAND
PAIRS_Y = 32
F32 = jnp.float32
BF16 = jnp.bfloat16
VMEM_LIMIT = 56 * 1024 * 1024


@functools.cache
def tables():
    index = np.arange(N)
    phase = (index[:, None] * index[None, :]) % N
    angle = np.float32(2.0 * math.pi / N) * phase.astype(np.float32)
    cosine = np.cos(angle).astype(np.float32)
    sine = np.sin(angle).astype(np.float32)
    eye_x = np.eye(XL, dtype=np.float32)
    z_plain = np.concatenate([cosine[:HALF].T, -sine[:HALF].T], axis=1)
    z_turned = np.concatenate([z_plain[:, HALF:], -z_plain[:, :HALF]], axis=1)
    mz = np.zeros((SHARE, 2, N, 2, 2, SHARE, N), np.float32)
    for a in range(SHARE):
        for p in range(2):
            mz[a, p, :, 0, p, a, :] = z_plain
            mz[a, p, :, 1, p, a, :] = z_turned
    mzt = np.zeros((2, SHARE, N, SHARE, 2, N), np.float32)
    for a in range(SHARE):
        for p in range(2):
            mzt[p, a, :, a, p, :] = z_plain.T
    by_parity = np.stack([cosine, sine], axis=1).reshape(N, 2, PAIRS_Y, 2)
    ky = np.einsum("ktjp,xw->kxtpjw", by_parity, eye_x)
    signed = np.stack([cosine, -sine], axis=1).reshape(N, 2, PAIRS_Y, 2)
    kyt = np.einsum("ktjp,xw->pjxtkw", signed, eye_x)
    by_slab = np.stack([cosine, sine], axis=1).reshape(N, 2, GRID, XL)
    kx = np.einsum("ktgx,lm->kltgmx", by_slab, eye_x)
    signed_slab = np.stack([cosine, -sine], axis=1).reshape(N, 2, GRID, XL)
    kxt = np.einsum("ktgx,lm->gmxtkl", signed_slab, eye_x)
    turn = np.zeros((SHARE, 2, HALF, SHARE, 2, HALF), np.float32)
    for a in range(SHARE):
        turn[a, 1, :, a, 0, :] = np.eye(HALF)
        turn[a, 0, :, a, 1, :] = -np.eye(HALF)
    shapes = {
        "mz": (mz, 512, 1024),
        "mzt": (mzt, 512, 512),
        "ky": (ky, 512, 1024),
        "kyt": (kyt, 512, 1024),
        "kx": (kx, 512, 1024),
        "kxt": (kxt, 512, 1024),
        "turn": (turn, 256, 256),
    }
    return {n: v.reshape(r, c).astype(BF16) for n, (v, r, c) in shapes.items()}


def dot(a, b):
    return jnp.dot(a, b, preferred_element_type=F32)


def forward_body(u_ref, o_ref, mz_ref, ky_ref, out_ref):
    orbital = o_ref[...].astype(F32)
    columns = []
    for a in range(SHARE):
        density = u_ref[a].astype(F32) * orbital
        columns.append(
            jnp.concatenate([density[:, 128 * j : 128 * (j + 1)] for j in range(PAIRS_Y)], axis=0)
        )
    density = jnp.concatenate(columns, axis=1).astype(BF16)
    zfreq = dot(density, mz_ref[...]).astype(BF16)
    stacked = jnp.concatenate([zfreq[:, 256 * i : 256 * (i + 1)] for i in range(4)], axis=0)
    out_ref[...] = dot(ky_ref[...], stacked).astype(BF16)


def middle_body(y_ref, w_ref, turn_ref, kx_ref, kxt_ref, out_ref):
    turn = turn_ref[...]
    yfreq = y_ref[...]
    both = jnp.concatenate([yfreq, dot(yfreq, turn).astype(BF16)], axis=0)
    potential = (dot(kx_ref[...], both) * w_ref[...]).astype(BF16)
    both = jnp.concatenate([potential, dot(potential, turn).astype(BF16)], axis=0)
    out_ref[...] = dot(kxt_ref[...], both).astype(BF16)


def backward_body(h_ref, o_ref, turn_ref, kyt_ref, mzt_ref, out_ref):
    orbital = o_ref[...].astype(F32)
    freq = h_ref[...]
    both = jnp.concatenate([freq, dot(freq, turn_ref[...]).astype(BF16)], axis=0)
    zfreq = dot(kyt_ref[...], both).astype(BF16)
    zfreq = jnp.concatenate([zfreq[:256], zfreq[256:]], axis=1)
    value = dot(zfreq, mzt_ref[...])
    for a in range(SHARE):
        rows = [value[8 * j : 8 * (j + 1), 128 * a : 128 * (a + 1)] for j in range(PAIRS_Y)]
        out_ref[a] = (jnp.concatenate(rows, axis=1) * orbital).astype(BF16)


def whole_call(body, shape, dtype, *args):
    return pl.pallas_call(
        body,
        out_shape=jax.ShapeDtypeStruct(shape, dtype),
        in_specs=[pl.BlockSpec(memory_space=pltpu.VMEM)] * len(args),
        out_specs=pl.BlockSpec(memory_space=pltpu.VMEM),
        compiler_params=pltpu.CompilerParams(vmem_limit_bytes=VMEM_LIMIT),
    )(*args)


def slab_body(steps, pieces, *refs):
    place_ref, u_ref, amp_ref = refs[:3]
    w_refs = refs[3 : 3 + pieces]
    out_ref, total = refs[3 + pieces :]
    step = pl.program_id(0)

    @pl.when(step == 0)
    def _():
        total[...] = jnp.zeros_like(total)

    bands, _, lanes = u_ref.shape
    left = u_ref[...].reshape(bands * XL, lanes)
    right = jnp.concatenate([w[...].reshape(-1, lanes) for w in w_refs], axis=0)
    total[...] += lax.dot_general(left, right, (((1,), (1,)), ((), ())), preferred_element_type=F32)

    @pl.when(step == steps - 1)
    def _():
        gram = total[...]
        row = lax.broadcasted_iota(jnp.int32, gram.shape, 0) % XL
        col = lax.broadcasted_iota(jnp.int32, gram.shape, 1) % XL
        gram = jnp.where(row == col, gram, 0.0)
        gram = jnp.sum(gram.reshape(bands, XL, ABLK * XL), axis=1)
        halves = []
        for half in range(2):
            spot = place_ref[...] + ABLK * half
            lane = lax.broadcasted_iota(jnp.int32, (ABLK * XL, 128), 1)
            pick = (lane == spot).astype(F32)
            halves.append(jnp.dot(gram, pick, precision=lax.Precision.HIGHEST, preferred_element_type=F32))
        slab = jnp.concatenate(halves, axis=0)
        high = slab.astype(BF16)
        low = (slab - high.astype(F32)).astype(BF16)
        amp = amp_ref[...]
        out_ref[...] = (dot(amp, high) + dot(amp, low)).astype(BF16)


def slab_call(place, fields, amp, parts):
    bands = fields.shape[0]
    lanes = 512
    steps = N * N // lanes
    counts = [p.shape[0] for p in parts]
    return pl.pallas_call(
        functools.partial(slab_body, steps, len(parts)),
        out_shape=jax.ShapeDtypeStruct((1024, 128), BF16),
        grid=(steps,),
        in_specs=[
            pl.BlockSpec((ABLK * XL, 1), lambda s: (0, 0)),
            pl.BlockSpec((bands, XL, lanes), lambda s: (0, 0, s)),
            pl.BlockSpec((1024, 256), lambda s: (0, 0)),
        ]
        + [pl.BlockSpec((n, XL, lanes), lambda s: (0, 0, s)) for n in counts],
        out_specs=pl.BlockSpec((1024, 128), lambda s: (0, 0)),
        scratch_shapes=[pltpu.VMEM((bands * XL, ABLK * XL), F32)],
        compiler_params=pltpu.CompilerParams(vmem_limit_bytes=VMEM_LIMIT),
    )(place, fields, amp, *parts)


def band_shift(value, dy, dh, dc):
    pairs = []
    for y in range(4):
        for h in range(2):
            for c in range(2):
                pairs.append((4 * y + 2 * h + c, 4 * ((y + dy) % 4) + 2 * ((h + dh) % 2) + (c + dc) % 2))
    return lax.ppermute(value, "band", pairs)


def rows(value, start, count):
    return lax.dynamic_slice_in_dim(value, start, count, 0)


def signed_freq(index):
    return (index + N // 2) % N - N // 2


def per_device(virtual_field, occupied_field, amplitudes, ablock, pairs, kept_cells):
    const = {n: jnp.asarray(v) for n, v in tables().items()}
    band = lax.axis_index("band")
    grid = lax.axis_index("grid")
    my_y, my_h, my_c = band // 4, (band // 2) % 2, band % 2
    local_bands = virtual_field.shape[0]
    occ_local = occupied_field.shape[0]
    block_start = ablock[0] * ABLK
    owner = block_start // local_bands
    own_y, own_h, own_c = owner // 4, (owner // 2) % 2, owner % 2
    first = block_start % local_bands

    with jax.named_scope("block_scatter"):
        got = band_shift(rows(virtual_field, first + 32 * (1 - my_c), 32), 0, 0, 1)
        mine = rows(virtual_field, first + 32 * my_c, 32)
        mine = jnp.where(own_c == my_c, mine, got)
        cand = [rows(mine, 8 * my_y, 8)]
        for k in (1, 3, 2):
            cand.append(band_shift(rows(mine, 8 * ((my_y + k) % 4), 8), k, 0, 0))
        away = (my_y - own_y) % 4
        mine = jnp.where(
            away == 0, cand[0], jnp.where(away == 1, cand[1], jnp.where(away == 3, cand[2], cand[3]))
        )
        got = band_shift(rows(mine, 4 * (1 - my_h), 4), 0, 1, 0)
        mine = jnp.where(own_h == my_h, rows(mine, 4 * my_h, 4), got)

    with jax.named_scope("orbitals"):
        index = pairs[0]
        local = jnp.clip(index - band * occ_local, 0, occ_local - 1)
        chosen = jnp.concatenate([rows(occupied_field, local[k], 1) for k in range(2)], axis=0)
        chosen = chosen.reshape(2, XL, BAND, 256).transpose(2, 0, 1, 3)
        chosen = lax.all_to_all(chosen, "band", 0, 0, tiled=True)
        piece = [rows(chosen, index[k] // occ_local, 1)[0, k] for k in range(2)]
        kept = kept_cells[0]
        in_x = (kept[None, :] // 16 == jnp.arange(N, dtype=jnp.int32)[:, None]).astype(BF16)
        in_c = (kept[:, None] % 16 == jnp.arange(16, dtype=jnp.int32)[None, :]).astype(BF16)
        mask = dot(in_x, in_c).astype(BF16).reshape(XL, 128)
        mask = jnp.concatenate([mask, jnp.zeros_like(mask)], axis=1)
        piece = jnp.stack(piece + [mask])
        spread = lax.all_to_all(
            jnp.broadcast_to(piece[None], (BAND,) + piece.shape), "band", 0, 0, tiled=True
        )
        orbitals = spread[:, :2].transpose(1, 2, 0, 3).reshape(2, XL, N * N)
        masks = spread[:, 2, :, :128].reshape(BAND, N, 16).transpose(1, 0, 2).reshape(N * GRID, HALF)
        cell = jnp.arange(N * GRID, dtype=jnp.int32)[:, None]
        freq_x = signed_freq(cell // GRID)
        freq_y = signed_freq(grid * GRID + cell % GRID)
        freq_z = jnp.arange(HALF, dtype=jnp.int32)[None, :]
        squared = (freq_x**2 + freq_y**2 + freq_z**2).astype(F32)
        weights = masks.astype(F32) / (float(N * N * N) * (squared + 1.0))
        weights = jnp.tile(weights, (1, 2 * SHARE))

    with jax.named_scope("amplitudes"):
        amp = amplitudes[0].T.reshape(128, 256)
        amp = lax.all_gather(amp, "grid", axis=0, tiled=True)

    with jax.named_scope("transform"):
        freq = whole_call(forward_body, (512, 256), BF16, mine, orbitals[0], const["mz"], const["ky"])
        freq = lax.all_to_all(freq, "grid", 0, 0, tiled=True)
        freq = whole_call(
            middle_body, (512, 256), BF16, freq, weights, const["turn"], const["kx"], const["kxt"]
        )
        freq = lax.all_to_all(freq, "grid", 0, 0, tiled=True)
        potential = whole_call(
            backward_body,
            (SHARE, XL, N * N),
            BF16,
            freq,
            orbitals[1],
            const["turn"],
            const["kyt"],
            const["mzt"],
        )

    with jax.named_scope("block_gather"):
        near = [potential, band_shift(potential, 0, 1, 0)]
        parts = [(0, h, 0, v) for h, v in enumerate(near)]
        for h in range(2):
            for k in (1, 3, 2):
                parts.append((k, h, 0, band_shift(near[h], k, 0, 0)))
        parts += [(k, h, 1, band_shift(v, 0, 0, 1)) for k, h, _, v in parts]
        row = jnp.arange(SHARE * XL, dtype=jnp.int32) // XL
        place = jnp.concatenate(
            [32 * (my_c ^ c) + 8 * ((my_y - k) % 4) + 4 * (my_h ^ h) + row for k, h, c, _ in parts]
        )

    with jax.named_scope("slab_ladder"):
        terms = slab_call(place[:, None], virtual_field, amp, [v for *_, v in parts])
        terms = lax.all_to_all(
            terms.reshape(GRID * BAND, XL, 128), ("grid", "band"), 0, 0, tiled=True
        )
        ladder = jnp.sum(terms.astype(F32), axis=0)
        return ladder.reshape(1, 16, ABLK)


def solution(mesh):
    in_specs = (
        P("band", "grid", None),
        P("band", "grid", None),
        P(None, "band", "grid"),
        P(),
        P(),
        P(("grid", "band"), None),
    )
    out_specs = P(None, ("grid", "band"), None)
    return jax.shard_map(
        per_device, mesh=mesh, in_specs=in_specs, out_specs=out_specs, check_vma=False
    )
```

time: 822 us -> 187 us (0.23); the launches traced: 813 us -> 187 us
  waiting for transfers between devices: 312 us -> 30.7 us
  local copies, waits for them, and re-layouts: 190 us -> 13.7 us
  other arithmetic: 110 us -> 4.83 us
  matrix products: 101 us -> 0.3 us
  starting transfers between devices: 10.2 us -> 58.6 us
  blocking collectives: 74.9 us -> 46.4 us
  Pallas kernels: 0 us -> 22.8 us
    psum x1 -> x0, waiting for transfers between devices: 145 us -> none  [spread(): return lax.psum(jnp.where(mine, value, jnp.zeros_like(value)), axis)]
    dot_general x8 -> x1, matrix products: 101 us -> 0.3 us  [dot(): return jnp.dot(a, b, preferred_element_type=F32)]
    all_to_all x1 -> x4, waiting for transfers between devices: 109 us -> 10.1 us  [the longest x2 10.1 us: per_device(): freq = lax.all_to_all(freq, 'grid', 0, 0, tiled=True)]
    psum x1 -> x0, blocking collectives: 74.9 us -> none  [per_device(): slab_whole = lax.psum(partial_slab, ('grid', 'band'))]
    unnamed x3 -> x0, waiting for transfers between devices: 58.5 us -> none
    another operation x6 -> x1, other arithmetic: 45.1 us -> 0.01 us  [per_device(): piece = jnp.stack(piece + [mask])]
    sub x2 -> x0, local copies, waits for them, and re-layouts: 43.4 us -> none  [per_device(): imag_part = with_cosine[:, :, 1] - with_sine[:, :, 0]]
    convert_element_type x5, local copies, waits for them, and re-layouts: 40.5 us -> 0.82 us  [the longest x4 0.72 us: per_device(): weights = masks.astype(F32) / (float(N * N * N) * (squared + 1.0))]
  transfers between devices with their start and end apart: 3 -> 24, of which waited for: 3 -> 5; matrix products, arithmetic and copies ran while one was open for 2% -> 7% of each run, Pallas kernels for 0% -> 0%
where the time goes in v1:
time: 187 us
  starting transfers between devices  58.6 us (31%)
  blocking collectives  46.4 us (25%)
  waiting for transfers between devices  30.7 us (16%)
  Pallas kernels  22.8 us (12%)
  local copies, waits for them, and re-layouts  13.7 us (7%)
  between operations  9.88 us (5%)
  other arithmetic  4.83 us (3%)
    ppermute x20, starting transfers between devices, band_shift(): return lax.ppermute(value, 'band', pairs)  37 us
    all_gather x1, blocking collectives, per_device(): amp = lax.all_gather(amp, 'grid', axis=0, tiled=True)  25.4 us
    all_to_all x1, blocking collectives, per_device(): lax.all_to_all(terms.reshape(GRID * BAND, XL, 128), ('grid', 'band'), 0,...  21.1 us
    ppermute x20, waiting for transfers between devices, band_shift(): return lax.ppermute(value, 'band', pairs)  20.6 us
    pallas_call x1, Pallas kernels, slab_call(): pl.pallas_call(functools.partial(slab_body, steps, len(parts)), out_shape...  12.5 us
    pallas_call x3, Pallas kernels, whole_call(): pl.pallas_call(body, out_shape=jax.ShapeDtypeStruct(shape, dtype), in_spe...  10.3 us
    all_to_all x2, waiting for transfers between devices, per_device(): freq = lax.all_to_all(freq, 'grid', 0, 0, tiled=True)  10.1 us
    all_to_all x2, starting transfers between devices, per_device(): freq = lax.all_to_all(freq, 'grid', 0, 0, tiled=True)  8.47 us
  transfers between devices with their start and end apart: 24, of which 5 were waited for; matrix products, arithmetic and copies ran while one was open for 7% of the time, Pallas kernels for 0%

profile of v1, /device:TPU:1, one launch (start us, length us, event | category | flops | bytes accessed | tf_op | source)
XLA Modules:
  0.0 187.3 jit_solution(4006297514649269322)
XLA Ops:
  0.7 1.7 constant_dynamic-slice_fusion.6
  2.5 1.5 collective-permute-start
  9.8 7.1 %all-to-all-start = ((bf16[16,2,8,256]{3,2,1,0:T(8,128)(2,1)}), bf16[16,2,8,256]{3,2,1,0:T(8,128)(2,1)S(1)}, u32[]{:S(2)}, u32[]{:S(2)}) async-start(bf16[16,2,8,256]{3,2,1,0:T(8,128)(2,1)} %copy.49), calls=%async_computation | async-start | bytes 262144 | tf_op jit(solution)/shard_map/orbitals/all_to_all | solution.py:222
  17.9 2.5 %dynamic-slice_select_fusion = bf16[32,8,4096]{2,1,0:T(8,128)(2,1)S(1)} fusion(bf16[32,8,4096]{2,1,0:T(8,128)(2,1)} %collective-permute-done, bf16[128,8,4096]{2,1,0:T(8,128)(2,1)} %refs_1_.1, s32[]{:T(128)S(6)} %select_n.280, pred[]{:T(512)S(6)} %eq.76), kind=kLoop, calls=%fused_computation | loop fusion | flops 1048576 | bytes 6291461 | tf_op jit(solution)/shard_map/block_scatter/jit(_where)/select_n | solution.py:206
  20.3 1.0 constant_dynamic-slice_fusion.3
  21.3 1.4 collective-permute-start.1
  22.7 1.3 collective-permute-start.2
  24.0 1.7 collective-permute-start.3
  31.8 6.0 %all-to-all-start.1 = ((bf16[16,3,8,256]{3,2,1,0:T(8,128)(2,1)}), bf16[16,3,8,256]{3,2,1,0:T(8,128)(2,1)S(1)}, u32[]{:S(2)}, u32[]{:S(2)}) async-start(bf16[16,3,8,256]{3,2,1,0:T(8,128)(2,1)} %broadcast_in_dim.5), calls=%async_computation.1 | async-start | bytes 393216 | tf_op jit(solution)/shard_map/orbitals/all_to_all | solution.py:230
  37.9 12.1 %collective-permute-done.3 = bf16[8,8,4096]{2,1,0:T(8,128)(2,1)} collective-permute-done((bf16[8,8,4096]{2,1,0:T(8,128)(2,1)S(1)}, bf16[8,8,4096]{2,1,0:T(8,128)(2,1)}, u32[]{:S(2)}, u32[]{:S(2)}) %collective-permute-start.3) | collective-permute-done | bytes 524320 | tf_op jit(solution)/shard_map/block_scatter/ppermute | solution.py:180
  50.0 1.3 select_select_fusion
  51.3 2.8 %collective-permute-start.4 = (bf16[4,8,4096]{2,1,0:T(8,128)(2,1)S(1)}, bf16[4,8,4096]{2,1,0:T(8,128)(2,1)S(1)}, u32[]{:S(2)}, u32[]{:S(2)}) collective-permute-start(bf16[4,8,4096]{2,1,0:T(8,128)(2,1)S(1)} %constant_dynamic-slice_fusion.2), channel_id=1, source_target_pairs={{0,2},{1,3},{2,0},{3,1},{4,6},{5,7},{6,4},{7,5},{8,10},{9,11},{10,... | collective-permute-start | bytes 786440 | tf_op jit(solution)/shard_map/block_scatter/ppermute | solution.py:180
  54.8 5.2 %collective-permute-done.4 = bf16[4,8,4096]{2,1,0:T(8,128)(2,1)S(1)} collective-permute-done((bf16[4,8,4096]{2,1,0:T(8,128)(2,1)S(1)}, bf16[4,8,4096]{2,1,0:T(8,128)(2,1)S(1)}, u32[]{:S(2)}, u32[]{:S(2)}) %collective-permute-start.4) | collective-permute-done | bytes 262176 | tf_op jit(solution)/shard_map/block_scatter/ppermute | solution.py:180
  60.7 3.2 %transform.3 = bf16[512,256]{1,0:T(8,128)(2,1)} custom-call(bf16[4,8,4096]{2,1,0:T(8,128)(2,1)} %dynamic-slice_select_fusion.1.u_ref, bf16[8,4096]{1,0:T(8,128)(2,1)} %bitcast.49, bf16[512,1024]{1,0:T(8,128)(2,1)} %constant.275.clone.mz_ref, bf16[512,1024]{1,0:T(8,128)(2,1)} %constant.277.clone.ky_ref), custom_call_target="tpu_custom_call" | custom-call | tf_op jit(solution)/shard_map/transform/pallas_call | solution.py:109
  63.9 5.1 %all-to-all-start.2 = ((bf16[8,64,256]{2,1,0:T(8,128)(2,1)}), bf16[8,64,256]{2,1,0:T(8,128)(2,1)S(1)}, u32[]{:S(2)}, u32[]{:S(2)}) async-start(bf16[8,64,256]{2,1,0:T(8,128)(2,1)} %bitcast.44), calls=%async_computation.2 | async-start | bytes 524288 | tf_op jit(solution)/shard_map/transform/all_to_all | solution.py:249
  69.9 1.0 copy.53.w_ref
  70.9 4.1 %all-to-all-done.2 = bf16[8,64,256]{2,1,0:T(8,128)(2,1)S(1)} async-done(((bf16[8,64,256]{2,1,0:T(8,128)(2,1)}), bf16[8,64,256]{2,1,0:T(8,128)(2,1)S(1)}, u32[]{:S(2)}, u32[]{:S(2)}) %all-to-all-start.2) | async-done | bytes 262176 | tf_op jit(solution)/shard_map/transform/all_to_all | solution.py:249
  75.7 4.0 %transform.4 = bf16[512,256]{1,0:T(8,128)(2,1)} custom-call(bf16[512,256]{1,0:T(8,128)(2,1)} %bitcast.43, f32[512,256]{1,0:T(8,128)} %copy.53.w_ref, bf16[256,256]{1,0:T(8,128)(2,1)} %constant.281.clone.turn_ref, bf16[512,1024]{1,0:T(8,128)(2,1)} %constant.279.clone.kx_ref, bf16[512,1024]{1,0:T(8,128)(2,1)} %constant.280.clone.kxt_ref), custom_call_target="tpu_custom_call" | custom-call | tf_op jit(solution)/shard_map/transform/pallas_call | solution.py:109
  79.7 3.4 %all-to-all-start.3 = ((bf16[8,64,256]{2,1,0:T(8,128)(2,1)}), bf16[8,64,256]{2,1,0:T(8,128)(2,1)S(1)}, u32[]{:S(2)}, u32[]{:S(2)}) async-start(bf16[8,64,256]{2,1,0:T(8,128)(2,1)} %bitcast.42), calls=%async_computation.3 | async-start | bytes 524288 | tf_op jit(solution)/shard_map/transform/all_to_all | solution.py:253
  83.2 5.9 %all-to-all-done.3 = bf16[8,64,256]{2,1,0:T(8,128)(2,1)S(1)} async-done(((bf16[8,64,256]{2,1,0:T(8,128)(2,1)}), bf16[8,64,256]{2,1,0:T(8,128)(2,1)S(1)}, u32[]{:S(2)}, u32[]{:S(2)}) %all-to-all-start.3) | async-done | bytes 262176 | tf_op jit(solution)/shard_map/transform/all_to_all | solution.py:253
  89.9 3.1 %transform.5.refs_3_ = bf16[4,8,4096]{2,1,0:T(8,128)(2,1)} custom-call(bf16[512,256]{1,0:T(8,128)(2,1)} %bitcast.41, bf16[8,4096]{1,0:T(8,128)(2,1)} %bitcast.48, bf16[256,256]{1,0:T(8,128)(2,1)} %constant.281.clone.turn_ref, bf16[512,1024]{1,0:T(8,128)(2,1)} %constant.278.clone.kyt_ref, bf16[512,512]{1,0:T(8,128)(2,1)} %constant.276.clone.mzt_ref), custom_call_target="tpu_custom_call" | custom-call | tf_op jit(solution)/shard_map/transform/pallas_call | solution.py:109
  93.0 3.3 %collective-permute-start.5 = (bf16[4,8,4096]{2,1,0:T(8,128)(2,1)}, bf16[4,8,4096]{2,1,0:T(8,128)(2,1)S(1)}, u32[]{:S(2)}, u32[]{:S(2)}) collective-permute-start(bf16[4,8,4096]{2,1,0:T(8,128)(2,1)} %transform.5.refs_3_), channel_id=1, source_target_pairs={{0,2},{1,3},{2,0},{3,1},{4,6},{5,7},{6,4},{7,5},{8,10},{9,11},{10,... | collective-permute-start | bytes 786440 | tf_op jit(solution)/shard_map/block_gather/ppermute | solution.py:180
  96.3 2.7 %collective-permute-start.7 = (bf16[4,8,4096]{2,1,0:T(8,128)(2,1)}, bf16[4,8,4096]{2,1,0:T(8,128)(2,1)S(1)}, u32[]{:S(2)}, u32[]{:S(2)}) collective-permute-start(bf16[4,8,4096]{2,1,0:T(8,128)(2,1)} %transform.5.refs_3_), channel_id=1, source_target_pairs={{0,12},{1,13},{2,14},{3,15},{4,0},{5,1},{6,2},{7,3},{8,4},{9,5},{1... | collective-permute-start | bytes 786440 | tf_op jit(solution)/shard_map/block_gather/ppermute | solution.py:180
  99.0 5.1 %collective-permute-start.12 = (bf16[4,8,4096]{2,1,0:T(8,128)(2,1)}, bf16[4,8,4096]{2,1,0:T(8,128)(2,1)S(1)}, u32[]{:S(2)}, u32[]{:S(2)}) collective-permute-start(bf16[4,8,4096]{2,1,0:T(8,128)(2,1)} %transform.5.refs_3_), channel_id=1, source_target_pairs={{0,1},{1,0},{2,3},{3,2},{4,5},{5,4},{6,7},{7,6},{8,9},{9,8},{10,11... | collective-permute-start | bytes 786440 | tf_op jit(solution)/shard_map/block_gather/ppermute | solution.py:180
  104.8 2.0 %collective-permute-start.10 = (bf16[4,8,4096]{2,1,0:T(8,128)(2,1)S(1)}, bf16[4,8,4096]{2,1,0:T(8,128)(2,1)S(1)}, u32[]{:S(2)}, u32[]{:S(2)}) collective-permute-start(bf16[4,8,4096]{2,1,0:T(8,128)(2,1)S(1)} %collective-permute-done.5.refs_4_), channel_id=1, source_target_pairs={{0,12},{1,13},{2,14},{3,15},{4,0},{5,1},{6,2},{7,3},{8,4},{9,5},{1... | collective-permute-start | bytes 786440 | tf_op jit(solution)/shard_map/block_gather/ppermute | solution.py:180
  106.8 2.0 %collective-permute-start.11 = (bf16[4,8,4096]{2,1,0:T(8,128)(2,1)S(1)}, bf16[4,8,4096]{2,1,0:T(8,128)(2,1)S(1)}, u32[]{:S(2)}, u32[]{:S(2)}) collective-permute-start(bf16[4,8,4096]{2,1,0:T(8,128)(2,1)S(1)} %collective-permute-done.5.refs_4_), channel_id=1, source_target_pairs={{0,8},{1,9},{2,10},{3,11},{4,12},{5,13},{6,14},{7,15},{8,0},{9,1},... | collective-permute-start | bytes 786440 | tf_op jit(solution)/shard_map/block_gather/ppermute | solution.py:180
  108.9 6.5 %collective-permute-start.13 = (bf16[4,8,4096]{2,1,0:T(8,128)(2,1)S(1)}, bf16[4,8,4096]{2,1,0:T(8,128)(2,1)S(1)}, u32[]{:S(2)}, u32[]{:S(2)}) collective-permute-start(bf16[4,8,4096]{2,1,0:T(8,128)(2,1)S(1)} %collective-permute-done.5.refs_4_), channel_id=1, source_target_pairs={{0,1},{1,0},{2,3},{3,2},{4,5},{5,4},{6,7},{7,6},{8,9},{9,8},{10,11... | collective-permute-start | bytes 786440 | tf_op jit(solution)/shard_map/block_gather/ppermute | solution.py:180
  115.5 3.3 %collective-permute-done.9.refs_8_ = bf16[4,8,4096]{2,1,0:T(8,128)(2,1)S(1)} collective-permute-done((bf16[4,8,4096]{2,1,0:T(8,128)(2,1)S(1)}, bf16[4,8,4096]{2,1,0:T(8,128)(2,1)S(1)}, u32[]{:S(2)}, u32[]{:S(2)}) %collective-permute-start.9) | collective-permute-done | bytes 262176 | tf_op jit(solution)/shard_map/block_gather/ppermute | solution.py:180
  118.8 4.9 %collective-permute-start.15 = (bf16[4,8,4096]{2,1,0:T(8,128)(2,1)S(1)}, bf16[4,8,4096]{2,1,0:T(8,128)(2,1)S(1)}, u32[]{:S(2)}, u32[]{:S(2)}) collective-permute-start(bf16[4,8,4096]{2,1,0:T(8,128)(2,1)S(1)} %collective-permute-done.7.refs_6_), channel_id=1, source_target_pairs={{0,1},{1,0},{2,3},{3,2},{4,5},{5,4},{6,7},{7,6},{8,9},{9,8},{10,11... | collective-permute-start | bytes 786440 | tf_op jit(solution)/shard_map/block_gather/ppermute | solution.py:180
  126.6 25.4 %all_gather.3.refs_2_ = bf16[1024,256]{1,0:T(8,128)(2,1)} all-gather(bf16[128,256]{1,0:T(8,128)(2,1)S(1)} %reshape.217), channel_id=1, replica_groups=mesh['grid'=8,'band'=16] {'grid'}, dimensions={0}, use_global_device_ids=true | all-gather | bytes 589824 | tf_op jit(solution)/shard_map/amplitudes/all_gather | solution.py:245
  152.9 12.5 %slab_ladder.1 = bf16[1024,128]{1,0:T(8,128)(2,1)} custom-call(s32[512,1]{1,0:T(8,128)} %copy.54.refs_0_, bf16[128,8,4096]{2,1,0:T(8,128)(2,1)} %refs_1_.1, bf16[1024,256]{1,0:T(8,128)(2,1)} %all_gather.3.refs_2_, bf16[4,8,4096]{2,1,0:T(8,128)(2,1)} %transform.5.refs_3_, bf16[4,8,4096]{2,1,0:T(8,128)(2,1)} %copy-done.2, bf16[4,8,4096]{2,1,0:T(8,128)(2,1)} %copy-done.3, ...), custom_call_target="tpu_custom_call" | custom-call | tf_op jit(solution)/shard_map/slab_ladder/pallas_call | solution.py:158
  165.4 21.1 %all_to_all.37 = bf16[128,8,128]{2,1,0:T(8,128)(2,1)S(1)} all-to-all(bf16[128,8,128]{2,1,0:T(8,128)(2,1)} %bitcast.45), channel_id=1, replica_groups=mesh['grid'=8,'band'=16] {'grid','band'}, dimensions={0} | all-to-all | bytes 524288 | tf_op jit(solution)/shard_map/slab_ladder/all_to_all | solution.py:279
  (104 shorter events, 13.2 us)
Async XLA Ops:
  2.5 15.4 %collective-permute-start = (bf16[32,8,4096]{2,1,0:T(8,128)(2,1)S(1)}, bf16[32,8,4096]{2,1,0:T(8,128)(2,1)}, u32[]{:S(2)}, u32[]{:S(2)}) collective-permute-start(bf16[32,8,4096]{2,1,0:T(8,128)(2,1)S(1)} %constant_dynamic-slice_fusion.6), channel_id=1, source_target_pairs={{0,1},{1,0},{2,3},{3,2},{4,5},{5,4},{6,7},{7,6},{8,9},{9,8},{10,11... | collective-permute-start | bytes 6291464 | tf_op jit(solution)/shard_map/block_scatter/ppermute | solution.py:180
  9.8 21.3 %all-to-all-start = ((bf16[16,2,8,256]{3,2,1,0:T(8,128)(2,1)}), bf16[16,2,8,256]{3,2,1,0:T(8,128)(2,1)S(1)}, u32[]{:S(2)}, u32[]{:S(2)}) async-start(bf16[16,2,8,256]{3,2,1,0:T(8,128)(2,1)} %copy.49), calls=%async_computation | async-start | bytes 262144 | tf_op jit(solution)/shard_map/orbitals/all_to_all | solution.py:222
  21.3 16.6 %collective-permute-start.1 = (bf16[8,8,4096]{2,1,0:T(8,128)(2,1)}, bf16[8,8,4096]{2,1,0:T(8,128)(2,1)}, u32[]{:S(2)}, u32[]{:S(2)}) collective-permute-start(bf16[8,8,4096]{2,1,0:T(8,128)(2,1)} %get-tuple-element.7), channel_id=1, source_target_pairs={{0,4},{1,5},{2,6},{3,7},{4,8},{5,9},{6,10},{7,11},{8,12},{9,13},{1... | collective-permute-start | bytes 1572872 | tf_op jit(solution)/shard_map/block_scatter/ppermute | solution.py:180
  22.7 15.2 %collective-permute-start.2 = (bf16[8,8,4096]{2,1,0:T(8,128)(2,1)S(1)}, bf16[8,8,4096]{2,1,0:T(8,128)(2,1)}, u32[]{:S(2)}, u32[]{:S(2)}) collective-permute-start(bf16[8,8,4096]{2,1,0:T(8,128)(2,1)S(1)} %get-tuple-element.6), channel_id=1, source_target_pairs={{0,12},{1,13},{2,14},{3,15},{4,0},{5,1},{6,2},{7,3},{8,4},{9,5},{1... | collective-permute-start | bytes 1572872 | tf_op jit(solution)/shard_map/block_scatter/ppermute | solution.py:180
  24.0 26.0 %collective-permute-start.3 = (bf16[8,8,4096]{2,1,0:T(8,128)(2,1)S(1)}, bf16[8,8,4096]{2,1,0:T(8,128)(2,1)}, u32[]{:S(2)}, u32[]{:S(2)}) collective-permute-start(bf16[8,8,4096]{2,1,0:T(8,128)(2,1)S(1)} %get-tuple-element.5), channel_id=1, source_target_pairs={{0,8},{1,9},{2,10},{3,11},{4,12},{5,13},{6,14},{7,15},{8,0},{9,1},... | collective-permute-start | bytes 1572872 | tf_op jit(solution)/shard_map/block_scatter/ppermute | solution.py:180
  31.8 22.3 %all-to-all-start.1 = ((bf16[16,3,8,256]{3,2,1,0:T(8,128)(2,1)}), bf16[16,3,8,256]{3,2,1,0:T(8,128)(2,1)S(1)}, u32[]{:S(2)}, u32[]{:S(2)}) async-start(bf16[16,3,8,256]{3,2,1,0:T(8,128)(2,1)} %broadcast_in_dim.5), calls=%async_computation.1 | async-start | bytes 393216 | tf_op jit(solution)/shard_map/orbitals/all_to_all | solution.py:230
  51.3 8.6 %collective-permute-start.4 = (bf16[4,8,4096]{2,1,0:T(8,128)(2,1)S(1)}, bf16[4,8,4096]{2,1,0:T(8,128)(2,1)S(1)}, u32[]{:S(2)}, u32[]{:S(2)}) collective-permute-start(bf16[4,8,4096]{2,1,0:T(8,128)(2,1)S(1)} %constant_dynamic-slice_fusion.2), channel_id=1, source_target_pairs={{0,2},{1,3},{2,0},{3,1},{4,6},{5,7},{6,4},{7,5},{8,10},{9,11},{10,... | collective-permute-start | bytes 786440 | tf_op jit(solution)/shard_map/block_scatter/ppermute | solution.py:180
  63.9 11.1 %all-to-all-start.2 = ((bf16[8,64,256]{2,1,0:T(8,128)(2,1)}), bf16[8,64,256]{2,1,0:T(8,128)(2,1)S(1)}, u32[]{:S(2)}, u32[]{:S(2)}) async-start(bf16[8,64,256]{2,1,0:T(8,128)(2,1)} %bitcast.44), calls=%async_computation.2 | async-start | bytes 524288 | tf_op jit(solution)/shard_map/transform/all_to_all | solution.py:249
  79.7 9.4 %all-to-all-start.3 = ((bf16[8,64,256]{2,1,0:T(8,128)(2,1)}), bf16[8,64,256]{2,1,0:T(8,128)(2,1)S(1)}, u32[]{:S(2)}, u32[]{:S(2)}) async-start(bf16[8,64,256]{2,1,0:T(8,128)(2,1)} %bitcast.42), calls=%async_computation.3 | async-start | bytes 524288 | tf_op jit(solution)/shard_map/transform/all_to_all | solution.py:253
  93.0 11.1 %collective-permute-start.5 = (bf16[4,8,4096]{2,1,0:T(8,128)(2,1)}, bf16[4,8,4096]{2,1,0:T(8,128)(2,1)S(1)}, u32[]{:S(2)}, u32[]{:S(2)}) collective-permute-start(bf16[4,8,4096]{2,1,0:T(8,128)(2,1)} %transform.5.refs_3_), channel_id=1, source_target_pairs={{0,2},{1,3},{2,0},{3,1},{4,6},{5,7},{6,4},{7,5},{8,10},{9,11},{10,... | collective-permute-start | bytes 786440 | tf_op jit(solution)/shard_map/block_gather/ppermute | solution.py:180
  96.3 8.5 %collective-permute-start.6 = (bf16[4,8,4096]{2,1,0:T(8,128)(2,1)}, bf16[4,8,4096]{2,1,0:T(8,128)(2,1)S(1)}, u32[]{:S(2)}, u32[]{:S(2)}) collective-permute-start(bf16[4,8,4096]{2,1,0:T(8,128)(2,1)} %transform.5.refs_3_), channel_id=1, source_target_pairs={{0,4},{1,5},{2,6},{3,7},{4,8},{5,9},{6,10},{7,11},{8,12},{9,13},{1... | collective-permute-start | bytes 786440 | tf_op jit(solution)/shard_map/block_gather/ppermute | solution.py:180
  96.3 10.6 %collective-permute-start.7 = (bf16[4,8,4096]{2,1,0:T(8,128)(2,1)}, bf16[4,8,4096]{2,1,0:T(8,128)(2,1)S(1)}, u32[]{:S(2)}, u32[]{:S(2)}) collective-permute-start(bf16[4,8,4096]{2,1,0:T(8,128)(2,1)} %transform.5.refs_3_), channel_id=1, source_target_pairs={{0,12},{1,13},{2,14},{3,15},{4,0},{5,1},{6,2},{7,3},{8,4},{9,5},{1... | collective-permute-start | bytes 786440 | tf_op jit(solution)/shard_map/block_gather/ppermute | solution.py:180
  99.0 9.9 %collective-permute-start.8 = (bf16[4,8,4096]{2,1,0:T(8,128)(2,1)}, bf16[4,8,4096]{2,1,0:T(8,128)(2,1)S(1)}, u32[]{:S(2)}, u32[]{:S(2)}) collective-permute-start(bf16[4,8,4096]{2,1,0:T(8,128)(2,1)} %transform.5.refs_3_), channel_id=1, source_target_pairs={{0,8},{1,9},{2,10},{3,11},{4,12},{5,13},{6,14},{7,15},{8,0},{9,1},... | collective-permute-start | bytes 786440 | tf_op jit(solution)/shard_map/block_gather/ppermute | solution.py:180
  99.0 16.4 %collective-permute-start.12 = (bf16[4,8,4096]{2,1,0:T(8,128)(2,1)}, bf16[4,8,4096]{2,1,0:T(8,128)(2,1)S(1)}, u32[]{:S(2)}, u32[]{:S(2)}) collective-permute-start(bf16[4,8,4096]{2,1,0:T(8,128)(2,1)} %transform.5.refs_3_), channel_id=1, source_target_pairs={{0,1},{1,0},{2,3},{3,2},{4,5},{5,4},{6,7},{7,6},{8,9},{9,8},{10,11... | collective-permute-start | bytes 786440 | tf_op jit(solution)/shard_map/block_gather/ppermute | solution.py:180
  104.1 48.0 %copy-start.2 = (bf16[4,8,4096]{2,1,0:T(8,128)(2,1)}, bf16[4,8,4096]{2,1,0:T(8,128)(2,1)S(1)}, u32[]{:S(2)}) copy-start(bf16[4,8,4096]{2,1,0:T(8,128)(2,1)S(1)} %collective-permute-done.5.refs_4_) | copy-start | bytes 786436
  104.1 14.7 %collective-permute-start.9 = (bf16[4,8,4096]{2,1,0:T(8,128)(2,1)S(1)}, bf16[4,8,4096]{2,1,0:T(8,128)(2,1)S(1)}, u32[]{:S(2)}, u32[]{:S(2)}) collective-permute-start(bf16[4,8,4096]{2,1,0:T(8,128)(2,1)S(1)} %collective-permute-done.5.refs_4_), channel_id=1, source_target_pairs={{0,4},{1,5},{2,6},{3,7},{4,8},{5,9},{6,10},{7,11},{8,12},{9,13},{1... | collective-permute-start | bytes 786440 | tf_op jit(solution)/shard_map/block_gather/ppermute | solution.py:180
  104.8 47.3 %copy-start.3 = (bf16[4,8,4096]{2,1,0:T(8,128)(2,1)}, bf16[4,8,4096]{2,1,0:T(8,128)(2,1)S(1)}, u32[]{:S(2)}) copy-start(bf16[4,8,4096]{2,1,0:T(8,128)(2,1)S(1)} %collective-permute-done.6.refs_5_) | copy-start | bytes 786436
  104.8 18.8 %collective-permute-start.10 = (bf16[4,8,4096]{2,1,0:T(8,128)(2,1)S(1)}, bf16[4,8,4096]{2,1,0:T(8,128)(2,1)S(1)}, u32[]{:S(2)}, u32[]{:S(2)}) collective-permute-start(bf16[4,8,4096]{2,1,0:T(8,128)(2,1)S(1)} %collective-permute-done.5.refs_4_), channel_id=1, source_target_pairs={{0,12},{1,13},{2,14},{3,15},{4,0},{5,1},{6,2},{7,3},{8,4},{9,5},{1... | collective-permute-start | bytes 786440 | tf_op jit(solution)/shard_map/block_gather/ppermute | solution.py:180
  106.8 45.2 %copy-start.4 = (bf16[4,8,4096]{2,1,0:T(8,128)(2,1)}, bf16[4,8,4096]{2,1,0:T(8,128)(2,1)S(1)}, u32[]{:S(2)}) copy-start(bf16[4,8,4096]{2,1,0:T(8,128)(2,1)S(1)} %collective-permute-done.7.refs_6_) | copy-start | bytes 786436
  106.8 16.9 %collective-permute-start.11 = (bf16[4,8,4096]{2,1,0:T(8,128)(2,1)S(1)}, bf16[4,8,4096]{2,1,0:T(8,128)(2,1)S(1)}, u32[]{:S(2)}, u32[]{:S(2)}) collective-permute-start(bf16[4,8,4096]{2,1,0:T(8,128)(2,1)S(1)} %collective-permute-done.5.refs_4_), channel_id=1, source_target_pairs={{0,8},{1,9},{2,10},{3,11},{4,12},{5,13},{6,14},{7,15},{8,0},{9,1},... | collective-permute-start | bytes 786440 | tf_op jit(solution)/shard_map/block_gather/ppermute | solution.py:180
  108.9 43.2 %copy-start.5 = (bf16[4,8,4096]{2,1,0:T(8,128)(2,1)}, bf16[4,8,4096]{2,1,0:T(8,128)(2,1)S(1)}, u32[]{:S(2)}) copy-start(bf16[4,8,4096]{2,1,0:T(8,128)(2,1)S(1)} %collective-permute-done.8.refs_7_) | copy-start | bytes 786436
  108.9 15.3 %collective-permute-start.13 = (bf16[4,8,4096]{2,1,0:T(8,128)(2,1)S(1)}, bf16[4,8,4096]{2,1,0:T(8,128)(2,1)S(1)}, u32[]{:S(2)}, u32[]{:S(2)}) collective-permute-start(bf16[4,8,4096]{2,1,0:T(8,128)(2,1)S(1)} %collective-permute-done.5.refs_4_), channel_id=1, source_target_pairs={{0,1},{1,0},{2,3},{3,2},{4,5},{5,4},{6,7},{7,6},{8,9},{9,8},{10,11... | collective-permute-start | bytes 786440 | tf_op jit(solution)/shard_map/block_gather/ppermute | solution.py:180
  115.4 36.7 %copy-start.6 = (bf16[4,8,4096]{2,1,0:T(8,128)(2,1)}, bf16[4,8,4096]{2,1,0:T(8,128)(2,1)S(1)}, u32[]{:S(2)}) copy-start(bf16[4,8,4096]{2,1,0:T(8,128)(2,1)S(1)} %collective-permute-done.12.refs_11_) | copy-start | bytes 786436
  115.4 8.9 %collective-permute-start.14 = (bf16[4,8,4096]{2,1,0:T(8,128)(2,1)S(1)}, bf16[4,8,4096]{2,1,0:T(8,128)(2,1)S(1)}, u32[]{:S(2)}, u32[]{:S(2)}) collective-permute-start(bf16[4,8,4096]{2,1,0:T(8,128)(2,1)S(1)} %collective-permute-done.6.refs_5_), channel_id=1, source_target_pairs={{0,1},{1,0},{2,3},{3,2},{4,5},{5,4},{6,7},{7,6},{8,9},{9,8},{10,11... | collective-permute-start | bytes 786440 | tf_op jit(solution)/shard_map/block_gather/ppermute | solution.py:180
  118.8 33.3 %copy-start.7 = (bf16[4,8,4096]{2,1,0:T(8,128)(2,1)}, bf16[4,8,4096]{2,1,0:T(8,128)(2,1)S(1)}, u32[]{:S(2)}) copy-start(bf16[4,8,4096]{2,1,0:T(8,128)(2,1)S(1)} %collective-permute-done.9.refs_8_) | copy-start | bytes 786436
  118.8 33.2 %collective-permute-start.15 = (bf16[4,8,4096]{2,1,0:T(8,128)(2,1)S(1)}, bf16[4,8,4096]{2,1,0:T(8,128)(2,1)S(1)}, u32[]{:S(2)}, u32[]{:S(2)}) collective-permute-start(bf16[4,8,4096]{2,1,0:T(8,128)(2,1)S(1)} %collective-permute-done.7.refs_6_), channel_id=1, source_target_pairs={{0,1},{1,0},{2,3},{3,2},{4,5},{5,4},{6,7},{7,6},{8,9},{9,8},{10,11... | collective-permute-start | bytes 786440 | tf_op jit(solution)/shard_map/block_gather/ppermute | solution.py:180
  123.7 28.5 %copy-start.8 = (bf16[4,8,4096]{2,1,0:T(8,128)(2,1)}, bf16[4,8,4096]{2,1,0:T(8,128)(2,1)S(1)}, u32[]{:S(2)}) copy-start(bf16[4,8,4096]{2,1,0:T(8,128)(2,1)S(1)} %collective-permute-done.10.refs_9_) | copy-start | bytes 786436
  123.7 28.3 %collective-permute-start.16 = (bf16[4,8,4096]{2,1,0:T(8,128)(2,1)S(1)}, bf16[4,8,4096]{2,1,0:T(8,128)(2,1)S(1)}, u32[]{:S(2)}, u32[]{:S(2)}) collective-permute-start(bf16[4,8,4096]{2,1,0:T(8,128)(2,1)S(1)} %collective-permute-done.8.refs_7_), channel_id=1, source_target_pairs={{0,1},{1,0},{2,3},{3,2},{4,5},{5,4},{6,7},{7,6},{8,9},{9,8},{10,11... | collective-permute-start | bytes 786440 | tf_op jit(solution)/shard_map/block_gather/ppermute | solution.py:180
  123.8 28.4 %copy-start.9 = (bf16[4,8,4096]{2,1,0:T(8,128)(2,1)}, bf16[4,8,4096]{2,1,0:T(8,128)(2,1)S(1)}, u32[]{:S(2)}) copy-start(bf16[4,8,4096]{2,1,0:T(8,128)(2,1)S(1)} %collective-permute-done.11.refs_10_) | copy-start | bytes 786436
  123.8 28.3 %collective-permute-start.17 = (bf16[4,8,4096]{2,1,0:T(8,128)(2,1)S(1)}, bf16[4,8,4096]{2,1,0:T(8,128)(2,1)S(1)}, u32[]{:S(2)}, u32[]{:S(2)}) collective-permute-start(bf16[4,8,4096]{2,1,0:T(8,128)(2,1)S(1)} %collective-permute-done.9.refs_8_), channel_id=1, source_target_pairs={{0,1},{1,0},{2,3},{3,2},{4,5},{5,4},{6,7},{7,6},{8,9},{9,8},{10,11... | collective-permute-start | bytes 786440 | tf_op jit(solution)/shard_map/block_gather/ppermute | solution.py:180
  124.2 27.9 %collective-permute-start.18 = (bf16[4,8,4096]{2,1,0:T(8,128)(2,1)S(1)}, bf16[4,8,4096]{2,1,0:T(8,128)(2,1)}, u32[]{:S(2)}, u32[]{:S(2)}) collective-permute-start(bf16[4,8,4096]{2,1,0:T(8,128)(2,1)S(1)} %collective-permute-done.10.refs_9_), channel_id=1, source_target_pairs={{0,1},{1,0},{2,3},{3,2},{4,5},{5,4},{6,7},{7,6},{8,9},{9,8},{10,11... | collective-permute-start | bytes 786440 | tf_op jit(solution)/shard_map/block_gather/ppermute | solution.py:180
  124.3 27.8 %collective-permute-start.19 = (bf16[4,8,4096]{2,1,0:T(8,128)(2,1)S(1)}, bf16[4,8,4096]{2,1,0:T(8,128)(2,1)}, u32[]{:S(2)}, u32[]{:S(2)}) collective-permute-start(bf16[4,8,4096]{2,1,0:T(8,128)(2,1)S(1)} %collective-permute-done.11.refs_10_), channel_id=1, source_target_pairs={{0,1},{1,0},{2,3},{3,2},{4,5},{5,4},{6,7},{7,6},{8,9},{9,8},{10,11... | collective-permute-start | bytes 786440 | tf_op jit(solution)/shard_map/block_gather/ppermute | solution.py:180
  (9 other events, 79.7 us)

commit v2 on v1

v2 whole, which is shorter than its diff:
```python
import functools
import math

import jax
import jax.numpy as jnp
import numpy as np
from jax import lax
from jax.experimental import pallas as pl
from jax.experimental.pallas import tpu as pltpu
from jax.sharding import PartitionSpec as P


N = 64
HALF = 32
ABLK = 64
GRID = 8
BAND = 16
XL = 8
SHARE = ABLK // BAND
PAIRS_Y = 32
F32 = jnp.float32
BF16 = jnp.bfloat16
VMEM_LIMIT = 16 * 1024 * 1024


@functools.cache
def tables():
    index = np.arange(N)
    phase = (index[:, None] * index[None, :]) % N
    angle = np.float32(2.0 * math.pi / N) * phase.astype(np.float32)
    cosine = np.cos(angle).astype(np.float32)
    sine = np.sin(angle).astype(np.float32)
    eye_x = np.eye(XL, dtype=np.float32)
    z_plain = np.concatenate([cosine[:HALF].T, -sine[:HALF].T], axis=1)
    z_turned = np.concatenate([z_plain[:, HALF:], -z_plain[:, :HALF]], axis=1)
    mz = np.zeros((SHARE, 2, N, 2, 2, SHARE, N), np.float32)
    for a in range(SHARE):
        for p in range(2):
            mz[a, p, :, 0, p, a, :] = z_plain
            mz[a, p, :, 1, p, a, :] = z_turned
    mzt = np.zeros((2, SHARE, N, SHARE, 2, N), np.float32)
    for a in range(SHARE):
        for p in range(2):
            mzt[p, a, :, a, p, :] = z_plain.T
    by_parity = np.stack([cosine, sine], axis=1).reshape(N, 2, PAIRS_Y, 2)
    ky = np.einsum("ktjp,xw->kxtpjw", by_parity, eye_x)
    signed = np.stack([cosine, -sine], axis=1).reshape(N, 2, PAIRS_Y, 2)
    kyt = np.einsum("ktjp,xw->pjxtkw", signed, eye_x)
    by_slab = np.stack([cosine, sine], axis=1).reshape(N, 2, GRID, XL)
    kx = np.einsum("ktgx,lm->lktgmx", by_slab, eye_x)
    signed_slab = np.stack([cosine, -sine], axis=1).reshape(N, 2, GRID, XL)
    kxt = np.einsum("ktgx,lm->gmxtlk", signed_slab, eye_x)
    turn = np.zeros((SHARE, 2, HALF, SHARE, 2, HALF), np.float32)
    for a in range(SHARE):
        turn[a, 1, :, a, 0, :] = np.eye(HALF)
        turn[a, 0, :, a, 1, :] = -np.eye(HALF)
    shapes = {
        "mz": (mz, 512, 1024),
        "mzt": (mzt, 512, 512),
        "ky": (ky, 512, 1024),
        "kyt": (kyt, 512, 1024),
        "kx": (kx, 512, 1024),
        "kxt": (kxt, 512, 1024),
        "turn": (turn, 256, 256),
    }
    return {n: v.reshape(r, c).astype(BF16) for n, (v, r, c) in shapes.items()}


def dot(a, b):
    return jnp.dot(a, b, preferred_element_type=F32)


def signed_freq(index):
    return (index + N // 2) % N - N // 2


def position():
    band = lax.axis_index("band")
    return band // 4, (band // 2) % 2, band % 2


def root_of(device):
    return device // 4, (device // 2) % 2, device % 2


def copies(sems, jobs):
    waits = []
    for slot, (target, choices) in enumerate(jobs):
        for condition, source in choices:
            move = pltpu.make_async_copy(source, target, sems.at[slot])
            if condition is None:
                move.start()
            else:
                pl.when(condition)(move.start)
        waits.append(pltpu.make_async_copy(target, target, sems.at[slot]))
    return waits


def through(bounce, sems, jobs, between=None):
    inner, row = [], 0
    for target, choices in jobs:
        inner.append((bounce.at[row : row + target.shape[0]], choices))
        row += target.shape[0]
    moves = copies(sems, inner)
    out = between() if between else []
    for slot, move in enumerate(moves):
        move.wait()
        target = jobs[slot][0]
        out.append(pltpu.make_async_copy(inner[slot][0], target, sems.at[len(jobs) + slot]))
        out[-1].start()
    wait_all(out)


def added(marks, sems, groups):
    def between():
        moves, slot = [], 0
        for sources, _ in groups:
            part = [(marks.at[slot + i : slot + i + 1], [(None, v)]) for i, v in enumerate(sources)]
            moves.append((slot, copies(sems.at[slot : slot + len(part)], part)))
            slot += len(part)
        out = []
        for (first, waits), (sources, targets) in zip(moves, groups, strict=True):
            wait_all(waits)
            total = marks[first].astype(F32)
            for i in range(1, len(sources)):
                total += marks[first + i].astype(F32)
            marks[first] = total.astype(BF16)
            for target in targets:
                out.append(pltpu.make_async_copy(marks.at[first : first + 1], target, sems.at[slot]))
                out[-1].start()
                slot += 1
        return out

    return between


def wait_all(waits):
    for move in waits:
        move.wait()


class Roots:
    def __init__(self, ablock_ref, pairs_ref, fields, occupied):
        self.y, self.h, self.c = position()
        self.fields, self.occupied = fields, occupied
        start = ablock_ref[0] * ABLK
        self.first = start % fields.shape[0]
        devices = [start // fields.shape[0]]
        self.local = []
        for k in range(2):
            index = pairs_ref[0, k]
            devices.append(index // occupied.shape[0])
            self.local.append(index % occupied.shape[0])
        roots = [root_of(d) for d in devices]
        self.away = [(self.y - y + 4) % 4 for y, _, _ in roots]
        self.same_h = [h == self.h for _, h, _ in roots]
        self.same_c = [c == self.c for _, _, c in roots]

    def block(self, core, dy, h, count):
        start = self.first + 32 * core + 8 * ((self.y + dy) % 4) + 4 * h
        return self.fields.at[pl.ds(start, count)]

    def orbital(self, k):
        return self.occupied.at[pl.ds(self.local[k], 1)]


def send_core_body(
    ablock_ref, pairs_ref, kept_ref, fields, occupied, up, down, across, stay, orbitals, bounce, marks, sems
):
    def between():
        kept = kept_ref[...]
        in_x = (lax.broadcasted_iota(jnp.int32, (N, kept.shape[1]), 0) == kept // 16).astype(BF16)
        in_c = lax.broadcasted_iota(jnp.int32, (128, kept.shape[1]), 0) % 16 == kept % 16
        mask = lax.dot_general(
            in_x, in_c.astype(BF16), (((1,), (1,)), ((), ())), preferred_element_type=F32
        )
        row = lax.broadcasted_iota(jnp.int32, mask.shape, 0)
        lane = lax.broadcasted_iota(jnp.int32, mask.shape, 1)
        mask = jnp.where(row % XL == lane // 16, mask, 0.0)
        tile = jnp.sum(mask.reshape(XL, XL, 128), axis=1)
        here = lax.axis_index("band")
        tiles = [jnp.where(here == n, tile, 0.0) for n in range(2 * BAND)]
        marks[0] = jnp.concatenate(tiles, axis=1).astype(BF16)
        move = pltpu.make_async_copy(marks, orbitals.at[2:], sems.at[16])
        move.start()
        return [move]

    at = Roots(ablock_ref, pairs_ref, fields, occupied)
    other, here, there = 1 - at.c, at.h, 1 - at.h
    jobs = [
        (up, at.block(other, 1, 0, 8)),
        (down, at.block(other, 3, 0, 8)),
        (across.at[:4], at.block(other, 0, there, 4)),
        (across.at[4:], at.block(other, 2, there, 4)),
        (orbitals.at[:1], at.orbital(0)),
        (orbitals.at[1:2], at.orbital(1)),
        (stay.at[:4], at.block(other, 0, here, 4)),
        (stay.at[4:], at.block(other, 2, here, 4)),
    ]
    through(bounce, sems, [(t, [(None, v)]) for t, v in jobs], between)


def send_first_body(
    ablock_ref,
    pairs_ref,
    fields,
    occupied,
    got_up,
    got_down,
    got_across,
    sent_orbitals,
    got_orbitals,
    up,
    down,
    across,
    bounce,
    marks,
    sems,
):
    at = Roots(ablock_ref, pairs_ref, fields, occupied)
    there = 1 - at.h
    mine, theirs = at.same_c[0], jnp.logical_not(at.same_c[0])
    jobs = [
        (up.at[:8], [(mine, at.block(at.c, 1, 0, 8)), (theirs, got_up)]),
        (down.at[:8], [(mine, at.block(at.c, 3, 0, 8)), (theirs, got_down)]),
        (across.at[:4], [(mine, at.block(at.c, 0, there, 4)), (theirs, got_across.at[:4])]),
        (across.at[4:8], [(mine, at.block(at.c, 2, there, 4)), (theirs, got_across.at[4:])]),
    ]
    for target in (up, down, across):
        for k in range(2):
            own = at.same_c[1 + k]
            jobs.append(
                (
                    target.at[8 + k : 9 + k],
                    [(own, at.orbital(k)), (jnp.logical_not(own), got_orbitals.at[k : k + 1])],
                )
            )
    groups = [([sent_orbitals.at[2:], got_orbitals.at[2:]], [v.at[10:] for v in (up, down, across)])]
    through(bounce, sems, jobs, added(marks, sems.at[20:], groups))


def send_second_body(
    ablock_ref,
    pairs_ref,
    fields,
    occupied,
    got_stay,
    sent_orbitals,
    got_orbitals,
    crossed,
    below,
    above,
    far,
    turn,
    bounce,
    marks,
    sems,
):
    at = Roots(ablock_ref, pairs_ref, fields, occupied)
    not_ = jnp.logical_not
    here, there = at.h, 1 - at.h
    same_h, same_c = at.same_h[0], at.same_c[0]
    jobs = [
        (
            far.at[:4],
            [
                (same_h & same_c, at.block(at.c, 2, here, 4)),
                (same_h & not_(same_c), got_stay.at[4:]),
                (not_(same_h), crossed.at[4:8]),
            ],
        ),
        (
            turn.at[:4],
            [
                (at.away[0] == 1, below.at[pl.ds(4 * there, 4)]),
                (at.away[0] != 1, above.at[pl.ds(4 * there, 4)]),
            ],
        ),
    ]
    for k in range(2):
        same_h, same_c, away = at.same_h[1 + k], at.same_c[1 + k], at.away[1 + k]
        row = slice(8 + k, 9 + k)
        jobs.append(
            (
                far.at[4 + k : 5 + k],
                [
                    (same_h & same_c, at.orbital(k)),
                    (same_h & not_(same_c), got_orbitals.at[k : k + 1]),
                    (not_(same_h), crossed.at[row]),
                ],
            )
        )
        jobs.append((turn.at[4 + k : 5 + k], [(away == 1, below.at[row]), (away != 1, above.at[row])]))
    groups = [
        ([sent_orbitals.at[2:], got_orbitals.at[2:], crossed.at[10:]], [far.at[6:]]),
        ([below.at[10:], above.at[10:]], [turn.at[6:]]),
    ]
    through(bounce, sems, jobs, added(marks, sems.at[12:], groups))


def forward_body(
    ablock_ref,
    pairs_ref,
    fields,
    occupied,
    got_stay,
    got_orbitals,
    crossed,
    below,
    above,
    far,
    turned,
    mz_hbm,
    ky_hbm,
    out_ref,
    second_ref,
    u_ref,
    o_ref,
    mz_ref,
    ky_ref,
    sems,
):
    at = Roots(ablock_ref, pairs_ref, fields, occupied)
    not_ = jnp.logical_not

    def arrived(k, rows_far, near_own, near_core, near_cross, side, side_turned):
        away, same_h, same_c = at.away[k], at.same_h[k], at.same_c[k]
        return [
            ((away == 0) & same_h & same_c, near_own),
            ((away == 0) & same_h & not_(same_c), near_core),
            ((away == 0) & not_(same_h), near_cross),
            (away == 2, rows_far),
            ((away == 1) & same_h, below.at[side]),
            ((away == 3) & same_h, above.at[side]),
            ((away % 2 == 1) & not_(same_h), side_turned),
        ]

    jobs = [
        (
            u_ref,
            arrived(
                0,
                far.at[:4],
                at.block(at.c, 0, at.h, 4),
                got_stay.at[:4],
                crossed.at[:4],
                pl.ds(4 * at.h, 4),
                turned.at[:4],
            ),
        )
    ]
    for k, target in enumerate((o_ref, second_ref)):
        jobs.append(
            (
                target,
                arrived(
                    1 + k,
                    far.at[4 + k : 5 + k],
                    at.orbital(k),
                    got_orbitals.at[k : k + 1],
                    crossed.at[8 + k : 9 + k],
                    pl.ds(8 + k, 1),
                    turned.at[4 + k : 5 + k],
                ),
            )
        )
    jobs += [(mz_ref, [(None, mz_hbm)]), (ky_ref, [(None, ky_hbm)])]
    u_wait, o_wait, second_wait, mz_wait, ky_wait = copies(sems, jobs)
    u_wait.wait()
    o_wait.wait()
    orbital = o_ref[0].astype(F32)
    columns = []
    for a in range(SHARE):
        density = u_ref[a].astype(F32) * orbital
        columns.append(
            jnp.concatenate([density[:, 128 * j : 128 * (j + 1)] for j in range(PAIRS_Y)], axis=0)
        )
    density = jnp.concatenate(columns, axis=1).astype(BF16)
    mz_wait.wait()
    zfreq = dot(density, mz_ref[...]).astype(BF16)
    stacked = jnp.concatenate([zfreq[:, 256 * i : 256 * (i + 1)] for i in range(4)], axis=0)
    ky_wait.wait()
    out_ref[...] = dot(ky_ref[...], stacked).astype(BF16)
    second_wait.wait()


def middle_body(y_ref, weight_ref, turn_ref, kx_hbm, kxt_hbm, out_ref, kx_ref, kxt_ref, sems):
    kx_wait, kxt_wait = copies(sems, [(kx_ref, [(None, kx_hbm)]), (kxt_ref, [(None, kxt_hbm)])])
    turn = turn_ref[...]
    yfreq = y_ref[...]
    both = jnp.concatenate([yfreq, dot(yfreq, turn).astype(BF16)], axis=0)
    weights = jnp.concatenate([weight_ref[...], weight_ref[...]], axis=1)
    kx_wait.wait()
    potential = (dot(kx_ref[...], both) * weights).astype(BF16)
    both = jnp.concatenate([potential, dot(potential, turn).astype(BF16)], axis=0)
    kxt_wait.wait()
    out_ref[...] = dot(kxt_ref[...], both).astype(BF16)


def backward_body(h_ref, o_ref, turn_ref, kyt_hbm, mzt_hbm, out_ref, kyt_ref, mzt_ref, sems):
    kyt_wait, mzt_wait = copies(sems, [(kyt_ref, [(None, kyt_hbm)]), (mzt_ref, [(None, mzt_hbm)])])
    orbital = o_ref[0].astype(F32)
    freq = h_ref[...]
    both = jnp.concatenate([freq, dot(freq, turn_ref[...]).astype(BF16)], axis=0)
    kyt_wait.wait()
    zfreq = dot(kyt_ref[...], both).astype(BF16)
    zfreq = jnp.concatenate([zfreq[:256], zfreq[256:]], axis=1)
    mzt_wait.wait()
    value = dot(zfreq, mzt_ref[...])
    for a in range(SHARE):
        rows = [value[8 * j : 8 * (j + 1), 128 * a : 128 * (a + 1)] for j in range(PAIRS_Y)]
        out_ref[a] = (jnp.concatenate(rows, axis=1) * orbital).astype(BF16)


def weight_body(sent_orbitals, got_orbitals, crossed, below, above, far, turned, out_ref, marks, sems):
    sources = [sent_orbitals.at[2:], got_orbitals.at[2:], crossed.at[10:], below.at[10:], above.at[10:]]
    sources += [far.at[6:], turned.at[6:]]
    wait_all(copies(sems, [(marks.at[i : i + 1], [(None, v)]) for i, v in enumerate(sources)]))
    total = sum(marks[i].astype(F32) for i in range(len(sources)))
    tiles = jnp.concatenate([total[:, 128 * n : 128 * (n + 1)] for n in range(BAND)], axis=0).astype(BF16)
    shape = (BAND * N, BAND * XL)
    row = lax.broadcasted_iota(jnp.int32, shape, 0)
    lane = lax.broadcasted_iota(jnp.int32, shape, 1)
    spread = dot((row // XL == lane).astype(BF16), tiles)
    spread = jnp.where(row % XL == lane // 16, spread, 0.0).astype(BF16)
    row = lax.broadcasted_iota(jnp.int32, (128, 128), 0)
    lane = lax.broadcasted_iota(jnp.int32, (128, 128), 1)
    spread = dot(spread, (row % 16 == lane % 16).astype(BF16))
    low = lax.broadcasted_iota(jnp.int32, (N, 128), 1) % HALF < 16
    blocks = [spread[N * n : N * (n + 1)] for n in range(BAND)]
    kept = jnp.concatenate([jnp.where(low, blocks[2 * m], blocks[2 * m + 1]) for m in range(XL)], axis=0)
    shape = (N * XL, 128)
    row = lax.broadcasted_iota(jnp.int32, shape, 0)
    lane = lax.broadcasted_iota(jnp.int32, shape, 1)
    freq_x = signed_freq(row % N)
    freq_y = signed_freq(lax.axis_index("grid") * XL + row // N)
    freq_z = lane % HALF
    squared = (freq_x * freq_x + freq_y * freq_y + freq_z * freq_z).astype(F32)
    out_ref[...] = kept / (float(N * N * N) * (squared + 1.0))


def copy_body(source, target, sems):
    wait_all(copies(sems, [(target, [(None, source)])]))


SMEM, VMEM, HBM = pltpu.SMEM, pltpu.VMEM, pltpu.HBM
PLANE = (XL, N * N)


def call(body, spaces, outs, out_spaces, scratch, args, dtype=BF16):
    many = len(outs) > 1
    shapes = [jax.ShapeDtypeStruct(o, dtype) for o in outs]
    specs = [pl.BlockSpec(memory_space=m) for m in out_spaces]
    return pl.pallas_call(
        body,
        out_shape=shapes if many else shapes[0],
        in_specs=[pl.BlockSpec(memory_space=m) for m in spaces],
        out_specs=specs if many else specs[0],
        scratch_shapes=scratch,
        compiler_params=pltpu.CompilerParams(vmem_limit_bytes=VMEM_LIMIT),
    )(*args)


def slab_body(last, names, u_ref, *refs):
    pieces = 2 * len(names)
    w_refs, extra = refs[:pieces], refs[pieces:-2]
    out_ref, total = refs[-2:]
    lanes = 2048
    for s in range(N * N // lanes):
        part = pl.ds(s * lanes, lanes)
        right = jnp.concatenate([w[:, part] for w in w_refs], axis=0)
        gram = lax.dot_general(u_ref[:, part], right, (((1,), (1,)), ((), ())), preferred_element_type=F32)
        if s == 0:
            total[...] = gram
        else:
            total[...] += gram
    gram = total[...]
    wide = gram.shape[1]
    row = lax.broadcasted_iota(jnp.int32, gram.shape, 0) % XL
    col = lax.broadcasted_iota(jnp.int32, gram.shape, 1) % XL
    gram = jnp.where(row == col, gram, 0.0)
    gram = jnp.sum(gram.reshape(gram.shape[0] // XL, XL, wide), axis=1)
    y, h, c = position()
    row = lax.broadcasted_iota(jnp.int32, (SHARE * XL, 128), 0) // XL
    lane = lax.broadcasted_iota(jnp.int32, (SHARE * XL, 128), 1) % ABLK
    pick = []
    for dy, dh in names:
        for dc in range(2):
            first = 32 * ((c + dc) % 2) + 8 * ((y - dy + 4) % 4) + 4 * ((h + dh) % 2)
            pick.append((lane == first + row).astype(F32))
    pick = jnp.concatenate(pick, axis=0)
    slab = jnp.dot(gram, pick, precision=lax.Precision.HIGHEST, preferred_element_type=F32)
    if extra:
        slab = slab + extra[0][...]
    if not last:
        out_ref[...] = slab
    else:
        lane = lax.broadcasted_iota(jnp.int32, slab.shape, 1)
        zero = jnp.zeros_like(slab)
        slab = jnp.concatenate(
            [jnp.where(lane < ABLK, slab, zero), jnp.where(lane < ABLK, zero, slab)], axis=0
        )
        high = slab.astype(BF16)
        low = (slab - high.astype(F32)).astype(BF16)
        amp = extra[1][...].reshape(1024, 256)
        out_ref[...] = (dot(amp, high) + dot(amp, low)).astype(BF16)


def slab_call(names, fields, parts, extra=()):
    last = len(extra) > 1
    tall = fields.shape[0]
    wide = sum(p.shape[0] for p in parts)
    out = (1024, 128) if last else (tall // XL, 128)
    args = (fields, *parts, *extra)
    return pl.pallas_call(
        functools.partial(slab_body, last, names),
        out_shape=jax.ShapeDtypeStruct(out, BF16 if last else F32),
        in_specs=[pl.BlockSpec(memory_space=VMEM)] * len(args),
        out_specs=pl.BlockSpec(memory_space=VMEM),
        scratch_shapes=[VMEM((tall, wide), F32)],
        compiler_params=pltpu.CompilerParams(vmem_limit_bytes=24 * 1024 * 1024),
        cost_estimate=pl.CostEstimate(
            flops=2 * tall * wide * N * N, bytes_accessed=2 * tall * N * N, transcendentals=0
        ),
    )(*args)


def band_shift(value, dy, dh, dc):
    pairs = []
    for y in range(4):
        for h in range(2):
            for c in range(2):
                pairs.append((4 * y + 2 * h + c, 4 * ((y + dy) % 4) + 2 * ((h + dh) % 2) + (c + dc) % 2))
    return lax.ppermute(value, "band", pairs)


def per_device(virtual_field, occupied_field, amplitudes, ablock, pairs, kept_cells):
    far_memory = lambda v: pltpu.with_memory_space_constraint(v, HBM)
    const = {n: jnp.asarray(v) if n == "turn" else far_memory(jnp.asarray(v)) for n, v in tables().items()}
    roots = (ablock, pairs, far_memory(virtual_field), far_memory(occupied_field))
    root_spaces = [SMEM, SMEM, pl.ANY, pl.ANY]

    with jax.named_scope("block_scatter"):
        sems = lambda n: [pltpu.SemaphoreType.DMA((n,))]
        bounce = lambda n, marks, k: [VMEM((n,) + PLANE, BF16), VMEM((marks,) + PLANE, BF16)] + sems(k)
        eight = (8,) + PLANE
        sent = call(
            send_core_body,
            [SMEM, SMEM, VMEM, pl.ANY, pl.ANY],
            [eight] * 4 + [(3,) + PLANE],
            [pl.ANY] * 5,
            bounce(34, 1, 17),
            roots[:2] + (kept_cells,) + roots[2:],
        )
        order = (0, 1, 2, 4, 3)
        got = {k: band_shift(sent[k], 0, 0, 1) for k in order}
        sent_orbitals = sent[4]
        sent = call(
            send_first_body,
            root_spaces + [pl.ANY] * 5,
            [(11,) + PLANE] * 3,
            [pl.ANY] * 3,
            bounce(30, 2, 25),
            roots + (got[0], got[1], got[2], sent_orbitals, got[4]),
        )
        sent, amp = lax.optimization_barrier((sent, amplitudes[0]))
        amp = jnp.broadcast_to(amp.T.reshape(1, 128, 256), (GRID, 128, 256))
        crossed = band_shift(sent[2], 0, 1, 0)
        below = band_shift(sent[0], 1, 0, 0)
        above = band_shift(sent[1], 3, 0, 0)
        amp = lax.all_to_all(amp, "grid", 0, 0, tiled=True)
        sent = call(
            send_second_body,
            root_spaces + [pl.ANY] * 6,
            [(7,) + PLANE] * 2,
            [pl.ANY] * 2,
            bounce(12, 5, 19),
            roots + (got[3], sent_orbitals, got[4], crossed, below, above),
        )
        far = band_shift(sent[0], 2, 0, 0)
        turned = band_shift(sent[1], 0, 1, 0)
        far, turned, amp = lax.optimization_barrier((far, turned, amp))

    with jax.named_scope("transform"):
        big = VMEM((512, 1024), BF16)
        freq, second = call(
            forward_body,
            root_spaces + [pl.ANY] * 9,
            [(512, 256), (1,) + PLANE],
            [VMEM, VMEM],
            [VMEM((SHARE,) + PLANE, BF16), VMEM((1,) + PLANE, BF16), big, big] + sems(5),
            roots + (got[3], got[4], crossed, below, above, far, turned, const["mz"], const["ky"]),
        )
        freq = lax.all_to_all(freq, "grid", 0, 0, tiled=True)
        weights = call(
            weight_body,
            [pl.ANY] * 7,
            [(N * XL, 128)],
            [VMEM],
            [VMEM((7,) + PLANE, BF16)] + sems(7),
            (sent_orbitals, got[4], crossed, below, above, far, turned),
            F32,
        )
        freq = call(
            middle_body,
            [VMEM] * 3 + [pl.ANY] * 2,
            [(512, 256)],
            [VMEM],
            [big, big] + sems(2),
            (freq, weights, const["turn"], const["kx"], const["kxt"]),
        )
        freq = lax.all_to_all(freq, "grid", 0, 0, tiled=True)
        potential = call(
            backward_body,
            [VMEM] * 3 + [pl.ANY] * 2,
            [(SHARE,) + PLANE],
            [VMEM],
            [big, VMEM((512, 512), BF16)] + sems(2),
            (freq, second, const["turn"], const["kyt"], const["mzt"]),
        )

    with jax.named_scope("block_gather"):
        early, late = ((0, 0), (2, 0), (1, 0), (3, 0), (0, 1)), ((2, 1), (1, 1), (3, 1))
        shape = (virtual_field.shape[0] * XL, N * N)
        potential, fields = lax.optimization_barrier(
            (potential.reshape(SHARE * XL, N * N), virtual_field.reshape(shape))
        )
        fields = call(copy_body, [pl.ANY], [shape], [pl.ANY], sems(1), (far_memory(fields),))
        part = {(0, 0): potential}
        for k in (2, 1, 3):
            part[k, 0] = band_shift(potential, k, 0, 0)
        part[0, 1] = band_shift(potential, 0, 1, 0)

        def contract(names, *extra):
            pieces = [w for name in names for w in (part[name], band_shift(part[name], 0, 0, 1))]
            return slab_call(names, fields, pieces, extra)

        part[2, 0], part[0, 1], fields = lax.optimization_barrier((part[2, 0], part[0, 1], fields))
        part[2, 1] = band_shift(part[2, 0], 0, 1, 0)
        for k in (1, 3):
            part[k, 1] = band_shift(part[0, 1], k, 0, 0)
        slab = contract(early)
        *got, slab = lax.optimization_barrier([part[name] for name in late] + [slab])
        part.update(zip(late, got))
        terms = contract(late, slab, amp)

    with jax.named_scope("ladder"):
        terms = lax.all_to_all(
            terms.reshape(GRID * BAND, XL, 128), ("grid", "band"), 0, 0, tiled=True
        )
        ladder = jnp.sum(terms.astype(F32), axis=0)
        return ladder.reshape(1, 16, ABLK)


def solution(mesh):
    in_specs = (
        P("band", "grid", None),
        P("band", "grid", None),
        P(None, "band", "grid"),
        P(),
        P(),
        P(("grid", "band"), None),
    )
    out_specs = P(None, ("grid", "band"), None)
    return jax.shard_map(
        per_device, mesh=mesh, in_specs=in_specs, out_specs=out_specs, check_vma=False
    )
```

time: 187 us -> 135 us (0.72)
  blocking collectives: 46.4 us -> 25.4 us
  starting transfers between devices: 58.6 us -> 43.1 us
  Pallas kernels: 22.8 us -> 32.2 us
  between operations: 9.88 us -> 0.86 us
  local copies, waits for them, and re-layouts: 13.7 us -> 7.01 us
  waiting for transfers between devices: 30.7 us -> 25.9 us
  other arithmetic: 4.83 us -> 0.14 us
    all_gather x1 -> x0, blocking collectives: 25.4 us -> none  [per_device(): amp = lax.all_gather(amp, 'grid', axis=0, tiled=True)]
    pallas_call x4 -> x10, Pallas kernels: 22.8 us -> 32.2 us  [the longest x8 23.3 us: call(): pl.pallas_call(body, out_shape=shapes if many else shapes[0], in_specs=[p...]
    all_to_all x0 -> x1, blocking collectives: none -> 8.49 us  [per_device(): freq = lax.all_to_all(freq, 'grid', 0, 0, tiled=True)]
    all_to_all x2 -> x1, starting transfers between devices: 13.2 us -> 5.06 us  [per_device(): amp = lax.all_to_all(amp, 'grid', 0, 0, tiled=True)]
    all_to_all x2 -> x1, waiting for transfers between devices: 10.1 us -> 3.42 us  [per_device(): freq = lax.all_to_all(freq, 'grid', 0, 0, tiled=True)]
    select_n x5 -> x0, other arithmetic: 4.52 us -> none  [the longest x1 2.47 us: per_device(): mine = jnp.where(own_c == my_c, mine, got)]
    all_to_all x1, blocking collectives: 21.1 us -> 16.9 us  [per_device(): lax.all_to_all(terms.reshape(GRID * BAND, XL, 128), ('grid', 'band'), 0,...]
    ppermute x20 -> x25, starting transfers between devices: 37 us -> 32.9 us  [band_shift(): return lax.ppermute(value, 'band', pairs)]
  transfers between devices with their start and end apart: 24 -> 27, of which waited for: 5 -> 10; matrix products, arithmetic and copies ran while one was open for 7% -> 1% of each run, Pallas kernels for 0% -> 10%
where the time goes in v2:
time: 135 us
  starting transfers between devices  43.1 us (32%)
  Pallas kernels  32.2 us (24%)
  waiting for transfers between devices  25.9 us (19%)
  blocking collectives  25.4 us (19%)
  local copies, waits for them, and re-layouts  7.01 us (5%)
    ppermute x25, starting transfers between devices, band_shift(): return lax.ppermute(value, 'band', pairs)  32.9 us
    pallas_call x8, Pallas kernels, call(): pl.pallas_call(body, out_shape=shapes if many else shapes[0], in_specs=[p...  23.3 us
    ppermute x25, waiting for transfers between devices, band_shift(): return lax.ppermute(value, 'band', pairs)  22.5 us
    all_to_all x1, blocking collectives, per_device(): lax.all_to_all(terms.reshape(GRID * BAND, XL, 128), ('grid', 'band'), 0,...  16.9 us
    pallas_call x2, Pallas kernels, slab_call(): pl.pallas_call(functools.partial(slab_body, last, names), out_shape=jax.S...  8.96 us
    all_to_all x1, blocking collectives, per_device(): freq = lax.all_to_all(freq, 'grid', 0, 0, tiled=True)  8.49 us
    unnamed x22, local copies, waits for them, and re-layouts  5.35 us
    all_to_all x1, starting transfers between devices, per_device(): amp = lax.all_to_all(amp, 'grid', 0, 0, tiled=True)  5.06 us
  transfers between devices with their start and end apart: 27, of which 10 were waited for; matrix products, arithmetic and copies ran while one was open for 1% of the time, Pallas kernels for 10%

profile of v2, /device:TPU:1, one launch (start us, length us, event | category | flops | bytes accessed | tf_op | source)
XLA Modules:
  0.0 134.6 jit_solution(1032727996346058743)
XLA Ops:
  2.0 3.2 %block_scatter.3 = (bf16[8,8,4096]{2,1,0:T(8,128)(2,1)S(1)}, bf16[8,8,4096]{2,1,0:T(8,128)(2,1)S(1)}, bf16[8,8,4096]{2,1,0:T(8,128)(2,1)S(1)}, bf16[8,8,4096]{2,1,0:T(8,128)(2,1)}, bf16[3,8,4096]{2,1,0:T(8,128)(2,1)S(1)}) custom-call(s32[1]{0:T(128)S(6)} %copy.15.ablock_ref, s32[1,2]{1,0:T(1,128)S(1)} %copy-done.7, s32[1,512]{1,0:T(1,128)S(1)} %copy-done.9, ...), custom_call_target="tpu_custom_call" | custom-call | tf_op jit(solution)/shard_map/block_scatter/pallas_call | solution.py:454
  5.3 1.5 %collective-permute-start.2 = (bf16[8,8,4096]{2,1,0:T(8,128)(2,1)S(1)}, bf16[8,8,4096]{2,1,0:T(8,128)(2,1)S(1)}, u32[]{:S(2)}, u32[]{:S(2)}) collective-permute-start(bf16[8,8,4096]{2,1,0:T(8,128)(2,1)S(1)} %get-tuple-element.35), channel_id=1, source_target_pairs={{0,1},{1,0},{2,3},{3,2},{4,5},{5,4},{6,7},{7,6},{8,9},{9,8},{10,11... | collective-permute-start | bytes 1572872 | tf_op jit(solution)/shard_map/block_scatter/ppermute | solution.py:534
  7.4 2.7 %collective-permute-done.1.got_orbitals = bf16[3,8,4096]{2,1,0:T(8,128)(2,1)S(1)} collective-permute-done((bf16[3,8,4096]{2,1,0:T(8,128)(2,1)S(1)}, bf16[3,8,4096]{2,1,0:T(8,128)(2,1)S(1)}, u32[]{:S(2)}, u32[]{:S(2)}) %collective-permute-start.1) | collective-permute-done | bytes 196640 | tf_op jit(solution)/shard_map/block_scatter/ppermute | solution.py:534
  10.1 3.0 %block_scatter.4 = (bf16[11,8,4096]{2,1,0:T(8,128)(2,1)}, bf16[11,8,4096]{2,1,0:T(8,128)(2,1)}, bf16[11,8,4096]{2,1,0:T(8,128)(2,1)}) custom-call(s32[1]{0:T(128)S(6)} %copy.15.ablock_ref, s32[1,2]{1,0:T(1,128)S(1)} %copy-done.7, bf16[128,8,4096]{2,1,0:T(8,128)(2,1)} %fields.7, bf16[16,8,4096]{2,1,0:T(8,128)(2,1)} %occupied.7, ...), custom_call_target="tpu_custom_call" | custom-call | tf_op jit(solution)/shard_map/block_scatter/pallas_call | solution.py:454
  13.1 2.9 %collective-permute-start.5 = (bf16[11,8,4096]{2,1,0:T(8,128)(2,1)}, bf16[11,8,4096]{2,1,0:T(8,128)(2,1)S(1)}, u32[]{:S(2)}, u32[]{:S(2)}) collective-permute-start(bf16[11,8,4096]{2,1,0:T(8,128)(2,1)} %get-tuple-element.41), channel_id=1, source_target_pairs={{0,2},{1,3},{2,0},{3,1},{4,6},{5,7},{6,4},{7,5},{8,10},{9,11},{10,... | collective-permute-start | bytes 2162696 | tf_op jit(solution)/shard_map/block_scatter/ppermute | solution.py:534
  16.0 1.3 collective-permute-start.6
  17.3 1.4 %collective-permute-start.7 = (bf16[11,8,4096]{2,1,0:T(8,128)(2,1)}, bf16[11,8,4096]{2,1,0:T(8,128)(2,1)S(1)}, u32[]{:S(2)}, u32[]{:S(2)}) collective-permute-start(bf16[11,8,4096]{2,1,0:T(8,128)(2,1)} %get-tuple-element.43), channel_id=1, source_target_pairs={{0,12},{1,13},{2,14},{3,15},{4,0},{5,1},{6,2},{7,3},{8,4},{9,5},{1... | collective-permute-start | bytes 2162696 | tf_op jit(solution)/shard_map/block_scatter/ppermute | solution.py:534
  18.8 1.6 %collective-permute-start = (bf16[8,8,4096]{2,1,0:T(8,128)(2,1)}, bf16[8,8,4096]{2,1,0:T(8,128)(2,1)S(1)}, u32[]{:S(2)}, u32[]{:S(2)}) collective-permute-start(bf16[8,8,4096]{2,1,0:T(8,128)(2,1)} %get-tuple-element.33), channel_id=1, source_target_pairs={{0,1},{1,0},{2,3},{3,2},{4,5},{5,4},{6,7},{7,6},{8,9},{9,8},{10,11... | collective-permute-start | bytes 1572872 | tf_op jit(solution)/shard_map/block_scatter/ppermute | solution.py:534
  21.4 5.1 %all-to-all-start = ((bf16[8,128,256]{2,1,0:T(8,128)(2,1)}), bf16[8,128,256]{2,1,0:T(8,128)(2,1)S(1)}, u32[]{:S(2)}, u32[]{:S(2)}) async-start(bf16[8,128,256]{2,1,0:T(8,128)(2,1)} %broadcast_in_dim.8), calls=%async_computation | async-start | bytes 1048576 | tf_op jit(solution)/shard_map/block_scatter/all_to_all | solution.py:571
  26.4 5.4 %collective-permute-done.5.crossed = bf16[11,8,4096]{2,1,0:T(8,128)(2,1)S(1)} collective-permute-done((bf16[11,8,4096]{2,1,0:T(8,128)(2,1)}, bf16[11,8,4096]{2,1,0:T(8,128)(2,1)S(1)}, u32[]{:S(2)}, u32[]{:S(2)}) %collective-permute-start.5) | collective-permute-done | bytes 720928 | tf_op jit(solution)/shard_map/block_scatter/ppermute | solution.py:534
  31.8 2.3 %collective-permute-done.6.below = bf16[11,8,4096]{2,1,0:T(8,128)(2,1)S(1)} collective-permute-done((bf16[11,8,4096]{2,1,0:T(8,128)(2,1)}, bf16[11,8,4096]{2,1,0:T(8,128)(2,1)S(1)}, u32[]{:S(2)}, u32[]{:S(2)}) %collective-permute-start.6) | collective-permute-done | bytes 720928 | tf_op jit(solution)/shard_map/block_scatter/ppermute | solution.py:534
  35.1 2.6 %block_scatter.5 = (bf16[7,8,4096]{2,1,0:T(8,128)(2,1)}, bf16[7,8,4096]{2,1,0:T(8,128)(2,1)}) custom-call(s32[1]{0:T(128)S(6)} %copy.15.ablock_ref, s32[1,2]{1,0:T(1,128)S(1)} %copy-done.8, bf16[128,8,4096]{2,1,0:T(8,128)(2,1)} %fields.7, bf16[16,8,4096]{2,1,0:T(8,128)(2,1)} %occupied.7, bf16[8,8,4096]{2,1,0:T(8,128)(2,1)S(1)} %collective-permute-done.got_stay, ...), custom_call_target="tpu_custom_call" | custom-call | tf_op jit(solution)/shard_map/block_scatter/pallas_call | solution.py:454
  37.7 2.4 %collective-permute-start.8 = (bf16[7,8,4096]{2,1,0:T(8,128)(2,1)}, bf16[7,8,4096]{2,1,0:T(8,128)(2,1)}, u32[]{:S(2)}, u32[]{:S(2)}) collective-permute-start(bf16[7,8,4096]{2,1,0:T(8,128)(2,1)} %get-tuple-element.44), channel_id=1, source_target_pairs={{0,8},{1,9},{2,10},{3,11},{4,12},{5,13},{6,14},{7,15},{8,0},{9,1},... | collective-permute-start | bytes 1376264 | tf_op jit(solution)/shard_map/block_scatter/ppermute | solution.py:534
  41.2 8.5 %collective-permute-done.8.far = bf16[7,8,4096]{2,1,0:T(8,128)(2,1)} collective-permute-done((bf16[7,8,4096]{2,1,0:T(8,128)(2,1)}, bf16[7,8,4096]{2,1,0:T(8,128)(2,1)}, u32[]{:S(2)}, u32[]{:S(2)}) %collective-permute-start.8) | collective-permute-done | bytes 458784 | tf_op jit(solution)/shard_map/block_scatter/ppermute | solution.py:534
  49.7 1.7 %collective-permute-done.9.turned = bf16[7,8,4096]{2,1,0:T(8,128)(2,1)} collective-permute-done((bf16[7,8,4096]{2,1,0:T(8,128)(2,1)}, bf16[7,8,4096]{2,1,0:T(8,128)(2,1)}, u32[]{:S(2)}, u32[]{:S(2)}) %collective-permute-start.9) | collective-permute-done | bytes 458784 | tf_op jit(solution)/shard_map/block_scatter/ppermute | solution.py:534
  51.4 3.0 %transform.4 = (bf16[512,256]{1,0:T(8,128)(2,1)S(1)}, bf16[1,8,4096]{2,1,0:T(8,128)(2,1)S(1)}) custom-call(s32[1]{0:T(128)S(6)} %copy.15.ablock_ref, s32[1,2]{1,0:T(1,128)S(1)} %copy-done.8, bf16[128,8,4096]{2,1,0:T(8,128)(2,1)} %fields.7, bf16[16,8,4096]{2,1,0:T(8,128)(2,1)} %occupied.7, bf16[8,8,4096]{2,1,0:T(8,128)(2,1)S(1)} %collective-permute-done.got_stay, ...), custom_call_target="tpu_custom_call" | custom-call | tf_op jit(solution)/shard_map/transform/pallas_call | solution.py:454
  55.7 5.1 %all-to-all-start.1 = ((bf16[8,64,256]{2,1,0:T(8,128)(2,1)}), bf16[8,64,256]{2,1,0:T(8,128)(2,1)}, u32[]{:S(2)}, u32[]{:S(2)}) async-start(bf16[8,64,256]{2,1,0:T(8,128)(2,1)} %bitcast.18), calls=%async_computation.1 | async-start | bytes 524288 | tf_op jit(solution)/shard_map/transform/all_to_all | solution.py:594
  61.7 1.8 %transform.5.weight_ref = f32[512,128]{1,0:T(8,128)S(1)} custom-call(bf16[3,8,4096]{2,1,0:T(8,128)(2,1)S(1)} %copy-done.2, bf16[3,8,4096]{2,1,0:T(8,128)(2,1)S(1)} %collective-permute-done.1.got_orbitals, bf16[11,8,4096]{2,1,0:T(8,128)(2,1)S(1)} %collective-permute-done.5.crossed, bf16[11,8,4096]{2,1,0:T(8,128)(2,1)S(1)} %collective-permute-done.6.below, ...), custom_call_target="tpu_custom_call" | custom-call | tf_op jit(solution)/shard_map/transform/pallas_call | solution.py:454
  63.5 3.4 %all-to-all-done.1 = bf16[8,64,256]{2,1,0:T(8,128)(2,1)} async-done(((bf16[8,64,256]{2,1,0:T(8,128)(2,1)}), bf16[8,64,256]{2,1,0:T(8,128)(2,1)}, u32[]{:S(2)}, u32[]{:S(2)}) %all-to-all-start.1) | async-done | bytes 262176 | tf_op jit(solution)/shard_map/transform/all_to_all | solution.py:594
  67.0 3.7 %transform.6 = bf16[512,256]{1,0:T(8,128)(2,1)S(1)} custom-call(bf16[512,256]{1,0:T(8,128)(2,1)} %bitcast.3.y_ref, f32[512,128]{1,0:T(8,128)S(1)} %transform.5.weight_ref, bf16[256,256]{1,0:T(8,128)(2,1)S(1)} %copy-done.3, bf16[512,1024]{1,0:T(8,128)(2,1)} %constant.20.clone.kx_hbm, bf16[512,1024]{1,0:T(8,128)(2,1)} %constant.21.clone.kxt_hbm), custom_call_target="tpu_custom_call" | custom-call | tf_op jit(solution)/shard_map/transform/pallas_call | solution.py:454
  70.7 8.5 %all_to_all.32 = bf16[8,64,256]{2,1,0:T(8,128)(2,1)S(1)} all-to-all(bf16[8,64,256]{2,1,0:T(8,128)(2,1)S(1)} %bitcast.16), channel_id=1, replica_groups=mesh['grid'=8,'band'=16] {'grid'}, dimensions={0} | all-to-all | bytes 524288 | tf_op jit(solution)/shard_map/transform/all_to_all | solution.py:612
  80.0 2.4 %transform.7 = bf16[4,8,4096]{2,1,0:T(8,128)(2,1)S(1)} custom-call(bf16[512,256]{1,0:T(8,128)(2,1)S(1)} %bitcast.15, bf16[1,8,4096]{2,1,0:T(8,128)(2,1)S(1)} %copy-done.6, bf16[256,256]{1,0:T(8,128)(2,1)S(1)} %copy-done.3, bf16[512,1024]{1,0:T(8,128)(2,1)} %constant.19.clone.kyt_hbm, bf16[512,512]{1,0:T(8,128)(2,1)} %constant.17.clone.mzt_hbm), custom_call_target="tpu_custom_call" | custom-call | tf_op jit(solution)/shard_map/transform/pallas_call | solution.py:454
  83.6 1.4 %collective-permute-start.11 = (bf16[32,4096]{1,0:T(8,128)(2,1)S(1)}, bf16[32,4096]{1,0:T(8,128)(2,1)S(1)}, u32[]{:S(2)}, u32[]{:S(2)}) collective-permute-start(bf16[32,4096]{1,0:T(8,128)(2,1)S(1)} %bitcast.10), channel_id=1, source_target_pairs={{0,2},{1,3},{2,0},{3,1},{4,6},{5,7},{6,4},{7,5},{8,10},{9,11},{10,... | collective-permute-start | bytes 786440 | tf_op jit(solution)/shard_map/block_gather/ppermute | solution.py:534
  85.7 2.0 %collective-permute-start.19 = (bf16[32,4096]{1,0:T(8,128)(2,1)S(1)}, bf16[32,4096]{1,0:T(8,128)(2,1)S(1)}, u32[]{:S(2)}, u32[]{:S(2)}) collective-permute-start(bf16[32,4096]{1,0:T(8,128)(2,1)S(1)} %bitcast.12), channel_id=1, source_target_pairs={{0,12},{1,13},{2,14},{3,15},{4,0},{5,1},{6,2},{7,3},{8,4},{9,5},{1... | collective-permute-start | bytes 786440 | tf_op jit(solution)/shard_map/block_gather/ppermute | solution.py:534
  87.7 7.3 %collective-permute-start.15 = (bf16[32,4096]{1,0:T(8,128)(2,1)S(1)}, bf16[32,4096]{1,0:T(8,128)(2,1)S(1)}, u32[]{:S(2)}, u32[]{:S(2)}) collective-permute-start(bf16[32,4096]{1,0:T(8,128)(2,1)S(1)} %bitcast.13), channel_id=1, source_target_pairs={{0,1},{1,0},{2,3},{3,2},{4,5},{5,4},{6,7},{7,6},{8,9},{9,8},{10,11... | collective-permute-start | bytes 786440 | tf_op jit(solution)/shard_map/block_gather/ppermute | solution.py:534
  95.0 3.4 %block_gather.3.u_ref = bf16[1024,4096]{1,0:T(8,128)(2,1)S(1)} custom-call(bf16[1024,4096]{1,0:T(8,128)(2,1)} %bitcast.19), custom_call_target="tpu_custom_call" | custom-call | tf_op jit(solution)/shard_map/block_gather/pallas_call | solution.py:454
  99.5 1.7 %collective-permute-start.12 = (bf16[32,4096]{1,0:T(8,128)(2,1)S(1)}, bf16[32,4096]{1,0:T(8,128)(2,1)S(1)}, u32[]{:S(2)}, u32[]{:S(2)}) collective-permute-start(bf16[32,4096]{1,0:T(8,128)(2,1)S(1)} %collective-permute-done.10.refs_2_), channel_id=1, source_target_pairs={{0,2},{1,3},{2,0},{3,1},{4,6},{5,7},{6,4},{7,5},{8,10},{9,11},{10,... | collective-permute-start | bytes 786440 | tf_op jit(solution)/shard_map/block_gather/ppermute | solution.py:534
  101.9 2.0 %collective-permute-start.14 = (bf16[32,4096]{1,0:T(8,128)(2,1)S(1)}, bf16[32,4096]{1,0:T(8,128)(2,1)S(1)}, u32[]{:S(2)}, u32[]{:S(2)}) collective-permute-start(bf16[32,4096]{1,0:T(8,128)(2,1)S(1)} %collective-permute-done.11.refs_8_), channel_id=1, source_target_pairs={{0,12},{1,13},{2,14},{3,15},{4,0},{5,1},{6,2},{7,3},{8,4},{9,5},{1... | collective-permute-start | bytes 786440 | tf_op jit(solution)/shard_map/block_gather/ppermute | solution.py:534
  103.9 5.2 %block_gather.4.refs_6_ = f32[128,128]{1,0:T(8,128)S(1)} custom-call(bf16[1024,4096]{1,0:T(8,128)(2,1)S(1)} %block_gather.3.u_ref, bf16[32,4096]{1,0:T(8,128)(2,1)S(1)} %bitcast.14, bf16[32,4096]{1,0:T(8,128)(2,1)S(1)} %collective-permute-done.15.refs_1_, bf16[32,4096]{1,0:T(8,128)(2,1)S(1)} %collective-permute-done.10.refs_2_, ...), custom_call_target="tpu_custom_call" | custom-call | flops 2684354560 | bytes 8388608 | tf_op jit(solution)/shard_map/block_gather/pallas_call | solution.py:515
  109.6 1.6 %collective-permute-start.22 = (bf16[32,4096]{1,0:T(8,128)(2,1)S(1)}, bf16[32,4096]{1,0:T(8,128)(2,1)S(1)}, u32[]{:S(2)}, u32[]{:S(2)}) collective-permute-start(bf16[32,4096]{1,0:T(8,128)(2,1)S(1)} %collective-permute-done.12.refs_0_), channel_id=1, source_target_pairs={{0,1},{1,0},{2,3},{3,2},{4,5},{5,4},{6,7},{7,6},{8,9},{9,8},{10,11... | collective-permute-start | bytes 786440 | tf_op jit(solution)/shard_map/block_gather/ppermute | solution.py:534
  113.1 3.8 %block_gather.5 = bf16[1024,128]{1,0:T(8,128)(2,1)S(1)} custom-call(bf16[1024,4096]{1,0:T(8,128)(2,1)S(1)} %block_gather.3.u_ref, bf16[32,4096]{1,0:T(8,128)(2,1)S(1)} %collective-permute-done.12.refs_0_, bf16[32,4096]{1,0:T(8,128)(2,1)S(1)} %collective-permute-done.22.refs_1_, bf16[32,4096]{1,0:T(8,128)(2,1)S(1)} %collective-permute-done.13.refs_2_, ...), custom_call_target="tpu_custom_call" | custom-call | flops 1610612736 | bytes 8388608 | tf_op jit(solution)/shard_map/block_gather/pallas_call | solution.py:515
  116.9 16.9 %all_to_all.33 = bf16[128,8,128]{2,1,0:T(8,128)(2,1)S(1)} all-to-all(bf16[128,8,128]{2,1,0:T(8,128)(2,1)S(1)} %bitcast.17), channel_id=1, replica_groups=mesh['grid'=8,'band'=16] {'grid','band'}, dimensions={0} | all-to-all | bytes 524288 | tf_op jit(solution)/shard_map/ladder/all_to_all | solution.py:648
  (61 shorter events, 14.8 us)
Async XLA Ops:
  2.0 18.4 %copy-start.10 = (bf16[1,128,256]{2,1,0:T(8,128)(2,1)S(1)}, bf16[1,128,256]{2,1,0:T(8,128)(2,1)}, u32[]{:S(2)}) copy-start(bf16[1,128,256]{2,1,0:T(8,128)(2,1)} %param.15) | copy-start | bytes 196612
  5.2 13.5 %copy-start = (bf16[3,8,4096]{2,1,0:T(8,128)(2,1)}, bf16[3,8,4096]{2,1,0:T(8,128)(2,1)S(1)}, u32[]{:S(2)}) copy-start(bf16[3,8,4096]{2,1,0:T(8,128)(2,1)S(1)} %get-tuple-element.34.sent_orbitals) | copy-start | bytes 589828
  5.3 28.9 %copy-start.8 = (s32[1,2]{1,0:T(1,128)S(1)}, s32[1,2]{1,0:T(1,128)}, u32[]{:S(2)}) copy-start(s32[1,2]{1,0:T(1,128)} %pairs_ref.7) | copy-start | bytes 28
  5.3 4.8 %collective-permute-start.2 = (bf16[8,8,4096]{2,1,0:T(8,128)(2,1)S(1)}, bf16[8,8,4096]{2,1,0:T(8,128)(2,1)S(1)}, u32[]{:S(2)}, u32[]{:S(2)}) collective-permute-start(bf16[8,8,4096]{2,1,0:T(8,128)(2,1)S(1)} %get-tuple-element.35), channel_id=1, source_target_pairs={{0,1},{1,0},{2,3},{3,2},{4,5},{5,4},{6,7},{7,6},{8,9},{9,8},{10,11... | collective-permute-start | bytes 1572872 | tf_op jit(solution)/shard_map/block_scatter/ppermute | solution.py:534
  6.8 3.3 %collective-permute-start.3 = (bf16[8,8,4096]{2,1,0:T(8,128)(2,1)S(1)}, bf16[8,8,4096]{2,1,0:T(8,128)(2,1)S(1)}, u32[]{:S(2)}, u32[]{:S(2)}) collective-permute-start(bf16[8,8,4096]{2,1,0:T(8,128)(2,1)S(1)} %get-tuple-element.36), channel_id=1, source_target_pairs={{0,1},{1,0},{2,3},{3,2},{4,5},{5,4},{6,7},{7,6},{8,9},{9,8},{10,11... | collective-permute-start | bytes 1572872 | tf_op jit(solution)/shard_map/block_scatter/ppermute | solution.py:534
  6.9 3.2 %collective-permute-start.4 = (bf16[8,8,4096]{2,1,0:T(8,128)(2,1)S(1)}, bf16[8,8,4096]{2,1,0:T(8,128)(2,1)S(1)}, u32[]{:S(2)}, u32[]{:S(2)}) collective-permute-start(bf16[8,8,4096]{2,1,0:T(8,128)(2,1)S(1)} %get-tuple-element.37), channel_id=1, source_target_pairs={{0,1},{1,0},{2,3},{3,2},{4,5},{5,4},{6,7},{7,6},{8,9},{9,8},{10,11... | collective-permute-start | bytes 1572872 | tf_op jit(solution)/shard_map/block_scatter/ppermute | solution.py:534
  7.3 2.8 %collective-permute-start.1 = (bf16[3,8,4096]{2,1,0:T(8,128)(2,1)S(1)}, bf16[3,8,4096]{2,1,0:T(8,128)(2,1)S(1)}, u32[]{:S(2)}, u32[]{:S(2)}) collective-permute-start(bf16[3,8,4096]{2,1,0:T(8,128)(2,1)S(1)} %get-tuple-element.34.sent_orbitals), channel_id=1, source_target_pairs={{0,1},{1,0},{2,3},{3,2},{4,5},{5,4},{6,7},{7,6},{8,9},{9,8},{10,11... | collective-permute-start | bytes 589832 | tf_op jit(solution)/shard_map/block_scatter/ppermute | solution.py:534
  13.1 18.7 %collective-permute-start.5 = (bf16[11,8,4096]{2,1,0:T(8,128)(2,1)}, bf16[11,8,4096]{2,1,0:T(8,128)(2,1)S(1)}, u32[]{:S(2)}, u32[]{:S(2)}) collective-permute-start(bf16[11,8,4096]{2,1,0:T(8,128)(2,1)} %get-tuple-element.41), channel_id=1, source_target_pairs={{0,2},{1,3},{2,0},{3,1},{4,6},{5,7},{6,4},{7,5},{8,10},{9,11},{10,... | collective-permute-start | bytes 2162696 | tf_op jit(solution)/shard_map/block_scatter/ppermute | solution.py:534
  16.0 18.1 %collective-permute-start.6 = (bf16[11,8,4096]{2,1,0:T(8,128)(2,1)}, bf16[11,8,4096]{2,1,0:T(8,128)(2,1)S(1)}, u32[]{:S(2)}, u32[]{:S(2)}) collective-permute-start(bf16[11,8,4096]{2,1,0:T(8,128)(2,1)} %get-tuple-element.42), channel_id=1, source_target_pairs={{0,4},{1,5},{2,6},{3,7},{4,8},{5,9},{6,10},{7,11},{8,12},{9,13},{1... | collective-permute-start | bytes 2162696 | tf_op jit(solution)/shard_map/block_scatter/ppermute | solution.py:534
  17.3 16.8 %collective-permute-start.7 = (bf16[11,8,4096]{2,1,0:T(8,128)(2,1)}, bf16[11,8,4096]{2,1,0:T(8,128)(2,1)S(1)}, u32[]{:S(2)}, u32[]{:S(2)}) collective-permute-start(bf16[11,8,4096]{2,1,0:T(8,128)(2,1)} %get-tuple-element.43), channel_id=1, source_target_pairs={{0,12},{1,13},{2,14},{3,15},{4,0},{5,1},{6,2},{7,3},{8,4},{9,5},{1... | collective-permute-start | bytes 2162696 | tf_op jit(solution)/shard_map/block_scatter/ppermute | solution.py:534
  18.8 7.6 %collective-permute-start = (bf16[8,8,4096]{2,1,0:T(8,128)(2,1)}, bf16[8,8,4096]{2,1,0:T(8,128)(2,1)S(1)}, u32[]{:S(2)}, u32[]{:S(2)}) collective-permute-start(bf16[8,8,4096]{2,1,0:T(8,128)(2,1)} %get-tuple-element.33), channel_id=1, source_target_pairs={{0,1},{1,0},{2,3},{3,2},{4,5},{5,4},{6,7},{7,6},{8,9},{9,8},{10,11... | collective-permute-start | bytes 1572872 | tf_op jit(solution)/shard_map/block_scatter/ppermute | solution.py:534
  21.4 19.8 %all-to-all-start = ((bf16[8,128,256]{2,1,0:T(8,128)(2,1)}), bf16[8,128,256]{2,1,0:T(8,128)(2,1)S(1)}, u32[]{:S(2)}, u32[]{:S(2)}) async-start(bf16[8,128,256]{2,1,0:T(8,128)(2,1)} %broadcast_in_dim.8), calls=%async_computation | async-start | bytes 1048576 | tf_op jit(solution)/shard_map/block_scatter/all_to_all | solution.py:571
  34.1 0.9 copy-start.1
  37.7 12.0 %collective-permute-start.8 = (bf16[7,8,4096]{2,1,0:T(8,128)(2,1)}, bf16[7,8,4096]{2,1,0:T(8,128)(2,1)}, u32[]{:S(2)}, u32[]{:S(2)}) collective-permute-start(bf16[7,8,4096]{2,1,0:T(8,128)(2,1)} %get-tuple-element.44), channel_id=1, source_target_pairs={{0,8},{1,9},{2,10},{3,11},{4,12},{5,13},{6,14},{7,15},{8,0},{9,1},... | collective-permute-start | bytes 1376264 | tf_op jit(solution)/shard_map/block_scatter/ppermute | solution.py:534
  40.1 26.9 %copy-start.3 = (bf16[256,256]{1,0:T(8,128)(2,1)S(1)}, bf16[256,256]{1,0:T(8,128)(2,1)}, u32[]{:S(2)}) copy-start(bf16[256,256]{1,0:T(8,128)(2,1)} %constant.22.clone.turn_ref) | copy-start | bytes 393220
  40.1 11.3 %collective-permute-start.9 = (bf16[7,8,4096]{2,1,0:T(8,128)(2,1)}, bf16[7,8,4096]{2,1,0:T(8,128)(2,1)}, u32[]{:S(2)}, u32[]{:S(2)}) collective-permute-start(bf16[7,8,4096]{2,1,0:T(8,128)(2,1)} %get-tuple-element.45), channel_id=1, source_target_pairs={{0,2},{1,3},{2,0},{3,1},{4,6},{5,7},{6,4},{7,5},{8,10},{9,11},{10,... | collective-permute-start | bytes 1376264 | tf_op jit(solution)/shard_map/block_scatter/ppermute | solution.py:534
  55.7 11.2 %all-to-all-start.1 = ((bf16[8,64,256]{2,1,0:T(8,128)(2,1)}), bf16[8,64,256]{2,1,0:T(8,128)(2,1)}, u32[]{:S(2)}, u32[]{:S(2)}) async-start(bf16[8,64,256]{2,1,0:T(8,128)(2,1)} %bitcast.18), calls=%async_computation.1 | async-start | bytes 524288 | tf_op jit(solution)/shard_map/transform/all_to_all | solution.py:594
  82.5 15.9 %collective-permute-start.10 = (bf16[32,4096]{1,0:T(8,128)(2,1)S(1)}, bf16[32,4096]{1,0:T(8,128)(2,1)S(1)}, u32[]{:S(2)}, u32[]{:S(2)}) collective-permute-start(bf16[32,4096]{1,0:T(8,128)(2,1)S(1)} %bitcast.9), channel_id=1, source_target_pairs={{0,8},{1,9},{2,10},{3,11},{4,12},{5,13},{6,14},{7,15},{8,0},{9,1},... | collective-permute-start | bytes 786440 | tf_op jit(solution)/shard_map/block_gather/ppermute | solution.py:534
  83.6 14.8 %collective-permute-start.11 = (bf16[32,4096]{1,0:T(8,128)(2,1)S(1)}, bf16[32,4096]{1,0:T(8,128)(2,1)S(1)}, u32[]{:S(2)}, u32[]{:S(2)}) collective-permute-start(bf16[32,4096]{1,0:T(8,128)(2,1)S(1)} %bitcast.10), channel_id=1, source_target_pairs={{0,2},{1,3},{2,0},{3,1},{4,6},{5,7},{6,4},{7,5},{8,10},{9,11},{10,... | collective-permute-start | bytes 786440 | tf_op jit(solution)/shard_map/block_gather/ppermute | solution.py:534
  85.0 14.0 %collective-permute-start.17 = (bf16[32,4096]{1,0:T(8,128)(2,1)S(1)}, bf16[32,4096]{1,0:T(8,128)(2,1)S(1)}, u32[]{:S(2)}, u32[]{:S(2)}) collective-permute-start(bf16[32,4096]{1,0:T(8,128)(2,1)S(1)} %bitcast.11), channel_id=1, source_target_pairs={{0,4},{1,5},{2,6},{3,7},{4,8},{5,9},{6,10},{7,11},{8,12},{9,13},{1... | collective-permute-start | bytes 786440 | tf_op jit(solution)/shard_map/block_gather/ppermute | solution.py:534
  85.7 13.7 %collective-permute-start.19 = (bf16[32,4096]{1,0:T(8,128)(2,1)S(1)}, bf16[32,4096]{1,0:T(8,128)(2,1)S(1)}, u32[]{:S(2)}, u32[]{:S(2)}) collective-permute-start(bf16[32,4096]{1,0:T(8,128)(2,1)S(1)} %bitcast.12), channel_id=1, source_target_pairs={{0,12},{1,13},{2,14},{3,15},{4,0},{5,1},{6,2},{7,3},{8,4},{9,5},{1... | collective-permute-start | bytes 786440 | tf_op jit(solution)/shard_map/block_gather/ppermute | solution.py:534
  87.7 11.8 %collective-permute-start.15 = (bf16[32,4096]{1,0:T(8,128)(2,1)S(1)}, bf16[32,4096]{1,0:T(8,128)(2,1)S(1)}, u32[]{:S(2)}, u32[]{:S(2)}) collective-permute-start(bf16[32,4096]{1,0:T(8,128)(2,1)S(1)} %bitcast.13), channel_id=1, source_target_pairs={{0,1},{1,0},{2,3},{3,2},{4,5},{5,4},{6,7},{7,6},{8,9},{9,8},{10,11... | collective-permute-start | bytes 786440 | tf_op jit(solution)/shard_map/block_gather/ppermute | solution.py:534
  98.4 2.9 %collective-permute-start.16 = (bf16[32,4096]{1,0:T(8,128)(2,1)S(1)}, bf16[32,4096]{1,0:T(8,128)(2,1)S(1)}, u32[]{:S(2)}, u32[]{:S(2)}) collective-permute-start(bf16[32,4096]{1,0:T(8,128)(2,1)S(1)} %collective-permute-done.10.refs_2_), channel_id=1, source_target_pairs={{0,1},{1,0},{2,3},{3,2},{4,5},{5,4},{6,7},{7,6},{8,9},{9,8},{10,11... | collective-permute-start | bytes 786440 | tf_op jit(solution)/shard_map/block_gather/ppermute | solution.py:534
  98.5 3.4 %collective-permute-start.21 = (bf16[32,4096]{1,0:T(8,128)(2,1)S(1)}, bf16[32,4096]{1,0:T(8,128)(2,1)S(1)}, u32[]{:S(2)}, u32[]{:S(2)}) collective-permute-start(bf16[32,4096]{1,0:T(8,128)(2,1)S(1)} %collective-permute-done.11.refs_8_), channel_id=1, source_target_pairs={{0,1},{1,0},{2,3},{3,2},{4,5},{5,4},{6,7},{7,6},{8,9},{9,8},{10,11... | collective-permute-start | bytes 786440 | tf_op jit(solution)/shard_map/block_gather/ppermute | solution.py:534
  99.0 5.0 %collective-permute-start.18 = (bf16[32,4096]{1,0:T(8,128)(2,1)S(1)}, bf16[32,4096]{1,0:T(8,128)(2,1)S(1)}, u32[]{:S(2)}, u32[]{:S(2)}) collective-permute-start(bf16[32,4096]{1,0:T(8,128)(2,1)S(1)} %collective-permute-done.17.refs_4_), channel_id=1, source_target_pairs={{0,1},{1,0},{2,3},{3,2},{4,5},{5,4},{6,7},{7,6},{8,9},{9,8},{10,11... | collective-permute-start | bytes 786440 | tf_op jit(solution)/shard_map/block_gather/ppermute | solution.py:534
  99.5 4.5 %collective-permute-start.20 = (bf16[32,4096]{1,0:T(8,128)(2,1)S(1)}, bf16[32,4096]{1,0:T(8,128)(2,1)S(1)}, u32[]{:S(2)}, u32[]{:S(2)}) collective-permute-start(bf16[32,4096]{1,0:T(8,128)(2,1)S(1)} %collective-permute-done.19.refs_6_), channel_id=1, source_target_pairs={{0,1},{1,0},{2,3},{3,2},{4,5},{5,4},{6,7},{7,6},{8,9},{9,8},{10,11... | collective-permute-start | bytes 786440 | tf_op jit(solution)/shard_map/block_gather/ppermute | solution.py:534
  99.5 9.6 %collective-permute-start.12 = (bf16[32,4096]{1,0:T(8,128)(2,1)S(1)}, bf16[32,4096]{1,0:T(8,128)(2,1)S(1)}, u32[]{:S(2)}, u32[]{:S(2)}) collective-permute-start(bf16[32,4096]{1,0:T(8,128)(2,1)S(1)} %collective-permute-done.10.refs_2_), channel_id=1, source_target_pairs={{0,2},{1,3},{2,0},{3,1},{4,6},{5,7},{6,4},{7,5},{8,10},{9,11},{10,... | collective-permute-start | bytes 786440 | tf_op jit(solution)/shard_map/block_gather/ppermute | solution.py:534
  101.3 8.3 %collective-permute-start.13 = (bf16[32,4096]{1,0:T(8,128)(2,1)S(1)}, bf16[32,4096]{1,0:T(8,128)(2,1)S(1)}, u32[]{:S(2)}, u32[]{:S(2)}) collective-permute-start(bf16[32,4096]{1,0:T(8,128)(2,1)S(1)} %collective-permute-done.11.refs_8_), channel_id=1, source_target_pairs={{0,4},{1,5},{2,6},{3,7},{4,8},{5,9},{6,10},{7,11},{8,12},{9,13},{1... | collective-permute-start | bytes 786440 | tf_op jit(solution)/shard_map/block_gather/ppermute | solution.py:534
  101.9 7.7 %collective-permute-start.14 = (bf16[32,4096]{1,0:T(8,128)(2,1)S(1)}, bf16[32,4096]{1,0:T(8,128)(2,1)S(1)}, u32[]{:S(2)}, u32[]{:S(2)}) collective-permute-start(bf16[32,4096]{1,0:T(8,128)(2,1)S(1)} %collective-permute-done.11.refs_8_), channel_id=1, source_target_pairs={{0,12},{1,13},{2,14},{3,15},{4,0},{5,1},{6,2},{7,3},{8,4},{9,5},{1... | collective-permute-start | bytes 786440 | tf_op jit(solution)/shard_map/block_gather/ppermute | solution.py:534
  109.6 2.7 %collective-permute-start.22 = (bf16[32,4096]{1,0:T(8,128)(2,1)S(1)}, bf16[32,4096]{1,0:T(8,128)(2,1)S(1)}, u32[]{:S(2)}, u32[]{:S(2)}) collective-permute-start(bf16[32,4096]{1,0:T(8,128)(2,1)S(1)} %collective-permute-done.12.refs_0_), channel_id=1, source_target_pairs={{0,1},{1,0},{2,3},{3,2},{4,5},{5,4},{6,7},{7,6},{8,9},{9,8},{10,11... | collective-permute-start | bytes 786440 | tf_op jit(solution)/shard_map/block_gather/ppermute | solution.py:534
  111.2 1.5 %collective-permute-start.23 = (bf16[32,4096]{1,0:T(8,128)(2,1)S(1)}, bf16[32,4096]{1,0:T(8,128)(2,1)S(1)}, u32[]{:S(2)}, u32[]{:S(2)}) collective-permute-start(bf16[32,4096]{1,0:T(8,128)(2,1)S(1)} %collective-permute-done.13.refs_2_), channel_id=1, source_target_pairs={{0,1},{1,0},{2,3},{3,2},{4,5},{5,4},{6,7},{7,6},{8,9},{9,8},{10,11... | collective-permute-start | bytes 786440 | tf_op jit(solution)/shard_map/block_gather/ppermute | solution.py:534
  111.2 1.9 %collective-permute-start.24 = (bf16[32,4096]{1,0:T(8,128)(2,1)S(1)}, bf16[32,4096]{1,0:T(8,128)(2,1)S(1)}, u32[]{:S(2)}, u32[]{:S(2)}) collective-permute-start(bf16[32,4096]{1,0:T(8,128)(2,1)S(1)} %collective-permute-done.14.refs_4_), channel_id=1, source_target_pairs={{0,1},{1,0},{2,3},{3,2},{4,5},{5,4},{6,7},{7,6},{8,9},{9,8},{10,11... | collective-permute-start | bytes 786440 | tf_op jit(solution)/shard_map/block_gather/ppermute | solution.py:534
  (6 other events, 4.4 us)

commit v3 on v2

--- a/solution.py
+++ b/solution.py
@@ -96,28 +96,34 @@
     return waits
 
 
-def through(bounce, sems, jobs, between=None):
+def through(bounce, sems, jobs, start=None):
     inner, row = [], 0
     for target, choices in jobs:
         inner.append((bounce.at[row : row + target.shape[0]], choices))
         row += target.shape[0]
     moves = copies(sems, inner)
-    out = between() if between else []
+    finish = start() if start else None
+    out = []
     for slot, move in enumerate(moves):
         move.wait()
         target = jobs[slot][0]
         out.append(pltpu.make_async_copy(inner[slot][0], target, sems.at[len(jobs) + slot]))
         out[-1].start()
+    if finish:
+        out += finish()
     wait_all(out)
 
 
 def added(marks, sems, groups):
-    def between():
+    def start():
         moves, slot = [], 0
         for sources, _ in groups:
             part = [(marks.at[slot + i : slot + i + 1], [(None, v)]) for i, v in enumerate(sources)]
             moves.append((slot, copies(sems.at[slot : slot + len(part)], part)))
             slot += len(part)
+        return functools.partial(finish, moves, slot)
+
+    def finish(moves, slot):
         out = []
         for (first, waits), (sources, targets) in zip(moves, groups, strict=True):
             wait_all(waits)
@@ -131,7 +137,7 @@
                 slot += 1
         return out
 
-    return between
+    return start
 
 
 def wait_all(waits):
@@ -164,10 +170,19 @@
         return self.occupied.at[pl.ds(self.local[k], 1)]
 
 
-def send_core_body(
-    ablock_ref, pairs_ref, kept_ref, fields, occupied, up, down, across, stay, orbitals, bounce, marks, sems
-):
-    def between():
+def core_a_body(ablock_ref, pairs_ref, kept_hbm, fields, occupied, out, bounce, marks, kept_ref, sems):
+    at = Roots(ablock_ref, pairs_ref, fields, occupied)
+    other, there = 1 - at.c, 1 - at.h
+    sources = [at.block(other, dy, there, 4) for dy in (1, 3, 2)]
+    jobs = [(out.at[4 * i : 4 * i + 4], [(None, v)]) for i, v in enumerate(sources)]
+    jobs.append((out.at[12:13], [(None, at.orbital(0))]))
+
+    def start():
+        (wait,) = copies(sems.at[9:], [(kept_ref, [(None, kept_hbm)])])
+        return functools.partial(finish, wait)
+
+    def finish(wait):
+        wait.wait()
         kept = kept_ref[...]
         in_x = (lax.broadcasted_iota(jnp.int32, (N, kept.shape[1]), 0) == kept // 16).astype(BF16)
         in_c = lax.broadcasted_iota(jnp.int32, (128, kept.shape[1]), 0) % 16 == kept % 16
@@ -178,75 +193,62 @@
         lane = lax.broadcasted_iota(jnp.int32, mask.shape, 1)
         mask = jnp.where(row % XL == lane // 16, mask, 0.0)
         tile = jnp.sum(mask.reshape(XL, XL, 128), axis=1)
-        here = lax.axis_index("band")
-        tiles = [jnp.where(here == n, tile, 0.0) for n in range(2 * BAND)]
+        band = lax.axis_index("band")
+        tiles = [jnp.where(band == n, tile, 0.0) for n in range(2 * BAND)]
         marks[0] = jnp.concatenate(tiles, axis=1).astype(BF16)
-        move = pltpu.make_async_copy(marks, orbitals.at[2:], sems.at[16])
+        move = pltpu.make_async_copy(marks, out.at[13:], sems.at[8])
         move.start()
         return [move]
 
+    through(bounce, sems, jobs, start)
+
+
+def core_b_body(ablock_ref, pairs_ref, fields, occupied, out, bounce, sems):
     at = Roots(ablock_ref, pairs_ref, fields, occupied)
     other, here, there = 1 - at.c, at.h, 1 - at.h
-    jobs = [
-        (up, at.block(other, 1, 0, 8)),
-        (down, at.block(other, 3, 0, 8)),
-        (across.at[:4], at.block(other, 0, there, 4)),
-        (across.at[4:], at.block(other, 2, there, 4)),
-        (orbitals.at[:1], at.orbital(0)),
-        (orbitals.at[1:2], at.orbital(1)),
-        (stay.at[:4], at.block(other, 0, here, 4)),
-        (stay.at[4:], at.block(other, 2, here, 4)),
-    ]
-    through(bounce, sems, [(t, [(None, v)]) for t, v in jobs], between)
-
-
-def send_first_body(
+    sources = [at.block(other, dy, h, 4) for dy, h in ((1, here), (3, here), (0, there), (2, here), (0, here))]
+    jobs = [(out.at[4 * i : 4 * i + 4], [(None, v)]) for i, v in enumerate(sources)]
+    jobs.append((out.at[20:], [(None, at.orbital(1))]))
+    through(bounce, sems, jobs)
+
+
+def first_a_body(
+    ablock_ref, pairs_ref, fields, occupied, sent_a, got_a, up, down, across, bounce, marks, sems
+):
+    at = Roots(ablock_ref, pairs_ref, fields, occupied)
+    mine, theirs = at.same_c[0], jnp.logical_not(at.same_c[0])
+    jobs = []
+    for i, (target, dy) in enumerate(((up, 1), (down, 3), (across, 2))):
+        own = at.block(at.c, dy, 1 - at.h, 4)
+        jobs.append((target.at[:4], [(mine, own), (theirs, got_a.at[4 * i : 4 * i + 4])]))
+    mine, theirs = at.same_c[1], jnp.logical_not(at.same_c[1])
+    for target in (up, down, across):
+        jobs.append((target.at[4:5], [(mine, at.orbital(0)), (theirs, got_a.at[12:13])]))
+    groups = [([sent_a.at[13:], got_a.at[13:]], [v.at[5:] for v in (up, down, across)])]
+    through(bounce, sems, jobs, added(marks, sems.at[12:], groups))
+
+
+def first_b_body(ablock_ref, pairs_ref, fields, occupied, got_b, up, down, across, bounce, sems):
+    at = Roots(ablock_ref, pairs_ref, fields, occupied)
+    mine, theirs = at.same_c[0], jnp.logical_not(at.same_c[0])
+    jobs = []
+    for i, (target, dy, h) in enumerate(((up, 1, at.h), (down, 3, at.h), (across, 0, 1 - at.h))):
+        own = at.block(at.c, dy, h, 4)
+        jobs.append((target.at[:4], [(mine, own), (theirs, got_b.at[4 * i : 4 * i + 4])]))
+    mine, theirs = at.same_c[2], jnp.logical_not(at.same_c[2])
+    for target in (up, down, across):
+        jobs.append((target.at[4:], [(mine, at.orbital(1)), (theirs, got_b.at[20:])]))
+    through(bounce, sems, jobs)
+
+
+def second_a_body(
     ablock_ref,
     pairs_ref,
     fields,
     occupied,
-    got_up,
-    got_down,
-    got_across,
-    sent_orbitals,
-    got_orbitals,
-    up,
-    down,
-    across,
-    bounce,
-    marks,
-    sems,
-):
-    at = Roots(ablock_ref, pairs_ref, fields, occupied)
-    there = 1 - at.h
-    mine, theirs = at.same_c[0], jnp.logical_not(at.same_c[0])
-    jobs = [
-        (up.at[:8], [(mine, at.block(at.c, 1, 0, 8)), (theirs, got_up)]),
-        (down.at[:8], [(mine, at.block(at.c, 3, 0, 8)), (theirs, got_down)]),
-        (across.at[:4], [(mine, at.block(at.c, 0, there, 4)), (theirs, got_across.at[:4])]),
-        (across.at[4:8], [(mine, at.block(at.c, 2, there, 4)), (theirs, got_across.at[4:])]),
-    ]
-    for target in (up, down, across):
-        for k in range(2):
-            own = at.same_c[1 + k]
-            jobs.append(
-                (
-                    target.at[8 + k : 9 + k],
-                    [(own, at.orbital(k)), (jnp.logical_not(own), got_orbitals.at[k : k + 1])],
-                )
-            )
-    groups = [([sent_orbitals.at[2:], got_orbitals.at[2:]], [v.at[10:] for v in (up, down, across)])]
-    through(bounce, sems, jobs, added(marks, sems.at[20:], groups))
-
-
-def send_second_body(
-    ablock_ref,
-    pairs_ref,
-    fields,
-    occupied,
-    got_stay,
-    sent_orbitals,
-    got_orbitals,
+    sent_a,
+    got_a,
+    got_b,
     crossed,
     below,
     above,
@@ -258,44 +260,73 @@
 ):
     at = Roots(ablock_ref, pairs_ref, fields, occupied)
     not_ = jnp.logical_not
-    here, there = at.h, 1 - at.h
-    same_h, same_c = at.same_h[0], at.same_c[0]
-    jobs = [
-        (
-            far.at[:4],
-            [
-                (same_h & same_c, at.block(at.c, 2, here, 4)),
-                (same_h & not_(same_c), got_stay.at[4:]),
-                (not_(same_h), crossed.at[4:8]),
-            ],
-        ),
-        (
-            turn.at[:4],
-            [
-                (at.away[0] == 1, below.at[pl.ds(4 * there, 4)]),
-                (at.away[0] != 1, above.at[pl.ds(4 * there, 4)]),
-            ],
-        ),
+    jobs = []
+    own_rows = (at.block(at.c, 2, at.h, 4), got_b.at[12:16], slice(0, 4))
+    own_orbital = (at.orbital(0), got_a.at[12:13], slice(4, 5))
+    for k, (own, core, part) in enumerate((own_rows, own_orbital)):
+        same_h, same_c = at.same_h[k], at.same_c[k]
+        choices = [(same_h & same_c, own), (same_h & not_(same_c), core), (not_(same_h), crossed.at[part])]
+        jobs.append((far.at[part], choices))
+        from_below = at.away[k] == 1
+        jobs.append((turn.at[part], [(from_below, below.at[part]), (not_(from_below), above.at[part])]))
+    groups = [
+        ([sent_a.at[13:], got_a.at[13:], crossed.at[5:]], [far.at[5:]]),
+        ([below.at[5:], above.at[5:]], [turn.at[5:]]),
     ]
-    for k in range(2):
-        same_h, same_c, away = at.same_h[1 + k], at.same_c[1 + k], at.away[1 + k]
-        row = slice(8 + k, 9 + k)
-        jobs.append(
-            (
-                far.at[4 + k : 5 + k],
-                [
-                    (same_h & same_c, at.orbital(k)),
-                    (same_h & not_(same_c), got_orbitals.at[k : k + 1]),
-                    (not_(same_h), crossed.at[row]),
-                ],
-            )
-        )
-        jobs.append((turn.at[4 + k : 5 + k], [(away == 1, below.at[row]), (away != 1, above.at[row])]))
-    groups = [
-        ([sent_orbitals.at[2:], got_orbitals.at[2:], crossed.at[10:]], [far.at[6:]]),
-        ([below.at[10:], above.at[10:]], [turn.at[6:]]),
+    through(bounce, sems, jobs, added(marks, sems.at[8:], groups))
+
+
+def second_b_body(
+    ablock_ref,
+    pairs_ref,
+    fields,
+    occupied,
+    got_b,
+    crossed,
+    below,
+    above,
+    amp_hbm,
+    far,
+    turn,
+    amp_out,
+    bounce,
+    amp_ref,
+    sems,
+):
+    at = Roots(ablock_ref, pairs_ref, fields, occupied)
+    not_ = jnp.logical_not
+    same_h, same_c, from_below = at.same_h[2], at.same_c[2], at.away[2] == 1
+    choices = [
+        (same_h & same_c, at.orbital(1)),
+        (same_h & not_(same_c), got_b.at[20:]),
+        (not_(same_h), crossed.at[4:]),
     ]
-    through(bounce, sems, jobs, added(marks, sems.at[12:], groups))
+    jobs = [(far, choices), (turn, [(from_below, below.at[4:]), (not_(from_below), above.at[4:])])]
+    (amp_wait,) = copies(sems.at[4:], [(amp_ref, [(None, amp_hbm.at[0])])])
+    through(bounce, sems, jobs)
+    amp_wait.wait()
+    row = lax.broadcasted_iota(jnp.int32, (128, 256), 0)
+    col = lax.broadcasted_iota(jnp.int32, (128, 256), 1)
+    over_c = (((1,), (1,)), ((), ()))
+    parity = [
+        lax.dot_general((col == 2 * row + p).astype(BF16), amp_ref[...], over_c, preferred_element_type=F32)
+        for p in range(2)
+    ]
+    amp_out[...] = jnp.concatenate(parity, axis=1).astype(BF16)
+
+
+def arrived(at, k, own, core, cross, far, below, above, turned):
+    not_ = jnp.logical_not
+    away, same_h, same_c = at.away[k], at.same_h[k], at.same_c[k]
+    return [
+        ((away == 0) & same_h & same_c, own),
+        ((away == 0) & same_h & not_(same_c), core),
+        ((away == 0) & not_(same_h), cross),
+        (away == 2, far),
+        ((away == 1) & same_h, below),
+        ((away == 3) & same_h, above),
+        ((away % 2 == 1) & not_(same_h), turned),
+    ]
 
 
 def forward_body(
@@ -303,69 +334,37 @@
     pairs_ref,
     fields,
     occupied,
-    got_stay,
-    got_orbitals,
-    crossed,
-    below,
-    above,
+    got_a,
+    got_b,
+    crossed_a,
+    below_a,
+    above_a,
+    crossed_b,
+    below_b,
+    above_b,
     far,
     turned,
+    amp_hbm,
     mz_hbm,
     ky_hbm,
-    out_ref,
-    second_ref,
+    out_hbm,
     u_ref,
     o_ref,
     mz_ref,
     ky_ref,
+    out_ref,
+    amp_ref,
     sems,
 ):
     at = Roots(ablock_ref, pairs_ref, fields, occupied)
-    not_ = jnp.logical_not
-
-    def arrived(k, rows_far, near_own, near_core, near_cross, side, side_turned):
-        away, same_h, same_c = at.away[k], at.same_h[k], at.same_c[k]
-        return [
-            ((away == 0) & same_h & same_c, near_own),
-            ((away == 0) & same_h & not_(same_c), near_core),
-            ((away == 0) & not_(same_h), near_cross),
-            (away == 2, rows_far),
-            ((away == 1) & same_h, below.at[side]),
-            ((away == 3) & same_h, above.at[side]),
-            ((away % 2 == 1) & not_(same_h), side_turned),
-        ]
-
+    rows = [v.at[:4] for v in (crossed_b, far, below_b, above_b, turned)]
+    orbital = [v.at[4:5] for v in (crossed_a, far, below_a, above_a, turned)]
     jobs = [
-        (
-            u_ref,
-            arrived(
-                0,
-                far.at[:4],
-                at.block(at.c, 0, at.h, 4),
-                got_stay.at[:4],
-                crossed.at[:4],
-                pl.ds(4 * at.h, 4),
-                turned.at[:4],
-            ),
-        )
+        (u_ref, arrived(at, 0, at.block(at.c, 0, at.h, 4), got_b.at[16:20], *rows)),
+        (o_ref, arrived(at, 1, at.orbital(0), got_a.at[12:13], *orbital)),
     ]
-    for k, target in enumerate((o_ref, second_ref)):
-        jobs.append(
-            (
-                target,
-                arrived(
-                    1 + k,
-                    far.at[4 + k : 5 + k],
-                    at.orbital(k),
-                    got_orbitals.at[k : k + 1],
-                    crossed.at[8 + k : 9 + k],
-                    pl.ds(8 + k, 1),
-                    turned.at[4 + k : 5 + k],
-                ),
-            )
-        )
-    jobs += [(mz_ref, [(None, mz_hbm)]), (ky_ref, [(None, ky_hbm)])]
-    u_wait, o_wait, second_wait, mz_wait, ky_wait = copies(sems, jobs)
+    jobs += [(mz_ref, [(None, mz_hbm)]), (ky_ref, [(None, ky_hbm)]), (amp_ref, [(None, amp_hbm)])]
+    u_wait, o_wait, mz_wait, ky_wait, amp_wait = copies(sems, jobs)
     u_wait.wait()
     o_wait.wait()
     orbital = o_ref[0].astype(F32)
@@ -380,41 +379,82 @@
     zfreq = dot(density, mz_ref[...]).astype(BF16)
     stacked = jnp.concatenate([zfreq[:, 256 * i : 256 * (i + 1)] for i in range(4)], axis=0)
     ky_wait.wait()
+    amp_wait.wait()
+    jobs = [(out_hbm.at[g, pl.ds(64, 128)], [(None, amp_ref)]) for g in range(GRID)]
+    out_waits = copies(sems.at[5:], jobs)
     out_ref[...] = dot(ky_ref[...], stacked).astype(BF16)
-    second_wait.wait()
-
-
-def middle_body(y_ref, weight_ref, turn_ref, kx_hbm, kxt_hbm, out_ref, kx_ref, kxt_ref, sems):
-    kx_wait, kxt_wait = copies(sems, [(kx_ref, [(None, kx_hbm)]), (kxt_ref, [(None, kxt_hbm)])])
+    jobs = [(out_hbm.at[g, pl.ds(0, 64)], [(None, out_ref.at[pl.ds(64 * g, 64)])]) for g in range(GRID)]
+    wait_all(out_waits + copies(sems.at[13:], jobs))
+
+
+def middle_body(
+    y_hbm, weight_ref, turn_hbm, kx_hbm, kxt_hbm, out_hbm, y_ref, turn_ref, kx_ref, kxt_ref, out_ref, sems
+):
+    jobs = [(y_ref, y_hbm.at[:, pl.ds(0, 64)]), (turn_ref, turn_hbm), (kx_ref, kx_hbm), (kxt_ref, kxt_hbm)]
+    y_wait, turn_wait, kx_wait, kxt_wait = copies(sems, [(t, [(None, v)]) for t, v in jobs])
+    weights = jnp.concatenate([weight_ref[...], weight_ref[...]], axis=1)
+    y_wait.wait()
+    turn_wait.wait()
     turn = turn_ref[...]
-    yfreq = y_ref[...]
+    yfreq = y_ref[...].reshape(512, 256)
     both = jnp.concatenate([yfreq, dot(yfreq, turn).astype(BF16)], axis=0)
-    weights = jnp.concatenate([weight_ref[...], weight_ref[...]], axis=1)
     kx_wait.wait()
     potential = (dot(kx_ref[...], both) * weights).astype(BF16)
     both = jnp.concatenate([potential, dot(potential, turn).astype(BF16)], axis=0)
     kxt_wait.wait()
     out_ref[...] = dot(kxt_ref[...], both).astype(BF16)
-
-
-def backward_body(h_ref, o_ref, turn_ref, kyt_hbm, mzt_hbm, out_ref, kyt_ref, mzt_ref, sems):
-    kyt_wait, mzt_wait = copies(sems, [(kyt_ref, [(None, kyt_hbm)]), (mzt_ref, [(None, mzt_hbm)])])
-    orbital = o_ref[0].astype(F32)
+    wait_all(copies(sems.at[4:], [(out_hbm, [(None, out_ref)])]))
+
+
+def backward_body(
+    ablock_ref,
+    pairs_ref,
+    fields,
+    occupied,
+    got_b,
+    crossed,
+    below,
+    above,
+    far,
+    turned,
+    turn_hbm,
+    kyt_hbm,
+    mzt_hbm,
+    h_ref,
+    out_ref,
+    o_ref,
+    turn_ref,
+    kyt_ref,
+    mzt_ref,
+    sems,
+):
+    at = Roots(ablock_ref, pairs_ref, fields, occupied)
+    rows = [v.at[4:] for v in (crossed, below, above)]
+    own, core = at.orbital(1), got_b.at[20:]
+    jobs = [
+        (o_ref, arrived(at, 2, own, core, rows[0], far, rows[1], rows[2], turned)),
+        (turn_ref, [(None, turn_hbm)]),
+        (kyt_ref, [(None, kyt_hbm)]),
+        (mzt_ref, [(None, mzt_hbm)]),
+    ]
+    o_wait, turn_wait, kyt_wait, mzt_wait = copies(sems, jobs)
     freq = h_ref[...]
+    turn_wait.wait()
     both = jnp.concatenate([freq, dot(freq, turn_ref[...]).astype(BF16)], axis=0)
     kyt_wait.wait()
     zfreq = dot(kyt_ref[...], both).astype(BF16)
     zfreq = jnp.concatenate([zfreq[:256], zfreq[256:]], axis=1)
     mzt_wait.wait()
     value = dot(zfreq, mzt_ref[...])
+    o_wait.wait()
+    orbital = o_ref[0].astype(F32)
     for a in range(SHARE):
         rows = [value[8 * j : 8 * (j + 1), 128 * a : 128 * (a + 1)] for j in range(PAIRS_Y)]
         out_ref[a] = (jnp.concatenate(rows, axis=1) * orbital).astype(BF16)
 
 
-def weight_body(sent_orbitals, got_orbitals, crossed, below, above, far, turned, out_ref, marks, sems):
-    sources = [sent_orbitals.at[2:], got_orbitals.at[2:], crossed.at[10:], below.at[10:], above.at[10:]]
-    sources += [far.at[6:], turned.at[6:]]
+def weight_body(sent_a, got_a, crossed, below, above, far, turned, out_ref, marks, sems):
+    sources = [sent_a.at[13:], got_a.at[13:]] + [v.at[5:] for v in (crossed, below, above, far, turned)]
     wait_all(copies(sems, [(marks.at[i : i + 1], [(None, v)]) for i, v in enumerate(sources)]))
     total = sum(marks[i].astype(F32) for i in range(len(sources)))
     tiles = jnp.concatenate([total[:, 128 * n : 128 * (n + 1)] for n in range(BAND)], axis=0).astype(BF16)
@@ -447,7 +487,7 @@
 PLANE = (XL, N * N)
 
 
-def call(body, spaces, outs, out_spaces, scratch, args, dtype=BF16):
+def call(body, spaces, outs, out_spaces, scratch, args, dtype=BF16, flops=10**8):
     many = len(outs) > 1
     shapes = [jax.ShapeDtypeStruct(o, dtype) for o in outs]
     specs = [pl.BlockSpec(memory_space=m) for m in out_spaces]
@@ -458,6 +498,7 @@
         out_specs=specs if many else specs[0],
         scratch_shapes=scratch,
         compiler_params=pltpu.CompilerParams(vmem_limit_bytes=VMEM_LIMIT),
+        cost_estimate=pl.CostEstimate(flops=flops, bytes_accessed=2**20, transcendentals=0),
     )(*args)
 
 
@@ -502,7 +543,7 @@
         )
         high = slab.astype(BF16)
         low = (slab - high.astype(F32)).astype(BF16)
-        amp = extra[1][...].reshape(1024, 256)
+        amp = extra[1][:, pl.ds(64, 128)].reshape(1024, 256)
         out_ref[...] = (dot(amp, high) + dot(amp, low)).astype(BF16)
 
 
@@ -536,87 +577,126 @@
 
 def per_device(virtual_field, occupied_field, amplitudes, ablock, pairs, kept_cells):
     far_memory = lambda v: pltpu.with_memory_space_constraint(v, HBM)
-    const = {n: jnp.asarray(v) if n == "turn" else far_memory(jnp.asarray(v)) for n, v in tables().items()}
+    const = {n: far_memory(jnp.asarray(v)) for n, v in tables().items()}
     roots = (ablock, pairs, far_memory(virtual_field), far_memory(occupied_field))
     root_spaces = [SMEM, SMEM, pl.ANY, pl.ANY]
 
     with jax.named_scope("block_scatter"):
         sems = lambda n: [pltpu.SemaphoreType.DMA((n,))]
-        bounce = lambda n, marks, k: [VMEM((n,) + PLANE, BF16), VMEM((marks,) + PLANE, BF16)] + sems(k)
-        eight = (8,) + PLANE
-        sent = call(
-            send_core_body,
-            [SMEM, SMEM, VMEM, pl.ANY, pl.ANY],
-            [eight] * 4 + [(3,) + PLANE],
-            [pl.ANY] * 5,
-            bounce(34, 1, 17),
-            roots[:2] + (kept_cells,) + roots[2:],
-        )
-        order = (0, 1, 2, 4, 3)
-        got = {k: band_shift(sent[k], 0, 0, 1) for k in order}
-        sent_orbitals = sent[4]
-        sent = call(
-            send_first_body,
-            root_spaces + [pl.ANY] * 5,
-            [(11,) + PLANE] * 3,
-            [pl.ANY] * 3,
-            bounce(30, 2, 25),
-            roots + (got[0], got[1], got[2], sent_orbitals, got[4]),
-        )
-        sent, amp = lax.optimization_barrier((sent, amplitudes[0]))
-        amp = jnp.broadcast_to(amp.T.reshape(1, 128, 256), (GRID, 128, 256))
-        crossed = band_shift(sent[2], 0, 1, 0)
-        below = band_shift(sent[0], 1, 0, 0)
-        above = band_shift(sent[1], 3, 0, 0)
-        amp = lax.all_to_all(amp, "grid", 0, 0, tiled=True)
-        sent = call(
-            send_second_body,
-            root_spaces + [pl.ANY] * 6,
-            [(7,) + PLANE] * 2,
-            [pl.ANY] * 2,
-            bounce(12, 5, 19),
-            roots + (got[3], sent_orbitals, got[4], crossed, below, above),
-        )
-        far = band_shift(sent[0], 2, 0, 0)
-        turned = band_shift(sent[1], 0, 1, 0)
-        far, turned, amp = lax.optimization_barrier((far, turned, amp))
+        rows = lambda n: (n,) + PLANE
+        held = lambda n: VMEM(rows(n), BF16)
+        hop = lambda body, spaces, out, scratch, *args, flops=10**8: call(
+            body, spaces, out, [pl.ANY] * len(out), scratch, args, flops=flops
+        )
+        any_ = [pl.ANY]
+        sent_a = hop(
+            core_a_body,
+            root_spaces[:2] + any_ * 3,
+            [rows(14)],
+            [held(13), held(1), VMEM(kept_cells.shape, jnp.int32)] + sems(10),
+            *roots[:2],
+            far_memory(kept_cells),
+            *roots[2:],
+        )
+        got_a = band_shift(sent_a, 0, 0, 1)
+        sent_b = call(
+            core_b_body, root_spaces, [rows(21)], any_, [held(21)] + sems(12), roots, flops=5 * 10**9
+        )
+        up, down, across = hop(
+            first_a_body,
+            root_spaces + any_ * 2,
+            [rows(6)] * 3,
+            [held(15), held(2)] + sems(17),
+            *roots,
+            sent_a,
+            got_a,
+        )
+        up, down, across, sent_b = lax.optimization_barrier((up, down, across, sent_b))
+        below_a = band_shift(up, 1, 0, 0)
+        above_a = band_shift(down, 3, 0, 0)
+        crossed_a = band_shift(across, 0, 1, 0)
+        got_b = band_shift(sent_b, 0, 0, 1)
+        up, down, across = hop(
+            first_b_body, root_spaces + any_, [rows(5)] * 3, [held(15)] + sems(12), *roots, got_b
+        )
+        below_b = band_shift(up, 1, 0, 0)
+        above_b = band_shift(down, 3, 0, 0)
+        crossed_b = band_shift(across, 0, 1, 0)
+        crossed_a, below_a, above_a, _ = lax.optimization_barrier((crossed_a, below_a, above_a, (up, down, across)))
+        far, turn = hop(
+            second_a_body,
+            root_spaces + any_ * 6,
+            [rows(6)] * 2,
+            [held(10), held(5)] + sems(15),
+            *roots,
+            sent_a,
+            got_a,
+            got_b,
+            crossed_a,
+            below_a,
+            above_a,
+            flops=10**10,
+        )
+        far_a = band_shift(far, 2, 0, 0)
+        turned_a = band_shift(turn, 0, 1, 0)
+        crossed_b, below_b, above_b, _ = lax.optimization_barrier((crossed_b, below_b, above_b, (far, turn)))
+        far, turn, amp = call(
+            second_b_body,
+            root_spaces + any_ * 5,
+            [rows(1), rows(1), (128, 256)],
+            any_ * 2 + [VMEM],
+            [held(2), VMEM((128, 256), BF16)] + sems(5),
+            (*roots, got_b, crossed_b, below_b, above_b, far_memory(amplitudes)),
+            flops=10**10,
+        )
+        far_b = band_shift(far, 2, 0, 0)
+        turned_b = band_shift(turn, 0, 1, 0)
+        far_a, turned_a, amp = lax.optimization_barrier((far_a, turned_a, amp))
 
     with jax.named_scope("transform"):
         big = VMEM((512, 1024), BF16)
-        freq, second = call(
+        from_all = (GRID, 64 + 128, 256)
+        freq = call(
             forward_body,
-            root_spaces + [pl.ANY] * 9,
-            [(512, 256), (1,) + PLANE],
-            [VMEM, VMEM],
-            [VMEM((SHARE,) + PLANE, BF16), VMEM((1,) + PLANE, BF16), big, big] + sems(5),
-            roots + (got[3], got[4], crossed, below, above, far, turned, const["mz"], const["ky"]),
+            root_spaces + any_ * 13,
+            [from_all],
+            any_,
+            [held(SHARE), held(1), big, big, VMEM((512, 256), BF16), VMEM((128, 256), BF16)] + sems(21),
+            roots
+            + (got_a, got_b, crossed_a, below_a, above_a, crossed_b, below_b, above_b, far_a, turned_a)
+            + (amp, const["mz"], const["ky"]),
+            flops=2 * 10**10,
         )
         freq = lax.all_to_all(freq, "grid", 0, 0, tiled=True)
+        amp = freq
         weights = call(
             weight_body,
-            [pl.ANY] * 7,
+            any_ * 7,
             [(N * XL, 128)],
             [VMEM],
-            [VMEM((7,) + PLANE, BF16)] + sems(7),
-            (sent_orbitals, got[4], crossed, below, above, far, turned),
+            [held(7)] + sems(7),
+            tuple(far_memory(v) for v in (sent_a, got_a, crossed_a, below_a, above_a, far_a, turned_a)),
             F32,
         )
         freq = call(
             middle_body,
-            [VMEM] * 3 + [pl.ANY] * 2,
+            any_ + [VMEM] + any_ * 3,
             [(512, 256)],
-            [VMEM],
-            [big, big] + sems(2),
+            any_,
+            [VMEM((GRID, 64, 256), BF16), VMEM((256, 256), BF16), big, big, VMEM((512, 256), BF16)] + sems(5),
             (freq, weights, const["turn"], const["kx"], const["kxt"]),
+            flops=10**10,
         )
         freq = lax.all_to_all(freq, "grid", 0, 0, tiled=True)
         potential = call(
             backward_body,
-            [VMEM] * 3 + [pl.ANY] * 2,
+            root_spaces + any_ * 9 + [VMEM],
             [(SHARE,) + PLANE],
             [VMEM],
-            [big, VMEM((512, 512), BF16)] + sems(2),
-            (freq, second, const["turn"], const["kyt"], const["mzt"]),
+            [held(1), VMEM((256, 256), BF16), big, VMEM((512, 512), BF16)] + sems(4),
+            roots
+            + tuple(far_memory(v) for v in (got_b, crossed_b, below_b, above_b, far_b, turned_b))
+            + (const["turn"], const["kyt"], const["mzt"], freq),
         )
 
     with jax.named_scope("block_gather"):

time: 135 us -> 133 us (0.985)
  blocking collectives: 25.4 us -> 19.1 us
  starting transfers between devices: 43.1 us -> 49 us
  local copies, waits for them, and re-layouts: 7.01 us -> 1.37 us
  Pallas kernels: 32.2 us -> 35.8 us
    all_to_all x1 -> x0, blocking collectives: 8.49 us -> none  [per_device(): freq = lax.all_to_all(freq, 'grid', 0, 0, tiled=True)]
    all_to_all x1 -> x2, starting transfers between devices: 5.06 us -> 11.5 us  [per_device(): freq = lax.all_to_all(freq, 'grid', 0, 0, tiled=True)]
    all_to_all x1 -> x0, starting transfers between devices: 5.06 us -> none  [per_device(): amp = lax.all_to_all(amp, 'grid', 0, 0, tiled=True)]
    ppermute x25 -> x27, waiting for transfers between devices: 22.5 us -> 17.8 us  [band_shift(): return lax.ppermute(value, 'band', pairs)]
    all_to_all x1 -> x2, waiting for transfers between devices: 3.42 us -> 8.1 us  [per_device(): freq = lax.all_to_all(freq, 'grid', 0, 0, tiled=True)]
    unnamed x22 -> x30, local copies, waits for them, and re-layouts: 5.35 us -> 0.7 us
    ppermute x25 -> x27, starting transfers between devices: 32.9 us -> 37.5 us  [band_shift(): return lax.ppermute(value, 'band', pairs)]
    pallas_call x8 -> x11, Pallas kernels: 23.3 us -> 26.9 us  [call(): pl.pallas_call(body, out_shape=shapes if many else shapes[0], in_specs=[p...]
  transfers between devices with their start and end apart: 27 -> 29, of which waited for: 10 -> 11; matrix products, arithmetic and copies ran while one was open for 1% -> 0% of each run, Pallas kernels for 10% -> 13%
where the time goes in v3:
time: 133 us; the launch traced here: 132 us
  starting transfers between devices  49 us (37%)
  Pallas kernels  35.8 us (27%)
  waiting for transfers between devices  25.9 us (19%)
  blocking collectives  19.1 us (14%)
  local copies, waits for them, and re-layouts  1.37 us (1%)
    ppermute x27, starting transfers between devices, band_shift(): return lax.ppermute(value, 'band', pairs)  37.5 us
    pallas_call x11, Pallas kernels, call(): pl.pallas_call(body, out_shape=shapes if many else shapes[0], in_specs=[p...  26.9 us
    all_to_all x1, blocking collectives, per_device(): lax.all_to_all(terms.reshape(GRID * BAND, XL, 128), ('grid', 'band'), 0,...  19.1 us
    ppermute x27, waiting for transfers between devices, band_shift(): return lax.ppermute(value, 'band', pairs)  17.8 us
    all_to_all x2, starting transfers between devices, per_device(): freq = lax.all_to_all(freq, 'grid', 0, 0, tiled=True)  11.5 us
    pallas_call x2, Pallas kernels, slab_call(): pl.pallas_call(functools.partial(slab_body, last, names), out_shape=jax.S...  8.96 us
    all_to_all x2, waiting for transfers between devices, per_device(): freq = lax.all_to_all(freq, 'grid', 0, 0, tiled=True)  8.1 us
  transfers between devices with their start and end apart: 29, of which 11 were waited for; matrix products, arithmetic and copies ran while one was open for 0% of the time, Pallas kernels for 13%

profile of v3, /device:TPU:1, one launch (start us, length us, event | category | flops | bytes accessed | tf_op | source)
XLA Modules:
  0.0 132.3 jit_solution(6152432133536785417)
XLA Ops:
  1.3 2.3 %block_scatter.6.sent_a = bf16[14,8,4096]{2,1,0:T(8,128)(2,1)S(1)} custom-call(s32[1]{0:T(128)S(6)} %copy.14.ablock_ref, s32[1,2]{1,0:T(1,128)S(1)} %copy-done.11, s32[1,512]{1,0:T(1,128)} %kept_hbm.1, bf16[128,8,4096]{2,1,0:T(8,128)(2,1)} %fields.15, bf16[16,8,4096]{2,1,0:T(8,128)(2,1)} %occupied.15), custom_call_target="tpu_custom_call" | custom-call | flops 100000000 | bytes 1048576 | tf_op jit(solution)/shard_map/block_scatter/pallas_call | solution.py:494
  3.6 1.5 %collective-permute-start = (bf16[14,8,4096]{2,1,0:T(8,128)(2,1)S(1)}, bf16[14,8,4096]{2,1,0:T(8,128)(2,1)S(1)}, u32[]{:S(2)}, u32[]{:S(2)}) collective-permute-start(bf16[14,8,4096]{2,1,0:T(8,128)(2,1)S(1)} %block_scatter.6.sent_a), channel_id=1, source_target_pairs={{0,1},{1,0},{2,3},{3,2},{4,5},{5,4},{6,7},{7,6},{8,9},{9,8},{10,11... | collective-permute-start | bytes 2752520 | tf_op jit(solution)/shard_map/block_scatter/ppermute | solution.py:575
  5.1 2.0 %block_scatter.8 = bf16[21,8,4096]{2,1,0:T(8,128)(2,1)S(1)} custom-call(s32[1]{0:T(128)S(6)} %copy.14.ablock_ref, s32[1,2]{1,0:T(1,128)S(1)} %copy-done.12, bf16[128,8,4096]{2,1,0:T(8,128)(2,1)} %fields.15, bf16[16,8,4096]{2,1,0:T(8,128)(2,1)} %occupied.15), custom_call_target="tpu_custom_call" | custom-call | flops 5000000000 | bytes 1048576 | tf_op jit(solution)/shard_map/block_scatter/pallas_call | solution.py:494
  7.2 2.1 %block_scatter.7 = (bf16[6,8,4096]{2,1,0:T(8,128)(2,1)S(1)}, bf16[6,8,4096]{2,1,0:T(8,128)(2,1)S(1)}, bf16[6,8,4096]{2,1,0:T(8,128)(2,1)S(1)}) custom-call(s32[1]{0:T(128)S(6)} %copy.14.ablock_ref, s32[1,2]{1,0:T(1,128)S(1)} %copy-done.12, bf16[128,8,4096]{2,1,0:T(8,128)(2,1)} %fields.15, bf16[16,8,4096]{2,1,0:T(8,128)(2,1)} %occupied.15, ...), custom_call_target="tpu_custom_call" | custom-call | flops 100000000 | bytes 1048576 | tf_op jit(solution)/shard_map/block_scatter/pallas_call | solution.py:494
  10.1 2.8 %collective-permute-start.5 = (bf16[6,8,4096]{2,1,0:T(8,128)(2,1)S(1)}, bf16[6,8,4096]{2,1,0:T(8,128)(2,1)S(1)}, u32[]{:S(2)}, u32[]{:S(2)}) collective-permute-start(bf16[6,8,4096]{2,1,0:T(8,128)(2,1)S(1)} %get-tuple-element.45), channel_id=1, source_target_pairs={{0,2},{1,3},{2,0},{3,1},{4,6},{5,7},{6,4},{7,5},{8,10},{9,11},{10,... | collective-permute-start | bytes 1179656 | tf_op jit(solution)/shard_map/block_scatter/ppermute | solution.py:575
  14.2 1.4 %collective-permute-start.7 = (bf16[6,8,4096]{2,1,0:T(8,128)(2,1)S(1)}, bf16[6,8,4096]{2,1,0:T(8,128)(2,1)S(1)}, u32[]{:S(2)}, u32[]{:S(2)}) collective-permute-start(bf16[6,8,4096]{2,1,0:T(8,128)(2,1)S(1)} %get-tuple-element.47), channel_id=1, source_target_pairs={{0,12},{1,13},{2,14},{3,15},{4,0},{5,1},{6,2},{7,3},{8,4},{9,5},{1... | collective-permute-start | bytes 1179656 | tf_op jit(solution)/shard_map/block_scatter/ppermute | solution.py:575
  18.4 3.9 %collective-permute-done.5.crossed.crossed_a = bf16[6,8,4096]{2,1,0:T(8,128)(2,1)S(1)} collective-permute-done((bf16[6,8,4096]{2,1,0:T(8,128)(2,1)S(1)}, bf16[6,8,4096]{2,1,0:T(8,128)(2,1)S(1)}, u32[]{:S(2)}, u32[]{:S(2)}) %collective-permute-start.5) | collective-permute-done | bytes 393248 | tf_op jit(solution)/shard_map/block_scatter/ppermute | solution.py:575
  22.3 2.8 %collective-permute-start.4 = (bf16[5,8,4096]{2,1,0:T(8,128)(2,1)S(1)}, bf16[5,8,4096]{2,1,0:T(8,128)(2,1)S(1)}, u32[]{:S(2)}, u32[]{:S(2)}) collective-permute-start(bf16[5,8,4096]{2,1,0:T(8,128)(2,1)S(1)} %get-tuple-element.44), channel_id=1, source_target_pairs={{0,12},{1,13},{2,14},{3,15},{4,0},{5,1},{6,2},{7,3},{8,4},{9,5},{1... | collective-permute-start | bytes 983048 | tf_op jit(solution)/shard_map/block_scatter/ppermute | solution.py:575
  25.1 2.0 %block_scatter.10 = (bf16[6,8,4096]{2,1,0:T(8,128)(2,1)S(1)}, bf16[6,8,4096]{2,1,0:T(8,128)(2,1)S(1)}) custom-call(s32[1]{0:T(128)S(6)} %copy.14.ablock_ref, s32[1,2]{1,0:T(1,128)S(1)} %copy-done.12, bf16[128,8,4096]{2,1,0:T(8,128)(2,1)} %fields.15, bf16[16,8,4096]{2,1,0:T(8,128)(2,1)} %occupied.15, bf16[14,8,4096]{2,1,0:T(8,128)(2,1)S(1)} %block_scatter.6.sent_a, ...), custom_call_target="tpu_custom_call" | custom-call | flops 10000000000 | bytes 1048576 | tf_op jit(solution)/shard_map/block_scatter/pallas_call | solution.py:494
  27.1 1.8 %collective-permute-start.10 = (bf16[6,8,4096]{2,1,0:T(8,128)(2,1)S(1)}, bf16[6,8,4096]{2,1,0:T(8,128)(2,1)S(1)}, u32[]{:S(2)}, u32[]{:S(2)}) collective-permute-start(bf16[6,8,4096]{2,1,0:T(8,128)(2,1)S(1)} %get-tuple-element.51), channel_id=1, source_target_pairs={{0,8},{1,9},{2,10},{3,11},{4,12},{5,13},{6,14},{7,15},{8,0},{9,1},... | collective-permute-start | bytes 1179656 | tf_op jit(solution)/shard_map/block_scatter/ppermute | solution.py:575
  30.2 1.4 %collective-permute-done.3.below.below_b = bf16[5,8,4096]{2,1,0:T(8,128)(2,1)S(1)} collective-permute-done((bf16[5,8,4096]{2,1,0:T(8,128)(2,1)S(1)}, bf16[5,8,4096]{2,1,0:T(8,128)(2,1)S(1)}, u32[]{:S(2)}, u32[]{:S(2)}) %collective-permute-start.3) | collective-permute-done | bytes 327712 | tf_op jit(solution)/shard_map/block_scatter/ppermute | solution.py:575
  31.6 1.6 %block_scatter.11 = (bf16[1,8,4096]{2,1,0:T(8,128)(2,1)S(1)}, bf16[1,8,4096]{2,1,0:T(8,128)(2,1)S(1)}, bf16[128,256]{1,0:T(8,128)(2,1)S(1)}) custom-call(s32[1]{0:T(128)S(6)} %copy.14.ablock_ref, s32[1,2]{1,0:T(1,128)S(1)} %copy-done.12, bf16[128,8,4096]{2,1,0:T(8,128)(2,1)} %fields.15, bf16[16,8,4096]{2,1,0:T(8,128)(2,1)} %occupied.15, ...), custom_call_target="tpu_custom_call" | custom-call | flops 10000000000 | bytes 1048576 | tf_op jit(solution)/shard_map/block_scatter/pallas_call | solution.py:494
  33.2 7.9 %collective-permute-done.10.far = bf16[6,8,4096]{2,1,0:T(8,128)(2,1)S(1)} collective-permute-done((bf16[6,8,4096]{2,1,0:T(8,128)(2,1)S(1)}, bf16[6,8,4096]{2,1,0:T(8,128)(2,1)S(1)}, u32[]{:S(2)}, u32[]{:S(2)}) %collective-permute-start.10) | collective-permute-done | bytes 393248 | tf_op jit(solution)/shard_map/block_scatter/ppermute | solution.py:575
  41.2 3.8 %transform.4 = bf16[8,192,256]{2,1,0:T(8,128)(2,1)} custom-call(s32[1]{0:T(128)S(6)} %copy.14.ablock_ref, s32[1,2]{1,0:T(1,128)S(1)} %copy-done.12, bf16[128,8,4096]{2,1,0:T(8,128)(2,1)} %fields.15, bf16[16,8,4096]{2,1,0:T(8,128)(2,1)} %occupied.15, bf16[14,8,4096]{2,1,0:T(8,128)(2,1)S(1)} %collective-permute-done.got_a, ...), custom_call_target="tpu_custom_call" | custom-call | flops 20000000000 | bytes 1048576 | tf_op jit(solution)/shard_map/transform/pallas_call | solution.py:494
  45.1 5.0 %all-to-all-start = ((bf16[8,192,256]{2,1,0:T(8,128)(2,1)}), bf16[8,192,256]{2,1,0:T(8,128)(2,1)S(1)}, u32[]{:S(2)}, u32[]{:S(2)}) async-start(bf16[8,192,256]{2,1,0:T(8,128)(2,1)} %transform.4), calls=%async_computation | async-start | bytes 1572864 | tf_op jit(solution)/shard_map/transform/all_to_all | solution.py:670
  50.1 1.6 %transform.5.weight_ref = f32[512,128]{1,0:T(8,128)S(1)} custom-call(bf16[14,8,4096]{2,1,0:T(8,128)(2,1)} %copy-done, bf16[14,8,4096]{2,1,0:T(8,128)(2,1)} %copy-done.2, bf16[6,8,4096]{2,1,0:T(8,128)(2,1)} %copy-done.3, bf16[6,8,4096]{2,1,0:T(8,128)(2,1)} %copy-done.4, bf16[6,8,4096]{2,1,0:T(8,128)(2,1)} %copy-done.5, bf16[6,8,4096]{2,1,0:T(8,128)(2,1)} %copy-done.6, ...), custom_call_target="tpu_custom_call" | custom-call | flops 100000000 | bytes 1048576 | tf_op jit(solution)/shard_map/transform/pallas_call | solution.py:494
  51.7 6.7 %all-to-all-done.y_hbm.refs_7_ = bf16[8,192,256]{2,1,0:T(8,128)(2,1)S(1)} async-done(((bf16[8,192,256]{2,1,0:T(8,128)(2,1)}), bf16[8,192,256]{2,1,0:T(8,128)(2,1)S(1)}, u32[]{:S(2)}, u32[]{:S(2)}) %all-to-all-start) | async-done | bytes 786464 | tf_op jit(solution)/shard_map/transform/all_to_all | solution.py:670
  58.5 3.6 %transform.6 = bf16[512,256]{1,0:T(8,128)(2,1)} custom-call(bf16[8,192,256]{2,1,0:T(8,128)(2,1)S(1)} %all-to-all-done.y_hbm.refs_7_, f32[512,128]{1,0:T(8,128)S(1)} %transform.5.weight_ref, bf16[256,256]{1,0:T(8,128)(2,1)} %constant.22.clone.turn_hbm, bf16[512,1024]{1,0:T(8,128)(2,1)} %constant.20.clone.kx_hbm, bf16[512,1024]{1,0:T(8,128)(2,1)} %constant.21.clone.kxt_hbm), custom_call_target="tpu_custom_call" | custom-call | flops 10000000000 | bytes 1048576 | tf_op jit(solution)/shard_map/transform/pallas_call | solution.py:494
  62.1 6.5 %all-to-all-start.1 = ((bf16[8,64,256]{2,1,0:T(8,128)(2,1)}), bf16[8,64,256]{2,1,0:T(8,128)(2,1)S(1)}, u32[]{:S(2)}, u32[]{:S(2)}) async-start(bf16[8,64,256]{2,1,0:T(8,128)(2,1)} %bitcast), calls=%async_computation.1 | async-start | bytes 524288 | tf_op jit(solution)/shard_map/transform/all_to_all | solution.py:690
  68.5 2.5 %collective-permute-start.9 = (bf16[1,8,4096]{2,1,0:T(8,128)(2,1)S(1)}, bf16[1,8,4096]{2,1,0:T(8,128)(2,1)S(1)}, u32[]{:S(2)}, u32[]{:S(2)}) collective-permute-start(bf16[1,8,4096]{2,1,0:T(8,128)(2,1)S(1)} %get-tuple-element.57), channel_id=1, source_target_pairs={{0,2},{1,3},{2,0},{3,1},{4,6},{5,7},{6,4},{7,5},{8,10},{9,11},{10,... | collective-permute-start | bytes 196616 | tf_op jit(solution)/shard_map/block_scatter/ppermute | solution.py:575
  71.0 2.1 %collective-permute-done.8.far = bf16[1,8,4096]{2,1,0:T(8,128)(2,1)S(1)} collective-permute-done((bf16[1,8,4096]{2,1,0:T(8,128)(2,1)S(1)}, bf16[1,8,4096]{2,1,0:T(8,128)(2,1)S(1)}, u32[]{:S(2)}, u32[]{:S(2)}) %collective-permute-start.8) | collective-permute-done | bytes 65568 | tf_op jit(solution)/shard_map/block_scatter/ppermute | solution.py:575
  73.2 1.4 %all-to-all-done.1 = bf16[8,64,256]{2,1,0:T(8,128)(2,1)S(1)} async-done(((bf16[8,64,256]{2,1,0:T(8,128)(2,1)}), bf16[8,64,256]{2,1,0:T(8,128)(2,1)S(1)}, u32[]{:S(2)}, u32[]{:S(2)}) %all-to-all-start.1) | async-done | bytes 262176 | tf_op jit(solution)/shard_map/transform/all_to_all | solution.py:690
  74.6 3.0 %transform.7 = bf16[4,8,4096]{2,1,0:T(8,128)(2,1)S(1)} custom-call(s32[1]{0:T(128)S(6)} %copy.14.ablock_ref, s32[1,2]{1,0:T(1,128)S(1)} %copy-done.12, bf16[128,8,4096]{2,1,0:T(8,128)(2,1)} %fields.15, bf16[16,8,4096]{2,1,0:T(8,128)(2,1)} %occupied.15, bf16[21,8,4096]{2,1,0:T(8,128)(2,1)} %copy-done.1, bf16[5,8,4096]{2,1,0:T(8,128)(2,1)} %copy-done.8, ...), custom_call_target="tpu_custom_call" | custom-call | flops 100000000 | bytes 1048576 | tf_op jit(solution)/shard_map/transform/pallas_call | solution.py:494
  77.7 2.7 %collective-permute-start.12 = (bf16[32,4096]{1,0:T(8,128)(2,1)S(1)}, bf16[32,4096]{1,0:T(8,128)(2,1)S(1)}, u32[]{:S(2)}, u32[]{:S(2)}) collective-permute-start(bf16[32,4096]{1,0:T(8,128)(2,1)S(1)} %bitcast.5), channel_id=1, source_target_pairs={{0,8},{1,9},{2,10},{3,11},{4,12},{5,13},{6,14},{7,15},{8,0},{9,1},... | collective-permute-start | bytes 786440 | tf_op jit(solution)/shard_map/block_gather/ppermute | solution.py:575
  80.5 3.3 %collective-permute-start.19 = (bf16[32,4096]{1,0:T(8,128)(2,1)S(1)}, bf16[32,4096]{1,0:T(8,128)(2,1)S(1)}, u32[]{:S(2)}, u32[]{:S(2)}) collective-permute-start(bf16[32,4096]{1,0:T(8,128)(2,1)S(1)} %bitcast.7), channel_id=1, source_target_pairs={{0,4},{1,5},{2,6},{3,7},{4,8},{5,9},{6,10},{7,11},{8,12},{9,13},{1... | collective-permute-start | bytes 786440 | tf_op jit(solution)/shard_map/block_gather/ppermute | solution.py:575
  83.9 5.6 %collective-permute-start.17 = (bf16[32,4096]{1,0:T(8,128)(2,1)S(1)}, bf16[32,4096]{1,0:T(8,128)(2,1)S(1)}, u32[]{:S(2)}, u32[]{:S(2)}) collective-permute-start(bf16[32,4096]{1,0:T(8,128)(2,1)S(1)} %bitcast.9), channel_id=1, source_target_pairs={{0,1},{1,0},{2,3},{3,2},{4,5},{5,4},{6,7},{7,6},{8,9},{9,8},{10,11... | collective-permute-start | bytes 786440 | tf_op jit(solution)/shard_map/block_gather/ppermute | solution.py:575
  89.5 3.4 %block_gather.3.u_ref = bf16[1024,4096]{1,0:T(8,128)(2,1)S(1)} custom-call(bf16[1024,4096]{1,0:T(8,128)(2,1)} %bitcast.13), custom_call_target="tpu_custom_call" | custom-call | flops 100000000 | bytes 1048576 | tf_op jit(solution)/shard_map/block_gather/pallas_call | solution.py:494
  95.1 1.6 %collective-permute-start.14 = (bf16[32,4096]{1,0:T(8,128)(2,1)S(1)}, bf16[32,4096]{1,0:T(8,128)(2,1)S(1)}, u32[]{:S(2)}, u32[]{:S(2)}) collective-permute-start(bf16[32,4096]{1,0:T(8,128)(2,1)S(1)} %collective-permute-done.12.refs_2_), channel_id=1, source_target_pairs={{0,2},{1,3},{2,0},{3,1},{4,6},{5,7},{6,4},{7,5},{8,10},{9,11},{10,... | collective-permute-start | bytes 786440 | tf_op jit(solution)/shard_map/block_gather/ppermute | solution.py:575
  97.0 2.4 %collective-permute-start.16 = (bf16[32,4096]{1,0:T(8,128)(2,1)S(1)}, bf16[32,4096]{1,0:T(8,128)(2,1)S(1)}, u32[]{:S(2)}, u32[]{:S(2)}) collective-permute-start(bf16[32,4096]{1,0:T(8,128)(2,1)S(1)} %collective-permute-done.13.refs_8_), channel_id=1, source_target_pairs={{0,12},{1,13},{2,14},{3,15},{4,0},{5,1},{6,2},{7,3},{8,4},{9,5},{1... | collective-permute-start | bytes 786440 | tf_op jit(solution)/shard_map/block_gather/ppermute | solution.py:575
  99.4 5.2 %block_gather.4.refs_6_ = f32[128,128]{1,0:T(8,128)S(1)} custom-call(bf16[1024,4096]{1,0:T(8,128)(2,1)S(1)} %block_gather.3.u_ref, bf16[32,4096]{1,0:T(8,128)(2,1)S(1)} %bitcast.10, bf16[32,4096]{1,0:T(8,128)(2,1)S(1)} %collective-permute-done.17.refs_1_, bf16[32,4096]{1,0:T(8,128)(2,1)S(1)} %collective-permute-done.12.refs_2_, ...), custom_call_target="tpu_custom_call" | custom-call | flops 2684354560 | bytes 8388608 | tf_op jit(solution)/shard_map/block_gather/pallas_call | solution.py:556
  108.6 3.8 %block_gather.5 = bf16[1024,128]{1,0:T(8,128)(2,1)S(1)} custom-call(bf16[1024,4096]{1,0:T(8,128)(2,1)S(1)} %block_gather.3.u_ref, bf16[32,4096]{1,0:T(8,128)(2,1)S(1)} %collective-permute-done.14.refs_0_, bf16[32,4096]{1,0:T(8,128)(2,1)S(1)} %collective-permute-done.24.refs_1_, bf16[32,4096]{1,0:T(8,128)(2,1)S(1)} %collective-permute-done.15.refs_2_, ...), custom_call_target="tpu_custom_call" | custom-call | flops 1610612736 | bytes 8388608 | tf_op jit(solution)/shard_map/block_gather/pallas_call | solution.py:556
  112.4 19.1 %all_to_all.21 = bf16[128,8,128]{2,1,0:T(8,128)(2,1)S(1)} all-to-all(bf16[128,8,128]{2,1,0:T(8,128)(2,1)S(1)} %bitcast.12), channel_id=1, replica_groups=mesh['grid'=8,'band'=16] {'grid','band'}, dimensions={0} | all-to-all | bytes 524288 | tf_op jit(solution)/shard_map/ladder/all_to_all | solution.py:728
  (72 shorter events, 14.2 us)
Async XLA Ops:
  3.6 21.5 %copy-start = (bf16[14,8,4096]{2,1,0:T(8,128)(2,1)}, bf16[14,8,4096]{2,1,0:T(8,128)(2,1)S(1)}, u32[]{:S(2)}) copy-start(bf16[14,8,4096]{2,1,0:T(8,128)(2,1)S(1)} %block_scatter.6.sent_a) | copy-start | bytes 2752516
  3.6 3.6 %collective-permute-start = (bf16[14,8,4096]{2,1,0:T(8,128)(2,1)S(1)}, bf16[14,8,4096]{2,1,0:T(8,128)(2,1)S(1)}, u32[]{:S(2)}, u32[]{:S(2)}) collective-permute-start(bf16[14,8,4096]{2,1,0:T(8,128)(2,1)S(1)} %block_scatter.6.sent_a), channel_id=1, source_target_pairs={{0,1},{1,0},{2,3},{3,2},{4,5},{5,4},{6,7},{7,6},{8,9},{9,8},{10,11... | collective-permute-start | bytes 2752520 | tf_op jit(solution)/shard_map/block_scatter/ppermute | solution.py:575
  7.2 33.9 %copy-start.2 = (bf16[14,8,4096]{2,1,0:T(8,128)(2,1)}, bf16[14,8,4096]{2,1,0:T(8,128)(2,1)S(1)}, u32[]{:S(2)}) copy-start(bf16[14,8,4096]{2,1,0:T(8,128)(2,1)S(1)} %collective-permute-done.got_a) | copy-start | bytes 2752516
  9.4 6.3 %collective-permute-start.1 = (bf16[21,8,4096]{2,1,0:T(8,128)(2,1)S(1)}, bf16[21,8,4096]{2,1,0:T(8,128)(2,1)S(1)}, u32[]{:S(2)}, u32[]{:S(2)}) collective-permute-start(bf16[21,8,4096]{2,1,0:T(8,128)(2,1)S(1)} %block_scatter.8), channel_id=1, source_target_pairs={{0,1},{1,0},{2,3},{3,2},{4,5},{5,4},{6,7},{7,6},{8,9},{9,8},{10,11... | collective-permute-start | bytes 4128776 | tf_op jit(solution)/shard_map/block_scatter/ppermute | solution.py:575
  10.1 12.2 %collective-permute-start.5 = (bf16[6,8,4096]{2,1,0:T(8,128)(2,1)S(1)}, bf16[6,8,4096]{2,1,0:T(8,128)(2,1)S(1)}, u32[]{:S(2)}, u32[]{:S(2)}) collective-permute-start(bf16[6,8,4096]{2,1,0:T(8,128)(2,1)S(1)} %get-tuple-element.45), channel_id=1, source_target_pairs={{0,2},{1,3},{2,0},{3,1},{4,6},{5,7},{6,4},{7,5},{8,10},{9,11},{10,... | collective-permute-start | bytes 1179656 | tf_op jit(solution)/shard_map/block_scatter/ppermute | solution.py:575
  12.9 12.2 %collective-permute-start.6 = (bf16[6,8,4096]{2,1,0:T(8,128)(2,1)S(1)}, bf16[6,8,4096]{2,1,0:T(8,128)(2,1)S(1)}, u32[]{:S(2)}, u32[]{:S(2)}) collective-permute-start(bf16[6,8,4096]{2,1,0:T(8,128)(2,1)S(1)} %get-tuple-element.46), channel_id=1, source_target_pairs={{0,4},{1,5},{2,6},{3,7},{4,8},{5,9},{6,10},{7,11},{8,12},{9,13},{1... | collective-permute-start | bytes 1179656 | tf_op jit(solution)/shard_map/block_scatter/ppermute | solution.py:575
  14.2 10.9 %collective-permute-start.7 = (bf16[6,8,4096]{2,1,0:T(8,128)(2,1)S(1)}, bf16[6,8,4096]{2,1,0:T(8,128)(2,1)S(1)}, u32[]{:S(2)}, u32[]{:S(2)}) collective-permute-start(bf16[6,8,4096]{2,1,0:T(8,128)(2,1)S(1)} %get-tuple-element.47), channel_id=1, source_target_pairs={{0,12},{1,13},{2,14},{3,15},{4,0},{5,1},{6,2},{7,3},{8,4},{9,5},{1... | collective-permute-start | bytes 1179656 | tf_op jit(solution)/shard_map/block_scatter/ppermute | solution.py:575
  15.7 25.5 %copy-start.1 = (bf16[21,8,4096]{2,1,0:T(8,128)(2,1)}, bf16[21,8,4096]{2,1,0:T(8,128)(2,1)S(1)}, u32[]{:S(2)}) copy-start(bf16[21,8,4096]{2,1,0:T(8,128)(2,1)S(1)} %collective-permute-done.1.got_b) | copy-start | bytes 4128772
  17.0 13.2 %collective-permute-start.2 = (bf16[5,8,4096]{2,1,0:T(8,128)(2,1)S(1)}, bf16[5,8,4096]{2,1,0:T(8,128)(2,1)S(1)}, u32[]{:S(2)}, u32[]{:S(2)}) collective-permute-start(bf16[5,8,4096]{2,1,0:T(8,128)(2,1)S(1)} %get-tuple-element.42), channel_id=1, source_target_pairs={{0,2},{1,3},{2,0},{3,1},{4,6},{5,7},{6,4},{7,5},{8,10},{9,11},{10,... | collective-permute-start | bytes 983048 | tf_op jit(solution)/shard_map/block_scatter/ppermute | solution.py:575
  17.3 14.3 %collective-permute-start.3 = (bf16[5,8,4096]{2,1,0:T(8,128)(2,1)S(1)}, bf16[5,8,4096]{2,1,0:T(8,128)(2,1)S(1)}, u32[]{:S(2)}, u32[]{:S(2)}) collective-permute-start(bf16[5,8,4096]{2,1,0:T(8,128)(2,1)S(1)} %get-tuple-element.43), channel_id=1, source_target_pairs={{0,4},{1,5},{2,6},{3,7},{4,8},{5,9},{6,10},{7,11},{8,12},{9,13},{1... | collective-permute-start | bytes 983048 | tf_op jit(solution)/shard_map/block_scatter/ppermute | solution.py:575
  22.3 9.4 %collective-permute-start.4 = (bf16[5,8,4096]{2,1,0:T(8,128)(2,1)S(1)}, bf16[5,8,4096]{2,1,0:T(8,128)(2,1)S(1)}, u32[]{:S(2)}, u32[]{:S(2)}) collective-permute-start(bf16[5,8,4096]{2,1,0:T(8,128)(2,1)S(1)} %get-tuple-element.44), channel_id=1, source_target_pairs={{0,12},{1,13},{2,14},{3,15},{4,0},{5,1},{6,2},{7,3},{8,4},{9,5},{1... | collective-permute-start | bytes 983048 | tf_op jit(solution)/shard_map/block_scatter/ppermute | solution.py:575
  27.1 14.0 %collective-permute-start.10 = (bf16[6,8,4096]{2,1,0:T(8,128)(2,1)S(1)}, bf16[6,8,4096]{2,1,0:T(8,128)(2,1)S(1)}, u32[]{:S(2)}, u32[]{:S(2)}) collective-permute-start(bf16[6,8,4096]{2,1,0:T(8,128)(2,1)S(1)} %get-tuple-element.51), channel_id=1, source_target_pairs={{0,8},{1,9},{2,10},{3,11},{4,12},{5,13},{6,14},{7,15},{8,0},{9,1},... | collective-permute-start | bytes 1179656 | tf_op jit(solution)/shard_map/block_scatter/ppermute | solution.py:575
  29.0 12.2 %collective-permute-start.11 = (bf16[6,8,4096]{2,1,0:T(8,128)(2,1)S(1)}, bf16[6,8,4096]{2,1,0:T(8,128)(2,1)S(1)}, u32[]{:S(2)}, u32[]{:S(2)}) collective-permute-start(bf16[6,8,4096]{2,1,0:T(8,128)(2,1)S(1)} %get-tuple-element.52), channel_id=1, source_target_pairs={{0,2},{1,3},{2,0},{3,1},{4,6},{5,7},{6,4},{7,5},{8,10},{9,11},{10,... | collective-permute-start | bytes 1179656 | tf_op jit(solution)/shard_map/block_scatter/ppermute | solution.py:575
  45.1 13.4 %all-to-all-start = ((bf16[8,192,256]{2,1,0:T(8,128)(2,1)}), bf16[8,192,256]{2,1,0:T(8,128)(2,1)S(1)}, u32[]{:S(2)}, u32[]{:S(2)}) async-start(bf16[8,192,256]{2,1,0:T(8,128)(2,1)} %transform.4), calls=%async_computation | async-start | bytes 1572864 | tf_op jit(solution)/shard_map/transform/all_to_all | solution.py:670
  62.1 12.5 %all-to-all-start.1 = ((bf16[8,64,256]{2,1,0:T(8,128)(2,1)}), bf16[8,64,256]{2,1,0:T(8,128)(2,1)S(1)}, u32[]{:S(2)}, u32[]{:S(2)}) async-start(bf16[8,64,256]{2,1,0:T(8,128)(2,1)} %bitcast), calls=%async_computation.1 | async-start | bytes 524288 | tf_op jit(solution)/shard_map/transform/all_to_all | solution.py:690
  68.5 4.6 %collective-permute-start.8 = (bf16[1,8,4096]{2,1,0:T(8,128)(2,1)S(1)}, bf16[1,8,4096]{2,1,0:T(8,128)(2,1)S(1)}, u32[]{:S(2)}, u32[]{:S(2)}) collective-permute-start(bf16[1,8,4096]{2,1,0:T(8,128)(2,1)S(1)} %get-tuple-element.56), channel_id=1, source_target_pairs={{0,8},{1,9},{2,10},{3,11},{4,12},{5,13},{6,14},{7,15},{8,0},{9,1},... | collective-permute-start | bytes 196616 | tf_op jit(solution)/shard_map/block_scatter/ppermute | solution.py:575
  68.5 4.7 %collective-permute-start.9 = (bf16[1,8,4096]{2,1,0:T(8,128)(2,1)S(1)}, bf16[1,8,4096]{2,1,0:T(8,128)(2,1)S(1)}, u32[]{:S(2)}, u32[]{:S(2)}) collective-permute-start(bf16[1,8,4096]{2,1,0:T(8,128)(2,1)S(1)} %get-tuple-element.57), channel_id=1, source_target_pairs={{0,2},{1,3},{2,0},{3,1},{4,6},{5,7},{6,4},{7,5},{8,10},{9,11},{10,... | collective-permute-start | bytes 196616 | tf_op jit(solution)/shard_map/block_scatter/ppermute | solution.py:575
  77.7 15.2 %collective-permute-start.12 = (bf16[32,4096]{1,0:T(8,128)(2,1)S(1)}, bf16[32,4096]{1,0:T(8,128)(2,1)S(1)}, u32[]{:S(2)}, u32[]{:S(2)}) collective-permute-start(bf16[32,4096]{1,0:T(8,128)(2,1)S(1)} %bitcast.5), channel_id=1, source_target_pairs={{0,8},{1,9},{2,10},{3,11},{4,12},{5,13},{6,14},{7,15},{8,0},{9,1},... | collective-permute-start | bytes 786440 | tf_op jit(solution)/shard_map/block_gather/ppermute | solution.py:575
  80.3 12.6 %collective-permute-start.13 = (bf16[32,4096]{1,0:T(8,128)(2,1)S(1)}, bf16[32,4096]{1,0:T(8,128)(2,1)S(1)}, u32[]{:S(2)}, u32[]{:S(2)}) collective-permute-start(bf16[32,4096]{1,0:T(8,128)(2,1)S(1)} %bitcast.6), channel_id=1, source_target_pairs={{0,2},{1,3},{2,0},{3,1},{4,6},{5,7},{6,4},{7,5},{8,10},{9,11},{10,... | collective-permute-start | bytes 786440 | tf_op jit(solution)/shard_map/block_gather/ppermute | solution.py:575
  80.5 13.0 %collective-permute-start.19 = (bf16[32,4096]{1,0:T(8,128)(2,1)S(1)}, bf16[32,4096]{1,0:T(8,128)(2,1)S(1)}, u32[]{:S(2)}, u32[]{:S(2)}) collective-permute-start(bf16[32,4096]{1,0:T(8,128)(2,1)S(1)} %bitcast.7), channel_id=1, source_target_pairs={{0,4},{1,5},{2,6},{3,7},{4,8},{5,9},{6,10},{7,11},{8,12},{9,13},{1... | collective-permute-start | bytes 786440 | tf_op jit(solution)/shard_map/block_gather/ppermute | solution.py:575
  83.9 10.0 %collective-permute-start.21 = (bf16[32,4096]{1,0:T(8,128)(2,1)S(1)}, bf16[32,4096]{1,0:T(8,128)(2,1)S(1)}, u32[]{:S(2)}, u32[]{:S(2)}) collective-permute-start(bf16[32,4096]{1,0:T(8,128)(2,1)S(1)} %bitcast.8), channel_id=1, source_target_pairs={{0,12},{1,13},{2,14},{3,15},{4,0},{5,1},{6,2},{7,3},{8,4},{9,5},{1... | collective-permute-start | bytes 786440 | tf_op jit(solution)/shard_map/block_gather/ppermute | solution.py:575
  83.9 11.2 %collective-permute-start.17 = (bf16[32,4096]{1,0:T(8,128)(2,1)S(1)}, bf16[32,4096]{1,0:T(8,128)(2,1)S(1)}, u32[]{:S(2)}, u32[]{:S(2)}) collective-permute-start(bf16[32,4096]{1,0:T(8,128)(2,1)S(1)} %bitcast.9), channel_id=1, source_target_pairs={{0,1},{1,0},{2,3},{3,2},{4,5},{5,4},{6,7},{7,6},{8,9},{9,8},{10,11... | collective-permute-start | bytes 786440 | tf_op jit(solution)/shard_map/block_gather/ppermute | solution.py:575
  92.9 3.8 %collective-permute-start.18 = (bf16[32,4096]{1,0:T(8,128)(2,1)S(1)}, bf16[32,4096]{1,0:T(8,128)(2,1)S(1)}, u32[]{:S(2)}, u32[]{:S(2)}) collective-permute-start(bf16[32,4096]{1,0:T(8,128)(2,1)S(1)} %collective-permute-done.12.refs_2_), channel_id=1, source_target_pairs={{0,1},{1,0},{2,3},{3,2},{4,5},{5,4},{6,7},{7,6},{8,9},{9,8},{10,11... | collective-permute-start | bytes 786440 | tf_op jit(solution)/shard_map/block_gather/ppermute | solution.py:575
  93.0 4.0 %collective-permute-start.23 = (bf16[32,4096]{1,0:T(8,128)(2,1)S(1)}, bf16[32,4096]{1,0:T(8,128)(2,1)S(1)}, u32[]{:S(2)}, u32[]{:S(2)}) collective-permute-start(bf16[32,4096]{1,0:T(8,128)(2,1)S(1)} %collective-permute-done.13.refs_8_), channel_id=1, source_target_pairs={{0,1},{1,0},{2,3},{3,2},{4,5},{5,4},{6,7},{7,6},{8,9},{9,8},{10,11... | collective-permute-start | bytes 786440 | tf_op jit(solution)/shard_map/block_gather/ppermute | solution.py:575
  93.5 5.9 %collective-permute-start.20 = (bf16[32,4096]{1,0:T(8,128)(2,1)S(1)}, bf16[32,4096]{1,0:T(8,128)(2,1)S(1)}, u32[]{:S(2)}, u32[]{:S(2)}) collective-permute-start(bf16[32,4096]{1,0:T(8,128)(2,1)S(1)} %collective-permute-done.19.refs_4_), channel_id=1, source_target_pairs={{0,1},{1,0},{2,3},{3,2},{4,5},{5,4},{6,7},{7,6},{8,9},{9,8},{10,11... | collective-permute-start | bytes 786440 | tf_op jit(solution)/shard_map/block_gather/ppermute | solution.py:575
  93.9 5.5 %collective-permute-start.22 = (bf16[32,4096]{1,0:T(8,128)(2,1)S(1)}, bf16[32,4096]{1,0:T(8,128)(2,1)S(1)}, u32[]{:S(2)}, u32[]{:S(2)}) collective-permute-start(bf16[32,4096]{1,0:T(8,128)(2,1)S(1)} %collective-permute-done.21.refs_6_), channel_id=1, source_target_pairs={{0,1},{1,0},{2,3},{3,2},{4,5},{5,4},{6,7},{7,6},{8,9},{9,8},{10,11... | collective-permute-start | bytes 786440 | tf_op jit(solution)/shard_map/block_gather/ppermute | solution.py:575
  95.1 9.5 %collective-permute-start.14 = (bf16[32,4096]{1,0:T(8,128)(2,1)S(1)}, bf16[32,4096]{1,0:T(8,128)(2,1)S(1)}, u32[]{:S(2)}, u32[]{:S(2)}) collective-permute-start(bf16[32,4096]{1,0:T(8,128)(2,1)S(1)} %collective-permute-done.12.refs_2_), channel_id=1, source_target_pairs={{0,2},{1,3},{2,0},{3,1},{4,6},{5,7},{6,4},{7,5},{8,10},{9,11},{10,... | collective-permute-start | bytes 786440 | tf_op jit(solution)/shard_map/block_gather/ppermute | solution.py:575
  96.7 8.8 %collective-permute-start.15 = (bf16[32,4096]{1,0:T(8,128)(2,1)S(1)}, bf16[32,4096]{1,0:T(8,128)(2,1)S(1)}, u32[]{:S(2)}, u32[]{:S(2)}) collective-permute-start(bf16[32,4096]{1,0:T(8,128)(2,1)S(1)} %collective-permute-done.13.refs_8_), channel_id=1, source_target_pairs={{0,4},{1,5},{2,6},{3,7},{4,8},{5,9},{6,10},{7,11},{8,12},{9,13},{1... | collective-permute-start | bytes 786440 | tf_op jit(solution)/shard_map/block_gather/ppermute | solution.py:575
  97.0 8.6 %collective-permute-start.16 = (bf16[32,4096]{1,0:T(8,128)(2,1)S(1)}, bf16[32,4096]{1,0:T(8,128)(2,1)S(1)}, u32[]{:S(2)}, u32[]{:S(2)}) collective-permute-start(bf16[32,4096]{1,0:T(8,128)(2,1)S(1)} %collective-permute-done.13.refs_8_), channel_id=1, source_target_pairs={{0,12},{1,13},{2,14},{3,15},{4,0},{5,1},{6,2},{7,3},{8,4},{9,5},{1... | collective-permute-start | bytes 786440 | tf_op jit(solution)/shard_map/block_gather/ppermute | solution.py:575
  105.6 2.3 %collective-permute-start.24 = (bf16[32,4096]{1,0:T(8,128)(2,1)S(1)}, bf16[32,4096]{1,0:T(8,128)(2,1)S(1)}, u32[]{:S(2)}, u32[]{:S(2)}) collective-permute-start(bf16[32,4096]{1,0:T(8,128)(2,1)S(1)} %collective-permute-done.14.refs_0_), channel_id=1, source_target_pairs={{0,1},{1,0},{2,3},{3,2},{4,5},{5,4},{6,7},{7,6},{8,9},{9,8},{10,11... | collective-permute-start | bytes 786440 | tf_op jit(solution)/shard_map/block_gather/ppermute | solution.py:575
  106.7 1.5 %collective-permute-start.25 = (bf16[32,4096]{1,0:T(8,128)(2,1)S(1)}, bf16[32,4096]{1,0:T(8,128)(2,1)S(1)}, u32[]{:S(2)}, u32[]{:S(2)}) collective-permute-start(bf16[32,4096]{1,0:T(8,128)(2,1)S(1)} %collective-permute-done.15.refs_2_), channel_id=1, source_target_pairs={{0,1},{1,0},{2,3},{3,2},{4,5},{5,4},{6,7},{7,6},{8,9},{9,8},{10,11... | collective-permute-start | bytes 786440 | tf_op jit(solution)/shard_map/block_gather/ppermute | solution.py:575
  106.7 1.9 %collective-permute-start.26 = (bf16[32,4096]{1,0:T(8,128)(2,1)S(1)}, bf16[32,4096]{1,0:T(8,128)(2,1)S(1)}, u32[]{:S(2)}, u32[]{:S(2)}) collective-permute-start(bf16[32,4096]{1,0:T(8,128)(2,1)S(1)} %collective-permute-done.16.refs_4_), channel_id=1, source_target_pairs={{0,1},{1,0},{2,3},{3,2},{4,5},{5,4},{6,7},{7,6},{8,9},{9,8},{10,11... | collective-permute-start | bytes 786440 | tf_op jit(solution)/shard_map/block_gather/ppermute | solution.py:575
  (12 other events, 97.8 us)

commit v4 on v3

--- a/solution.py
+++ b/solution.py
@@ -96,22 +96,12 @@
     return waits
 
 
-def through(bounce, sems, jobs, start=None):
-    inner, row = [], 0
-    for target, choices in jobs:
-        inner.append((bounce.at[row : row + target.shape[0]], choices))
-        row += target.shape[0]
-    moves = copies(sems, inner)
+def gather(sems, jobs, start=None):
     finish = start() if start else None
-    out = []
-    for slot, move in enumerate(moves):
-        move.wait()
-        target = jobs[slot][0]
-        out.append(pltpu.make_async_copy(inner[slot][0], target, sems.at[len(jobs) + slot]))
-        out[-1].start()
+    moves = copies(sems, jobs)
     if finish:
-        out += finish()
-    wait_all(out)
+        moves += finish()
+    wait_all(moves)
 
 
 def added(marks, sems, groups):
@@ -170,7 +160,7 @@
         return self.occupied.at[pl.ds(self.local[k], 1)]
 
 
-def core_a_body(ablock_ref, pairs_ref, kept_hbm, fields, occupied, out, bounce, marks, kept_ref, sems):
+def core_a_body(ablock_ref, pairs_ref, kept_hbm, fields, occupied, out, marks, kept_ref, sems):
     at = Roots(ablock_ref, pairs_ref, fields, occupied)
     other, there = 1 - at.c, 1 - at.h
     sources = [at.block(other, dy, there, 4) for dy in (1, 3, 2)]
@@ -200,20 +190,31 @@
         move.start()
         return [move]
 
-    through(bounce, sems, jobs, start)
-
-
-def core_b_body(ablock_ref, pairs_ref, fields, occupied, out, bounce, sems):
+    gather(sems, jobs, start)
+
+
+def core_b_body(ablock_ref, pairs_ref, fields, occupied, amp_hbm, out, amp_out, amp_ref, sems):
     at = Roots(ablock_ref, pairs_ref, fields, occupied)
     other, here, there = 1 - at.c, at.h, 1 - at.h
     sources = [at.block(other, dy, h, 4) for dy, h in ((1, here), (3, here), (0, there), (2, here), (0, here))]
     jobs = [(out.at[4 * i : 4 * i + 4], [(None, v)]) for i, v in enumerate(sources)]
     jobs.append((out.at[20:], [(None, at.orbital(1))]))
-    through(bounce, sems, jobs)
+    moves = copies(sems, jobs)
+    (amp_wait,) = copies(sems.at[6:], [(amp_ref, [(None, amp_hbm.at[0])])])
+    amp_wait.wait()
+    row = lax.broadcasted_iota(jnp.int32, (128, 256), 0)
+    col = lax.broadcasted_iota(jnp.int32, (128, 256), 1)
+    over_c = (((1,), (1,)), ((), ()))
+    parity = [
+        lax.dot_general((col == 2 * row + p).astype(BF16), amp_ref[...], over_c, preferred_element_type=F32)
+        for p in range(2)
+    ]
+    amp_out[...] = jnp.concatenate(parity, axis=1).astype(BF16)
+    wait_all(moves)
 
 
 def first_a_body(
-    ablock_ref, pairs_ref, fields, occupied, sent_a, got_a, up, down, across, bounce, marks, sems
+    ablock_ref, pairs_ref, fields, occupied, sent_a, got_a, up, down, across, marks, sems
 ):
     at = Roots(ablock_ref, pairs_ref, fields, occupied)
     mine, theirs = at.same_c[0], jnp.logical_not(at.same_c[0])
@@ -225,10 +226,10 @@
     for target in (up, down, across):
         jobs.append((target.at[4:5], [(mine, at.orbital(0)), (theirs, got_a.at[12:13])]))
     groups = [([sent_a.at[13:], got_a.at[13:]], [v.at[5:] for v in (up, down, across)])]
-    through(bounce, sems, jobs, added(marks, sems.at[12:], groups))
-
-
-def first_b_body(ablock_ref, pairs_ref, fields, occupied, got_b, up, down, across, bounce, sems):
+    gather(sems, jobs, added(marks, sems.at[12:], groups))
+
+
+def first_b_body(ablock_ref, pairs_ref, fields, occupied, got_b, up, down, across, sems):
     at = Roots(ablock_ref, pairs_ref, fields, occupied)
     mine, theirs = at.same_c[0], jnp.logical_not(at.same_c[0])
     jobs = []
@@ -238,7 +239,7 @@
     mine, theirs = at.same_c[2], jnp.logical_not(at.same_c[2])
     for target in (up, down, across):
         jobs.append((target.at[4:], [(mine, at.orbital(1)), (theirs, got_b.at[20:])]))
-    through(bounce, sems, jobs)
+    gather(sems, jobs)
 
 
 def second_a_body(
@@ -254,7 +255,6 @@
     above,
     far,
     turn,
-    bounce,
     marks,
     sems,
 ):
@@ -273,46 +273,7 @@
         ([sent_a.at[13:], got_a.at[13:], crossed.at[5:]], [far.at[5:]]),
         ([below.at[5:], above.at[5:]], [turn.at[5:]]),
     ]
-    through(bounce, sems, jobs, added(marks, sems.at[8:], groups))
-
-
-def second_b_body(
-    ablock_ref,
-    pairs_ref,
-    fields,
-    occupied,
-    got_b,
-    crossed,
-    below,
-    above,
-    amp_hbm,
-    far,
-    turn,
-    amp_out,
-    bounce,
-    amp_ref,
-    sems,
-):
-    at = Roots(ablock_ref, pairs_ref, fields, occupied)
-    not_ = jnp.logical_not
-    same_h, same_c, from_below = at.same_h[2], at.same_c[2], at.away[2] == 1
-    choices = [
-        (same_h & same_c, at.orbital(1)),
-        (same_h & not_(same_c), got_b.at[20:]),
-        (not_(same_h), crossed.at[4:]),
-    ]
-    jobs = [(far, choices), (turn, [(from_below, below.at[4:]), (not_(from_below), above.at[4:])])]
-    (amp_wait,) = copies(sems.at[4:], [(amp_ref, [(None, amp_hbm.at[0])])])
-    through(bounce, sems, jobs)
-    amp_wait.wait()
-    row = lax.broadcasted_iota(jnp.int32, (128, 256), 0)
-    col = lax.broadcasted_iota(jnp.int32, (128, 256), 1)
-    over_c = (((1,), (1,)), ((), ()))
-    parity = [
-        lax.dot_general((col == 2 * row + p).astype(BF16), amp_ref[...], over_c, preferred_element_type=F32)
-        for p in range(2)
-    ]
-    amp_out[...] = jnp.concatenate(parity, axis=1).astype(BF16)
+    gather(sems, jobs, added(marks, sems.at[8:], groups))
 
 
 def arrived(at, k, own, core, cross, far, below, above, turned):
@@ -334,6 +295,7 @@
     pairs_ref,
     fields,
     occupied,
+    sent_a,
     got_a,
     got_b,
     crossed_a,
@@ -348,12 +310,17 @@
     mz_hbm,
     ky_hbm,
     out_hbm,
+    tiles_ref,
+    second_ref,
+    far_ref,
+    turn_ref,
     u_ref,
     o_ref,
     mz_ref,
     ky_ref,
     out_ref,
     amp_ref,
+    marks,
     sems,
 ):
     at = Roots(ablock_ref, pairs_ref, fields, occupied)
@@ -365,6 +332,18 @@
     ]
     jobs += [(mz_ref, [(None, mz_hbm)]), (ky_ref, [(None, ky_hbm)]), (amp_ref, [(None, amp_hbm)])]
     u_wait, o_wait, mz_wait, ky_wait, amp_wait = copies(sems, jobs)
+    sources = [sent_a.at[13:], got_a.at[13:]] + [v.at[5:] for v in (crossed_a, below_a, above_a, far, turned)]
+    mark_waits = copies(sems.at[21:], [(marks.at[i : i + 1], [(None, v)]) for i, v in enumerate(sources)])
+    own, core = at.orbital(1), got_b.at[20:]
+    crossed, below, above = (v.at[4:] for v in (crossed_b, below_b, above_b))
+    not_ = jnp.logical_not
+    same_h, same_c, from_below = at.same_h[2], at.same_c[2], at.away[2] == 1
+    jobs = [
+        (second_ref, arrived(at, 2, own, core, crossed, own, below, above, own)),
+        (far_ref, [(same_h & same_c, own), (same_h & not_(same_c), core), (not_(same_h), crossed)]),
+        (turn_ref, [(from_below, below), (not_(from_below), above)]),
+    ]
+    second_waits = copies(sems.at[28:], jobs)
     u_wait.wait()
     o_wait.wait()
     orbital = o_ref[0].astype(F32)
@@ -375,6 +354,10 @@
             jnp.concatenate([density[:, 128 * j : 128 * (j + 1)] for j in range(PAIRS_Y)], axis=0)
         )
     density = jnp.concatenate(columns, axis=1).astype(BF16)
+    wait_all(mark_waits)
+    total = sum(marks[i].astype(F32) for i in range(len(sources)))
+    tiles = jnp.concatenate([total[:, 128 * n : 128 * (n + 1)] for n in range(BAND)], axis=0)
+    tiles_ref[...] = tiles.astype(BF16)
     mz_wait.wait()
     zfreq = dot(density, mz_ref[...]).astype(BF16)
     stacked = jnp.concatenate([zfreq[:, 256 * i : 256 * (i + 1)] for i in range(4)], axis=0)
@@ -384,7 +367,7 @@
     out_waits = copies(sems.at[5:], jobs)
     out_ref[...] = dot(ky_ref[...], stacked).astype(BF16)
     jobs = [(out_hbm.at[g, pl.ds(0, 64)], [(None, out_ref.at[pl.ds(64 * g, 64)])]) for g in range(GRID)]
-    wait_all(out_waits + copies(sems.at[13:], jobs))
+    wait_all(out_waits + second_waits + copies(sems.at[13:], jobs))
 
 
 def middle_body(
@@ -411,10 +394,7 @@
     pairs_ref,
     fields,
     occupied,
-    got_b,
-    crossed,
-    below,
-    above,
+    second,
     far,
     turned,
     turn_hbm,
@@ -429,10 +409,8 @@
     sems,
 ):
     at = Roots(ablock_ref, pairs_ref, fields, occupied)
-    rows = [v.at[4:] for v in (crossed, below, above)]
-    own, core = at.orbital(1), got_b.at[20:]
     jobs = [
-        (o_ref, arrived(at, 2, own, core, rows[0], far, rows[1], rows[2], turned)),
+        (o_ref, arrived(at, 2, second, second, second, far, second, second, turned)),
         (turn_ref, [(None, turn_hbm)]),
         (kyt_ref, [(None, kyt_hbm)]),
         (mzt_ref, [(None, mzt_hbm)]),
@@ -453,11 +431,8 @@
         out_ref[a] = (jnp.concatenate(rows, axis=1) * orbital).astype(BF16)
 
 
-def weight_body(sent_a, got_a, crossed, below, above, far, turned, out_ref, marks, sems):
-    sources = [sent_a.at[13:], got_a.at[13:]] + [v.at[5:] for v in (crossed, below, above, far, turned)]
-    wait_all(copies(sems, [(marks.at[i : i + 1], [(None, v)]) for i, v in enumerate(sources)]))
-    total = sum(marks[i].astype(F32) for i in range(len(sources)))
-    tiles = jnp.concatenate([total[:, 128 * n : 128 * (n + 1)] for n in range(BAND)], axis=0).astype(BF16)
+def weight_body(tiles_ref, out_ref):
+    tiles = tiles_ref[...]
     shape = (BAND * N, BAND * XL)
     row = lax.broadcasted_iota(jnp.int32, shape, 0)
     lane = lax.broadcasted_iota(jnp.int32, shape, 1)
@@ -477,6 +452,10 @@
     freq_z = lane % HALF
     squared = (freq_x * freq_x + freq_y * freq_y + freq_z * freq_z).astype(F32)
     out_ref[...] = kept / (float(N * N * N) * (squared + 1.0))
+
+
+def arrival_body(first, second, third, amp_ref, out_ref):
+    out_ref[...] = amp_ref[...]
 
 
 def copy_body(source, target, sems):
@@ -593,20 +572,26 @@
             core_a_body,
             root_spaces[:2] + any_ * 3,
             [rows(14)],
-            [held(13), held(1), VMEM(kept_cells.shape, jnp.int32)] + sems(10),
+            [held(1), VMEM(kept_cells.shape, jnp.int32)] + sems(10),
             *roots[:2],
             far_memory(kept_cells),
             *roots[2:],
         )
         got_a = band_shift(sent_a, 0, 0, 1)
-        sent_b = call(
-            core_b_body, root_spaces, [rows(21)], any_, [held(21)] + sems(12), roots, flops=5 * 10**9
+        sent_b, amp = call(
+            core_b_body,
+            root_spaces + any_,
+            [rows(21), (128, 256)],
+            any_ + [VMEM],
+            [VMEM((128, 256), BF16)] + sems(7),
+            roots + (far_memory(amplitudes),),
+            flops=5 * 10**9,
         )
         up, down, across = hop(
             first_a_body,
             root_spaces + any_ * 2,
             [rows(6)] * 3,
-            [held(15), held(2)] + sems(17),
+            [held(2)] + sems(17),
             *roots,
             sent_a,
             got_a,
@@ -617,7 +602,7 @@
         crossed_a = band_shift(across, 0, 1, 0)
         got_b = band_shift(sent_b, 0, 0, 1)
         up, down, across = hop(
-            first_b_body, root_spaces + any_, [rows(5)] * 3, [held(15)] + sems(12), *roots, got_b
+            first_b_body, root_spaces + any_, [rows(5)] * 3, sems(6), *roots, got_b
         )
         below_b = band_shift(up, 1, 0, 0)
         above_b = band_shift(down, 3, 0, 0)
@@ -627,7 +612,7 @@
             second_a_body,
             root_spaces + any_ * 6,
             [rows(6)] * 2,
-            [held(10), held(5)] + sems(15),
+            [held(5)] + sems(15),
             *roots,
             sent_a,
             got_a,
@@ -639,43 +624,36 @@
         )
         far_a = band_shift(far, 2, 0, 0)
         turned_a = band_shift(turn, 0, 1, 0)
-        crossed_b, below_b, above_b, _ = lax.optimization_barrier((crossed_b, below_b, above_b, (far, turn)))
-        far, turn, amp = call(
-            second_b_body,
-            root_spaces + any_ * 5,
-            [rows(1), rows(1), (128, 256)],
-            any_ * 2 + [VMEM],
-            [held(2), VMEM((128, 256), BF16)] + sems(5),
-            (*roots, got_b, crossed_b, below_b, above_b, far_memory(amplitudes)),
-            flops=10**10,
-        )
-        far_b = band_shift(far, 2, 0, 0)
-        turned_b = band_shift(turn, 0, 1, 0)
+
+        behind = (crossed_b, below_b, above_b, amp)
+        amp = call(arrival_body, any_ * 3 + [VMEM], [(128, 256)], [VMEM], [], behind, flops=10**10)
         far_a, turned_a, amp = lax.optimization_barrier((far_a, turned_a, amp))
 
     with jax.named_scope("transform"):
         big = VMEM((512, 1024), BF16)
         from_all = (GRID, 64 + 128, 256)
-        freq = call(
+        freq, tiles, second, far, turn = call(
             forward_body,
-            root_spaces + any_ * 13,
-            [from_all],
-            any_,
-            [held(SHARE), held(1), big, big, VMEM((512, 256), BF16), VMEM((128, 256), BF16)] + sems(21),
+            root_spaces + any_ * 14,
+            [from_all, (BAND * XL, 128)] + [rows(1)] * 3,
+            any_ + [VMEM] * 4,
+            [held(SHARE), held(1), big, big, VMEM((512, 256), BF16), VMEM((128, 256), BF16), held(7)] + sems(31),
             roots
-            + (got_a, got_b, crossed_a, below_a, above_a, crossed_b, below_b, above_b, far_a, turned_a)
+            + (sent_a, got_a, got_b, crossed_a, below_a, above_a, crossed_b, below_b, above_b, far_a, turned_a)
             + (amp, const["mz"], const["ky"]),
             flops=2 * 10**10,
         )
         freq = lax.all_to_all(freq, "grid", 0, 0, tiled=True)
         amp = freq
+        far_b = band_shift(far, 2, 0, 0)
+        turned_b = band_shift(turn, 0, 1, 0)
         weights = call(
             weight_body,
-            any_ * 7,
+            [VMEM],
             [(N * XL, 128)],
             [VMEM],
-            [held(7)] + sems(7),
-            tuple(far_memory(v) for v in (sent_a, got_a, crossed_a, below_a, above_a, far_a, turned_a)),
+            [],
+            (tiles,),
             F32,
         )
         freq = call(
@@ -690,12 +668,12 @@
         freq = lax.all_to_all(freq, "grid", 0, 0, tiled=True)
         potential = call(
             backward_body,
-            root_spaces + any_ * 9 + [VMEM],
+            root_spaces + any_ * 6 + [VMEM],
             [(SHARE,) + PLANE],
             [VMEM],
             [held(1), VMEM((256, 256), BF16), big, VMEM((512, 512), BF16)] + sems(4),
             roots
-            + tuple(far_memory(v) for v in (got_b, crossed_b, below_b, above_b, far_b, turned_b))
+            + (second, far_b, turned_b)
             + (const["turn"], const["kyt"], const["mzt"], freq),
         )
 

time: 133 us -> 131 us (0.985)
  waiting for transfers between devices: 25.9 us -> 29.8 us
  Pallas kernels: 35.8 us -> 32.7 us
  starting transfers between devices: 49 us -> 46.5 us
    pallas_call x11, Pallas kernels: 26.9 us -> 23.7 us  [call(): pl.pallas_call(body, out_shape=shapes if many else shapes[0], in_specs=[p...]
    ppermute x27, waiting for transfers between devices: 17.8 us -> 20.6 us  [band_shift(): return lax.ppermute(value, 'band', pairs)]
    ppermute x27, starting transfers between devices: 37.5 us -> 34.8 us  [band_shift(): return lax.ppermute(value, 'band', pairs)]
  transfers between devices with their start and end apart: 29 -> 29, of which waited for: 11 -> 12; matrix products, arithmetic and copies ran while one was open for 0% -> 0% of each run, Pallas kernels for 13% -> 11%
where the time goes in v4:
time: 131 us; the launch traced here: 130 us
  starting transfers between devices  46.5 us (35%)
  Pallas kernels  32.7 us (25%)
  waiting for transfers between devices  29.8 us (23%)
  blocking collectives  18.9 us (14%)
  local copies, waits for them, and re-layouts  1.32 us (1%)
    ppermute x27, starting transfers between devices, band_shift(): return lax.ppermute(value, 'band', pairs)  34.8 us
    pallas_call x11, Pallas kernels, call(): pl.pallas_call(body, out_shape=shapes if many else shapes[0], in_specs=[p...  23.7 us
    ppermute x27, waiting for transfers between devices, band_shift(): return lax.ppermute(value, 'band', pairs)  20.6 us
    all_to_all x1, blocking collectives, per_device(): lax.all_to_all(terms.reshape(GRID * BAND, XL, 128), ('grid', 'band'), 0,...  18.9 us
    all_to_all x2, starting transfers between devices, per_device(): freq = lax.all_to_all(freq, 'grid', 0, 0, tiled=True)  11.7 us
    all_to_all x2, waiting for transfers between devices, per_device(): freq = lax.all_to_all(freq, 'grid', 0, 0, tiled=True)  9.11 us
    pallas_call x2, Pallas kernels, slab_call(): pl.pallas_call(functools.partial(slab_body, last, names), out_shape=jax.S...  8.96 us
  transfers between devices with their start and end apart: 29, of which 12 were waited for; matrix products, arithmetic and copies ran while one was open for 0% of the time, Pallas kernels for 11%

profile of v4, /device:TPU:1, one launch (start us, length us, event | category | flops | bytes accessed | tf_op | source)
XLA Modules:
  0.0 130.1 jit_solution(17479197870622339828)
XLA Ops:
  1.3 1.8 %block_scatter.6.sent_a = bf16[14,8,4096]{2,1,0:T(8,128)(2,1)S(1)} custom-call(s32[1]{0:T(128)S(6)} %copy.14.ablock_ref, s32[1,2]{1,0:T(1,128)S(1)} %copy-done, s32[1,512]{1,0:T(1,128)} %kept_hbm.1, bf16[128,8,4096]{2,1,0:T(8,128)(2,1)} %fields.13, bf16[16,8,4096]{2,1,0:T(8,128)(2,1)} %occupied.13), custom_call_target="tpu_custom_call" | custom-call | flops 100000000 | bytes 1048576 | tf_op jit(solution)/shard_map/block_scatter/pallas_call | solution.py:473
  3.1 1.5 %collective-permute-start = (bf16[14,8,4096]{2,1,0:T(8,128)(2,1)S(1)}, bf16[14,8,4096]{2,1,0:T(8,128)(2,1)S(1)}, u32[]{:S(2)}, u32[]{:S(2)}) collective-permute-start(bf16[14,8,4096]{2,1,0:T(8,128)(2,1)S(1)} %block_scatter.6.sent_a), channel_id=1, source_target_pairs={{0,1},{1,0},{2,3},{3,2},{4,5},{5,4},{6,7},{7,6},{8,9},{9,8},{10,11... | collective-permute-start | bytes 2752520 | tf_op jit(solution)/shard_map/block_scatter/ppermute | solution.py:554
  4.6 2.1 %block_scatter.8 = (bf16[21,8,4096]{2,1,0:T(8,128)(2,1)S(1)}, bf16[128,256]{1,0:T(8,128)(2,1)S(1)}) custom-call(s32[1]{0:T(128)S(6)} %copy.14.ablock_ref, s32[1,2]{1,0:T(1,128)S(1)} %copy-done, bf16[128,8,4096]{2,1,0:T(8,128)(2,1)} %fields.13, bf16[16,8,4096]{2,1,0:T(8,128)(2,1)} %occupied.13, bf16[1,128,256]{2,1,0:T(8,128)(2,1)} %amp_hbm.1), custom_call_target="tpu_custom_call" | custom-call | flops 5000000000 | bytes 1048576 | tf_op jit(solution)/shard_map/block_scatter/pallas_call | solution.py:473
  6.7 2.0 %block_scatter.7 = (bf16[6,8,4096]{2,1,0:T(8,128)(2,1)S(1)}, bf16[6,8,4096]{2,1,0:T(8,128)(2,1)S(1)}, bf16[6,8,4096]{2,1,0:T(8,128)(2,1)S(1)}) custom-call(s32[1]{0:T(128)S(6)} %copy.14.ablock_ref, s32[1,2]{1,0:T(1,128)S(1)} %copy-done, bf16[128,8,4096]{2,1,0:T(8,128)(2,1)} %fields.13, bf16[16,8,4096]{2,1,0:T(8,128)(2,1)} %occupied.13, ...), custom_call_target="tpu_custom_call" | custom-call | flops 100000000 | bytes 1048576 | tf_op jit(solution)/shard_map/block_scatter/pallas_call | solution.py:473
  9.1 2.8 %collective-permute-start.2 = (bf16[6,8,4096]{2,1,0:T(8,128)(2,1)S(1)}, bf16[6,8,4096]{2,1,0:T(8,128)(2,1)S(1)}, u32[]{:S(2)}, u32[]{:S(2)}) collective-permute-start(bf16[6,8,4096]{2,1,0:T(8,128)(2,1)S(1)} %get-tuple-element.44), channel_id=1, source_target_pairs={{0,2},{1,3},{2,0},{3,1},{4,6},{5,7},{6,4},{7,5},{8,10},{9,11},{10,... | collective-permute-start | bytes 1179656 | tf_op jit(solution)/shard_map/block_scatter/ppermute | solution.py:554
  11.9 1.3 collective-permute-start.3
  13.2 1.4 %collective-permute-start.4 = (bf16[6,8,4096]{2,1,0:T(8,128)(2,1)S(1)}, bf16[6,8,4096]{2,1,0:T(8,128)(2,1)S(1)}, u32[]{:S(2)}, u32[]{:S(2)}) collective-permute-start(bf16[6,8,4096]{2,1,0:T(8,128)(2,1)S(1)} %get-tuple-element.46), channel_id=1, source_target_pairs={{0,12},{1,13},{2,14},{3,15},{4,0},{5,1},{6,2},{7,3},{8,4},{9,5},{1... | collective-permute-start | bytes 1179656 | tf_op jit(solution)/shard_map/block_scatter/ppermute | solution.py:554
  14.6 1.7 %block_scatter.9 = (bf16[5,8,4096]{2,1,0:T(8,128)(2,1)S(1)}, bf16[5,8,4096]{2,1,0:T(8,128)(2,1)S(1)}, bf16[5,8,4096]{2,1,0:T(8,128)(2,1)S(1)}) custom-call(s32[1]{0:T(128)S(6)} %copy.14.ablock_ref, s32[1,2]{1,0:T(1,128)S(1)} %copy-done, bf16[128,8,4096]{2,1,0:T(8,128)(2,1)} %fields.13, bf16[16,8,4096]{2,1,0:T(8,128)(2,1)} %occupied.13, ...), custom_call_target="tpu_custom_call" | custom-call | flops 100000000 | bytes 1048576 | tf_op jit(solution)/shard_map/block_scatter/pallas_call | solution.py:473
  17.9 3.2 %collective-permute-done.2.crossed.crossed_a = bf16[6,8,4096]{2,1,0:T(8,128)(2,1)S(1)} collective-permute-done((bf16[6,8,4096]{2,1,0:T(8,128)(2,1)S(1)}, bf16[6,8,4096]{2,1,0:T(8,128)(2,1)S(1)}, u32[]{:S(2)}, u32[]{:S(2)}) %collective-permute-start.2) | collective-permute-done | bytes 393248 | tf_op jit(solution)/shard_map/block_scatter/ppermute | solution.py:554
  21.0 2.8 %collective-permute-start.7 = (bf16[5,8,4096]{2,1,0:T(8,128)(2,1)S(1)}, bf16[5,8,4096]{2,1,0:T(8,128)(2,1)S(1)}, u32[]{:S(2)}, u32[]{:S(2)}) collective-permute-start(bf16[5,8,4096]{2,1,0:T(8,128)(2,1)S(1)} %get-tuple-element.48), channel_id=1, source_target_pairs={{0,12},{1,13},{2,14},{3,15},{4,0},{5,1},{6,2},{7,3},{8,4},{9,5},{1... | collective-permute-start | bytes 983048 | tf_op jit(solution)/shard_map/block_scatter/ppermute | solution.py:554
  23.9 1.6 %block_scatter.10 = (bf16[6,8,4096]{2,1,0:T(8,128)(2,1)S(1)}, bf16[6,8,4096]{2,1,0:T(8,128)(2,1)S(1)}) custom-call(s32[1]{0:T(128)S(6)} %copy.14.ablock_ref, s32[1,2]{1,0:T(1,128)S(1)} %copy-done, bf16[128,8,4096]{2,1,0:T(8,128)(2,1)} %fields.13, bf16[16,8,4096]{2,1,0:T(8,128)(2,1)} %occupied.13, bf16[14,8,4096]{2,1,0:T(8,128)(2,1)S(1)} %block_scatter.6.sent_a, ...), custom_call_target="tpu_custom_call" | custom-call | flops 10000000000 | bytes 1048576 | tf_op jit(solution)/shard_map/block_scatter/pallas_call | solution.py:473
  25.5 1.9 %collective-permute-start.8 = (bf16[6,8,4096]{2,1,0:T(8,128)(2,1)S(1)}, bf16[6,8,4096]{2,1,0:T(8,128)(2,1)S(1)}, u32[]{:S(2)}, u32[]{:S(2)}) collective-permute-start(bf16[6,8,4096]{2,1,0:T(8,128)(2,1)S(1)} %get-tuple-element.53), channel_id=1, source_target_pairs={{0,8},{1,9},{2,10},{3,11},{4,12},{5,13},{6,14},{7,15},{8,0},{9,1},... | collective-permute-start | bytes 1179656 | tf_op jit(solution)/shard_map/block_scatter/ppermute | solution.py:554
  27.4 1.8 %collective-permute-start.9 = (bf16[6,8,4096]{2,1,0:T(8,128)(2,1)S(1)}, bf16[6,8,4096]{2,1,0:T(8,128)(2,1)S(1)}, u32[]{:S(2)}, u32[]{:S(2)}) collective-permute-start(bf16[6,8,4096]{2,1,0:T(8,128)(2,1)S(1)} %get-tuple-element.54), channel_id=1, source_target_pairs={{0,2},{1,3},{2,0},{3,1},{4,6},{5,7},{6,4},{7,5},{8,10},{9,11},{10,... | collective-permute-start | bytes 1179656 | tf_op jit(solution)/shard_map/block_scatter/ppermute | solution.py:554
  30.4 9.5 %collective-permute-done.8.far = bf16[6,8,4096]{2,1,0:T(8,128)(2,1)S(1)} collective-permute-done((bf16[6,8,4096]{2,1,0:T(8,128)(2,1)S(1)}, bf16[6,8,4096]{2,1,0:T(8,128)(2,1)S(1)}, u32[]{:S(2)}, u32[]{:S(2)}) %collective-permute-start.8) | collective-permute-done | bytes 393248 | tf_op jit(solution)/shard_map/block_scatter/ppermute | solution.py:554
  40.0 3.9 %transform.4 = (bf16[8,192,256]{2,1,0:T(8,128)(2,1)}, bf16[128,128]{1,0:T(8,128)(2,1)S(1)}, bf16[1,8,4096]{2,1,0:T(8,128)(2,1)S(1)}, bf16[1,8,4096]{2,1,0:T(8,128)(2,1)S(1)}, bf16[1,8,4096]{2,1,0:T(8,128)(2,1)S(1)}) custom-call(s32[1]{0:T(128)S(6)} %copy.14.ablock_ref, s32[1,2]{1,0:T(1,128)S(1)} %copy-done.1, bf16[128,8,4096]{2,1,0:T(8,128)(2,1)} %fields.13, ...), custom_call_target="tpu_custom_call" | custom-call | flops 20000000000 | bytes 1048576 | tf_op jit(solution)/shard_map/transform/pallas_call | solution.py:473
  43.9 5.1 %all-to-all-start = ((bf16[8,192,256]{2,1,0:T(8,128)(2,1)}), bf16[8,192,256]{2,1,0:T(8,128)(2,1)S(1)}, u32[]{:S(2)}, u32[]{:S(2)}) async-start(bf16[8,192,256]{2,1,0:T(8,128)(2,1)} %get-tuple-element.62), calls=%async_computation | async-start | bytes 1572864 | tf_op jit(solution)/shard_map/transform/all_to_all | solution.py:646
  49.4 8.3 %all-to-all-done.y_hbm.refs_7_ = bf16[8,192,256]{2,1,0:T(8,128)(2,1)S(1)} async-done(((bf16[8,192,256]{2,1,0:T(8,128)(2,1)}), bf16[8,192,256]{2,1,0:T(8,128)(2,1)S(1)}, u32[]{:S(2)}, u32[]{:S(2)}) %all-to-all-start) | async-done | bytes 786464 | tf_op jit(solution)/shard_map/transform/all_to_all | solution.py:646
  57.8 3.6 %transform.6 = bf16[512,256]{1,0:T(8,128)(2,1)} custom-call(bf16[8,192,256]{2,1,0:T(8,128)(2,1)S(1)} %all-to-all-done.y_hbm.refs_7_, f32[512,128]{1,0:T(8,128)S(1)} %transform.5.weight_ref, bf16[256,256]{1,0:T(8,128)(2,1)} %constant.22.clone.turn_hbm, bf16[512,1024]{1,0:T(8,128)(2,1)} %constant.20.clone.kx_hbm, bf16[512,1024]{1,0:T(8,128)(2,1)} %constant.21.clone.kxt_hbm), custom_call_target="tpu_custom_call" | custom-call | flops 10000000000 | bytes 1048576 | tf_op jit(solution)/shard_map/transform/pallas_call | solution.py:473
  61.3 6.6 %all-to-all-start.1 = ((bf16[8,64,256]{2,1,0:T(8,128)(2,1)}), bf16[8,64,256]{2,1,0:T(8,128)(2,1)S(1)}, u32[]{:S(2)}, u32[]{:S(2)}) async-start(bf16[8,64,256]{2,1,0:T(8,128)(2,1)} %bitcast), calls=%async_computation.1 | async-start | bytes 524288 | tf_op jit(solution)/shard_map/transform/all_to_all | solution.py:668
  68.7 3.8 %collective-permute-done.10.far = bf16[1,8,4096]{2,1,0:T(8,128)(2,1)S(1)} collective-permute-done((bf16[1,8,4096]{2,1,0:T(8,128)(2,1)S(1)}, bf16[1,8,4096]{2,1,0:T(8,128)(2,1)S(1)}, u32[]{:S(2)}, u32[]{:S(2)}) %collective-permute-start.10) | collective-permute-done | bytes 65568 | tf_op jit(solution)/shard_map/transform/ppermute | solution.py:554
  74.0 3.1 %transform.7 = bf16[4,8,4096]{2,1,0:T(8,128)(2,1)S(1)} custom-call(s32[1]{0:T(128)S(6)} %copy.14.ablock_ref, s32[1,2]{1,0:T(1,128)S(1)} %copy-done.1, bf16[128,8,4096]{2,1,0:T(8,128)(2,1)} %fields.13, bf16[16,8,4096]{2,1,0:T(8,128)(2,1)} %occupied.13, bf16[1,8,4096]{2,1,0:T(8,128)(2,1)S(1)} %get-tuple-element.59.second, ...), custom_call_target="tpu_custom_call" | custom-call | flops 100000000 | bytes 1048576 | tf_op jit(solution)/shard_map/transform/pallas_call | solution.py:473
  77.1 1.8 %collective-permute-start.12 = (bf16[32,4096]{1,0:T(8,128)(2,1)S(1)}, bf16[32,4096]{1,0:T(8,128)(2,1)S(1)}, u32[]{:S(2)}, u32[]{:S(2)}) collective-permute-start(bf16[32,4096]{1,0:T(8,128)(2,1)S(1)} %bitcast.5), channel_id=1, source_target_pairs={{0,8},{1,9},{2,10},{3,11},{4,12},{5,13},{6,14},{7,15},{8,0},{9,1},... | collective-permute-start | bytes 786440 | tf_op jit(solution)/shard_map/block_gather/ppermute | solution.py:554
  79.4 2.0 %collective-permute-start.19 = (bf16[32,4096]{1,0:T(8,128)(2,1)S(1)}, bf16[32,4096]{1,0:T(8,128)(2,1)S(1)}, u32[]{:S(2)}, u32[]{:S(2)}) collective-permute-start(bf16[32,4096]{1,0:T(8,128)(2,1)S(1)} %bitcast.7), channel_id=1, source_target_pairs={{0,4},{1,5},{2,6},{3,7},{4,8},{5,9},{6,10},{7,11},{8,12},{9,13},{1... | collective-permute-start | bytes 786440 | tf_op jit(solution)/shard_map/block_gather/ppermute | solution.py:554
  82.1 4.3 %collective-permute-start.17 = (bf16[32,4096]{1,0:T(8,128)(2,1)S(1)}, bf16[32,4096]{1,0:T(8,128)(2,1)S(1)}, u32[]{:S(2)}, u32[]{:S(2)}) collective-permute-start(bf16[32,4096]{1,0:T(8,128)(2,1)S(1)} %bitcast.9), channel_id=1, source_target_pairs={{0,1},{1,0},{2,3},{3,2},{4,5},{5,4},{6,7},{7,6},{8,9},{9,8},{10,11... | collective-permute-start | bytes 786440 | tf_op jit(solution)/shard_map/block_gather/ppermute | solution.py:554
  86.4 3.4 %block_gather.3.u_ref = bf16[1024,4096]{1,0:T(8,128)(2,1)S(1)} custom-call(bf16[1024,4096]{1,0:T(8,128)(2,1)} %bitcast.13), custom_call_target="tpu_custom_call" | custom-call | flops 100000000 | bytes 1048576 | tf_op jit(solution)/shard_map/block_gather/pallas_call | solution.py:473
  90.7 2.3 %collective-permute-start.20 = (bf16[32,4096]{1,0:T(8,128)(2,1)S(1)}, bf16[32,4096]{1,0:T(8,128)(2,1)S(1)}, u32[]{:S(2)}, u32[]{:S(2)}) collective-permute-start(bf16[32,4096]{1,0:T(8,128)(2,1)S(1)} %collective-permute-done.19.refs_4_), channel_id=1, source_target_pairs={{0,1},{1,0},{2,3},{3,2},{4,5},{5,4},{6,7},{7,6},{8,9},{9,8},{10,11... | collective-permute-start | bytes 786440 | tf_op jit(solution)/shard_map/block_gather/ppermute | solution.py:554
  93.1 1.6 %collective-permute-start.14 = (bf16[32,4096]{1,0:T(8,128)(2,1)S(1)}, bf16[32,4096]{1,0:T(8,128)(2,1)S(1)}, u32[]{:S(2)}, u32[]{:S(2)}) collective-permute-start(bf16[32,4096]{1,0:T(8,128)(2,1)S(1)} %collective-permute-done.12.refs_2_), channel_id=1, source_target_pairs={{0,2},{1,3},{2,0},{3,1},{4,6},{5,7},{6,4},{7,5},{8,10},{9,11},{10,... | collective-permute-start | bytes 786440 | tf_op jit(solution)/shard_map/block_gather/ppermute | solution.py:554
  95.5 2.0 %collective-permute-start.16 = (bf16[32,4096]{1,0:T(8,128)(2,1)S(1)}, bf16[32,4096]{1,0:T(8,128)(2,1)S(1)}, u32[]{:S(2)}, u32[]{:S(2)}) collective-permute-start(bf16[32,4096]{1,0:T(8,128)(2,1)S(1)} %collective-permute-done.13.refs_8_), channel_id=1, source_target_pairs={{0,12},{1,13},{2,14},{3,15},{4,0},{5,1},{6,2},{7,3},{8,4},{9,5},{1... | collective-permute-start | bytes 786440 | tf_op jit(solution)/shard_map/block_gather/ppermute | solution.py:554
  97.5 5.2 %block_gather.4.refs_6_ = f32[128,128]{1,0:T(8,128)S(1)} custom-call(bf16[1024,4096]{1,0:T(8,128)(2,1)S(1)} %block_gather.3.u_ref, bf16[32,4096]{1,0:T(8,128)(2,1)S(1)} %bitcast.10, bf16[32,4096]{1,0:T(8,128)(2,1)S(1)} %collective-permute-done.17.refs_1_, bf16[32,4096]{1,0:T(8,128)(2,1)S(1)} %collective-permute-done.12.refs_2_, ...), custom_call_target="tpu_custom_call" | custom-call | flops 2684354560 | bytes 8388608 | tf_op jit(solution)/shard_map/block_gather/pallas_call | solution.py:535
  103.1 1.5 %collective-permute-start.24 = (bf16[32,4096]{1,0:T(8,128)(2,1)S(1)}, bf16[32,4096]{1,0:T(8,128)(2,1)S(1)}, u32[]{:S(2)}, u32[]{:S(2)}) collective-permute-start(bf16[32,4096]{1,0:T(8,128)(2,1)S(1)} %collective-permute-done.14.refs_0_), channel_id=1, source_target_pairs={{0,1},{1,0},{2,3},{3,2},{4,5},{5,4},{6,7},{7,6},{8,9},{9,8},{10,11... | collective-permute-start | bytes 786440 | tf_op jit(solution)/shard_map/block_gather/ppermute | solution.py:554
  106.6 3.8 %block_gather.5 = bf16[1024,128]{1,0:T(8,128)(2,1)S(1)} custom-call(bf16[1024,4096]{1,0:T(8,128)(2,1)S(1)} %block_gather.3.u_ref, bf16[32,4096]{1,0:T(8,128)(2,1)S(1)} %collective-permute-done.14.refs_0_, bf16[32,4096]{1,0:T(8,128)(2,1)S(1)} %collective-permute-done.24.refs_1_, bf16[32,4096]{1,0:T(8,128)(2,1)S(1)} %collective-permute-done.15.refs_2_, ...), custom_call_target="tpu_custom_call" | custom-call | flops 1610612736 | bytes 8388608 | tf_op jit(solution)/shard_map/block_gather/pallas_call | solution.py:535
  110.4 18.9 %all_to_all.21 = bf16[128,8,128]{2,1,0:T(8,128)(2,1)S(1)} all-to-all(bf16[128,8,128]{2,1,0:T(8,128)(2,1)S(1)} %bitcast.12), channel_id=1, replica_groups=mesh['grid'=8,'band'=16] {'grid','band'}, dimensions={0} | all-to-all | bytes 524288 | tf_op jit(solution)/shard_map/ladder/all_to_all | solution.py:706
  (46 shorter events, 12.7 us)
Async XLA Ops:
  0.7 0.7 copy-start
  3.1 3.6 %collective-permute-start = (bf16[14,8,4096]{2,1,0:T(8,128)(2,1)S(1)}, bf16[14,8,4096]{2,1,0:T(8,128)(2,1)S(1)}, u32[]{:S(2)}, u32[]{:S(2)}) collective-permute-start(bf16[14,8,4096]{2,1,0:T(8,128)(2,1)S(1)} %block_scatter.6.sent_a), channel_id=1, source_target_pairs={{0,1},{1,0},{2,3},{3,2},{4,5},{5,4},{6,7},{7,6},{8,9},{9,8},{10,11... | collective-permute-start | bytes 2752520 | tf_op jit(solution)/shard_map/block_scatter/ppermute | solution.py:554
  8.7 5.9 %collective-permute-start.1 = (bf16[21,8,4096]{2,1,0:T(8,128)(2,1)S(1)}, bf16[21,8,4096]{2,1,0:T(8,128)(2,1)S(1)}, u32[]{:S(2)}, u32[]{:S(2)}) collective-permute-start(bf16[21,8,4096]{2,1,0:T(8,128)(2,1)S(1)} %get-tuple-element.43), channel_id=1, source_target_pairs={{0,1},{1,0},{2,3},{3,2},{4,5},{5,4},{6,7},{7,6},{8,9},{9,8},{10,11... | collective-permute-start | bytes 4128776 | tf_op jit(solution)/shard_map/block_scatter/ppermute | solution.py:554
  9.1 12.0 %collective-permute-start.2 = (bf16[6,8,4096]{2,1,0:T(8,128)(2,1)S(1)}, bf16[6,8,4096]{2,1,0:T(8,128)(2,1)S(1)}, u32[]{:S(2)}, u32[]{:S(2)}) collective-permute-start(bf16[6,8,4096]{2,1,0:T(8,128)(2,1)S(1)} %get-tuple-element.44), channel_id=1, source_target_pairs={{0,2},{1,3},{2,0},{3,1},{4,6},{5,7},{6,4},{7,5},{8,10},{9,11},{10,... | collective-permute-start | bytes 1179656 | tf_op jit(solution)/shard_map/block_scatter/ppermute | solution.py:554
  11.9 12.0 %collective-permute-start.3 = (bf16[6,8,4096]{2,1,0:T(8,128)(2,1)S(1)}, bf16[6,8,4096]{2,1,0:T(8,128)(2,1)S(1)}, u32[]{:S(2)}, u32[]{:S(2)}) collective-permute-start(bf16[6,8,4096]{2,1,0:T(8,128)(2,1)S(1)} %get-tuple-element.45), channel_id=1, source_target_pairs={{0,4},{1,5},{2,6},{3,7},{4,8},{5,9},{6,10},{7,11},{8,12},{9,13},{1... | collective-permute-start | bytes 1179656 | tf_op jit(solution)/shard_map/block_scatter/ppermute | solution.py:554
  13.2 10.7 %collective-permute-start.4 = (bf16[6,8,4096]{2,1,0:T(8,128)(2,1)S(1)}, bf16[6,8,4096]{2,1,0:T(8,128)(2,1)S(1)}, u32[]{:S(2)}, u32[]{:S(2)}) collective-permute-start(bf16[6,8,4096]{2,1,0:T(8,128)(2,1)S(1)} %get-tuple-element.46), channel_id=1, source_target_pairs={{0,12},{1,13},{2,14},{3,15},{4,0},{5,1},{6,2},{7,3},{8,4},{9,5},{1... | collective-permute-start | bytes 1179656 | tf_op jit(solution)/shard_map/block_scatter/ppermute | solution.py:554
  16.4 12.8 %collective-permute-start.5 = (bf16[5,8,4096]{2,1,0:T(8,128)(2,1)S(1)}, bf16[5,8,4096]{2,1,0:T(8,128)(2,1)S(1)}, u32[]{:S(2)}, u32[]{:S(2)}) collective-permute-start(bf16[5,8,4096]{2,1,0:T(8,128)(2,1)S(1)} %get-tuple-element.49), channel_id=1, source_target_pairs={{0,2},{1,3},{2,0},{3,1},{4,6},{5,7},{6,4},{7,5},{8,10},{9,11},{10,... | collective-permute-start | bytes 983048 | tf_op jit(solution)/shard_map/block_scatter/ppermute | solution.py:554
  16.7 13.7 %collective-permute-start.6 = (bf16[5,8,4096]{2,1,0:T(8,128)(2,1)S(1)}, bf16[5,8,4096]{2,1,0:T(8,128)(2,1)S(1)}, u32[]{:S(2)}, u32[]{:S(2)}) collective-permute-start(bf16[5,8,4096]{2,1,0:T(8,128)(2,1)S(1)} %get-tuple-element.47), channel_id=1, source_target_pairs={{0,4},{1,5},{2,6},{3,7},{4,8},{5,9},{6,10},{7,11},{8,12},{9,13},{1... | collective-permute-start | bytes 983048 | tf_op jit(solution)/shard_map/block_scatter/ppermute | solution.py:554
  21.0 9.4 %collective-permute-start.7 = (bf16[5,8,4096]{2,1,0:T(8,128)(2,1)S(1)}, bf16[5,8,4096]{2,1,0:T(8,128)(2,1)S(1)}, u32[]{:S(2)}, u32[]{:S(2)}) collective-permute-start(bf16[5,8,4096]{2,1,0:T(8,128)(2,1)S(1)} %get-tuple-element.48), channel_id=1, source_target_pairs={{0,12},{1,13},{2,14},{3,15},{4,0},{5,1},{6,2},{7,3},{8,4},{9,5},{1... | collective-permute-start | bytes 983048 | tf_op jit(solution)/shard_map/block_scatter/ppermute | solution.py:554
  25.5 14.4 %collective-permute-start.8 = (bf16[6,8,4096]{2,1,0:T(8,128)(2,1)S(1)}, bf16[6,8,4096]{2,1,0:T(8,128)(2,1)S(1)}, u32[]{:S(2)}, u32[]{:S(2)}) collective-permute-start(bf16[6,8,4096]{2,1,0:T(8,128)(2,1)S(1)} %get-tuple-element.53), channel_id=1, source_target_pairs={{0,8},{1,9},{2,10},{3,11},{4,12},{5,13},{6,14},{7,15},{8,0},{9,1},... | collective-permute-start | bytes 1179656 | tf_op jit(solution)/shard_map/block_scatter/ppermute | solution.py:554
  27.4 12.6 %collective-permute-start.9 = (bf16[6,8,4096]{2,1,0:T(8,128)(2,1)S(1)}, bf16[6,8,4096]{2,1,0:T(8,128)(2,1)S(1)}, u32[]{:S(2)}, u32[]{:S(2)}) collective-permute-start(bf16[6,8,4096]{2,1,0:T(8,128)(2,1)S(1)} %get-tuple-element.54), channel_id=1, source_target_pairs={{0,2},{1,3},{2,0},{3,1},{4,6},{5,7},{6,4},{7,5},{8,10},{9,11},{10,... | collective-permute-start | bytes 1179656 | tf_op jit(solution)/shard_map/block_scatter/ppermute | solution.py:554
  30.4 9.5 %copy-start.1 = (s32[1,2]{1,0:T(1,128)S(1)}, s32[1,2]{1,0:T(1,128)}, u32[]{:S(2)}) copy-start(s32[1,2]{1,0:T(1,128)} %pairs_ref.13) | copy-start | bytes 28
  43.9 13.9 %all-to-all-start = ((bf16[8,192,256]{2,1,0:T(8,128)(2,1)}), bf16[8,192,256]{2,1,0:T(8,128)(2,1)S(1)}, u32[]{:S(2)}, u32[]{:S(2)}) async-start(bf16[8,192,256]{2,1,0:T(8,128)(2,1)} %get-tuple-element.62), calls=%async_computation | async-start | bytes 1572864 | tf_op jit(solution)/shard_map/transform/all_to_all | solution.py:646
  61.3 12.7 %all-to-all-start.1 = ((bf16[8,64,256]{2,1,0:T(8,128)(2,1)}), bf16[8,64,256]{2,1,0:T(8,128)(2,1)S(1)}, u32[]{:S(2)}, u32[]{:S(2)}) async-start(bf16[8,64,256]{2,1,0:T(8,128)(2,1)} %bitcast), calls=%async_computation.1 | async-start | bytes 524288 | tf_op jit(solution)/shard_map/transform/all_to_all | solution.py:668
  67.9 4.6 %collective-permute-start.10 = (bf16[1,8,4096]{2,1,0:T(8,128)(2,1)S(1)}, bf16[1,8,4096]{2,1,0:T(8,128)(2,1)S(1)}, u32[]{:S(2)}, u32[]{:S(2)}) collective-permute-start(bf16[1,8,4096]{2,1,0:T(8,128)(2,1)S(1)} %get-tuple-element.60), channel_id=1, source_target_pairs={{0,8},{1,9},{2,10},{3,11},{4,12},{5,13},{6,14},{7,15},{8,0},{9,1},... | collective-permute-start | bytes 196616 | tf_op jit(solution)/shard_map/transform/ppermute | solution.py:554
  67.9 5.3 %collective-permute-start.11 = (bf16[1,8,4096]{2,1,0:T(8,128)(2,1)S(1)}, bf16[1,8,4096]{2,1,0:T(8,128)(2,1)S(1)}, u32[]{:S(2)}, u32[]{:S(2)}) collective-permute-start(bf16[1,8,4096]{2,1,0:T(8,128)(2,1)S(1)} %get-tuple-element.61), channel_id=1, source_target_pairs={{0,2},{1,3},{2,0},{3,1},{4,6},{5,7},{6,4},{7,5},{8,10},{9,11},{10,... | collective-permute-start | bytes 196616 | tf_op jit(solution)/shard_map/transform/ppermute | solution.py:554
  77.1 12.7 %collective-permute-start.12 = (bf16[32,4096]{1,0:T(8,128)(2,1)S(1)}, bf16[32,4096]{1,0:T(8,128)(2,1)S(1)}, u32[]{:S(2)}, u32[]{:S(2)}) collective-permute-start(bf16[32,4096]{1,0:T(8,128)(2,1)S(1)} %bitcast.5), channel_id=1, source_target_pairs={{0,8},{1,9},{2,10},{3,11},{4,12},{5,13},{6,14},{7,15},{8,0},{9,1},... | collective-permute-start | bytes 786440 | tf_op jit(solution)/shard_map/block_gather/ppermute | solution.py:554
  79.0 10.8 %collective-permute-start.13 = (bf16[32,4096]{1,0:T(8,128)(2,1)S(1)}, bf16[32,4096]{1,0:T(8,128)(2,1)S(1)}, u32[]{:S(2)}, u32[]{:S(2)}) collective-permute-start(bf16[32,4096]{1,0:T(8,128)(2,1)S(1)} %bitcast.6), channel_id=1, source_target_pairs={{0,2},{1,3},{2,0},{3,1},{4,6},{5,7},{6,4},{7,5},{8,10},{9,11},{10,... | collective-permute-start | bytes 786440 | tf_op jit(solution)/shard_map/block_gather/ppermute | solution.py:554
  79.4 11.3 %collective-permute-start.19 = (bf16[32,4096]{1,0:T(8,128)(2,1)S(1)}, bf16[32,4096]{1,0:T(8,128)(2,1)S(1)}, u32[]{:S(2)}, u32[]{:S(2)}) collective-permute-start(bf16[32,4096]{1,0:T(8,128)(2,1)S(1)} %bitcast.7), channel_id=1, source_target_pairs={{0,4},{1,5},{2,6},{3,7},{4,8},{5,9},{6,10},{7,11},{8,12},{9,13},{1... | collective-permute-start | bytes 786440 | tf_op jit(solution)/shard_map/block_gather/ppermute | solution.py:554
  81.4 11.7 %collective-permute-start.21 = (bf16[32,4096]{1,0:T(8,128)(2,1)S(1)}, bf16[32,4096]{1,0:T(8,128)(2,1)S(1)}, u32[]{:S(2)}, u32[]{:S(2)}) collective-permute-start(bf16[32,4096]{1,0:T(8,128)(2,1)S(1)} %bitcast.8), channel_id=1, source_target_pairs={{0,12},{1,13},{2,14},{3,15},{4,0},{5,1},{6,2},{7,3},{8,4},{9,5},{1... | collective-permute-start | bytes 786440 | tf_op jit(solution)/shard_map/block_gather/ppermute | solution.py:554
  82.1 11.0 %collective-permute-start.17 = (bf16[32,4096]{1,0:T(8,128)(2,1)S(1)}, bf16[32,4096]{1,0:T(8,128)(2,1)S(1)}, u32[]{:S(2)}, u32[]{:S(2)}) collective-permute-start(bf16[32,4096]{1,0:T(8,128)(2,1)S(1)} %bitcast.9), channel_id=1, source_target_pairs={{0,1},{1,0},{2,3},{3,2},{4,5},{5,4},{6,7},{7,6},{8,9},{9,8},{10,11... | collective-permute-start | bytes 786440 | tf_op jit(solution)/shard_map/block_gather/ppermute | solution.py:554
  89.8 4.8 %collective-permute-start.18 = (bf16[32,4096]{1,0:T(8,128)(2,1)S(1)}, bf16[32,4096]{1,0:T(8,128)(2,1)S(1)}, u32[]{:S(2)}, u32[]{:S(2)}) collective-permute-start(bf16[32,4096]{1,0:T(8,128)(2,1)S(1)} %collective-permute-done.12.refs_2_), channel_id=1, source_target_pairs={{0,1},{1,0},{2,3},{3,2},{4,5},{5,4},{6,7},{7,6},{8,9},{9,8},{10,11... | collective-permute-start | bytes 786440 | tf_op jit(solution)/shard_map/block_gather/ppermute | solution.py:554
  90.5 5.0 %collective-permute-start.23 = (bf16[32,4096]{1,0:T(8,128)(2,1)S(1)}, bf16[32,4096]{1,0:T(8,128)(2,1)S(1)}, u32[]{:S(2)}, u32[]{:S(2)}) collective-permute-start(bf16[32,4096]{1,0:T(8,128)(2,1)S(1)} %collective-permute-done.13.refs_8_), channel_id=1, source_target_pairs={{0,1},{1,0},{2,3},{3,2},{4,5},{5,4},{6,7},{7,6},{8,9},{9,8},{10,11... | collective-permute-start | bytes 786440 | tf_op jit(solution)/shard_map/block_gather/ppermute | solution.py:554
  90.7 6.7 %collective-permute-start.20 = (bf16[32,4096]{1,0:T(8,128)(2,1)S(1)}, bf16[32,4096]{1,0:T(8,128)(2,1)S(1)}, u32[]{:S(2)}, u32[]{:S(2)}) collective-permute-start(bf16[32,4096]{1,0:T(8,128)(2,1)S(1)} %collective-permute-done.19.refs_4_), channel_id=1, source_target_pairs={{0,1},{1,0},{2,3},{3,2},{4,5},{5,4},{6,7},{7,6},{8,9},{9,8},{10,11... | collective-permute-start | bytes 786440 | tf_op jit(solution)/shard_map/block_gather/ppermute | solution.py:554
  93.1 4.4 %collective-permute-start.22 = (bf16[32,4096]{1,0:T(8,128)(2,1)S(1)}, bf16[32,4096]{1,0:T(8,128)(2,1)S(1)}, u32[]{:S(2)}, u32[]{:S(2)}) collective-permute-start(bf16[32,4096]{1,0:T(8,128)(2,1)S(1)} %collective-permute-done.21.refs_6_), channel_id=1, source_target_pairs={{0,1},{1,0},{2,3},{3,2},{4,5},{5,4},{6,7},{7,6},{8,9},{9,8},{10,11... | collective-permute-start | bytes 786440 | tf_op jit(solution)/shard_map/block_gather/ppermute | solution.py:554
  93.1 9.6 %collective-permute-start.14 = (bf16[32,4096]{1,0:T(8,128)(2,1)S(1)}, bf16[32,4096]{1,0:T(8,128)(2,1)S(1)}, u32[]{:S(2)}, u32[]{:S(2)}) collective-permute-start(bf16[32,4096]{1,0:T(8,128)(2,1)S(1)} %collective-permute-done.12.refs_2_), channel_id=1, source_target_pairs={{0,2},{1,3},{2,0},{3,1},{4,6},{5,7},{6,4},{7,5},{8,10},{9,11},{10,... | collective-permute-start | bytes 786440 | tf_op jit(solution)/shard_map/block_gather/ppermute | solution.py:554
  94.7 8.5 %collective-permute-start.15 = (bf16[32,4096]{1,0:T(8,128)(2,1)S(1)}, bf16[32,4096]{1,0:T(8,128)(2,1)S(1)}, u32[]{:S(2)}, u32[]{:S(2)}) collective-permute-start(bf16[32,4096]{1,0:T(8,128)(2,1)S(1)} %collective-permute-done.13.refs_8_), channel_id=1, source_target_pairs={{0,4},{1,5},{2,6},{3,7},{4,8},{5,9},{6,10},{7,11},{8,12},{9,13},{1... | collective-permute-start | bytes 786440 | tf_op jit(solution)/shard_map/block_gather/ppermute | solution.py:554
  95.5 7.7 %collective-permute-start.16 = (bf16[32,4096]{1,0:T(8,128)(2,1)S(1)}, bf16[32,4096]{1,0:T(8,128)(2,1)S(1)}, u32[]{:S(2)}, u32[]{:S(2)}) collective-permute-start(bf16[32,4096]{1,0:T(8,128)(2,1)S(1)} %collective-permute-done.13.refs_8_), channel_id=1, source_target_pairs={{0,12},{1,13},{2,14},{3,15},{4,0},{5,1},{6,2},{7,3},{8,4},{9,5},{1... | collective-permute-start | bytes 786440 | tf_op jit(solution)/shard_map/block_gather/ppermute | solution.py:554
  103.1 2.7 %collective-permute-start.24 = (bf16[32,4096]{1,0:T(8,128)(2,1)S(1)}, bf16[32,4096]{1,0:T(8,128)(2,1)S(1)}, u32[]{:S(2)}, u32[]{:S(2)}) collective-permute-start(bf16[32,4096]{1,0:T(8,128)(2,1)S(1)} %collective-permute-done.14.refs_0_), channel_id=1, source_target_pairs={{0,1},{1,0},{2,3},{3,2},{4,5},{5,4},{6,7},{7,6},{8,9},{9,8},{10,11... | collective-permute-start | bytes 786440 | tf_op jit(solution)/shard_map/block_gather/ppermute | solution.py:554
  104.7 1.5 %collective-permute-start.25 = (bf16[32,4096]{1,0:T(8,128)(2,1)S(1)}, bf16[32,4096]{1,0:T(8,128)(2,1)S(1)}, u32[]{:S(2)}, u32[]{:S(2)}) collective-permute-start(bf16[32,4096]{1,0:T(8,128)(2,1)S(1)} %collective-permute-done.15.refs_2_), channel_id=1, source_target_pairs={{0,1},{1,0},{2,3},{3,2},{4,5},{5,4},{6,7},{7,6},{8,9},{9,8},{10,11... | collective-permute-start | bytes 786440 | tf_op jit(solution)/shard_map/block_gather/ppermute | solution.py:554
  104.7 1.9 %collective-permute-start.26 = (bf16[32,4096]{1,0:T(8,128)(2,1)S(1)}, bf16[32,4096]{1,0:T(8,128)(2,1)S(1)}, u32[]{:S(2)}, u32[]{:S(2)}) collective-permute-start(bf16[32,4096]{1,0:T(8,128)(2,1)S(1)} %collective-permute-done.16.refs_4_), channel_id=1, source_target_pairs={{0,1},{1,0},{2,3},{3,2},{4,5},{5,4},{6,7},{7,6},{8,9},{9,8},{10,11... | collective-permute-start | bytes 786440 | tf_op jit(solution)/shard_map/block_gather/ppermute | solution.py:554

commit v5 on v4

--- a/solution.py
+++ b/solution.py
@@ -104,32 +104,6 @@
     wait_all(moves)
 
 
-def added(marks, sems, groups):
-    def start():
-        moves, slot = [], 0
-        for sources, _ in groups:
-            part = [(marks.at[slot + i : slot + i + 1], [(None, v)]) for i, v in enumerate(sources)]
-            moves.append((slot, copies(sems.at[slot : slot + len(part)], part)))
-            slot += len(part)
-        return functools.partial(finish, moves, slot)
-
-    def finish(moves, slot):
-        out = []
-        for (first, waits), (sources, targets) in zip(moves, groups, strict=True):
-            wait_all(waits)
-            total = marks[first].astype(F32)
-            for i in range(1, len(sources)):
-                total += marks[first + i].astype(F32)
-            marks[first] = total.astype(BF16)
-            for target in targets:
-                out.append(pltpu.make_async_copy(marks.at[first : first + 1], target, sems.at[slot]))
-                out[-1].start()
-                slot += 1
-        return out
-
-    return start
-
-
 def wait_all(waits):
     for move in waits:
         move.wait()
@@ -164,8 +138,8 @@
     at = Roots(ablock_ref, pairs_ref, fields, occupied)
     other, there = 1 - at.c, 1 - at.h
     sources = [at.block(other, dy, there, 4) for dy in (1, 3, 2)]
-    jobs = [(out.at[4 * i : 4 * i + 4], [(None, v)]) for i, v in enumerate(sources)]
-    jobs.append((out.at[12:13], [(None, at.orbital(0))]))
+    jobs = [(plane(out, pl.ds(4 * i, 4)), [(None, v)]) for i, v in enumerate(sources)]
+    jobs.append((plane(out, pl.ds(12, 1)), [(None, at.orbital(0))]))
 
     def start():
         (wait,) = copies(sems.at[9:], [(kept_ref, [(None, kept_hbm)])])
@@ -182,11 +156,8 @@
         row = lax.broadcasted_iota(jnp.int32, mask.shape, 0)
         lane = lax.broadcasted_iota(jnp.int32, mask.shape, 1)
         mask = jnp.where(row % XL == lane // 16, mask, 0.0)
-        tile = jnp.sum(mask.reshape(XL, XL, 128), axis=1)
-        band = lax.axis_index("band")
-        tiles = [jnp.where(band == n, tile, 0.0) for n in range(2 * BAND)]
-        marks[0] = jnp.concatenate(tiles, axis=1).astype(BF16)
-        move = pltpu.make_async_copy(marks, out.at[13:], sems.at[8])
+        marks[0] = jnp.sum(mask.reshape(XL, XL, 128), axis=1).astype(BF16)
+        move = pltpu.make_async_copy(marks, marks_of(out, pl.ds(0, 1)), sems.at[8])
         move.start()
         return [move]
 
@@ -213,20 +184,26 @@
     wait_all(moves)
 
 
-def first_a_body(
-    ablock_ref, pairs_ref, fields, occupied, sent_a, got_a, up, down, across, marks, sems
-):
+def own_marks(at, target, sent_a, got_a):
+    return [
+        (marks_of(target, pl.ds(at.c, 1)), [(None, marks_of(sent_a, pl.ds(0, 1)))]),
+        (marks_of(target, pl.ds(1 - at.c, 1)), [(None, marks_of(got_a, pl.ds(0, 1)))]),
+    ]
+
+
+def first_a_body(ablock_ref, pairs_ref, fields, occupied, sent_a, got_a, up, down, across, sems):
     at = Roots(ablock_ref, pairs_ref, fields, occupied)
     mine, theirs = at.same_c[0], jnp.logical_not(at.same_c[0])
     jobs = []
     for i, (target, dy) in enumerate(((up, 1), (down, 3), (across, 2))):
         own = at.block(at.c, dy, 1 - at.h, 4)
-        jobs.append((target.at[:4], [(mine, own), (theirs, got_a.at[4 * i : 4 * i + 4])]))
+        jobs.append((plane(target, pl.ds(0, 4)), [(mine, own), (theirs, plane(got_a, pl.ds(4 * i, 4)))]))
     mine, theirs = at.same_c[1], jnp.logical_not(at.same_c[1])
     for target in (up, down, across):
-        jobs.append((target.at[4:5], [(mine, at.orbital(0)), (theirs, got_a.at[12:13])]))
-    groups = [([sent_a.at[13:], got_a.at[13:]], [v.at[5:] for v in (up, down, across)])]
-    gather(sems, jobs, added(marks, sems.at[12:], groups))
+        partner = plane(got_a, pl.ds(12, 1))
+        jobs.append((plane(target, pl.ds(4, 1)), [(mine, at.orbital(0)), (theirs, partner)]))
+        jobs += own_marks(at, target, sent_a, got_a)
+    gather(sems, jobs)
 
 
 def first_b_body(ablock_ref, pairs_ref, fields, occupied, got_b, up, down, across, sems):
@@ -243,37 +220,25 @@
 
 
 def second_a_body(
-    ablock_ref,
-    pairs_ref,
-    fields,
-    occupied,
-    sent_a,
-    got_a,
-    got_b,
-    crossed,
-    below,
-    above,
-    far,
-    turn,
-    marks,
-    sems,
+    ablock_ref, pairs_ref, fields, occupied, sent_a, got_a, got_b, crossed, below, above, far, turn, sems
 ):
     at = Roots(ablock_ref, pairs_ref, fields, occupied)
     not_ = jnp.logical_not
     jobs = []
-    own_rows = (at.block(at.c, 2, at.h, 4), got_b.at[12:16], slice(0, 4))
-    own_orbital = (at.orbital(0), got_a.at[12:13], slice(4, 5))
+    own_rows = (at.block(at.c, 2, at.h, 4), got_b.at[12:16], pl.ds(0, 4))
+    own_orbital = (at.orbital(0), plane(got_a, pl.ds(12, 1)), pl.ds(4, 1))
     for k, (own, core, part) in enumerate((own_rows, own_orbital)):
         same_h, same_c = at.same_h[k], at.same_c[k]
-        choices = [(same_h & same_c, own), (same_h & not_(same_c), core), (not_(same_h), crossed.at[part])]
-        jobs.append((far.at[part], choices))
+        other = plane(crossed, part)
+        choices = [(same_h & same_c, own), (same_h & not_(same_c), core), (not_(same_h), other)]
+        jobs.append((plane(far, part), choices))
         from_below = at.away[k] == 1
-        jobs.append((turn.at[part], [(from_below, below.at[part]), (not_(from_below), above.at[part])]))
-    groups = [
-        ([sent_a.at[13:], got_a.at[13:], crossed.at[5:]], [far.at[5:]]),
-        ([below.at[5:], above.at[5:]], [turn.at[5:]]),
-    ]
-    gather(sems, jobs, added(marks, sems.at[8:], groups))
+        choices = [(from_below, plane(below, part)), (not_(from_below), plane(above, part))]
+        jobs.append((plane(turn, part), choices))
+    jobs += own_marks(at, far, sent_a, got_a)
+    for target, first, source in ((far, 2, crossed), (turn, 0, below), (turn, 2, above)):
+        jobs.append((marks_of(target, pl.ds(first, 2)), [(None, marks_of(source, pl.ds(0, 2)))]))
+    gather(sems, jobs)
 
 
 def arrived(at, k, own, core, cross, far, below, above, turned):
@@ -320,20 +285,27 @@
     ky_ref,
     out_ref,
     amp_ref,
-    marks,
     sems,
 ):
     at = Roots(ablock_ref, pairs_ref, fields, occupied)
-    rows = [v.at[:4] for v in (crossed_b, far, below_b, above_b, turned)]
-    orbital = [v.at[4:5] for v in (crossed_a, far, below_a, above_a, turned)]
+    rows = [crossed_b.at[:4], plane(far, pl.ds(0, 4)), below_b.at[:4], above_b.at[:4], plane(turned, pl.ds(0, 4))]
+    orbital = [plane(v, pl.ds(4, 1)) for v in (crossed_a, far, below_a, above_a, turned)]
     jobs = [
         (u_ref, arrived(at, 0, at.block(at.c, 0, at.h, 4), got_b.at[16:20], *rows)),
-        (o_ref, arrived(at, 1, at.orbital(0), got_a.at[12:13], *orbital)),
+        (o_ref, arrived(at, 1, at.orbital(0), plane(got_a, pl.ds(12, 1)), *orbital)),
     ]
     jobs += [(mz_ref, [(None, mz_hbm)]), (ky_ref, [(None, ky_hbm)]), (amp_ref, [(None, amp_hbm)])]
     u_wait, o_wait, mz_wait, ky_wait, amp_wait = copies(sems, jobs)
-    sources = [sent_a.at[13:], got_a.at[13:]] + [v.at[5:] for v in (crossed_a, below_a, above_a, far, turned)]
-    mark_waits = copies(sems.at[21:], [(marks.at[i : i + 1], [(None, v)]) for i, v in enumerate(sources)])
+    device = lambda dy, dh, c: 4 * ((at.y + dy) % 4) + 2 * ((at.h + dh) % 2) + c
+    jobs = [
+        (tiles_ref.at[pl.ds(device(0, 0, at.c), 1)], [(None, marks_of(sent_a, pl.ds(0, 1)))]),
+        (tiles_ref.at[pl.ds(device(0, 0, 1 - at.c), 1)], [(None, marks_of(got_a, pl.ds(0, 1)))]),
+    ]
+    pairs = [(0, 1, crossed_a, 0), (3, 0, below_a, 0), (1, 0, above_a, 0), (2, 0, far, 0), (2, 1, far, 2)]
+    for dy, dh, source, first in pairs + [(3, 1, turned, 0), (1, 1, turned, 2)]:
+        place = tiles_ref.at[pl.ds(device(dy, dh, 0), 2)]
+        jobs.append((place, [(None, marks_of(source, pl.ds(first, 2)))]))
+    mark_waits = copies(sems.at[21:], jobs)
     own, core = at.orbital(1), got_b.at[20:]
     crossed, below, above = (v.at[4:] for v in (crossed_b, below_b, above_b))
     not_ = jnp.logical_not
@@ -343,7 +315,7 @@
         (far_ref, [(same_h & same_c, own), (same_h & not_(same_c), core), (not_(same_h), crossed)]),
         (turn_ref, [(from_below, below), (not_(from_below), above)]),
     ]
-    second_waits = copies(sems.at[28:], jobs)
+    second_waits = copies(sems.at[30:], jobs)
     u_wait.wait()
     o_wait.wait()
     orbital = o_ref[0].astype(F32)
@@ -354,10 +326,6 @@
             jnp.concatenate([density[:, 128 * j : 128 * (j + 1)] for j in range(PAIRS_Y)], axis=0)
         )
     density = jnp.concatenate(columns, axis=1).astype(BF16)
-    wait_all(mark_waits)
-    total = sum(marks[i].astype(F32) for i in range(len(sources)))
-    tiles = jnp.concatenate([total[:, 128 * n : 128 * (n + 1)] for n in range(BAND)], axis=0)
-    tiles_ref[...] = tiles.astype(BF16)
     mz_wait.wait()
     zfreq = dot(density, mz_ref[...]).astype(BF16)
     stacked = jnp.concatenate([zfreq[:, 256 * i : 256 * (i + 1)] for i in range(4)], axis=0)
@@ -367,7 +335,7 @@
     out_waits = copies(sems.at[5:], jobs)
     out_ref[...] = dot(ky_ref[...], stacked).astype(BF16)
     jobs = [(out_hbm.at[g, pl.ds(0, 64)], [(None, out_ref.at[pl.ds(64 * g, 64)])]) for g in range(GRID)]
-    wait_all(out_waits + second_waits + copies(sems.at[13:], jobs))
+    wait_all(out_waits + mark_waits + second_waits + copies(sems.at[13:], jobs))
 
 
 def middle_body(
@@ -432,7 +400,7 @@
 
 
 def weight_body(tiles_ref, out_ref):
-    tiles = tiles_ref[...]
+    tiles = tiles_ref[...].astype(F32).reshape(BAND * XL, 128).astype(BF16)
     shape = (BAND * N, BAND * XL)
     row = lax.broadcasted_iota(jnp.int32, shape, 0)
     lane = lax.broadcasted_iota(jnp.int32, shape, 1)
@@ -464,6 +432,16 @@
 
 SMEM, VMEM, HBM = pltpu.SMEM, pltpu.VMEM, pltpu.HBM
 PLANE = (XL, N * N)
+LONG = (XL, N * N + 128)
+GRIDPOINTS, MARKS = pl.ds(0, N * N), pl.ds(N * N, 128)
+
+
+def plane(ref, *index):
+    return ref.at[*index, :, GRIDPOINTS]
+
+
+def marks_of(ref, *index):
+    return ref.at[*index, :, MARKS]
 
 
 def call(body, spaces, outs, out_spaces, scratch, args, dtype=BF16, flops=10**8):
@@ -571,8 +549,8 @@
         sent_a = hop(
             core_a_body,
             root_spaces[:2] + any_ * 3,
-            [rows(14)],
-            [held(1), VMEM(kept_cells.shape, jnp.int32)] + sems(10),
+            [(13,) + LONG],
+            [VMEM((1, XL, 128), BF16), VMEM(kept_cells.shape, jnp.int32)] + sems(10),
             *roots[:2],
             far_memory(kept_cells),
             *roots[2:],
@@ -590,8 +568,8 @@
         up, down, across = hop(
             first_a_body,
             root_spaces + any_ * 2,
-            [rows(6)] * 3,
-            [held(2)] + sems(17),
+            [(5,) + LONG] * 3,
+            sems(12),
             *roots,
             sent_a,
             got_a,
@@ -611,8 +589,8 @@
         far, turn = hop(
             second_a_body,
             root_spaces + any_ * 6,
-            [rows(6)] * 2,
-            [held(5)] + sems(15),
+            [(5,) + LONG] * 2,
+            sems(9),
             *roots,
             sent_a,
             got_a,
@@ -635,9 +613,9 @@
         freq, tiles, second, far, turn = call(
             forward_body,
             root_spaces + any_ * 14,
-            [from_all, (BAND * XL, 128)] + [rows(1)] * 3,
+            [from_all, (BAND, XL, 128)] + [rows(1)] * 3,
             any_ + [VMEM] * 4,
-            [held(SHARE), held(1), big, big, VMEM((512, 256), BF16), VMEM((128, 256), BF16), held(7)] + sems(31),
+            [held(SHARE), held(1), big, big, VMEM((512, 256), BF16), VMEM((128, 256), BF16)] + sems(33),
             roots
             + (sent_a, got_a, got_b, crossed_a, below_a, above_a, crossed_b, below_b, above_b, far_a, turned_a)
             + (amp, const["mz"], const["ky"]),

time: 131 us -> 128 us (0.977)
  waiting for transfers between devices: 29.8 us -> 26.4 us
    ppermute x27, waiting for transfers between devices: 20.6 us -> 17.1 us  [band_shift(): return lax.ppermute(value, 'band', pairs)]
  transfers between devices with their start and end apart: 29 -> 29, of which waited for: 12 -> 11; matrix products, arithmetic and copies ran while one was open for 0% -> 0% of each run, Pallas kernels for 11% -> 11%
where the time goes in v5:
time: 128 us; the launch traced here: 127 us
  starting transfers between devices  47.2 us (37%)
  Pallas kernels  32.4 us (25%)
  waiting for transfers between devices  26.4 us (21%)
  blocking collectives  18.9 us (15%)
  local copies, waits for them, and re-layouts  1.32 us (1%)
    ppermute x27, starting transfers between devices, band_shift(): return lax.ppermute(value, 'band', pairs)  35.5 us
    pallas_call x11, Pallas kernels, call(): pl.pallas_call(body, out_shape=shapes if many else shapes[0], in_specs=[p...  23.5 us
    all_to_all x1, blocking collectives, per_device(): lax.all_to_all(terms.reshape(GRID * BAND, XL, 128), ('grid', 'band'), 0,...  18.9 us
    ppermute x27, waiting for transfers between devices, band_shift(): return lax.ppermute(value, 'band', pairs)  17.1 us
    all_to_all x2, starting transfers between devices, per_device(): freq = lax.all_to_all(freq, 'grid', 0, 0, tiled=True)  11.7 us
    all_to_all x2, waiting for transfers between devices, per_device(): freq = lax.all_to_all(freq, 'grid', 0, 0, tiled=True)  9.24 us
    pallas_call x2, Pallas kernels, slab_call(): pl.pallas_call(functools.partial(slab_body, last, names), out_shape=jax.S...  8.96 us
  transfers between devices with their start and end apart: 29, of which 11 were waited for; matrix products, arithmetic and copies ran while one was open for 0% of the time, Pallas kernels for 11%

profile of v5, /device:TPU:1, one launch (start us, length us, event | category | flops | bytes accessed | tf_op | source)
XLA Modules:
  0.0 127.1 jit_solution(9481864428727467468)
XLA Ops:
  1.3 1.8 %block_scatter.6.sent_a = bf16[13,8,4224]{2,1,0:T(8,128)(2,1)S(1)} custom-call(s32[1]{0:T(128)S(6)} %copy.14.ablock_ref, s32[1,2]{1,0:T(1,128)S(1)} %copy-done, s32[1,512]{1,0:T(1,128)} %kept_hbm.1, bf16[128,8,4096]{2,1,0:T(8,128)(2,1)} %fields.13, bf16[16,8,4096]{2,1,0:T(8,128)(2,1)} %occupied.13), custom_call_target="tpu_custom_call" | custom-call | flops 100000000 | bytes 1048576 | tf_op jit(solution)/shard_map/block_scatter/pallas_call | solution.py:451
  3.1 1.5 %collective-permute-start = (bf16[13,8,4224]{2,1,0:T(8,128)(2,1)S(1)}, bf16[13,8,4224]{2,1,0:T(8,128)(2,1)S(1)}, u32[]{:S(2)}, u32[]{:S(2)}) collective-permute-start(bf16[13,8,4224]{2,1,0:T(8,128)(2,1)S(1)} %block_scatter.6.sent_a), channel_id=1, source_target_pairs={{0,1},{1,0},{2,3},{3,2},{4,5},{5,4},{6,7},{7,6},{8,9},{9,8},{10,11... | collective-permute-start | bytes 2635784 | tf_op jit(solution)/shard_map/block_scatter/ppermute | solution.py:532
  4.6 2.1 %block_scatter.8 = (bf16[21,8,4096]{2,1,0:T(8,128)(2,1)S(1)}, bf16[128,256]{1,0:T(8,128)(2,1)S(1)}) custom-call(s32[1]{0:T(128)S(6)} %copy.14.ablock_ref, s32[1,2]{1,0:T(1,128)S(1)} %copy-done, bf16[128,8,4096]{2,1,0:T(8,128)(2,1)} %fields.13, bf16[16,8,4096]{2,1,0:T(8,128)(2,1)} %occupied.13, bf16[1,128,256]{2,1,0:T(8,128)(2,1)} %amp_hbm.1), custom_call_target="tpu_custom_call" | custom-call | flops 5000000000 | bytes 1048576 | tf_op jit(solution)/shard_map/block_scatter/pallas_call | solution.py:451
  6.7 1.8 %block_scatter.7 = (bf16[5,8,4224]{2,1,0:T(8,128)(2,1)S(1)}, bf16[5,8,4224]{2,1,0:T(8,128)(2,1)S(1)}, bf16[5,8,4224]{2,1,0:T(8,128)(2,1)S(1)}) custom-call(s32[1]{0:T(128)S(6)} %copy.14.ablock_ref, s32[1,2]{1,0:T(1,128)S(1)} %copy-done, bf16[128,8,4096]{2,1,0:T(8,128)(2,1)} %fields.13, bf16[16,8,4096]{2,1,0:T(8,128)(2,1)} %occupied.13, ...), custom_call_target="tpu_custom_call" | custom-call | flops 100000000 | bytes 1048576 | tf_op jit(solution)/shard_map/block_scatter/pallas_call | solution.py:451
  8.6 2.9 %collective-permute-start.2 = (bf16[5,8,4224]{2,1,0:T(8,128)(2,1)S(1)}, bf16[5,8,4224]{2,1,0:T(8,128)(2,1)S(1)}, u32[]{:S(2)}, u32[]{:S(2)}) collective-permute-start(bf16[5,8,4224]{2,1,0:T(8,128)(2,1)S(1)} %get-tuple-element.44), channel_id=1, source_target_pairs={{0,2},{1,3},{2,0},{3,1},{4,6},{5,7},{6,4},{7,5},{8,10},{9,11},{10,... | collective-permute-start | bytes 1013768 | tf_op jit(solution)/shard_map/block_scatter/ppermute | solution.py:532
  12.8 1.4 %collective-permute-start.4 = (bf16[5,8,4224]{2,1,0:T(8,128)(2,1)S(1)}, bf16[5,8,4224]{2,1,0:T(8,128)(2,1)S(1)}, u32[]{:S(2)}, u32[]{:S(2)}) collective-permute-start(bf16[5,8,4224]{2,1,0:T(8,128)(2,1)S(1)} %get-tuple-element.46), channel_id=1, source_target_pairs={{0,12},{1,13},{2,14},{3,15},{4,0},{5,1},{6,2},{7,3},{8,4},{9,5},{1... | collective-permute-start | bytes 1013768 | tf_op jit(solution)/shard_map/block_scatter/ppermute | solution.py:532
  14.2 1.7 %block_scatter.9 = (bf16[5,8,4096]{2,1,0:T(8,128)(2,1)S(1)}, bf16[5,8,4096]{2,1,0:T(8,128)(2,1)S(1)}, bf16[5,8,4096]{2,1,0:T(8,128)(2,1)S(1)}) custom-call(s32[1]{0:T(128)S(6)} %copy.14.ablock_ref, s32[1,2]{1,0:T(1,128)S(1)} %copy-done, bf16[128,8,4096]{2,1,0:T(8,128)(2,1)} %fields.13, bf16[16,8,4096]{2,1,0:T(8,128)(2,1)} %occupied.13, ...), custom_call_target="tpu_custom_call" | custom-call | flops 100000000 | bytes 1048576 | tf_op jit(solution)/shard_map/block_scatter/pallas_call | solution.py:451
  17.7 1.6 %collective-permute-done.2.crossed.crossed_a = bf16[5,8,4224]{2,1,0:T(8,128)(2,1)S(1)} collective-permute-done((bf16[5,8,4224]{2,1,0:T(8,128)(2,1)S(1)}, bf16[5,8,4224]{2,1,0:T(8,128)(2,1)S(1)}, u32[]{:S(2)}, u32[]{:S(2)}) %collective-permute-start.2) | collective-permute-done | bytes 337952 | tf_op jit(solution)/shard_map/block_scatter/ppermute | solution.py:532
  19.3 2.8 %collective-permute-start.7 = (bf16[5,8,4096]{2,1,0:T(8,128)(2,1)S(1)}, bf16[5,8,4096]{2,1,0:T(8,128)(2,1)S(1)}, u32[]{:S(2)}, u32[]{:S(2)}) collective-permute-start(bf16[5,8,4096]{2,1,0:T(8,128)(2,1)S(1)} %get-tuple-element.48), channel_id=1, source_target_pairs={{0,12},{1,13},{2,14},{3,15},{4,0},{5,1},{6,2},{7,3},{8,4},{9,5},{1... | collective-permute-start | bytes 983048 | tf_op jit(solution)/shard_map/block_scatter/ppermute | solution.py:532
  22.1 1.6 %block_scatter.10 = (bf16[5,8,4224]{2,1,0:T(8,128)(2,1)S(1)}, bf16[5,8,4224]{2,1,0:T(8,128)(2,1)S(1)}) custom-call(s32[1]{0:T(128)S(6)} %copy.14.ablock_ref, s32[1,2]{1,0:T(1,128)S(1)} %copy-done, bf16[128,8,4096]{2,1,0:T(8,128)(2,1)} %fields.13, bf16[16,8,4096]{2,1,0:T(8,128)(2,1)} %occupied.13, bf16[13,8,4224]{2,1,0:T(8,128)(2,1)S(1)} %block_scatter.6.sent_a, ...), custom_call_target="tpu_custom_call" | custom-call | flops 10000000000 | bytes 1048576 | tf_op jit(solution)/shard_map/block_scatter/pallas_call | solution.py:451
  23.8 1.8 %collective-permute-start.8 = (bf16[5,8,4224]{2,1,0:T(8,128)(2,1)S(1)}, bf16[5,8,4224]{2,1,0:T(8,128)(2,1)S(1)}, u32[]{:S(2)}, u32[]{:S(2)}) collective-permute-start(bf16[5,8,4224]{2,1,0:T(8,128)(2,1)S(1)} %get-tuple-element.53), channel_id=1, source_target_pairs={{0,8},{1,9},{2,10},{3,11},{4,12},{5,13},{6,14},{7,15},{8,0},{9,1},... | collective-permute-start | bytes 1013768 | tf_op jit(solution)/shard_map/block_scatter/ppermute | solution.py:532
  26.9 1.8 %collective-permute-done.6.second.below_b = bf16[5,8,4096]{2,1,0:T(8,128)(2,1)S(1)} collective-permute-done((bf16[5,8,4096]{2,1,0:T(8,128)(2,1)S(1)}, bf16[5,8,4096]{2,1,0:T(8,128)(2,1)S(1)}, u32[]{:S(2)}, u32[]{:S(2)}) %collective-permute-start.6) | collective-permute-done | bytes 327712 | tf_op jit(solution)/shard_map/block_scatter/ppermute | solution.py:532
  28.6 8.3 %collective-permute-done.8.far = bf16[5,8,4224]{2,1,0:T(8,128)(2,1)S(1)} collective-permute-done((bf16[5,8,4224]{2,1,0:T(8,128)(2,1)S(1)}, bf16[5,8,4224]{2,1,0:T(8,128)(2,1)S(1)}, u32[]{:S(2)}, u32[]{:S(2)}) %collective-permute-start.8) | collective-permute-done | bytes 337952 | tf_op jit(solution)/shard_map/block_scatter/ppermute | solution.py:532
  37.0 3.9 %transform.4 = (bf16[8,192,256]{2,1,0:T(8,128)(2,1)}, bf16[16,8,128]{2,1,0:T(8,128)(2,1)S(1)}, bf16[1,8,4096]{2,1,0:T(8,128)(2,1)S(1)}, bf16[1,8,4096]{2,1,0:T(8,128)(2,1)S(1)}, bf16[1,8,4096]{2,1,0:T(8,128)(2,1)S(1)}) custom-call(s32[1]{0:T(128)S(6)} %copy.14.ablock_ref, s32[1,2]{1,0:T(1,128)S(1)} %copy-done.1, bf16[128,8,4096]{2,1,0:T(8,128)(2,1)} %fields.13, ...), custom_call_target="tpu_custom_call" | custom-call | flops 20000000000 | bytes 1048576 | tf_op jit(solution)/shard_map/transform/pallas_call | solution.py:451
  40.9 5.1 %all-to-all-start = ((bf16[8,192,256]{2,1,0:T(8,128)(2,1)}), bf16[8,192,256]{2,1,0:T(8,128)(2,1)S(1)}, u32[]{:S(2)}, u32[]{:S(2)}) async-start(bf16[8,192,256]{2,1,0:T(8,128)(2,1)} %get-tuple-element.62), calls=%async_computation | async-start | bytes 1572864 | tf_op jit(solution)/shard_map/transform/all_to_all | solution.py:624
  46.5 8.3 %all-to-all-done.y_hbm.refs_7_ = bf16[8,192,256]{2,1,0:T(8,128)(2,1)S(1)} async-done(((bf16[8,192,256]{2,1,0:T(8,128)(2,1)}), bf16[8,192,256]{2,1,0:T(8,128)(2,1)S(1)}, u32[]{:S(2)}, u32[]{:S(2)}) %all-to-all-start) | async-done | bytes 786464 | tf_op jit(solution)/shard_map/transform/all_to_all | solution.py:624
  54.8 3.6 %transform.6 = bf16[512,256]{1,0:T(8,128)(2,1)} custom-call(bf16[8,192,256]{2,1,0:T(8,128)(2,1)S(1)} %all-to-all-done.y_hbm.refs_7_, f32[512,128]{1,0:T(8,128)S(1)} %transform.5.weight_ref, bf16[256,256]{1,0:T(8,128)(2,1)} %constant.22.clone.turn_hbm, bf16[512,1024]{1,0:T(8,128)(2,1)} %constant.20.clone.kx_hbm, bf16[512,1024]{1,0:T(8,128)(2,1)} %constant.21.clone.kxt_hbm), custom_call_target="tpu_custom_call" | custom-call | flops 10000000000 | bytes 1048576 | tf_op jit(solution)/shard_map/transform/pallas_call | solution.py:451
  58.3 6.6 %all-to-all-start.1 = ((bf16[8,64,256]{2,1,0:T(8,128)(2,1)}), bf16[8,64,256]{2,1,0:T(8,128)(2,1)S(1)}, u32[]{:S(2)}, u32[]{:S(2)}) async-start(bf16[8,64,256]{2,1,0:T(8,128)(2,1)} %bitcast), calls=%async_computation.1 | async-start | bytes 524288 | tf_op jit(solution)/shard_map/transform/all_to_all | solution.py:646
  66.4 3.1 %collective-permute-done.10.far = bf16[1,8,4096]{2,1,0:T(8,128)(2,1)S(1)} collective-permute-done((bf16[1,8,4096]{2,1,0:T(8,128)(2,1)S(1)}, bf16[1,8,4096]{2,1,0:T(8,128)(2,1)S(1)}, u32[]{:S(2)}, u32[]{:S(2)}) %collective-permute-start.10) | collective-permute-done | bytes 65568 | tf_op jit(solution)/shard_map/transform/ppermute | solution.py:532
  71.0 3.1 %transform.7 = bf16[4,8,4096]{2,1,0:T(8,128)(2,1)S(1)} custom-call(s32[1]{0:T(128)S(6)} %copy.14.ablock_ref, s32[1,2]{1,0:T(1,128)S(1)} %copy-done.1, bf16[128,8,4096]{2,1,0:T(8,128)(2,1)} %fields.13, bf16[16,8,4096]{2,1,0:T(8,128)(2,1)} %occupied.13, bf16[1,8,4096]{2,1,0:T(8,128)(2,1)S(1)} %get-tuple-element.59.second, ...), custom_call_target="tpu_custom_call" | custom-call | flops 100000000 | bytes 1048576 | tf_op jit(solution)/shard_map/transform/pallas_call | solution.py:451
  74.1 1.9 %collective-permute-start.12 = (bf16[32,4096]{1,0:T(8,128)(2,1)S(1)}, bf16[32,4096]{1,0:T(8,128)(2,1)S(1)}, u32[]{:S(2)}, u32[]{:S(2)}) collective-permute-start(bf16[32,4096]{1,0:T(8,128)(2,1)S(1)} %bitcast.5), channel_id=1, source_target_pairs={{0,8},{1,9},{2,10},{3,11},{4,12},{5,13},{6,14},{7,15},{8,0},{9,1},... | collective-permute-start | bytes 786440 | tf_op jit(solution)/shard_map/block_gather/ppermute | solution.py:532
  76.0 1.4 %collective-permute-start.13 = (bf16[32,4096]{1,0:T(8,128)(2,1)S(1)}, bf16[32,4096]{1,0:T(8,128)(2,1)S(1)}, u32[]{:S(2)}, u32[]{:S(2)}) collective-permute-start(bf16[32,4096]{1,0:T(8,128)(2,1)S(1)} %bitcast.6), channel_id=1, source_target_pairs={{0,2},{1,3},{2,0},{3,1},{4,6},{5,7},{6,4},{7,5},{8,10},{9,11},{10,... | collective-permute-start | bytes 786440 | tf_op jit(solution)/shard_map/block_gather/ppermute | solution.py:532
  78.0 2.1 %collective-permute-start.21 = (bf16[32,4096]{1,0:T(8,128)(2,1)S(1)}, bf16[32,4096]{1,0:T(8,128)(2,1)S(1)}, u32[]{:S(2)}, u32[]{:S(2)}) collective-permute-start(bf16[32,4096]{1,0:T(8,128)(2,1)S(1)} %bitcast.8), channel_id=1, source_target_pairs={{0,12},{1,13},{2,14},{3,15},{4,0},{5,1},{6,2},{7,3},{8,4},{9,5},{1... | collective-permute-start | bytes 786440 | tf_op jit(solution)/shard_map/block_gather/ppermute | solution.py:532
  80.1 4.0 %collective-permute-start.17 = (bf16[32,4096]{1,0:T(8,128)(2,1)S(1)}, bf16[32,4096]{1,0:T(8,128)(2,1)S(1)}, u32[]{:S(2)}, u32[]{:S(2)}) collective-permute-start(bf16[32,4096]{1,0:T(8,128)(2,1)S(1)} %bitcast.9), channel_id=1, source_target_pairs={{0,1},{1,0},{2,3},{3,2},{4,5},{5,4},{6,7},{7,6},{8,9},{9,8},{10,11... | collective-permute-start | bytes 786440 | tf_op jit(solution)/shard_map/block_gather/ppermute | solution.py:532
  84.1 3.4 %block_gather.3.u_ref = bf16[1024,4096]{1,0:T(8,128)(2,1)S(1)} custom-call(bf16[1024,4096]{1,0:T(8,128)(2,1)} %bitcast.13), custom_call_target="tpu_custom_call" | custom-call | flops 100000000 | bytes 1048576 | tf_op jit(solution)/shard_map/block_gather/pallas_call | solution.py:451
  88.1 2.0 %collective-permute-start.20 = (bf16[32,4096]{1,0:T(8,128)(2,1)S(1)}, bf16[32,4096]{1,0:T(8,128)(2,1)S(1)}, u32[]{:S(2)}, u32[]{:S(2)}) collective-permute-start(bf16[32,4096]{1,0:T(8,128)(2,1)S(1)} %collective-permute-done.19.refs_4_), channel_id=1, source_target_pairs={{0,1},{1,0},{2,3},{3,2},{4,5},{5,4},{6,7},{7,6},{8,9},{9,8},{10,11... | collective-permute-start | bytes 786440 | tf_op jit(solution)/shard_map/block_gather/ppermute | solution.py:532
  90.2 1.6 %collective-permute-start.14 = (bf16[32,4096]{1,0:T(8,128)(2,1)S(1)}, bf16[32,4096]{1,0:T(8,128)(2,1)S(1)}, u32[]{:S(2)}, u32[]{:S(2)}) collective-permute-start(bf16[32,4096]{1,0:T(8,128)(2,1)S(1)} %collective-permute-done.12.refs_2_), channel_id=1, source_target_pairs={{0,2},{1,3},{2,0},{3,1},{4,6},{5,7},{6,4},{7,5},{8,10},{9,11},{10,... | collective-permute-start | bytes 786440 | tf_op jit(solution)/shard_map/block_gather/ppermute | solution.py:532
  91.9 2.8 %collective-permute-start.16 = (bf16[32,4096]{1,0:T(8,128)(2,1)S(1)}, bf16[32,4096]{1,0:T(8,128)(2,1)S(1)}, u32[]{:S(2)}, u32[]{:S(2)}) collective-permute-start(bf16[32,4096]{1,0:T(8,128)(2,1)S(1)} %collective-permute-done.13.refs_8_), channel_id=1, source_target_pairs={{0,12},{1,13},{2,14},{3,15},{4,0},{5,1},{6,2},{7,3},{8,4},{9,5},{1... | collective-permute-start | bytes 786440 | tf_op jit(solution)/shard_map/block_gather/ppermute | solution.py:532
  94.6 5.2 %block_gather.4.refs_6_ = f32[128,128]{1,0:T(8,128)S(1)} custom-call(bf16[1024,4096]{1,0:T(8,128)(2,1)S(1)} %block_gather.3.u_ref, bf16[32,4096]{1,0:T(8,128)(2,1)S(1)} %bitcast.10, bf16[32,4096]{1,0:T(8,128)(2,1)S(1)} %collective-permute-done.17.refs_1_, bf16[32,4096]{1,0:T(8,128)(2,1)S(1)} %collective-permute-done.12.refs_2_, ...), custom_call_target="tpu_custom_call" | custom-call | flops 2684354560 | bytes 8388608 | tf_op jit(solution)/shard_map/block_gather/pallas_call | solution.py:513
  100.1 1.6 %collective-permute-start.24 = (bf16[32,4096]{1,0:T(8,128)(2,1)S(1)}, bf16[32,4096]{1,0:T(8,128)(2,1)S(1)}, u32[]{:S(2)}, u32[]{:S(2)}) collective-permute-start(bf16[32,4096]{1,0:T(8,128)(2,1)S(1)} %collective-permute-done.14.refs_0_), channel_id=1, source_target_pairs={{0,1},{1,0},{2,3},{3,2},{4,5},{5,4},{6,7},{7,6},{8,9},{9,8},{10,11... | collective-permute-start | bytes 786440 | tf_op jit(solution)/shard_map/block_gather/ppermute | solution.py:532
  103.6 3.8 %block_gather.5 = bf16[1024,128]{1,0:T(8,128)(2,1)S(1)} custom-call(bf16[1024,4096]{1,0:T(8,128)(2,1)S(1)} %block_gather.3.u_ref, bf16[32,4096]{1,0:T(8,128)(2,1)S(1)} %collective-permute-done.14.refs_0_, bf16[32,4096]{1,0:T(8,128)(2,1)S(1)} %collective-permute-done.24.refs_1_, bf16[32,4096]{1,0:T(8,128)(2,1)S(1)} %collective-permute-done.15.refs_2_, ...), custom_call_target="tpu_custom_call" | custom-call | flops 1610612736 | bytes 8388608 | tf_op jit(solution)/shard_map/block_gather/pallas_call | solution.py:513
  107.4 18.9 %all_to_all.21 = bf16[128,8,128]{2,1,0:T(8,128)(2,1)S(1)} all-to-all(bf16[128,8,128]{2,1,0:T(8,128)(2,1)S(1)} %bitcast.12), channel_id=1, replica_groups=mesh['grid'=8,'band'=16] {'grid','band'}, dimensions={0} | all-to-all | bytes 524288 | tf_op jit(solution)/shard_map/ladder/all_to_all | solution.py:684
  (46 shorter events, 12.9 us)
Async XLA Ops:
  0.7 0.7 copy-start
  3.1 3.6 %collective-permute-start = (bf16[13,8,4224]{2,1,0:T(8,128)(2,1)S(1)}, bf16[13,8,4224]{2,1,0:T(8,128)(2,1)S(1)}, u32[]{:S(2)}, u32[]{:S(2)}) collective-permute-start(bf16[13,8,4224]{2,1,0:T(8,128)(2,1)S(1)} %block_scatter.6.sent_a), channel_id=1, source_target_pairs={{0,1},{1,0},{2,3},{3,2},{4,5},{5,4},{6,7},{7,6},{8,9},{9,8},{10,11... | collective-permute-start | bytes 2635784 | tf_op jit(solution)/shard_map/block_scatter/ppermute | solution.py:532
  8.5 5.7 %collective-permute-start.1 = (bf16[21,8,4096]{2,1,0:T(8,128)(2,1)S(1)}, bf16[21,8,4096]{2,1,0:T(8,128)(2,1)S(1)}, u32[]{:S(2)}, u32[]{:S(2)}) collective-permute-start(bf16[21,8,4096]{2,1,0:T(8,128)(2,1)S(1)} %get-tuple-element.43), channel_id=1, source_target_pairs={{0,1},{1,0},{2,3},{3,2},{4,5},{5,4},{6,7},{7,6},{8,9},{9,8},{10,11... | collective-permute-start | bytes 4128776 | tf_op jit(solution)/shard_map/block_scatter/ppermute | solution.py:532
  8.6 10.7 %collective-permute-start.2 = (bf16[5,8,4224]{2,1,0:T(8,128)(2,1)S(1)}, bf16[5,8,4224]{2,1,0:T(8,128)(2,1)S(1)}, u32[]{:S(2)}, u32[]{:S(2)}) collective-permute-start(bf16[5,8,4224]{2,1,0:T(8,128)(2,1)S(1)} %get-tuple-element.44), channel_id=1, source_target_pairs={{0,2},{1,3},{2,0},{3,1},{4,6},{5,7},{6,4},{7,5},{8,10},{9,11},{10,... | collective-permute-start | bytes 1013768 | tf_op jit(solution)/shard_map/block_scatter/ppermute | solution.py:532
  11.5 10.6 %collective-permute-start.3 = (bf16[5,8,4224]{2,1,0:T(8,128)(2,1)S(1)}, bf16[5,8,4224]{2,1,0:T(8,128)(2,1)S(1)}, u32[]{:S(2)}, u32[]{:S(2)}) collective-permute-start(bf16[5,8,4224]{2,1,0:T(8,128)(2,1)S(1)} %get-tuple-element.45), channel_id=1, source_target_pairs={{0,4},{1,5},{2,6},{3,7},{4,8},{5,9},{6,10},{7,11},{8,12},{9,13},{1... | collective-permute-start | bytes 1013768 | tf_op jit(solution)/shard_map/block_scatter/ppermute | solution.py:532
  12.8 9.3 %collective-permute-start.4 = (bf16[5,8,4224]{2,1,0:T(8,128)(2,1)S(1)}, bf16[5,8,4224]{2,1,0:T(8,128)(2,1)S(1)}, u32[]{:S(2)}, u32[]{:S(2)}) collective-permute-start(bf16[5,8,4224]{2,1,0:T(8,128)(2,1)S(1)} %get-tuple-element.46), channel_id=1, source_target_pairs={{0,12},{1,13},{2,14},{3,15},{4,0},{5,1},{6,2},{7,3},{8,4},{9,5},{1... | collective-permute-start | bytes 1013768 | tf_op jit(solution)/shard_map/block_scatter/ppermute | solution.py:532
  16.0 10.9 %collective-permute-start.5 = (bf16[5,8,4096]{2,1,0:T(8,128)(2,1)S(1)}, bf16[5,8,4096]{2,1,0:T(8,128)(2,1)S(1)}, u32[]{:S(2)}, u32[]{:S(2)}) collective-permute-start(bf16[5,8,4096]{2,1,0:T(8,128)(2,1)S(1)} %get-tuple-element.49), channel_id=1, source_target_pairs={{0,2},{1,3},{2,0},{3,1},{4,6},{5,7},{6,4},{7,5},{8,10},{9,11},{10,... | collective-permute-start | bytes 983048 | tf_op jit(solution)/shard_map/block_scatter/ppermute | solution.py:532
  16.4 12.3 %collective-permute-start.6 = (bf16[5,8,4096]{2,1,0:T(8,128)(2,1)S(1)}, bf16[5,8,4096]{2,1,0:T(8,128)(2,1)S(1)}, u32[]{:S(2)}, u32[]{:S(2)}) collective-permute-start(bf16[5,8,4096]{2,1,0:T(8,128)(2,1)S(1)} %get-tuple-element.47), channel_id=1, source_target_pairs={{0,4},{1,5},{2,6},{3,7},{4,8},{5,9},{6,10},{7,11},{8,12},{9,13},{1... | collective-permute-start | bytes 983048 | tf_op jit(solution)/shard_map/block_scatter/ppermute | solution.py:532
  19.3 9.4 %collective-permute-start.7 = (bf16[5,8,4096]{2,1,0:T(8,128)(2,1)S(1)}, bf16[5,8,4096]{2,1,0:T(8,128)(2,1)S(1)}, u32[]{:S(2)}, u32[]{:S(2)}) collective-permute-start(bf16[5,8,4096]{2,1,0:T(8,128)(2,1)S(1)} %get-tuple-element.48), channel_id=1, source_target_pairs={{0,12},{1,13},{2,14},{3,15},{4,0},{5,1},{6,2},{7,3},{8,4},{9,5},{1... | collective-permute-start | bytes 983048 | tf_op jit(solution)/shard_map/block_scatter/ppermute | solution.py:532
  23.8 13.2 %collective-permute-start.8 = (bf16[5,8,4224]{2,1,0:T(8,128)(2,1)S(1)}, bf16[5,8,4224]{2,1,0:T(8,128)(2,1)S(1)}, u32[]{:S(2)}, u32[]{:S(2)}) collective-permute-start(bf16[5,8,4224]{2,1,0:T(8,128)(2,1)S(1)} %get-tuple-element.53), channel_id=1, source_target_pairs={{0,8},{1,9},{2,10},{3,11},{4,12},{5,13},{6,14},{7,15},{8,0},{9,1},... | collective-permute-start | bytes 1013768 | tf_op jit(solution)/shard_map/block_scatter/ppermute | solution.py:532
  25.6 11.4 %collective-permute-start.9 = (bf16[5,8,4224]{2,1,0:T(8,128)(2,1)S(1)}, bf16[5,8,4224]{2,1,0:T(8,128)(2,1)S(1)}, u32[]{:S(2)}, u32[]{:S(2)}) collective-permute-start(bf16[5,8,4224]{2,1,0:T(8,128)(2,1)S(1)} %get-tuple-element.54), channel_id=1, source_target_pairs={{0,2},{1,3},{2,0},{3,1},{4,6},{5,7},{6,4},{7,5},{8,10},{9,11},{10,... | collective-permute-start | bytes 1013768 | tf_op jit(solution)/shard_map/block_scatter/ppermute | solution.py:532
  28.6 8.4 %copy-start.1 = (s32[1,2]{1,0:T(1,128)S(1)}, s32[1,2]{1,0:T(1,128)}, u32[]{:S(2)}) copy-start(s32[1,2]{1,0:T(1,128)} %pairs_ref.13) | copy-start | bytes 28
  40.9 13.9 %all-to-all-start = ((bf16[8,192,256]{2,1,0:T(8,128)(2,1)}), bf16[8,192,256]{2,1,0:T(8,128)(2,1)S(1)}, u32[]{:S(2)}, u32[]{:S(2)}) async-start(bf16[8,192,256]{2,1,0:T(8,128)(2,1)} %get-tuple-element.62), calls=%async_computation | async-start | bytes 1572864 | tf_op jit(solution)/shard_map/transform/all_to_all | solution.py:624
  58.3 12.7 %all-to-all-start.1 = ((bf16[8,64,256]{2,1,0:T(8,128)(2,1)}), bf16[8,64,256]{2,1,0:T(8,128)(2,1)S(1)}, u32[]{:S(2)}, u32[]{:S(2)}) async-start(bf16[8,64,256]{2,1,0:T(8,128)(2,1)} %bitcast), calls=%async_computation.1 | async-start | bytes 524288 | tf_op jit(solution)/shard_map/transform/all_to_all | solution.py:646
  64.9 4.6 %collective-permute-start.10 = (bf16[1,8,4096]{2,1,0:T(8,128)(2,1)S(1)}, bf16[1,8,4096]{2,1,0:T(8,128)(2,1)S(1)}, u32[]{:S(2)}, u32[]{:S(2)}) collective-permute-start(bf16[1,8,4096]{2,1,0:T(8,128)(2,1)S(1)} %get-tuple-element.60), channel_id=1, source_target_pairs={{0,8},{1,9},{2,10},{3,11},{4,12},{5,13},{6,14},{7,15},{8,0},{9,1},... | collective-permute-start | bytes 196616 | tf_op jit(solution)/shard_map/transform/ppermute | solution.py:532
  65.0 5.1 %collective-permute-start.11 = (bf16[1,8,4096]{2,1,0:T(8,128)(2,1)S(1)}, bf16[1,8,4096]{2,1,0:T(8,128)(2,1)S(1)}, u32[]{:S(2)}, u32[]{:S(2)}) collective-permute-start(bf16[1,8,4096]{2,1,0:T(8,128)(2,1)S(1)} %get-tuple-element.61), channel_id=1, source_target_pairs={{0,2},{1,3},{2,0},{3,1},{4,6},{5,7},{6,4},{7,5},{8,10},{9,11},{10,... | collective-permute-start | bytes 196616 | tf_op jit(solution)/shard_map/transform/ppermute | solution.py:532
  74.1 13.4 %collective-permute-start.12 = (bf16[32,4096]{1,0:T(8,128)(2,1)S(1)}, bf16[32,4096]{1,0:T(8,128)(2,1)S(1)}, u32[]{:S(2)}, u32[]{:S(2)}) collective-permute-start(bf16[32,4096]{1,0:T(8,128)(2,1)S(1)} %bitcast.5), channel_id=1, source_target_pairs={{0,8},{1,9},{2,10},{3,11},{4,12},{5,13},{6,14},{7,15},{8,0},{9,1},... | collective-permute-start | bytes 786440 | tf_op jit(solution)/shard_map/block_gather/ppermute | solution.py:532
  76.0 11.5 %collective-permute-start.13 = (bf16[32,4096]{1,0:T(8,128)(2,1)S(1)}, bf16[32,4096]{1,0:T(8,128)(2,1)S(1)}, u32[]{:S(2)}, u32[]{:S(2)}) collective-permute-start(bf16[32,4096]{1,0:T(8,128)(2,1)S(1)} %bitcast.6), channel_id=1, source_target_pairs={{0,2},{1,3},{2,0},{3,1},{4,6},{5,7},{6,4},{7,5},{8,10},{9,11},{10,... | collective-permute-start | bytes 786440 | tf_op jit(solution)/shard_map/block_gather/ppermute | solution.py:532
  77.4 10.7 %collective-permute-start.19 = (bf16[32,4096]{1,0:T(8,128)(2,1)S(1)}, bf16[32,4096]{1,0:T(8,128)(2,1)S(1)}, u32[]{:S(2)}, u32[]{:S(2)}) collective-permute-start(bf16[32,4096]{1,0:T(8,128)(2,1)S(1)} %bitcast.7), channel_id=1, source_target_pairs={{0,4},{1,5},{2,6},{3,7},{4,8},{5,9},{6,10},{7,11},{8,12},{9,13},{1... | collective-permute-start | bytes 786440 | tf_op jit(solution)/shard_map/block_gather/ppermute | solution.py:532
  78.0 12.1 %collective-permute-start.21 = (bf16[32,4096]{1,0:T(8,128)(2,1)S(1)}, bf16[32,4096]{1,0:T(8,128)(2,1)S(1)}, u32[]{:S(2)}, u32[]{:S(2)}) collective-permute-start(bf16[32,4096]{1,0:T(8,128)(2,1)S(1)} %bitcast.8), channel_id=1, source_target_pairs={{0,12},{1,13},{2,14},{3,15},{4,0},{5,1},{6,2},{7,3},{8,4},{9,5},{1... | collective-permute-start | bytes 786440 | tf_op jit(solution)/shard_map/block_gather/ppermute | solution.py:532
  80.1 10.1 %collective-permute-start.17 = (bf16[32,4096]{1,0:T(8,128)(2,1)S(1)}, bf16[32,4096]{1,0:T(8,128)(2,1)S(1)}, u32[]{:S(2)}, u32[]{:S(2)}) collective-permute-start(bf16[32,4096]{1,0:T(8,128)(2,1)S(1)} %bitcast.9), channel_id=1, source_target_pairs={{0,1},{1,0},{2,3},{3,2},{4,5},{5,4},{6,7},{7,6},{8,9},{9,8},{10,11... | collective-permute-start | bytes 786440 | tf_op jit(solution)/shard_map/block_gather/ppermute | solution.py:532
  87.5 4.3 %collective-permute-start.18 = (bf16[32,4096]{1,0:T(8,128)(2,1)S(1)}, bf16[32,4096]{1,0:T(8,128)(2,1)S(1)}, u32[]{:S(2)}, u32[]{:S(2)}) collective-permute-start(bf16[32,4096]{1,0:T(8,128)(2,1)S(1)} %collective-permute-done.12.refs_2_), channel_id=1, source_target_pairs={{0,1},{1,0},{2,3},{3,2},{4,5},{5,4},{6,7},{7,6},{8,9},{9,8},{10,11... | collective-permute-start | bytes 786440 | tf_op jit(solution)/shard_map/block_gather/ppermute | solution.py:532
  87.6 4.3 %collective-permute-start.23 = (bf16[32,4096]{1,0:T(8,128)(2,1)S(1)}, bf16[32,4096]{1,0:T(8,128)(2,1)S(1)}, u32[]{:S(2)}, u32[]{:S(2)}) collective-permute-start(bf16[32,4096]{1,0:T(8,128)(2,1)S(1)} %collective-permute-done.13.refs_8_), channel_id=1, source_target_pairs={{0,1},{1,0},{2,3},{3,2},{4,5},{5,4},{6,7},{7,6},{8,9},{9,8},{10,11... | collective-permute-start | bytes 786440 | tf_op jit(solution)/shard_map/block_gather/ppermute | solution.py:532
  88.1 6.5 %collective-permute-start.20 = (bf16[32,4096]{1,0:T(8,128)(2,1)S(1)}, bf16[32,4096]{1,0:T(8,128)(2,1)S(1)}, u32[]{:S(2)}, u32[]{:S(2)}) collective-permute-start(bf16[32,4096]{1,0:T(8,128)(2,1)S(1)} %collective-permute-done.19.refs_4_), channel_id=1, source_target_pairs={{0,1},{1,0},{2,3},{3,2},{4,5},{5,4},{6,7},{7,6},{8,9},{9,8},{10,11... | collective-permute-start | bytes 786440 | tf_op jit(solution)/shard_map/block_gather/ppermute | solution.py:532
  90.2 4.5 %collective-permute-start.22 = (bf16[32,4096]{1,0:T(8,128)(2,1)S(1)}, bf16[32,4096]{1,0:T(8,128)(2,1)S(1)}, u32[]{:S(2)}, u32[]{:S(2)}) collective-permute-start(bf16[32,4096]{1,0:T(8,128)(2,1)S(1)} %collective-permute-done.21.refs_6_), channel_id=1, source_target_pairs={{0,1},{1,0},{2,3},{3,2},{4,5},{5,4},{6,7},{7,6},{8,9},{9,8},{10,11... | collective-permute-start | bytes 786440 | tf_op jit(solution)/shard_map/block_gather/ppermute | solution.py:532
  90.2 9.6 %collective-permute-start.14 = (bf16[32,4096]{1,0:T(8,128)(2,1)S(1)}, bf16[32,4096]{1,0:T(8,128)(2,1)S(1)}, u32[]{:S(2)}, u32[]{:S(2)}) collective-permute-start(bf16[32,4096]{1,0:T(8,128)(2,1)S(1)} %collective-permute-done.12.refs_2_), channel_id=1, source_target_pairs={{0,2},{1,3},{2,0},{3,1},{4,6},{5,7},{6,4},{7,5},{8,10},{9,11},{10,... | collective-permute-start | bytes 786440 | tf_op jit(solution)/shard_map/block_gather/ppermute | solution.py:532
  91.8 8.3 %collective-permute-start.15 = (bf16[32,4096]{1,0:T(8,128)(2,1)S(1)}, bf16[32,4096]{1,0:T(8,128)(2,1)S(1)}, u32[]{:S(2)}, u32[]{:S(2)}) collective-permute-start(bf16[32,4096]{1,0:T(8,128)(2,1)S(1)} %collective-permute-done.13.refs_8_), channel_id=1, source_target_pairs={{0,4},{1,5},{2,6},{3,7},{4,8},{5,9},{6,10},{7,11},{8,12},{9,13},{1... | collective-permute-start | bytes 786440 | tf_op jit(solution)/shard_map/block_gather/ppermute | solution.py:532
  91.9 8.3 %collective-permute-start.16 = (bf16[32,4096]{1,0:T(8,128)(2,1)S(1)}, bf16[32,4096]{1,0:T(8,128)(2,1)S(1)}, u32[]{:S(2)}, u32[]{:S(2)}) collective-permute-start(bf16[32,4096]{1,0:T(8,128)(2,1)S(1)} %collective-permute-done.13.refs_8_), channel_id=1, source_target_pairs={{0,12},{1,13},{2,14},{3,15},{4,0},{5,1},{6,2},{7,3},{8,4},{9,5},{1... | collective-permute-start | bytes 786440 | tf_op jit(solution)/shard_map/block_gather/ppermute | solution.py:532
  100.1 2.7 %collective-permute-start.24 = (bf16[32,4096]{1,0:T(8,128)(2,1)S(1)}, bf16[32,4096]{1,0:T(8,128)(2,1)S(1)}, u32[]{:S(2)}, u32[]{:S(2)}) collective-permute-start(bf16[32,4096]{1,0:T(8,128)(2,1)S(1)} %collective-permute-done.14.refs_0_), channel_id=1, source_target_pairs={{0,1},{1,0},{2,3},{3,2},{4,5},{5,4},{6,7},{7,6},{8,9},{9,8},{10,11... | collective-permute-start | bytes 786440 | tf_op jit(solution)/shard_map/block_gather/ppermute | solution.py:532
  101.7 1.5 %collective-permute-start.25 = (bf16[32,4096]{1,0:T(8,128)(2,1)S(1)}, bf16[32,4096]{1,0:T(8,128)(2,1)S(1)}, u32[]{:S(2)}, u32[]{:S(2)}) collective-permute-start(bf16[32,4096]{1,0:T(8,128)(2,1)S(1)} %collective-permute-done.15.refs_2_), channel_id=1, source_target_pairs={{0,1},{1,0},{2,3},{3,2},{4,5},{5,4},{6,7},{7,6},{8,9},{9,8},{10,11... | collective-permute-start | bytes 786440 | tf_op jit(solution)/shard_map/block_gather/ppermute | solution.py:532
  101.7 1.9 %collective-permute-start.26 = (bf16[32,4096]{1,0:T(8,128)(2,1)S(1)}, bf16[32,4096]{1,0:T(8,128)(2,1)S(1)}, u32[]{:S(2)}, u32[]{:S(2)}) collective-permute-start(bf16[32,4096]{1,0:T(8,128)(2,1)S(1)} %collective-permute-done.16.refs_4_), channel_id=1, source_target_pairs={{0,1},{1,0},{2,3},{3,2},{4,5},{5,4},{6,7},{7,6},{8,9},{9,8},{10,11... | collective-permute-start | bytes 786440 | tf_op jit(solution)/shard_map/block_gather/ppermute | solution.py:532

commit v6 on v5

--- a/solution.py
+++ b/solution.py
@@ -117,7 +117,7 @@
         self.first = start % fields.shape[0]
         devices = [start // fields.shape[0]]
         self.local = []
-        for k in range(2):
+        for k in range(2 if pairs_ref is not None else 0):
             index = pairs_ref[0, k]
             devices.append(index // occupied.shape[0])
             self.local.append(index % occupied.shape[0])
@@ -134,12 +134,12 @@
         return self.occupied.at[pl.ds(self.local[k], 1)]
 
 
-def core_a_body(ablock_ref, pairs_ref, kept_hbm, fields, occupied, out, marks, kept_ref, sems):
-    at = Roots(ablock_ref, pairs_ref, fields, occupied)
+def core_a_body(ablock_ref, pairs_hbm, kept_hbm, fields, occupied, out, marks, kept_ref, pairs_ref, sems):
+    (pairs_wait,) = copies(sems.at[10:], [(pairs_ref, [(None, pairs_hbm)])])
+    at = Roots(ablock_ref, None, fields, occupied)
     other, there = 1 - at.c, 1 - at.h
     sources = [at.block(other, dy, there, 4) for dy in (1, 3, 2)]
     jobs = [(plane(out, pl.ds(4 * i, 4)), [(None, v)]) for i, v in enumerate(sources)]
-    jobs.append((plane(out, pl.ds(12, 1)), [(None, at.orbital(0))]))
 
     def start():
         (wait,) = copies(sems.at[9:], [(kept_ref, [(None, kept_hbm)])])
@@ -159,7 +159,9 @@
         marks[0] = jnp.sum(mask.reshape(XL, XL, 128), axis=1).astype(BF16)
         move = pltpu.make_async_copy(marks, marks_of(out, pl.ds(0, 1)), sems.at[8])
         move.start()
-        return [move]
+        pairs_wait.wait()
+        orbital = occupied.at[pl.ds(pairs_ref[0, 0] % occupied.shape[0], 1)]
+        return [move] + copies(sems.at[3:], [(plane(out, pl.ds(12, 1)), [(None, orbital)])])
 
     gather(sems, jobs, start)
 
@@ -548,10 +550,11 @@
         any_ = [pl.ANY]
         sent_a = hop(
             core_a_body,
-            root_spaces[:2] + any_ * 3,
+            [SMEM] + any_ * 4,
             [(13,) + LONG],
-            [VMEM((1, XL, 128), BF16), VMEM(kept_cells.shape, jnp.int32)] + sems(10),
-            *roots[:2],
+            [VMEM((1, XL, 128), BF16), VMEM(kept_cells.shape, jnp.int32), SMEM((1, 2), jnp.int32)] + sems(11),
+            ablock,
+            far_memory(pairs),
             far_memory(kept_cells),
             *roots[2:],
         )

time: 128 us -> 128 us (level)
  waiting for transfers between devices: 26.4 us -> 28.9 us
    ppermute x27, waiting for transfers between devices: 17.1 us -> 19.8 us  [band_shift(): return lax.ppermute(value, 'band', pairs)]
  transfers between devices with their start and end apart: 29 -> 29, of which waited for: 11 -> 12; matrix products, arithmetic and copies ran while one was open for 0% -> 0% of each run, Pallas kernels for 11% -> 11%
where the time goes in v6:
time: 128 us; the launch traced here: 127 us
  starting transfers between devices  46 us (36%)
  Pallas kernels  31.9 us (25%)
  waiting for transfers between devices  28.9 us (23%)
  blocking collectives  18.8 us (15%)
    ppermute x27, starting transfers between devices, band_shift(): return lax.ppermute(value, 'band', pairs)  34.3 us
    pallas_call x11, Pallas kernels, call(): pl.pallas_call(body, out_shape=shapes if many else shapes[0], in_specs=[p...  23 us
    ppermute x27, waiting for transfers between devices, band_shift(): return lax.ppermute(value, 'band', pairs)  19.8 us
    all_to_all x1, blocking collectives, per_device(): lax.all_to_all(terms.reshape(GRID * BAND, XL, 128), ('grid', 'band'), 0,...  18.8 us
    all_to_all x2, starting transfers between devices, per_device(): freq = lax.all_to_all(freq, 'grid', 0, 0, tiled=True)  11.7 us
    all_to_all x2, waiting for transfers between devices, per_device(): freq = lax.all_to_all(freq, 'grid', 0, 0, tiled=True)  9.05 us
    pallas_call x2, Pallas kernels, slab_call(): pl.pallas_call(functools.partial(slab_body, last, names), out_shape=jax.S...  8.96 us
  transfers between devices with their start and end apart: 29, of which 12 were waited for; matrix products, arithmetic and copies ran while one was open for 0% of the time, Pallas kernels for 11%

profile of v6, /device:TPU:1, one launch (start us, length us, event | category | flops | bytes accessed | tf_op | source)
XLA Modules:
  0.0 127.2 jit_solution(13416691378946643821)
XLA Ops:
  0.7 1.9 %block_scatter.6.sent_a = bf16[13,8,4224]{2,1,0:T(8,128)(2,1)S(1)} custom-call(s32[1]{0:T(128)S(6)} %copy.14.ablock_ref, s32[1,2]{1,0:T(1,128)} %pairs_ref.11, s32[1,512]{1,0:T(1,128)} %kept_hbm.1, bf16[128,8,4096]{2,1,0:T(8,128)(2,1)} %fields.13, bf16[16,8,4096]{2,1,0:T(8,128)(2,1)} %occupied.13), custom_call_target="tpu_custom_call" | custom-call | flops 100000000 | bytes 1048576 | tf_op jit(solution)/shard_map/block_scatter/pallas_call | solution.py:453
  2.6 1.5 %collective-permute-start = (bf16[13,8,4224]{2,1,0:T(8,128)(2,1)S(1)}, bf16[13,8,4224]{2,1,0:T(8,128)(2,1)S(1)}, u32[]{:S(2)}, u32[]{:S(2)}) collective-permute-start(bf16[13,8,4224]{2,1,0:T(8,128)(2,1)S(1)} %block_scatter.6.sent_a), channel_id=1, source_target_pairs={{0,1},{1,0},{2,3},{3,2},{4,5},{5,4},{6,7},{7,6},{8,9},{9,8},{10,11... | collective-permute-start | bytes 2635784 | tf_op jit(solution)/shard_map/block_scatter/ppermute | solution.py:534
  4.1 2.1 %block_scatter.8 = (bf16[21,8,4096]{2,1,0:T(8,128)(2,1)S(1)}, bf16[128,256]{1,0:T(8,128)(2,1)S(1)}) custom-call(s32[1]{0:T(128)S(6)} %copy.14.ablock_ref, s32[1,2]{1,0:T(1,128)S(1)} %copy-done, bf16[128,8,4096]{2,1,0:T(8,128)(2,1)} %fields.13, bf16[16,8,4096]{2,1,0:T(8,128)(2,1)} %occupied.13, bf16[1,128,256]{2,1,0:T(8,128)(2,1)} %amp_hbm.1), custom_call_target="tpu_custom_call" | custom-call | flops 5000000000 | bytes 1048576 | tf_op jit(solution)/shard_map/block_scatter/pallas_call | solution.py:453
  6.2 1.8 %block_scatter.7 = (bf16[5,8,4224]{2,1,0:T(8,128)(2,1)S(1)}, bf16[5,8,4224]{2,1,0:T(8,128)(2,1)S(1)}, bf16[5,8,4224]{2,1,0:T(8,128)(2,1)S(1)}) custom-call(s32[1]{0:T(128)S(6)} %copy.14.ablock_ref, s32[1,2]{1,0:T(1,128)S(1)} %copy-done, bf16[128,8,4096]{2,1,0:T(8,128)(2,1)} %fields.13, bf16[16,8,4096]{2,1,0:T(8,128)(2,1)} %occupied.13, ...), custom_call_target="tpu_custom_call" | custom-call | flops 100000000 | bytes 1048576 | tf_op jit(solution)/shard_map/block_scatter/pallas_call | solution.py:453
  8.3 2.8 %collective-permute-start.2 = (bf16[5,8,4224]{2,1,0:T(8,128)(2,1)S(1)}, bf16[5,8,4224]{2,1,0:T(8,128)(2,1)S(1)}, u32[]{:S(2)}, u32[]{:S(2)}) collective-permute-start(bf16[5,8,4224]{2,1,0:T(8,128)(2,1)S(1)} %get-tuple-element.44), channel_id=1, source_target_pairs={{0,2},{1,3},{2,0},{3,1},{4,6},{5,7},{6,4},{7,5},{8,10},{9,11},{10,... | collective-permute-start | bytes 1013768 | tf_op jit(solution)/shard_map/block_scatter/ppermute | solution.py:534
  11.1 1.3 %collective-permute-start.3 = (bf16[5,8,4224]{2,1,0:T(8,128)(2,1)S(1)}, bf16[5,8,4224]{2,1,0:T(8,128)(2,1)S(1)}, u32[]{:S(2)}, u32[]{:S(2)}) collective-permute-start(bf16[5,8,4224]{2,1,0:T(8,128)(2,1)S(1)} %get-tuple-element.45), channel_id=1, source_target_pairs={{0,4},{1,5},{2,6},{3,7},{4,8},{5,9},{6,10},{7,11},{8,12},{9,13},{1... | collective-permute-start | bytes 1013768 | tf_op jit(solution)/shard_map/block_scatter/ppermute | solution.py:534
  12.4 1.4 %collective-permute-start.4 = (bf16[5,8,4224]{2,1,0:T(8,128)(2,1)S(1)}, bf16[5,8,4224]{2,1,0:T(8,128)(2,1)S(1)}, u32[]{:S(2)}, u32[]{:S(2)}) collective-permute-start(bf16[5,8,4224]{2,1,0:T(8,128)(2,1)S(1)} %get-tuple-element.46), channel_id=1, source_target_pairs={{0,12},{1,13},{2,14},{3,15},{4,0},{5,1},{6,2},{7,3},{8,4},{9,5},{1... | collective-permute-start | bytes 1013768 | tf_op jit(solution)/shard_map/block_scatter/ppermute | solution.py:534
  13.9 1.7 %block_scatter.9 = (bf16[5,8,4096]{2,1,0:T(8,128)(2,1)S(1)}, bf16[5,8,4096]{2,1,0:T(8,128)(2,1)S(1)}, bf16[5,8,4096]{2,1,0:T(8,128)(2,1)S(1)}) custom-call(s32[1]{0:T(128)S(6)} %copy.14.ablock_ref, s32[1,2]{1,0:T(1,128)S(1)} %copy-done, bf16[128,8,4096]{2,1,0:T(8,128)(2,1)} %fields.13, bf16[16,8,4096]{2,1,0:T(8,128)(2,1)} %occupied.13, ...), custom_call_target="tpu_custom_call" | custom-call | flops 100000000 | bytes 1048576 | tf_op jit(solution)/shard_map/block_scatter/pallas_call | solution.py:453
  17.1 1.9 %collective-permute-done.2.crossed.crossed_a = bf16[5,8,4224]{2,1,0:T(8,128)(2,1)S(1)} collective-permute-done((bf16[5,8,4224]{2,1,0:T(8,128)(2,1)S(1)}, bf16[5,8,4224]{2,1,0:T(8,128)(2,1)S(1)}, u32[]{:S(2)}, u32[]{:S(2)}) %collective-permute-start.2) | collective-permute-done | bytes 337952 | tf_op jit(solution)/shard_map/block_scatter/ppermute | solution.py:534
  19.0 2.8 %collective-permute-start.7 = (bf16[5,8,4096]{2,1,0:T(8,128)(2,1)S(1)}, bf16[5,8,4096]{2,1,0:T(8,128)(2,1)S(1)}, u32[]{:S(2)}, u32[]{:S(2)}) collective-permute-start(bf16[5,8,4096]{2,1,0:T(8,128)(2,1)S(1)} %get-tuple-element.48), channel_id=1, source_target_pairs={{0,12},{1,13},{2,14},{3,15},{4,0},{5,1},{6,2},{7,3},{8,4},{9,5},{1... | collective-permute-start | bytes 983048 | tf_op jit(solution)/shard_map/block_scatter/ppermute | solution.py:534
  22.8 1.9 %collective-permute-start.8 = (bf16[5,8,4224]{2,1,0:T(8,128)(2,1)S(1)}, bf16[5,8,4224]{2,1,0:T(8,128)(2,1)S(1)}, u32[]{:S(2)}, u32[]{:S(2)}) collective-permute-start(bf16[5,8,4224]{2,1,0:T(8,128)(2,1)S(1)} %get-tuple-element.53), channel_id=1, source_target_pairs={{0,8},{1,9},{2,10},{3,11},{4,12},{5,13},{6,14},{7,15},{8,0},{9,1},... | collective-permute-start | bytes 1013768 | tf_op jit(solution)/shard_map/block_scatter/ppermute | solution.py:534
  24.6 2.0 %collective-permute-start.9 = (bf16[5,8,4224]{2,1,0:T(8,128)(2,1)S(1)}, bf16[5,8,4224]{2,1,0:T(8,128)(2,1)S(1)}, u32[]{:S(2)}, u32[]{:S(2)}) collective-permute-start(bf16[5,8,4224]{2,1,0:T(8,128)(2,1)S(1)} %get-tuple-element.54), channel_id=1, source_target_pairs={{0,2},{1,3},{2,0},{3,1},{4,6},{5,7},{6,4},{7,5},{8,10},{9,11},{10,... | collective-permute-start | bytes 1013768 | tf_op jit(solution)/shard_map/block_scatter/ppermute | solution.py:534
  26.7 1.7 %collective-permute-done.6.second.below_b = bf16[5,8,4096]{2,1,0:T(8,128)(2,1)S(1)} collective-permute-done((bf16[5,8,4096]{2,1,0:T(8,128)(2,1)S(1)}, bf16[5,8,4096]{2,1,0:T(8,128)(2,1)S(1)}, u32[]{:S(2)}, u32[]{:S(2)}) %collective-permute-start.6) | collective-permute-done | bytes 327712 | tf_op jit(solution)/shard_map/block_scatter/ppermute | solution.py:534
  28.4 8.3 %collective-permute-done.8.far = bf16[5,8,4224]{2,1,0:T(8,128)(2,1)S(1)} collective-permute-done((bf16[5,8,4224]{2,1,0:T(8,128)(2,1)S(1)}, bf16[5,8,4224]{2,1,0:T(8,128)(2,1)S(1)}, u32[]{:S(2)}, u32[]{:S(2)}) %collective-permute-start.8) | collective-permute-done | bytes 337952 | tf_op jit(solution)/shard_map/block_scatter/ppermute | solution.py:534
  36.7 4.0 %transform.4 = (bf16[8,192,256]{2,1,0:T(8,128)(2,1)}, bf16[16,8,128]{2,1,0:T(8,128)(2,1)S(1)}, bf16[1,8,4096]{2,1,0:T(8,128)(2,1)S(1)}, bf16[1,8,4096]{2,1,0:T(8,128)(2,1)S(1)}, bf16[1,8,4096]{2,1,0:T(8,128)(2,1)S(1)}) custom-call(s32[1]{0:T(128)S(6)} %copy.14.ablock_ref, s32[1,2]{1,0:T(1,128)S(1)} %copy-done, bf16[128,8,4096]{2,1,0:T(8,128)(2,1)} %fields.13, ...), custom_call_target="tpu_custom_call" | custom-call | flops 20000000000 | bytes 1048576 | tf_op jit(solution)/shard_map/transform/pallas_call | solution.py:453
  40.7 5.1 %all-to-all-start = ((bf16[8,192,256]{2,1,0:T(8,128)(2,1)}), bf16[8,192,256]{2,1,0:T(8,128)(2,1)S(1)}, u32[]{:S(2)}, u32[]{:S(2)}) async-start(bf16[8,192,256]{2,1,0:T(8,128)(2,1)} %get-tuple-element.62), calls=%async_computation | async-start | bytes 1572864 | tf_op jit(solution)/shard_map/transform/all_to_all | solution.py:627
  46.3 8.7 %all-to-all-done.y_hbm.refs_7_ = bf16[8,192,256]{2,1,0:T(8,128)(2,1)S(1)} async-done(((bf16[8,192,256]{2,1,0:T(8,128)(2,1)}), bf16[8,192,256]{2,1,0:T(8,128)(2,1)S(1)}, u32[]{:S(2)}, u32[]{:S(2)}) %all-to-all-start) | async-done | bytes 786464 | tf_op jit(solution)/shard_map/transform/all_to_all | solution.py:627
  55.0 3.6 %transform.6 = bf16[512,256]{1,0:T(8,128)(2,1)} custom-call(bf16[8,192,256]{2,1,0:T(8,128)(2,1)S(1)} %all-to-all-done.y_hbm.refs_7_, f32[512,128]{1,0:T(8,128)S(1)} %transform.5.weight_ref, bf16[256,256]{1,0:T(8,128)(2,1)} %constant.22.clone.turn_hbm, bf16[512,1024]{1,0:T(8,128)(2,1)} %constant.20.clone.kx_hbm, bf16[512,1024]{1,0:T(8,128)(2,1)} %constant.21.clone.kxt_hbm), custom_call_target="tpu_custom_call" | custom-call | flops 10000000000 | bytes 1048576 | tf_op jit(solution)/shard_map/transform/pallas_call | solution.py:453
  58.5 6.6 %all-to-all-start.1 = ((bf16[8,64,256]{2,1,0:T(8,128)(2,1)}), bf16[8,64,256]{2,1,0:T(8,128)(2,1)S(1)}, u32[]{:S(2)}, u32[]{:S(2)}) async-start(bf16[8,64,256]{2,1,0:T(8,128)(2,1)} %bitcast), calls=%async_computation.1 | async-start | bytes 524288 | tf_op jit(solution)/shard_map/transform/all_to_all | solution.py:649
  65.8 4.0 %collective-permute-done.10.far = bf16[1,8,4096]{2,1,0:T(8,128)(2,1)S(1)} collective-permute-done((bf16[1,8,4096]{2,1,0:T(8,128)(2,1)S(1)}, bf16[1,8,4096]{2,1,0:T(8,128)(2,1)S(1)}, u32[]{:S(2)}, u32[]{:S(2)}) %collective-permute-start.10) | collective-permute-done | bytes 65568 | tf_op jit(solution)/shard_map/transform/ppermute | solution.py:534
  71.4 3.1 %transform.7 = bf16[4,8,4096]{2,1,0:T(8,128)(2,1)S(1)} custom-call(s32[1]{0:T(128)S(6)} %copy.14.ablock_ref, s32[1,2]{1,0:T(1,128)S(1)} %copy-done, bf16[128,8,4096]{2,1,0:T(8,128)(2,1)} %fields.13, bf16[16,8,4096]{2,1,0:T(8,128)(2,1)} %occupied.13, bf16[1,8,4096]{2,1,0:T(8,128)(2,1)S(1)} %get-tuple-element.59.second, ...), custom_call_target="tpu_custom_call" | custom-call | flops 100000000 | bytes 1048576 | tf_op jit(solution)/shard_map/transform/pallas_call | solution.py:453
  74.5 1.7 %collective-permute-start.12 = (bf16[32,4096]{1,0:T(8,128)(2,1)S(1)}, bf16[32,4096]{1,0:T(8,128)(2,1)S(1)}, u32[]{:S(2)}, u32[]{:S(2)}) collective-permute-start(bf16[32,4096]{1,0:T(8,128)(2,1)S(1)} %bitcast.5), channel_id=1, source_target_pairs={{0,8},{1,9},{2,10},{3,11},{4,12},{5,13},{6,14},{7,15},{8,0},{9,1},... | collective-permute-start | bytes 786440 | tf_op jit(solution)/shard_map/block_gather/ppermute | solution.py:534
  78.1 1.4 %collective-permute-start.21 = (bf16[32,4096]{1,0:T(8,128)(2,1)S(1)}, bf16[32,4096]{1,0:T(8,128)(2,1)S(1)}, u32[]{:S(2)}, u32[]{:S(2)}) collective-permute-start(bf16[32,4096]{1,0:T(8,128)(2,1)S(1)} %bitcast.8), channel_id=1, source_target_pairs={{0,12},{1,13},{2,14},{3,15},{4,0},{5,1},{6,2},{7,3},{8,4},{9,5},{1... | collective-permute-start | bytes 786440 | tf_op jit(solution)/shard_map/block_gather/ppermute | solution.py:534
  79.5 4.0 %collective-permute-start.17 = (bf16[32,4096]{1,0:T(8,128)(2,1)S(1)}, bf16[32,4096]{1,0:T(8,128)(2,1)S(1)}, u32[]{:S(2)}, u32[]{:S(2)}) collective-permute-start(bf16[32,4096]{1,0:T(8,128)(2,1)S(1)} %bitcast.9), channel_id=1, source_target_pairs={{0,1},{1,0},{2,3},{3,2},{4,5},{5,4},{6,7},{7,6},{8,9},{9,8},{10,11... | collective-permute-start | bytes 786440 | tf_op jit(solution)/shard_map/block_gather/ppermute | solution.py:534
  83.5 3.4 %block_gather.3.u_ref = bf16[1024,4096]{1,0:T(8,128)(2,1)S(1)} custom-call(bf16[1024,4096]{1,0:T(8,128)(2,1)} %bitcast.13), custom_call_target="tpu_custom_call" | custom-call | flops 100000000 | bytes 1048576 | tf_op jit(solution)/shard_map/block_gather/pallas_call | solution.py:453
  88.4 2.0 %collective-permute-start.20 = (bf16[32,4096]{1,0:T(8,128)(2,1)S(1)}, bf16[32,4096]{1,0:T(8,128)(2,1)S(1)}, u32[]{:S(2)}, u32[]{:S(2)}) collective-permute-start(bf16[32,4096]{1,0:T(8,128)(2,1)S(1)} %collective-permute-done.19.refs_4_), channel_id=1, source_target_pairs={{0,1},{1,0},{2,3},{3,2},{4,5},{5,4},{6,7},{7,6},{8,9},{9,8},{10,11... | collective-permute-start | bytes 786440 | tf_op jit(solution)/shard_map/block_gather/ppermute | solution.py:534
  90.4 1.6 %collective-permute-start.14 = (bf16[32,4096]{1,0:T(8,128)(2,1)S(1)}, bf16[32,4096]{1,0:T(8,128)(2,1)S(1)}, u32[]{:S(2)}, u32[]{:S(2)}) collective-permute-start(bf16[32,4096]{1,0:T(8,128)(2,1)S(1)} %collective-permute-done.12.refs_2_), channel_id=1, source_target_pairs={{0,2},{1,3},{2,0},{3,1},{4,6},{5,7},{6,4},{7,5},{8,10},{9,11},{10,... | collective-permute-start | bytes 786440 | tf_op jit(solution)/shard_map/block_gather/ppermute | solution.py:534
  92.1 2.6 %collective-permute-start.16 = (bf16[32,4096]{1,0:T(8,128)(2,1)S(1)}, bf16[32,4096]{1,0:T(8,128)(2,1)S(1)}, u32[]{:S(2)}, u32[]{:S(2)}) collective-permute-start(bf16[32,4096]{1,0:T(8,128)(2,1)S(1)} %collective-permute-done.13.refs_8_), channel_id=1, source_target_pairs={{0,12},{1,13},{2,14},{3,15},{4,0},{5,1},{6,2},{7,3},{8,4},{9,5},{1... | collective-permute-start | bytes 786440 | tf_op jit(solution)/shard_map/block_gather/ppermute | solution.py:534
  94.7 5.2 %block_gather.4.refs_6_ = f32[128,128]{1,0:T(8,128)S(1)} custom-call(bf16[1024,4096]{1,0:T(8,128)(2,1)S(1)} %block_gather.3.u_ref, bf16[32,4096]{1,0:T(8,128)(2,1)S(1)} %bitcast.10, bf16[32,4096]{1,0:T(8,128)(2,1)S(1)} %collective-permute-done.17.refs_1_, bf16[32,4096]{1,0:T(8,128)(2,1)S(1)} %collective-permute-done.12.refs_2_, ...), custom_call_target="tpu_custom_call" | custom-call | flops 2684354560 | bytes 8388608 | tf_op jit(solution)/shard_map/block_gather/pallas_call | solution.py:515
  100.3 1.6 %collective-permute-start.24 = (bf16[32,4096]{1,0:T(8,128)(2,1)S(1)}, bf16[32,4096]{1,0:T(8,128)(2,1)S(1)}, u32[]{:S(2)}, u32[]{:S(2)}) collective-permute-start(bf16[32,4096]{1,0:T(8,128)(2,1)S(1)} %collective-permute-done.14.refs_0_), channel_id=1, source_target_pairs={{0,1},{1,0},{2,3},{3,2},{4,5},{5,4},{6,7},{7,6},{8,9},{9,8},{10,11... | collective-permute-start | bytes 786440 | tf_op jit(solution)/shard_map/block_gather/ppermute | solution.py:534
  103.8 3.8 %block_gather.5 = bf16[1024,128]{1,0:T(8,128)(2,1)S(1)} custom-call(bf16[1024,4096]{1,0:T(8,128)(2,1)S(1)} %block_gather.3.u_ref, bf16[32,4096]{1,0:T(8,128)(2,1)S(1)} %collective-permute-done.14.refs_0_, bf16[32,4096]{1,0:T(8,128)(2,1)S(1)} %collective-permute-done.24.refs_1_, bf16[32,4096]{1,0:T(8,128)(2,1)S(1)} %collective-permute-done.15.refs_2_, ...), custom_call_target="tpu_custom_call" | custom-call | flops 1610612736 | bytes 8388608 | tf_op jit(solution)/shard_map/block_gather/pallas_call | solution.py:515
  107.6 18.8 %all_to_all.21 = bf16[128,8,128]{2,1,0:T(8,128)(2,1)S(1)} all-to-all(bf16[128,8,128]{2,1,0:T(8,128)(2,1)S(1)} %bitcast.12), channel_id=1, replica_groups=mesh['grid'=8,'band'=16] {'grid','band'}, dimensions={0} | all-to-all | bytes 524288 | tf_op jit(solution)/shard_map/ladder/all_to_all | solution.py:687
  (44 shorter events, 12.2 us)
Async XLA Ops:
  0.0 4.1 %copy-start = (s32[1,2]{1,0:T(1,128)S(1)}, s32[1,2]{1,0:T(1,128)}, u32[]{:S(2)}) copy-start(s32[1,2]{1,0:T(1,128)} %pairs_ref.11) | copy-start | bytes 28
  2.6 3.6 %collective-permute-start = (bf16[13,8,4224]{2,1,0:T(8,128)(2,1)S(1)}, bf16[13,8,4224]{2,1,0:T(8,128)(2,1)S(1)}, u32[]{:S(2)}, u32[]{:S(2)}) collective-permute-start(bf16[13,8,4224]{2,1,0:T(8,128)(2,1)S(1)} %block_scatter.6.sent_a), channel_id=1, source_target_pairs={{0,1},{1,0},{2,3},{3,2},{4,5},{5,4},{6,7},{7,6},{8,9},{9,8},{10,11... | collective-permute-start | bytes 2635784 | tf_op jit(solution)/shard_map/block_scatter/ppermute | solution.py:534
  8.0 5.9 %collective-permute-start.1 = (bf16[21,8,4096]{2,1,0:T(8,128)(2,1)S(1)}, bf16[21,8,4096]{2,1,0:T(8,128)(2,1)S(1)}, u32[]{:S(2)}, u32[]{:S(2)}) collective-permute-start(bf16[21,8,4096]{2,1,0:T(8,128)(2,1)S(1)} %get-tuple-element.43), channel_id=1, source_target_pairs={{0,1},{1,0},{2,3},{3,2},{4,5},{5,4},{6,7},{7,6},{8,9},{9,8},{10,11... | collective-permute-start | bytes 4128776 | tf_op jit(solution)/shard_map/block_scatter/ppermute | solution.py:534
  8.3 10.7 %collective-permute-start.2 = (bf16[5,8,4224]{2,1,0:T(8,128)(2,1)S(1)}, bf16[5,8,4224]{2,1,0:T(8,128)(2,1)S(1)}, u32[]{:S(2)}, u32[]{:S(2)}) collective-permute-start(bf16[5,8,4224]{2,1,0:T(8,128)(2,1)S(1)} %get-tuple-element.44), channel_id=1, source_target_pairs={{0,2},{1,3},{2,0},{3,1},{4,6},{5,7},{6,4},{7,5},{8,10},{9,11},{10,... | collective-permute-start | bytes 1013768 | tf_op jit(solution)/shard_map/block_scatter/ppermute | solution.py:534
  11.1 10.7 %collective-permute-start.3 = (bf16[5,8,4224]{2,1,0:T(8,128)(2,1)S(1)}, bf16[5,8,4224]{2,1,0:T(8,128)(2,1)S(1)}, u32[]{:S(2)}, u32[]{:S(2)}) collective-permute-start(bf16[5,8,4224]{2,1,0:T(8,128)(2,1)S(1)} %get-tuple-element.45), channel_id=1, source_target_pairs={{0,4},{1,5},{2,6},{3,7},{4,8},{5,9},{6,10},{7,11},{8,12},{9,13},{1... | collective-permute-start | bytes 1013768 | tf_op jit(solution)/shard_map/block_scatter/ppermute | solution.py:534
  12.4 9.4 %collective-permute-start.4 = (bf16[5,8,4224]{2,1,0:T(8,128)(2,1)S(1)}, bf16[5,8,4224]{2,1,0:T(8,128)(2,1)S(1)}, u32[]{:S(2)}, u32[]{:S(2)}) collective-permute-start(bf16[5,8,4224]{2,1,0:T(8,128)(2,1)S(1)} %get-tuple-element.46), channel_id=1, source_target_pairs={{0,12},{1,13},{2,14},{3,15},{4,0},{5,1},{6,2},{7,3},{8,4},{9,5},{1... | collective-permute-start | bytes 1013768 | tf_op jit(solution)/shard_map/block_scatter/ppermute | solution.py:534
  15.6 11.1 %collective-permute-start.5 = (bf16[5,8,4096]{2,1,0:T(8,128)(2,1)S(1)}, bf16[5,8,4096]{2,1,0:T(8,128)(2,1)S(1)}, u32[]{:S(2)}, u32[]{:S(2)}) collective-permute-start(bf16[5,8,4096]{2,1,0:T(8,128)(2,1)S(1)} %get-tuple-element.49), channel_id=1, source_target_pairs={{0,2},{1,3},{2,0},{3,1},{4,6},{5,7},{6,4},{7,5},{8,10},{9,11},{10,... | collective-permute-start | bytes 983048 | tf_op jit(solution)/shard_map/block_scatter/ppermute | solution.py:534
  15.9 12.5 %collective-permute-start.6 = (bf16[5,8,4096]{2,1,0:T(8,128)(2,1)S(1)}, bf16[5,8,4096]{2,1,0:T(8,128)(2,1)S(1)}, u32[]{:S(2)}, u32[]{:S(2)}) collective-permute-start(bf16[5,8,4096]{2,1,0:T(8,128)(2,1)S(1)} %get-tuple-element.47), channel_id=1, source_target_pairs={{0,4},{1,5},{2,6},{3,7},{4,8},{5,9},{6,10},{7,11},{8,12},{9,13},{1... | collective-permute-start | bytes 983048 | tf_op jit(solution)/shard_map/block_scatter/ppermute | solution.py:534
  19.0 9.4 %collective-permute-start.7 = (bf16[5,8,4096]{2,1,0:T(8,128)(2,1)S(1)}, bf16[5,8,4096]{2,1,0:T(8,128)(2,1)S(1)}, u32[]{:S(2)}, u32[]{:S(2)}) collective-permute-start(bf16[5,8,4096]{2,1,0:T(8,128)(2,1)S(1)} %get-tuple-element.48), channel_id=1, source_target_pairs={{0,12},{1,13},{2,14},{3,15},{4,0},{5,1},{6,2},{7,3},{8,4},{9,5},{1... | collective-permute-start | bytes 983048 | tf_op jit(solution)/shard_map/block_scatter/ppermute | solution.py:534
  22.8 13.9 %collective-permute-start.8 = (bf16[5,8,4224]{2,1,0:T(8,128)(2,1)S(1)}, bf16[5,8,4224]{2,1,0:T(8,128)(2,1)S(1)}, u32[]{:S(2)}, u32[]{:S(2)}) collective-permute-start(bf16[5,8,4224]{2,1,0:T(8,128)(2,1)S(1)} %get-tuple-element.53), channel_id=1, source_target_pairs={{0,8},{1,9},{2,10},{3,11},{4,12},{5,13},{6,14},{7,15},{8,0},{9,1},... | collective-permute-start | bytes 1013768 | tf_op jit(solution)/shard_map/block_scatter/ppermute | solution.py:534
  24.6 12.1 %collective-permute-start.9 = (bf16[5,8,4224]{2,1,0:T(8,128)(2,1)S(1)}, bf16[5,8,4224]{2,1,0:T(8,128)(2,1)S(1)}, u32[]{:S(2)}, u32[]{:S(2)}) collective-permute-start(bf16[5,8,4224]{2,1,0:T(8,128)(2,1)S(1)} %get-tuple-element.54), channel_id=1, source_target_pairs={{0,2},{1,3},{2,0},{3,1},{4,6},{5,7},{6,4},{7,5},{8,10},{9,11},{10,... | collective-permute-start | bytes 1013768 | tf_op jit(solution)/shard_map/block_scatter/ppermute | solution.py:534
  40.7 14.3 %all-to-all-start = ((bf16[8,192,256]{2,1,0:T(8,128)(2,1)}), bf16[8,192,256]{2,1,0:T(8,128)(2,1)S(1)}, u32[]{:S(2)}, u32[]{:S(2)}) async-start(bf16[8,192,256]{2,1,0:T(8,128)(2,1)} %get-tuple-element.62), calls=%async_computation | async-start | bytes 1572864 | tf_op jit(solution)/shard_map/transform/all_to_all | solution.py:627
  58.5 12.8 %all-to-all-start.1 = ((bf16[8,64,256]{2,1,0:T(8,128)(2,1)}), bf16[8,64,256]{2,1,0:T(8,128)(2,1)S(1)}, u32[]{:S(2)}, u32[]{:S(2)}) async-start(bf16[8,64,256]{2,1,0:T(8,128)(2,1)} %bitcast), calls=%async_computation.1 | async-start | bytes 524288 | tf_op jit(solution)/shard_map/transform/all_to_all | solution.py:649
  65.2 4.6 %collective-permute-start.10 = (bf16[1,8,4096]{2,1,0:T(8,128)(2,1)S(1)}, bf16[1,8,4096]{2,1,0:T(8,128)(2,1)S(1)}, u32[]{:S(2)}, u32[]{:S(2)}) collective-permute-start(bf16[1,8,4096]{2,1,0:T(8,128)(2,1)S(1)} %get-tuple-element.60), channel_id=1, source_target_pairs={{0,8},{1,9},{2,10},{3,11},{4,12},{5,13},{6,14},{7,15},{8,0},{9,1},... | collective-permute-start | bytes 196616 | tf_op jit(solution)/shard_map/transform/ppermute | solution.py:534
  65.4 5.6 %collective-permute-start.11 = (bf16[1,8,4096]{2,1,0:T(8,128)(2,1)S(1)}, bf16[1,8,4096]{2,1,0:T(8,128)(2,1)S(1)}, u32[]{:S(2)}, u32[]{:S(2)}) collective-permute-start(bf16[1,8,4096]{2,1,0:T(8,128)(2,1)S(1)} %get-tuple-element.61), channel_id=1, source_target_pairs={{0,2},{1,3},{2,0},{3,1},{4,6},{5,7},{6,4},{7,5},{8,10},{9,11},{10,... | collective-permute-start | bytes 196616 | tf_op jit(solution)/shard_map/transform/ppermute | solution.py:534
  74.5 12.4 %collective-permute-start.12 = (bf16[32,4096]{1,0:T(8,128)(2,1)S(1)}, bf16[32,4096]{1,0:T(8,128)(2,1)S(1)}, u32[]{:S(2)}, u32[]{:S(2)}) collective-permute-start(bf16[32,4096]{1,0:T(8,128)(2,1)S(1)} %bitcast.5), channel_id=1, source_target_pairs={{0,8},{1,9},{2,10},{3,11},{4,12},{5,13},{6,14},{7,15},{8,0},{9,1},... | collective-permute-start | bytes 786440 | tf_op jit(solution)/shard_map/block_gather/ppermute | solution.py:534
  76.1 10.8 %collective-permute-start.13 = (bf16[32,4096]{1,0:T(8,128)(2,1)S(1)}, bf16[32,4096]{1,0:T(8,128)(2,1)S(1)}, u32[]{:S(2)}, u32[]{:S(2)}) collective-permute-start(bf16[32,4096]{1,0:T(8,128)(2,1)S(1)} %bitcast.6), channel_id=1, source_target_pairs={{0,2},{1,3},{2,0},{3,1},{4,6},{5,7},{6,4},{7,5},{8,10},{9,11},{10,... | collective-permute-start | bytes 786440 | tf_op jit(solution)/shard_map/block_gather/ppermute | solution.py:534
  76.8 11.6 %collective-permute-start.19 = (bf16[32,4096]{1,0:T(8,128)(2,1)S(1)}, bf16[32,4096]{1,0:T(8,128)(2,1)S(1)}, u32[]{:S(2)}, u32[]{:S(2)}) collective-permute-start(bf16[32,4096]{1,0:T(8,128)(2,1)S(1)} %bitcast.7), channel_id=1, source_target_pairs={{0,4},{1,5},{2,6},{3,7},{4,8},{5,9},{6,10},{7,11},{8,12},{9,13},{1... | collective-permute-start | bytes 786440 | tf_op jit(solution)/shard_map/block_gather/ppermute | solution.py:534
  78.1 12.3 %collective-permute-start.21 = (bf16[32,4096]{1,0:T(8,128)(2,1)S(1)}, bf16[32,4096]{1,0:T(8,128)(2,1)S(1)}, u32[]{:S(2)}, u32[]{:S(2)}) collective-permute-start(bf16[32,4096]{1,0:T(8,128)(2,1)S(1)} %bitcast.8), channel_id=1, source_target_pairs={{0,12},{1,13},{2,14},{3,15},{4,0},{5,1},{6,2},{7,3},{8,4},{9,5},{1... | collective-permute-start | bytes 786440 | tf_op jit(solution)/shard_map/block_gather/ppermute | solution.py:534
  79.5 10.9 %collective-permute-start.17 = (bf16[32,4096]{1,0:T(8,128)(2,1)S(1)}, bf16[32,4096]{1,0:T(8,128)(2,1)S(1)}, u32[]{:S(2)}, u32[]{:S(2)}) collective-permute-start(bf16[32,4096]{1,0:T(8,128)(2,1)S(1)} %bitcast.9), channel_id=1, source_target_pairs={{0,1},{1,0},{2,3},{3,2},{4,5},{5,4},{6,7},{7,6},{8,9},{9,8},{10,11... | collective-permute-start | bytes 786440 | tf_op jit(solution)/shard_map/block_gather/ppermute | solution.py:534
  86.9 5.1 %collective-permute-start.18 = (bf16[32,4096]{1,0:T(8,128)(2,1)S(1)}, bf16[32,4096]{1,0:T(8,128)(2,1)S(1)}, u32[]{:S(2)}, u32[]{:S(2)}) collective-permute-start(bf16[32,4096]{1,0:T(8,128)(2,1)S(1)} %collective-permute-done.12.refs_2_), channel_id=1, source_target_pairs={{0,1},{1,0},{2,3},{3,2},{4,5},{5,4},{6,7},{7,6},{8,9},{9,8},{10,11... | collective-permute-start | bytes 786440 | tf_op jit(solution)/shard_map/block_gather/ppermute | solution.py:534
  87.6 4.5 %collective-permute-start.23 = (bf16[32,4096]{1,0:T(8,128)(2,1)S(1)}, bf16[32,4096]{1,0:T(8,128)(2,1)S(1)}, u32[]{:S(2)}, u32[]{:S(2)}) collective-permute-start(bf16[32,4096]{1,0:T(8,128)(2,1)S(1)} %collective-permute-done.13.refs_8_), channel_id=1, source_target_pairs={{0,1},{1,0},{2,3},{3,2},{4,5},{5,4},{6,7},{7,6},{8,9},{9,8},{10,11... | collective-permute-start | bytes 786440 | tf_op jit(solution)/shard_map/block_gather/ppermute | solution.py:534
  88.4 6.3 %collective-permute-start.20 = (bf16[32,4096]{1,0:T(8,128)(2,1)S(1)}, bf16[32,4096]{1,0:T(8,128)(2,1)S(1)}, u32[]{:S(2)}, u32[]{:S(2)}) collective-permute-start(bf16[32,4096]{1,0:T(8,128)(2,1)S(1)} %collective-permute-done.19.refs_4_), channel_id=1, source_target_pairs={{0,1},{1,0},{2,3},{3,2},{4,5},{5,4},{6,7},{7,6},{8,9},{9,8},{10,11... | collective-permute-start | bytes 786440 | tf_op jit(solution)/shard_map/block_gather/ppermute | solution.py:534
  90.4 4.3 %collective-permute-start.22 = (bf16[32,4096]{1,0:T(8,128)(2,1)S(1)}, bf16[32,4096]{1,0:T(8,128)(2,1)S(1)}, u32[]{:S(2)}, u32[]{:S(2)}) collective-permute-start(bf16[32,4096]{1,0:T(8,128)(2,1)S(1)} %collective-permute-done.21.refs_6_), channel_id=1, source_target_pairs={{0,1},{1,0},{2,3},{3,2},{4,5},{5,4},{6,7},{7,6},{8,9},{9,8},{10,11... | collective-permute-start | bytes 786440 | tf_op jit(solution)/shard_map/block_gather/ppermute | solution.py:534
  90.4 9.4 %collective-permute-start.14 = (bf16[32,4096]{1,0:T(8,128)(2,1)S(1)}, bf16[32,4096]{1,0:T(8,128)(2,1)S(1)}, u32[]{:S(2)}, u32[]{:S(2)}) collective-permute-start(bf16[32,4096]{1,0:T(8,128)(2,1)S(1)} %collective-permute-done.12.refs_2_), channel_id=1, source_target_pairs={{0,2},{1,3},{2,0},{3,1},{4,6},{5,7},{6,4},{7,5},{8,10},{9,11},{10,... | collective-permute-start | bytes 786440 | tf_op jit(solution)/shard_map/block_gather/ppermute | solution.py:534
  92.0 8.3 %collective-permute-start.15 = (bf16[32,4096]{1,0:T(8,128)(2,1)S(1)}, bf16[32,4096]{1,0:T(8,128)(2,1)S(1)}, u32[]{:S(2)}, u32[]{:S(2)}) collective-permute-start(bf16[32,4096]{1,0:T(8,128)(2,1)S(1)} %collective-permute-done.13.refs_8_), channel_id=1, source_target_pairs={{0,4},{1,5},{2,6},{3,7},{4,8},{5,9},{6,10},{7,11},{8,12},{9,13},{1... | collective-permute-start | bytes 786440 | tf_op jit(solution)/shard_map/block_gather/ppermute | solution.py:534
  92.1 8.2 %collective-permute-start.16 = (bf16[32,4096]{1,0:T(8,128)(2,1)S(1)}, bf16[32,4096]{1,0:T(8,128)(2,1)S(1)}, u32[]{:S(2)}, u32[]{:S(2)}) collective-permute-start(bf16[32,4096]{1,0:T(8,128)(2,1)S(1)} %collective-permute-done.13.refs_8_), channel_id=1, source_target_pairs={{0,12},{1,13},{2,14},{3,15},{4,0},{5,1},{6,2},{7,3},{8,4},{9,5},{1... | collective-permute-start | bytes 786440 | tf_op jit(solution)/shard_map/block_gather/ppermute | solution.py:534
  100.3 2.7 %collective-permute-start.24 = (bf16[32,4096]{1,0:T(8,128)(2,1)S(1)}, bf16[32,4096]{1,0:T(8,128)(2,1)S(1)}, u32[]{:S(2)}, u32[]{:S(2)}) collective-permute-start(bf16[32,4096]{1,0:T(8,128)(2,1)S(1)} %collective-permute-done.14.refs_0_), channel_id=1, source_target_pairs={{0,1},{1,0},{2,3},{3,2},{4,5},{5,4},{6,7},{7,6},{8,9},{9,8},{10,11... | collective-permute-start | bytes 786440 | tf_op jit(solution)/shard_map/block_gather/ppermute | solution.py:534
  101.9 1.5 %collective-permute-start.25 = (bf16[32,4096]{1,0:T(8,128)(2,1)S(1)}, bf16[32,4096]{1,0:T(8,128)(2,1)S(1)}, u32[]{:S(2)}, u32[]{:S(2)}) collective-permute-start(bf16[32,4096]{1,0:T(8,128)(2,1)S(1)} %collective-permute-done.15.refs_2_), channel_id=1, source_target_pairs={{0,1},{1,0},{2,3},{3,2},{4,5},{5,4},{6,7},{7,6},{8,9},{9,8},{10,11... | collective-permute-start | bytes 786440 | tf_op jit(solution)/shard_map/block_gather/ppermute | solution.py:534
  101.9 1.9 %collective-permute-start.26 = (bf16[32,4096]{1,0:T(8,128)(2,1)S(1)}, bf16[32,4096]{1,0:T(8,128)(2,1)S(1)}, u32[]{:S(2)}, u32[]{:S(2)}) collective-permute-start(bf16[32,4096]{1,0:T(8,128)(2,1)S(1)} %collective-permute-done.16.refs_4_), channel_id=1, source_target_pairs={{0,1},{1,0},{2,3},{3,2},{4,5},{5,4},{6,7},{7,6},{8,9},{9,8},{10,11... | collective-permute-start | bytes 786440 | tf_op jit(solution)/shard_map/block_gather/ppermute | solution.py:534

commit v7 on v6

--- a/solution.py
+++ b/solution.py
@@ -465,15 +465,8 @@
     pieces = 2 * len(names)
     w_refs, extra = refs[:pieces], refs[pieces:-2]
     out_ref, total = refs[-2:]
-    lanes = 2048
-    for s in range(N * N // lanes):
-        part = pl.ds(s * lanes, lanes)
-        right = jnp.concatenate([w[:, part] for w in w_refs], axis=0)
-        gram = lax.dot_general(u_ref[:, part], right, (((1,), (1,)), ((), ())), preferred_element_type=F32)
-        if s == 0:
-            total[...] = gram
-        else:
-            total[...] += gram
+    right = jnp.concatenate([w[...] for w in w_refs], axis=0)
+    total[...] = lax.dot_general(u_ref[...], right, (((1,), (1,)), ((), ())), preferred_element_type=F32)
     gram = total[...]
     wide = gram.shape[1]
     row = lax.broadcasted_iota(jnp.int32, gram.shape, 0) % XL
@@ -487,9 +480,12 @@
     for dy, dh in names:
         for dc in range(2):
             first = 32 * ((c + dc) % 2) + 8 * ((y - dy + 4) % 4) + 4 * ((h + dh) % 2)
-            pick.append((lane == first + row).astype(F32))
+            pick.append((lane == first + row).astype(BF16))
     pick = jnp.concatenate(pick, axis=0)
-    slab = jnp.dot(gram, pick, precision=lax.Precision.HIGHEST, preferred_element_type=F32)
+    high = gram.astype(BF16)
+    rest = gram - high.astype(F32)
+    middle = rest.astype(BF16)
+    slab = dot(high, pick) + dot(middle, pick) + dot((rest - middle.astype(F32)).astype(BF16), pick)
     if extra:
         slab = slab + extra[0][...]
     if not last:

time: 128 us -> 129 us (level)
  starting transfers between devices: 46 us -> 47.6 us
    ppermute x27, starting transfers between devices: 34.3 us -> 36.2 us  [band_shift(): return lax.ppermute(value, 'band', pairs)]
  transfers between devices with their start and end apart: 29 -> 29, of which waited for: 12 -> 12; matrix products, arithmetic and copies ran while one was open for 0% -> 0% of each run, Pallas kernels for 11% -> 10%
where the time goes in v7:
time: 129 us; the launch traced here: 128 us
  starting transfers between devices  47.6 us (37%)
  Pallas kernels  31.7 us (25%)
  waiting for transfers between devices  28.1 us (22%)
  blocking collectives  18.8 us (15%)
    ppermute x27, starting transfers between devices, band_shift(): return lax.ppermute(value, 'band', pairs)  36.2 us
    pallas_call x11, Pallas kernels, call(): pl.pallas_call(body, out_shape=shapes if many else shapes[0], in_specs=[p...  22.1 us
    all_to_all x1, blocking collectives, per_device(): lax.all_to_all(terms.reshape(GRID * BAND, XL, 128), ('grid', 'band'), 0,...  18.8 us
    ppermute x27, waiting for transfers between devices, band_shift(): return lax.ppermute(value, 'band', pairs)  18.7 us
    all_to_all x2, starting transfers between devices, per_device(): freq = lax.all_to_all(freq, 'grid', 0, 0, tiled=True)  11.5 us
    pallas_call x2, Pallas kernels, slab_call(): pl.pallas_call(functools.partial(slab_body, last, names), out_shape=jax.S...  9.65 us
    all_to_all x2, waiting for transfers between devices, per_device(): freq = lax.all_to_all(freq, 'grid', 0, 0, tiled=True)  9.43 us
  transfers between devices with their start and end apart: 29, of which 12 were waited for; matrix products, arithmetic and copies ran while one was open for 0% of the time, Pallas kernels for 10%

profile of v7, /device:TPU:1, one launch (start us, length us, event | category | flops | bytes accessed | tf_op | source)
XLA Modules:
  0.0 127.9 jit_solution(13234187879070351944)
XLA Ops:
  0.7 1.9 %block_scatter.6.sent_a = bf16[13,8,4224]{2,1,0:T(8,128)(2,1)S(1)} custom-call(s32[1]{0:T(128)S(6)} %copy.14.ablock_ref, s32[1,2]{1,0:T(1,128)} %pairs_ref.11, s32[1,512]{1,0:T(1,128)} %kept_hbm.1, bf16[128,8,4096]{2,1,0:T(8,128)(2,1)} %fields.13, bf16[16,8,4096]{2,1,0:T(8,128)(2,1)} %occupied.13), custom_call_target="tpu_custom_call" | custom-call | flops 100000000 | bytes 1048576 | tf_op jit(solution)/shard_map/block_scatter/pallas_call | solution.py:453
  2.6 1.5 %collective-permute-start = (bf16[13,8,4224]{2,1,0:T(8,128)(2,1)S(1)}, bf16[13,8,4224]{2,1,0:T(8,128)(2,1)S(1)}, u32[]{:S(2)}, u32[]{:S(2)}) collective-permute-start(bf16[13,8,4224]{2,1,0:T(8,128)(2,1)S(1)} %block_scatter.6.sent_a), channel_id=1, source_target_pairs={{0,1},{1,0},{2,3},{3,2},{4,5},{5,4},{6,7},{7,6},{8,9},{9,8},{10,11... | collective-permute-start | bytes 2635784 | tf_op jit(solution)/shard_map/block_scatter/ppermute | solution.py:530
  4.1 2.1 %block_scatter.8 = (bf16[21,8,4096]{2,1,0:T(8,128)(2,1)S(1)}, bf16[128,256]{1,0:T(8,128)(2,1)S(1)}) custom-call(s32[1]{0:T(128)S(6)} %copy.14.ablock_ref, s32[1,2]{1,0:T(1,128)S(1)} %copy-done, bf16[128,8,4096]{2,1,0:T(8,128)(2,1)} %fields.13, bf16[16,8,4096]{2,1,0:T(8,128)(2,1)} %occupied.13, bf16[1,128,256]{2,1,0:T(8,128)(2,1)} %amp_hbm.1), custom_call_target="tpu_custom_call" | custom-call | flops 5000000000 | bytes 1048576 | tf_op jit(solution)/shard_map/block_scatter/pallas_call | solution.py:453
  6.2 1.7 %block_scatter.7 = (bf16[5,8,4224]{2,1,0:T(8,128)(2,1)S(1)}, bf16[5,8,4224]{2,1,0:T(8,128)(2,1)S(1)}, bf16[5,8,4224]{2,1,0:T(8,128)(2,1)S(1)}) custom-call(s32[1]{0:T(128)S(6)} %copy.14.ablock_ref, s32[1,2]{1,0:T(1,128)S(1)} %copy-done, bf16[128,8,4096]{2,1,0:T(8,128)(2,1)} %fields.13, bf16[16,8,4096]{2,1,0:T(8,128)(2,1)} %occupied.13, ...), custom_call_target="tpu_custom_call" | custom-call | flops 100000000 | bytes 1048576 | tf_op jit(solution)/shard_map/block_scatter/pallas_call | solution.py:453
  8.4 2.8 %collective-permute-start.2 = (bf16[5,8,4224]{2,1,0:T(8,128)(2,1)S(1)}, bf16[5,8,4224]{2,1,0:T(8,128)(2,1)S(1)}, u32[]{:S(2)}, u32[]{:S(2)}) collective-permute-start(bf16[5,8,4224]{2,1,0:T(8,128)(2,1)S(1)} %get-tuple-element.44), channel_id=1, source_target_pairs={{0,2},{1,3},{2,0},{3,1},{4,6},{5,7},{6,4},{7,5},{8,10},{9,11},{10,... | collective-permute-start | bytes 1013768 | tf_op jit(solution)/shard_map/block_scatter/ppermute | solution.py:530
  12.5 1.4 %collective-permute-start.4 = (bf16[5,8,4224]{2,1,0:T(8,128)(2,1)S(1)}, bf16[5,8,4224]{2,1,0:T(8,128)(2,1)S(1)}, u32[]{:S(2)}, u32[]{:S(2)}) collective-permute-start(bf16[5,8,4224]{2,1,0:T(8,128)(2,1)S(1)} %get-tuple-element.46), channel_id=1, source_target_pairs={{0,12},{1,13},{2,14},{3,15},{4,0},{5,1},{6,2},{7,3},{8,4},{9,5},{1... | collective-permute-start | bytes 1013768 | tf_op jit(solution)/shard_map/block_scatter/ppermute | solution.py:530
  16.3 3.1 %collective-permute-done.2.crossed.crossed_a = bf16[5,8,4224]{2,1,0:T(8,128)(2,1)S(1)} collective-permute-done((bf16[5,8,4224]{2,1,0:T(8,128)(2,1)S(1)}, bf16[5,8,4224]{2,1,0:T(8,128)(2,1)S(1)}, u32[]{:S(2)}, u32[]{:S(2)}) %collective-permute-start.2) | collective-permute-done | bytes 337952 | tf_op jit(solution)/shard_map/block_scatter/ppermute | solution.py:530
  19.4 2.8 %collective-permute-start.7 = (bf16[5,8,4096]{2,1,0:T(8,128)(2,1)S(1)}, bf16[5,8,4096]{2,1,0:T(8,128)(2,1)S(1)}, u32[]{:S(2)}, u32[]{:S(2)}) collective-permute-start(bf16[5,8,4096]{2,1,0:T(8,128)(2,1)S(1)} %get-tuple-element.48), channel_id=1, source_target_pairs={{0,12},{1,13},{2,14},{3,15},{4,0},{5,1},{6,2},{7,3},{8,4},{9,5},{1... | collective-permute-start | bytes 983048 | tf_op jit(solution)/shard_map/block_scatter/ppermute | solution.py:530
  23.1 1.9 %collective-permute-start.8 = (bf16[5,8,4224]{2,1,0:T(8,128)(2,1)S(1)}, bf16[5,8,4224]{2,1,0:T(8,128)(2,1)S(1)}, u32[]{:S(2)}, u32[]{:S(2)}) collective-permute-start(bf16[5,8,4224]{2,1,0:T(8,128)(2,1)S(1)} %get-tuple-element.53), channel_id=1, source_target_pairs={{0,8},{1,9},{2,10},{3,11},{4,12},{5,13},{6,14},{7,15},{8,0},{9,1},... | collective-permute-start | bytes 1013768 | tf_op jit(solution)/shard_map/block_scatter/ppermute | solution.py:530
  25.0 2.0 %collective-permute-start.9 = (bf16[5,8,4224]{2,1,0:T(8,128)(2,1)S(1)}, bf16[5,8,4224]{2,1,0:T(8,128)(2,1)S(1)}, u32[]{:S(2)}, u32[]{:S(2)}) collective-permute-start(bf16[5,8,4224]{2,1,0:T(8,128)(2,1)S(1)} %get-tuple-element.54), channel_id=1, source_target_pairs={{0,2},{1,3},{2,0},{3,1},{4,6},{5,7},{6,4},{7,5},{8,10},{9,11},{10,... | collective-permute-start | bytes 1013768 | tf_op jit(solution)/shard_map/block_scatter/ppermute | solution.py:530
  27.0 1.8 %collective-permute-done.6.second.below_b = bf16[5,8,4096]{2,1,0:T(8,128)(2,1)S(1)} collective-permute-done((bf16[5,8,4096]{2,1,0:T(8,128)(2,1)S(1)}, bf16[5,8,4096]{2,1,0:T(8,128)(2,1)S(1)}, u32[]{:S(2)}, u32[]{:S(2)}) %collective-permute-start.6) | collective-permute-done | bytes 327712 | tf_op jit(solution)/shard_map/block_scatter/ppermute | solution.py:530
  28.8 8.3 %collective-permute-done.8.far = bf16[5,8,4224]{2,1,0:T(8,128)(2,1)S(1)} collective-permute-done((bf16[5,8,4224]{2,1,0:T(8,128)(2,1)S(1)}, bf16[5,8,4224]{2,1,0:T(8,128)(2,1)S(1)}, u32[]{:S(2)}, u32[]{:S(2)}) %collective-permute-start.8) | collective-permute-done | bytes 337952 | tf_op jit(solution)/shard_map/block_scatter/ppermute | solution.py:530
  37.1 3.9 %transform.4 = (bf16[8,192,256]{2,1,0:T(8,128)(2,1)}, bf16[16,8,128]{2,1,0:T(8,128)(2,1)S(1)}, bf16[1,8,4096]{2,1,0:T(8,128)(2,1)S(1)}, bf16[1,8,4096]{2,1,0:T(8,128)(2,1)S(1)}, bf16[1,8,4096]{2,1,0:T(8,128)(2,1)S(1)}) custom-call(s32[1]{0:T(128)S(6)} %copy.14.ablock_ref, s32[1,2]{1,0:T(1,128)S(1)} %copy-done, bf16[128,8,4096]{2,1,0:T(8,128)(2,1)} %fields.13, ...), custom_call_target="tpu_custom_call" | custom-call | flops 20000000000 | bytes 1048576 | tf_op jit(solution)/shard_map/transform/pallas_call | solution.py:453
  41.1 5.1 %all-to-all-start = ((bf16[8,192,256]{2,1,0:T(8,128)(2,1)}), bf16[8,192,256]{2,1,0:T(8,128)(2,1)S(1)}, u32[]{:S(2)}, u32[]{:S(2)}) async-start(bf16[8,192,256]{2,1,0:T(8,128)(2,1)} %get-tuple-element.62), calls=%async_computation | async-start | bytes 1572864 | tf_op jit(solution)/shard_map/transform/all_to_all | solution.py:623
  46.6 8.9 %all-to-all-done.y_hbm.refs_7_ = bf16[8,192,256]{2,1,0:T(8,128)(2,1)S(1)} async-done(((bf16[8,192,256]{2,1,0:T(8,128)(2,1)}), bf16[8,192,256]{2,1,0:T(8,128)(2,1)S(1)}, u32[]{:S(2)}, u32[]{:S(2)}) %all-to-all-start) | async-done | bytes 786464 | tf_op jit(solution)/shard_map/transform/all_to_all | solution.py:623
  55.5 3.6 %transform.6 = bf16[512,256]{1,0:T(8,128)(2,1)} custom-call(bf16[8,192,256]{2,1,0:T(8,128)(2,1)S(1)} %all-to-all-done.y_hbm.refs_7_, f32[512,128]{1,0:T(8,128)S(1)} %transform.5.weight_ref, bf16[256,256]{1,0:T(8,128)(2,1)} %constant.22.clone.turn_hbm, bf16[512,1024]{1,0:T(8,128)(2,1)} %constant.20.clone.kx_hbm, bf16[512,1024]{1,0:T(8,128)(2,1)} %constant.21.clone.kxt_hbm), custom_call_target="tpu_custom_call" | custom-call | flops 10000000000 | bytes 1048576 | tf_op jit(solution)/shard_map/transform/pallas_call | solution.py:453
  59.1 6.4 %all-to-all-start.1 = ((bf16[8,64,256]{2,1,0:T(8,128)(2,1)}), bf16[8,64,256]{2,1,0:T(8,128)(2,1)S(1)}, u32[]{:S(2)}, u32[]{:S(2)}) async-start(bf16[8,64,256]{2,1,0:T(8,128)(2,1)} %bitcast), calls=%async_computation.1 | async-start | bytes 524288 | tf_op jit(solution)/shard_map/transform/all_to_all | solution.py:645
  65.6 1.9 %collective-permute-start.11 = (bf16[1,8,4096]{2,1,0:T(8,128)(2,1)S(1)}, bf16[1,8,4096]{2,1,0:T(8,128)(2,1)S(1)}, u32[]{:S(2)}, u32[]{:S(2)}) collective-permute-start(bf16[1,8,4096]{2,1,0:T(8,128)(2,1)S(1)} %get-tuple-element.61), channel_id=1, source_target_pairs={{0,2},{1,3},{2,0},{3,1},{4,6},{5,7},{6,4},{7,5},{8,10},{9,11},{10,... | collective-permute-start | bytes 196616 | tf_op jit(solution)/shard_map/transform/ppermute | solution.py:530
  67.5 2.6 %collective-permute-done.10.far = bf16[1,8,4096]{2,1,0:T(8,128)(2,1)S(1)} collective-permute-done((bf16[1,8,4096]{2,1,0:T(8,128)(2,1)S(1)}, bf16[1,8,4096]{2,1,0:T(8,128)(2,1)S(1)}, u32[]{:S(2)}, u32[]{:S(2)}) %collective-permute-start.10) | collective-permute-done | bytes 65568 | tf_op jit(solution)/shard_map/transform/ppermute | solution.py:530
  71.7 3.1 %transform.7 = bf16[4,8,4096]{2,1,0:T(8,128)(2,1)S(1)} custom-call(s32[1]{0:T(128)S(6)} %copy.14.ablock_ref, s32[1,2]{1,0:T(1,128)S(1)} %copy-done, bf16[128,8,4096]{2,1,0:T(8,128)(2,1)} %fields.13, bf16[16,8,4096]{2,1,0:T(8,128)(2,1)} %occupied.13, bf16[1,8,4096]{2,1,0:T(8,128)(2,1)S(1)} %get-tuple-element.59.second, ...), custom_call_target="tpu_custom_call" | custom-call | flops 100000000 | bytes 1048576 | tf_op jit(solution)/shard_map/transform/pallas_call | solution.py:453
  74.8 1.5 %collective-permute-start.12 = (bf16[32,4096]{1,0:T(8,128)(2,1)S(1)}, bf16[32,4096]{1,0:T(8,128)(2,1)S(1)}, u32[]{:S(2)}, u32[]{:S(2)}) collective-permute-start(bf16[32,4096]{1,0:T(8,128)(2,1)S(1)} %bitcast.5), channel_id=1, source_target_pairs={{0,8},{1,9},{2,10},{3,11},{4,12},{5,13},{6,14},{7,15},{8,0},{9,1},... | collective-permute-start | bytes 786440 | tf_op jit(solution)/shard_map/block_gather/ppermute | solution.py:530
  76.3 1.5 %collective-permute-start.13 = (bf16[32,4096]{1,0:T(8,128)(2,1)S(1)}, bf16[32,4096]{1,0:T(8,128)(2,1)S(1)}, u32[]{:S(2)}, u32[]{:S(2)}) collective-permute-start(bf16[32,4096]{1,0:T(8,128)(2,1)S(1)} %bitcast.6), channel_id=1, source_target_pairs={{0,2},{1,3},{2,0},{3,1},{4,6},{5,7},{6,4},{7,5},{8,10},{9,11},{10,... | collective-permute-start | bytes 786440 | tf_op jit(solution)/shard_map/block_gather/ppermute | solution.py:530
  78.9 1.6 %collective-permute-start.21 = (bf16[32,4096]{1,0:T(8,128)(2,1)S(1)}, bf16[32,4096]{1,0:T(8,128)(2,1)S(1)}, u32[]{:S(2)}, u32[]{:S(2)}) collective-permute-start(bf16[32,4096]{1,0:T(8,128)(2,1)S(1)} %bitcast.8), channel_id=1, source_target_pairs={{0,12},{1,13},{2,14},{3,15},{4,0},{5,1},{6,2},{7,3},{8,4},{9,5},{1... | collective-permute-start | bytes 786440 | tf_op jit(solution)/shard_map/block_gather/ppermute | solution.py:530
  80.5 3.7 %collective-permute-start.17 = (bf16[32,4096]{1,0:T(8,128)(2,1)S(1)}, bf16[32,4096]{1,0:T(8,128)(2,1)S(1)}, u32[]{:S(2)}, u32[]{:S(2)}) collective-permute-start(bf16[32,4096]{1,0:T(8,128)(2,1)S(1)} %bitcast.9), channel_id=1, source_target_pairs={{0,1},{1,0},{2,3},{3,2},{4,5},{5,4},{6,7},{7,6},{8,9},{9,8},{10,11... | collective-permute-start | bytes 786440 | tf_op jit(solution)/shard_map/block_gather/ppermute | solution.py:530
  84.2 3.4 %block_gather.3.u_ref = bf16[1024,4096]{1,0:T(8,128)(2,1)S(1)} custom-call(bf16[1024,4096]{1,0:T(8,128)(2,1)} %bitcast.13), custom_call_target="tpu_custom_call" | custom-call | flops 100000000 | bytes 1048576 | tf_op jit(solution)/shard_map/block_gather/pallas_call | solution.py:453
  88.5 2.2 %collective-permute-start.20 = (bf16[32,4096]{1,0:T(8,128)(2,1)S(1)}, bf16[32,4096]{1,0:T(8,128)(2,1)S(1)}, u32[]{:S(2)}, u32[]{:S(2)}) collective-permute-start(bf16[32,4096]{1,0:T(8,128)(2,1)S(1)} %collective-permute-done.19.refs_4_), channel_id=1, source_target_pairs={{0,1},{1,0},{2,3},{3,2},{4,5},{5,4},{6,7},{7,6},{8,9},{9,8},{10,11... | collective-permute-start | bytes 786440 | tf_op jit(solution)/shard_map/block_gather/ppermute | solution.py:530
  90.8 1.6 %collective-permute-start.14 = (bf16[32,4096]{1,0:T(8,128)(2,1)S(1)}, bf16[32,4096]{1,0:T(8,128)(2,1)S(1)}, u32[]{:S(2)}, u32[]{:S(2)}) collective-permute-start(bf16[32,4096]{1,0:T(8,128)(2,1)S(1)} %collective-permute-done.12.refs_2_), channel_id=1, source_target_pairs={{0,2},{1,3},{2,0},{3,1},{4,6},{5,7},{6,4},{7,5},{8,10},{9,11},{10,... | collective-permute-start | bytes 786440 | tf_op jit(solution)/shard_map/block_gather/ppermute | solution.py:530
  92.9 2.1 %collective-permute-start.16 = (bf16[32,4096]{1,0:T(8,128)(2,1)S(1)}, bf16[32,4096]{1,0:T(8,128)(2,1)S(1)}, u32[]{:S(2)}, u32[]{:S(2)}) collective-permute-start(bf16[32,4096]{1,0:T(8,128)(2,1)S(1)} %collective-permute-done.13.refs_8_), channel_id=1, source_target_pairs={{0,12},{1,13},{2,14},{3,15},{4,0},{5,1},{6,2},{7,3},{8,4},{9,5},{1... | collective-permute-start | bytes 786440 | tf_op jit(solution)/shard_map/block_gather/ppermute | solution.py:530
  95.0 5.6 %block_gather.4.refs_6_ = f32[128,128]{1,0:T(8,128)S(1)} custom-call(bf16[1024,4096]{1,0:T(8,128)(2,1)S(1)} %block_gather.3.u_ref, bf16[32,4096]{1,0:T(8,128)(2,1)S(1)} %bitcast.10, bf16[32,4096]{1,0:T(8,128)(2,1)S(1)} %collective-permute-done.17.refs_1_, bf16[32,4096]{1,0:T(8,128)(2,1)S(1)} %collective-permute-done.12.refs_2_, ...), custom_call_target="tpu_custom_call" | custom-call | flops 2684354560 | bytes 8388608 | tf_op jit(solution)/shard_map/block_gather/pallas_call | solution.py:511
  100.7 1.6 %collective-permute-start.24 = (bf16[32,4096]{1,0:T(8,128)(2,1)S(1)}, bf16[32,4096]{1,0:T(8,128)(2,1)S(1)}, u32[]{:S(2)}, u32[]{:S(2)}) collective-permute-start(bf16[32,4096]{1,0:T(8,128)(2,1)S(1)} %collective-permute-done.14.refs_0_), channel_id=1, source_target_pairs={{0,1},{1,0},{2,3},{3,2},{4,5},{5,4},{6,7},{7,6},{8,9},{9,8},{10,11... | collective-permute-start | bytes 786440 | tf_op jit(solution)/shard_map/block_gather/ppermute | solution.py:530
  104.2 4.1 %block_gather.5 = bf16[1024,128]{1,0:T(8,128)(2,1)S(1)} custom-call(bf16[1024,4096]{1,0:T(8,128)(2,1)S(1)} %block_gather.3.u_ref, bf16[32,4096]{1,0:T(8,128)(2,1)S(1)} %collective-permute-done.14.refs_0_, bf16[32,4096]{1,0:T(8,128)(2,1)S(1)} %collective-permute-done.24.refs_1_, bf16[32,4096]{1,0:T(8,128)(2,1)S(1)} %collective-permute-done.15.refs_2_, ...), custom_call_target="tpu_custom_call" | custom-call | flops 1610612736 | bytes 8388608 | tf_op jit(solution)/shard_map/block_gather/pallas_call | solution.py:511
  108.3 18.8 %all_to_all.21 = bf16[128,8,128]{2,1,0:T(8,128)(2,1)S(1)} all-to-all(bf16[128,8,128]{2,1,0:T(8,128)(2,1)S(1)} %bitcast.12), channel_id=1, replica_groups=mesh['grid'=8,'band'=16] {'grid','band'}, dimensions={0} | all-to-all | bytes 524288 | tf_op jit(solution)/shard_map/ladder/all_to_all | solution.py:683
  (44 shorter events, 12.6 us)
Async XLA Ops:
  0.0 4.1 %copy-start = (s32[1,2]{1,0:T(1,128)S(1)}, s32[1,2]{1,0:T(1,128)}, u32[]{:S(2)}) copy-start(s32[1,2]{1,0:T(1,128)} %pairs_ref.11) | copy-start | bytes 28
  2.6 3.6 %collective-permute-start = (bf16[13,8,4224]{2,1,0:T(8,128)(2,1)S(1)}, bf16[13,8,4224]{2,1,0:T(8,128)(2,1)S(1)}, u32[]{:S(2)}, u32[]{:S(2)}) collective-permute-start(bf16[13,8,4224]{2,1,0:T(8,128)(2,1)S(1)} %block_scatter.6.sent_a), channel_id=1, source_target_pairs={{0,1},{1,0},{2,3},{3,2},{4,5},{5,4},{6,7},{7,6},{8,9},{9,8},{10,11... | collective-permute-start | bytes 2635784 | tf_op jit(solution)/shard_map/block_scatter/ppermute | solution.py:530
  7.9 6.1 %collective-permute-start.1 = (bf16[21,8,4096]{2,1,0:T(8,128)(2,1)S(1)}, bf16[21,8,4096]{2,1,0:T(8,128)(2,1)S(1)}, u32[]{:S(2)}, u32[]{:S(2)}) collective-permute-start(bf16[21,8,4096]{2,1,0:T(8,128)(2,1)S(1)} %get-tuple-element.43), channel_id=1, source_target_pairs={{0,1},{1,0},{2,3},{3,2},{4,5},{5,4},{6,7},{7,6},{8,9},{9,8},{10,11... | collective-permute-start | bytes 4128776 | tf_op jit(solution)/shard_map/block_scatter/ppermute | solution.py:530
  8.4 11.0 %collective-permute-start.2 = (bf16[5,8,4224]{2,1,0:T(8,128)(2,1)S(1)}, bf16[5,8,4224]{2,1,0:T(8,128)(2,1)S(1)}, u32[]{:S(2)}, u32[]{:S(2)}) collective-permute-start(bf16[5,8,4224]{2,1,0:T(8,128)(2,1)S(1)} %get-tuple-element.44), channel_id=1, source_target_pairs={{0,2},{1,3},{2,0},{3,1},{4,6},{5,7},{6,4},{7,5},{8,10},{9,11},{10,... | collective-permute-start | bytes 1013768 | tf_op jit(solution)/shard_map/block_scatter/ppermute | solution.py:530
  11.2 11.0 %collective-permute-start.3 = (bf16[5,8,4224]{2,1,0:T(8,128)(2,1)S(1)}, bf16[5,8,4224]{2,1,0:T(8,128)(2,1)S(1)}, u32[]{:S(2)}, u32[]{:S(2)}) collective-permute-start(bf16[5,8,4224]{2,1,0:T(8,128)(2,1)S(1)} %get-tuple-element.45), channel_id=1, source_target_pairs={{0,4},{1,5},{2,6},{3,7},{4,8},{5,9},{6,10},{7,11},{8,12},{9,13},{1... | collective-permute-start | bytes 1013768 | tf_op jit(solution)/shard_map/block_scatter/ppermute | solution.py:530
  12.5 9.7 %collective-permute-start.4 = (bf16[5,8,4224]{2,1,0:T(8,128)(2,1)S(1)}, bf16[5,8,4224]{2,1,0:T(8,128)(2,1)S(1)}, u32[]{:S(2)}, u32[]{:S(2)}) collective-permute-start(bf16[5,8,4224]{2,1,0:T(8,128)(2,1)S(1)} %get-tuple-element.46), channel_id=1, source_target_pairs={{0,12},{1,13},{2,14},{3,15},{4,0},{5,1},{6,2},{7,3},{8,4},{9,5},{1... | collective-permute-start | bytes 1013768 | tf_op jit(solution)/shard_map/block_scatter/ppermute | solution.py:530
  14.9 12.0 %collective-permute-start.5 = (bf16[5,8,4096]{2,1,0:T(8,128)(2,1)S(1)}, bf16[5,8,4096]{2,1,0:T(8,128)(2,1)S(1)}, u32[]{:S(2)}, u32[]{:S(2)}) collective-permute-start(bf16[5,8,4096]{2,1,0:T(8,128)(2,1)S(1)} %get-tuple-element.49), channel_id=1, source_target_pairs={{0,2},{1,3},{2,0},{3,1},{4,6},{5,7},{6,4},{7,5},{8,10},{9,11},{10,... | collective-permute-start | bytes 983048 | tf_op jit(solution)/shard_map/block_scatter/ppermute | solution.py:530
  15.2 13.5 %collective-permute-start.6 = (bf16[5,8,4096]{2,1,0:T(8,128)(2,1)S(1)}, bf16[5,8,4096]{2,1,0:T(8,128)(2,1)S(1)}, u32[]{:S(2)}, u32[]{:S(2)}) collective-permute-start(bf16[5,8,4096]{2,1,0:T(8,128)(2,1)S(1)} %get-tuple-element.47), channel_id=1, source_target_pairs={{0,4},{1,5},{2,6},{3,7},{4,8},{5,9},{6,10},{7,11},{8,12},{9,13},{1... | collective-permute-start | bytes 983048 | tf_op jit(solution)/shard_map/block_scatter/ppermute | solution.py:530
  19.4 9.4 %collective-permute-start.7 = (bf16[5,8,4096]{2,1,0:T(8,128)(2,1)S(1)}, bf16[5,8,4096]{2,1,0:T(8,128)(2,1)S(1)}, u32[]{:S(2)}, u32[]{:S(2)}) collective-permute-start(bf16[5,8,4096]{2,1,0:T(8,128)(2,1)S(1)} %get-tuple-element.48), channel_id=1, source_target_pairs={{0,12},{1,13},{2,14},{3,15},{4,0},{5,1},{6,2},{7,3},{8,4},{9,5},{1... | collective-permute-start | bytes 983048 | tf_op jit(solution)/shard_map/block_scatter/ppermute | solution.py:530
  23.1 13.9 %collective-permute-start.8 = (bf16[5,8,4224]{2,1,0:T(8,128)(2,1)S(1)}, bf16[5,8,4224]{2,1,0:T(8,128)(2,1)S(1)}, u32[]{:S(2)}, u32[]{:S(2)}) collective-permute-start(bf16[5,8,4224]{2,1,0:T(8,128)(2,1)S(1)} %get-tuple-element.53), channel_id=1, source_target_pairs={{0,8},{1,9},{2,10},{3,11},{4,12},{5,13},{6,14},{7,15},{8,0},{9,1},... | collective-permute-start | bytes 1013768 | tf_op jit(solution)/shard_map/block_scatter/ppermute | solution.py:530
  25.0 12.1 %collective-permute-start.9 = (bf16[5,8,4224]{2,1,0:T(8,128)(2,1)S(1)}, bf16[5,8,4224]{2,1,0:T(8,128)(2,1)S(1)}, u32[]{:S(2)}, u32[]{:S(2)}) collective-permute-start(bf16[5,8,4224]{2,1,0:T(8,128)(2,1)S(1)} %get-tuple-element.54), channel_id=1, source_target_pairs={{0,2},{1,3},{2,0},{3,1},{4,6},{5,7},{6,4},{7,5},{8,10},{9,11},{10,... | collective-permute-start | bytes 1013768 | tf_op jit(solution)/shard_map/block_scatter/ppermute | solution.py:530
  41.1 14.5 %all-to-all-start = ((bf16[8,192,256]{2,1,0:T(8,128)(2,1)}), bf16[8,192,256]{2,1,0:T(8,128)(2,1)S(1)}, u32[]{:S(2)}, u32[]{:S(2)}) async-start(bf16[8,192,256]{2,1,0:T(8,128)(2,1)} %get-tuple-element.62), calls=%async_computation | async-start | bytes 1572864 | tf_op jit(solution)/shard_map/transform/all_to_all | solution.py:623
  59.1 12.6 %all-to-all-start.1 = ((bf16[8,64,256]{2,1,0:T(8,128)(2,1)}), bf16[8,64,256]{2,1,0:T(8,128)(2,1)S(1)}, u32[]{:S(2)}, u32[]{:S(2)}) async-start(bf16[8,64,256]{2,1,0:T(8,128)(2,1)} %bitcast), calls=%async_computation.1 | async-start | bytes 524288 | tf_op jit(solution)/shard_map/transform/all_to_all | solution.py:645
  65.5 4.6 %collective-permute-start.10 = (bf16[1,8,4096]{2,1,0:T(8,128)(2,1)S(1)}, bf16[1,8,4096]{2,1,0:T(8,128)(2,1)S(1)}, u32[]{:S(2)}, u32[]{:S(2)}) collective-permute-start(bf16[1,8,4096]{2,1,0:T(8,128)(2,1)S(1)} %get-tuple-element.60), channel_id=1, source_target_pairs={{0,8},{1,9},{2,10},{3,11},{4,12},{5,13},{6,14},{7,15},{8,0},{9,1},... | collective-permute-start | bytes 196616 | tf_op jit(solution)/shard_map/transform/ppermute | solution.py:530
  65.6 5.6 %collective-permute-start.11 = (bf16[1,8,4096]{2,1,0:T(8,128)(2,1)S(1)}, bf16[1,8,4096]{2,1,0:T(8,128)(2,1)S(1)}, u32[]{:S(2)}, u32[]{:S(2)}) collective-permute-start(bf16[1,8,4096]{2,1,0:T(8,128)(2,1)S(1)} %get-tuple-element.61), channel_id=1, source_target_pairs={{0,2},{1,3},{2,0},{3,1},{4,6},{5,7},{6,4},{7,5},{8,10},{9,11},{10,... | collective-permute-start | bytes 196616 | tf_op jit(solution)/shard_map/transform/ppermute | solution.py:530
  74.8 12.8 %collective-permute-start.12 = (bf16[32,4096]{1,0:T(8,128)(2,1)S(1)}, bf16[32,4096]{1,0:T(8,128)(2,1)S(1)}, u32[]{:S(2)}, u32[]{:S(2)}) collective-permute-start(bf16[32,4096]{1,0:T(8,128)(2,1)S(1)} %bitcast.5), channel_id=1, source_target_pairs={{0,8},{1,9},{2,10},{3,11},{4,12},{5,13},{6,14},{7,15},{8,0},{9,1},... | collective-permute-start | bytes 786440 | tf_op jit(solution)/shard_map/block_gather/ppermute | solution.py:530
  76.3 11.4 %collective-permute-start.13 = (bf16[32,4096]{1,0:T(8,128)(2,1)S(1)}, bf16[32,4096]{1,0:T(8,128)(2,1)S(1)}, u32[]{:S(2)}, u32[]{:S(2)}) collective-permute-start(bf16[32,4096]{1,0:T(8,128)(2,1)S(1)} %bitcast.6), channel_id=1, source_target_pairs={{0,2},{1,3},{2,0},{3,1},{4,6},{5,7},{6,4},{7,5},{8,10},{9,11},{10,... | collective-permute-start | bytes 786440 | tf_op jit(solution)/shard_map/block_gather/ppermute | solution.py:530
  77.8 10.7 %collective-permute-start.19 = (bf16[32,4096]{1,0:T(8,128)(2,1)S(1)}, bf16[32,4096]{1,0:T(8,128)(2,1)S(1)}, u32[]{:S(2)}, u32[]{:S(2)}) collective-permute-start(bf16[32,4096]{1,0:T(8,128)(2,1)S(1)} %bitcast.7), channel_id=1, source_target_pairs={{0,4},{1,5},{2,6},{3,7},{4,8},{5,9},{6,10},{7,11},{8,12},{9,13},{1... | collective-permute-start | bytes 786440 | tf_op jit(solution)/shard_map/block_gather/ppermute | solution.py:530
  78.9 11.9 %collective-permute-start.21 = (bf16[32,4096]{1,0:T(8,128)(2,1)S(1)}, bf16[32,4096]{1,0:T(8,128)(2,1)S(1)}, u32[]{:S(2)}, u32[]{:S(2)}) collective-permute-start(bf16[32,4096]{1,0:T(8,128)(2,1)S(1)} %bitcast.8), channel_id=1, source_target_pairs={{0,12},{1,13},{2,14},{3,15},{4,0},{5,1},{6,2},{7,3},{8,4},{9,5},{1... | collective-permute-start | bytes 786440 | tf_op jit(solution)/shard_map/block_gather/ppermute | solution.py:530
  80.5 10.3 %collective-permute-start.17 = (bf16[32,4096]{1,0:T(8,128)(2,1)S(1)}, bf16[32,4096]{1,0:T(8,128)(2,1)S(1)}, u32[]{:S(2)}, u32[]{:S(2)}) collective-permute-start(bf16[32,4096]{1,0:T(8,128)(2,1)S(1)} %bitcast.9), channel_id=1, source_target_pairs={{0,1},{1,0},{2,3},{3,2},{4,5},{5,4},{6,7},{7,6},{8,9},{9,8},{10,11... | collective-permute-start | bytes 786440 | tf_op jit(solution)/shard_map/block_gather/ppermute | solution.py:530
  87.7 4.7 %collective-permute-start.18 = (bf16[32,4096]{1,0:T(8,128)(2,1)S(1)}, bf16[32,4096]{1,0:T(8,128)(2,1)S(1)}, u32[]{:S(2)}, u32[]{:S(2)}) collective-permute-start(bf16[32,4096]{1,0:T(8,128)(2,1)S(1)} %collective-permute-done.12.refs_2_), channel_id=1, source_target_pairs={{0,1},{1,0},{2,3},{3,2},{4,5},{5,4},{6,7},{7,6},{8,9},{9,8},{10,11... | collective-permute-start | bytes 786440 | tf_op jit(solution)/shard_map/block_gather/ppermute | solution.py:530
  88.0 5.0 %collective-permute-start.23 = (bf16[32,4096]{1,0:T(8,128)(2,1)S(1)}, bf16[32,4096]{1,0:T(8,128)(2,1)S(1)}, u32[]{:S(2)}, u32[]{:S(2)}) collective-permute-start(bf16[32,4096]{1,0:T(8,128)(2,1)S(1)} %collective-permute-done.13.refs_8_), channel_id=1, source_target_pairs={{0,1},{1,0},{2,3},{3,2},{4,5},{5,4},{6,7},{7,6},{8,9},{9,8},{10,11... | collective-permute-start | bytes 786440 | tf_op jit(solution)/shard_map/block_gather/ppermute | solution.py:530
  88.5 6.5 %collective-permute-start.20 = (bf16[32,4096]{1,0:T(8,128)(2,1)S(1)}, bf16[32,4096]{1,0:T(8,128)(2,1)S(1)}, u32[]{:S(2)}, u32[]{:S(2)}) collective-permute-start(bf16[32,4096]{1,0:T(8,128)(2,1)S(1)} %collective-permute-done.19.refs_4_), channel_id=1, source_target_pairs={{0,1},{1,0},{2,3},{3,2},{4,5},{5,4},{6,7},{7,6},{8,9},{9,8},{10,11... | collective-permute-start | bytes 786440 | tf_op jit(solution)/shard_map/block_gather/ppermute | solution.py:530
  90.8 4.3 %collective-permute-start.22 = (bf16[32,4096]{1,0:T(8,128)(2,1)S(1)}, bf16[32,4096]{1,0:T(8,128)(2,1)S(1)}, u32[]{:S(2)}, u32[]{:S(2)}) collective-permute-start(bf16[32,4096]{1,0:T(8,128)(2,1)S(1)} %collective-permute-done.21.refs_6_), channel_id=1, source_target_pairs={{0,1},{1,0},{2,3},{3,2},{4,5},{5,4},{6,7},{7,6},{8,9},{9,8},{10,11... | collective-permute-start | bytes 786440 | tf_op jit(solution)/shard_map/block_gather/ppermute | solution.py:530
  90.8 9.8 %collective-permute-start.14 = (bf16[32,4096]{1,0:T(8,128)(2,1)S(1)}, bf16[32,4096]{1,0:T(8,128)(2,1)S(1)}, u32[]{:S(2)}, u32[]{:S(2)}) collective-permute-start(bf16[32,4096]{1,0:T(8,128)(2,1)S(1)} %collective-permute-done.12.refs_2_), channel_id=1, source_target_pairs={{0,2},{1,3},{2,0},{3,1},{4,6},{5,7},{6,4},{7,5},{8,10},{9,11},{10,... | collective-permute-start | bytes 786440 | tf_op jit(solution)/shard_map/block_gather/ppermute | solution.py:530
  92.3 8.3 %collective-permute-start.15 = (bf16[32,4096]{1,0:T(8,128)(2,1)S(1)}, bf16[32,4096]{1,0:T(8,128)(2,1)S(1)}, u32[]{:S(2)}, u32[]{:S(2)}) collective-permute-start(bf16[32,4096]{1,0:T(8,128)(2,1)S(1)} %collective-permute-done.13.refs_8_), channel_id=1, source_target_pairs={{0,4},{1,5},{2,6},{3,7},{4,8},{5,9},{6,10},{7,11},{8,12},{9,13},{1... | collective-permute-start | bytes 786440 | tf_op jit(solution)/shard_map/block_gather/ppermute | solution.py:530
  92.9 7.8 %collective-permute-start.16 = (bf16[32,4096]{1,0:T(8,128)(2,1)S(1)}, bf16[32,4096]{1,0:T(8,128)(2,1)S(1)}, u32[]{:S(2)}, u32[]{:S(2)}) collective-permute-start(bf16[32,4096]{1,0:T(8,128)(2,1)S(1)} %collective-permute-done.13.refs_8_), channel_id=1, source_target_pairs={{0,12},{1,13},{2,14},{3,15},{4,0},{5,1},{6,2},{7,3},{8,4},{9,5},{1... | collective-permute-start | bytes 786440 | tf_op jit(solution)/shard_map/block_gather/ppermute | solution.py:530
  100.7 2.7 %collective-permute-start.24 = (bf16[32,4096]{1,0:T(8,128)(2,1)S(1)}, bf16[32,4096]{1,0:T(8,128)(2,1)S(1)}, u32[]{:S(2)}, u32[]{:S(2)}) collective-permute-start(bf16[32,4096]{1,0:T(8,128)(2,1)S(1)} %collective-permute-done.14.refs_0_), channel_id=1, source_target_pairs={{0,1},{1,0},{2,3},{3,2},{4,5},{5,4},{6,7},{7,6},{8,9},{9,8},{10,11... | collective-permute-start | bytes 786440 | tf_op jit(solution)/shard_map/block_gather/ppermute | solution.py:530
  102.3 1.5 %collective-permute-start.25 = (bf16[32,4096]{1,0:T(8,128)(2,1)S(1)}, bf16[32,4096]{1,0:T(8,128)(2,1)S(1)}, u32[]{:S(2)}, u32[]{:S(2)}) collective-permute-start(bf16[32,4096]{1,0:T(8,128)(2,1)S(1)} %collective-permute-done.15.refs_2_), channel_id=1, source_target_pairs={{0,1},{1,0},{2,3},{3,2},{4,5},{5,4},{6,7},{7,6},{8,9},{9,8},{10,11... | collective-permute-start | bytes 786440 | tf_op jit(solution)/shard_map/block_gather/ppermute | solution.py:530
  102.3 1.9 %collective-permute-start.26 = (bf16[32,4096]{1,0:T(8,128)(2,1)S(1)}, bf16[32,4096]{1,0:T(8,128)(2,1)S(1)}, u32[]{:S(2)}, u32[]{:S(2)}) collective-permute-start(bf16[32,4096]{1,0:T(8,128)(2,1)S(1)} %collective-permute-done.16.refs_4_), channel_id=1, source_target_pairs={{0,1},{1,0},{2,3},{3,2},{4,5},{5,4},{6,7},{7,6},{8,9},{9,8},{10,11... | collective-permute-start | bytes 786440 | tf_op jit(solution)/shard_map/block_gather/ppermute | solution.py:530

commit v8 on v7

--- a/solution.py
+++ b/solution.py
@@ -662,9 +662,9 @@
         )
         fields = call(copy_body, [pl.ANY], [shape], [pl.ANY], sems(1), (far_memory(fields),))
         part = {(0, 0): potential}
+        part[0, 1] = band_shift(potential, 0, 1, 0)
         for k in (2, 1, 3):
             part[k, 0] = band_shift(potential, k, 0, 0)
-        part[0, 1] = band_shift(potential, 0, 1, 0)
 
         def contract(names, *extra):
             pieces = [w for name in names for w in (part[name], band_shift(part[name], 0, 0, 1))]

time: 129 us -> 128 us (level)
  starting transfers between devices: 47.6 us -> 45.6 us
  Pallas kernels: 31.7 us -> 33.1 us
    ppermute x27, starting transfers between devices: 36.2 us -> 34.1 us  [band_shift(): return lax.ppermute(value, 'band', pairs)]
    pallas_call x11, Pallas kernels: 22.1 us -> 23.4 us  [call(): pl.pallas_call(body, out_shape=shapes if many else shapes[0], in_specs=[p...]
  transfers between devices with their start and end apart: 29 -> 29, of which waited for: 12 -> 12; matrix products, arithmetic and copies ran while one was open for 0% -> 0% of each run, Pallas kernels for 10% -> 12%
where the time goes in v8:
time: 128 us
  starting transfers between devices  45.6 us (36%)
  Pallas kernels  33.1 us (26%)
  waiting for transfers between devices  28.8 us (22%)
  blocking collectives  18.8 us (15%)
    ppermute x27, starting transfers between devices, band_shift(): return lax.ppermute(value, 'band', pairs)  34.1 us
    pallas_call x11, Pallas kernels, call(): pl.pallas_call(body, out_shape=shapes if many else shapes[0], in_specs=[p...  23.4 us
    ppermute x27, waiting for transfers between devices, band_shift(): return lax.ppermute(value, 'band', pairs)  19.4 us
    all_to_all x1, blocking collectives, per_device(): lax.all_to_all(terms.reshape(GRID * BAND, XL, 128), ('grid', 'band'), 0,...  18.8 us
    all_to_all x2, starting transfers between devices, per_device(): freq = lax.all_to_all(freq, 'grid', 0, 0, tiled=True)  11.5 us
    pallas_call x2, Pallas kernels, slab_call(): pl.pallas_call(functools.partial(slab_body, last, names), out_shape=jax.S...  9.65 us
    all_to_all x2, waiting for transfers between devices, per_device(): freq = lax.all_to_all(freq, 'grid', 0, 0, tiled=True)  9.44 us
  transfers between devices with their start and end apart: 29, of which 12 were waited for; matrix products, arithmetic and copies ran while one was open for 0% of the time, Pallas kernels for 12%

profile of v8, /device:TPU:1, one launch (start us, length us, event | category | flops | bytes accessed | tf_op | source)
XLA Modules:
  0.0 127.9 jit_solution(13234187879070351944)
XLA Ops:
  0.7 1.9 %block_scatter.6.sent_a = bf16[13,8,4224]{2,1,0:T(8,128)(2,1)S(1)} custom-call(s32[1]{0:T(128)S(6)} %copy.14.ablock_ref, s32[1,2]{1,0:T(1,128)} %pairs_ref.11, s32[1,512]{1,0:T(1,128)} %kept_hbm.1, bf16[128,8,4096]{2,1,0:T(8,128)(2,1)} %fields.13, bf16[16,8,4096]{2,1,0:T(8,128)(2,1)} %occupied.13), custom_call_target="tpu_custom_call" | custom-call | flops 100000000 | bytes 1048576 | tf_op jit(solution)/shard_map/block_scatter/pallas_call | solution.py:453
  2.6 1.5 %collective-permute-start = (bf16[13,8,4224]{2,1,0:T(8,128)(2,1)S(1)}, bf16[13,8,4224]{2,1,0:T(8,128)(2,1)S(1)}, u32[]{:S(2)}, u32[]{:S(2)}) collective-permute-start(bf16[13,8,4224]{2,1,0:T(8,128)(2,1)S(1)} %block_scatter.6.sent_a), channel_id=1, source_target_pairs={{0,1},{1,0},{2,3},{3,2},{4,5},{5,4},{6,7},{7,6},{8,9},{9,8},{10,11... | collective-permute-start | bytes 2635784 | tf_op jit(solution)/shard_map/block_scatter/ppermute | solution.py:530
  4.1 2.1 %block_scatter.8 = (bf16[21,8,4096]{2,1,0:T(8,128)(2,1)S(1)}, bf16[128,256]{1,0:T(8,128)(2,1)S(1)}) custom-call(s32[1]{0:T(128)S(6)} %copy.14.ablock_ref, s32[1,2]{1,0:T(1,128)S(1)} %copy-done, bf16[128,8,4096]{2,1,0:T(8,128)(2,1)} %fields.13, bf16[16,8,4096]{2,1,0:T(8,128)(2,1)} %occupied.13, bf16[1,128,256]{2,1,0:T(8,128)(2,1)} %amp_hbm.1), custom_call_target="tpu_custom_call" | custom-call | flops 5000000000 | bytes 1048576 | tf_op jit(solution)/shard_map/block_scatter/pallas_call | solution.py:453
  6.2 1.7 %block_scatter.7 = (bf16[5,8,4224]{2,1,0:T(8,128)(2,1)S(1)}, bf16[5,8,4224]{2,1,0:T(8,128)(2,1)S(1)}, bf16[5,8,4224]{2,1,0:T(8,128)(2,1)S(1)}) custom-call(s32[1]{0:T(128)S(6)} %copy.14.ablock_ref, s32[1,2]{1,0:T(1,128)S(1)} %copy-done, bf16[128,8,4096]{2,1,0:T(8,128)(2,1)} %fields.13, bf16[16,8,4096]{2,1,0:T(8,128)(2,1)} %occupied.13, ...), custom_call_target="tpu_custom_call" | custom-call | flops 100000000 | bytes 1048576 | tf_op jit(solution)/shard_map/block_scatter/pallas_call | solution.py:453
  8.4 2.8 %collective-permute-start.2 = (bf16[5,8,4224]{2,1,0:T(8,128)(2,1)S(1)}, bf16[5,8,4224]{2,1,0:T(8,128)(2,1)S(1)}, u32[]{:S(2)}, u32[]{:S(2)}) collective-permute-start(bf16[5,8,4224]{2,1,0:T(8,128)(2,1)S(1)} %get-tuple-element.44), channel_id=1, source_target_pairs={{0,2},{1,3},{2,0},{3,1},{4,6},{5,7},{6,4},{7,5},{8,10},{9,11},{10,... | collective-permute-start | bytes 1013768 | tf_op jit(solution)/shard_map/block_scatter/ppermute | solution.py:530
  12.5 1.4 %collective-permute-start.4 = (bf16[5,8,4224]{2,1,0:T(8,128)(2,1)S(1)}, bf16[5,8,4224]{2,1,0:T(8,128)(2,1)S(1)}, u32[]{:S(2)}, u32[]{:S(2)}) collective-permute-start(bf16[5,8,4224]{2,1,0:T(8,128)(2,1)S(1)} %get-tuple-element.46), channel_id=1, source_target_pairs={{0,12},{1,13},{2,14},{3,15},{4,0},{5,1},{6,2},{7,3},{8,4},{9,5},{1... | collective-permute-start | bytes 1013768 | tf_op jit(solution)/shard_map/block_scatter/ppermute | solution.py:530
  14.0 1.6 %block_scatter.9 = (bf16[5,8,4096]{2,1,0:T(8,128)(2,1)S(1)}, bf16[5,8,4096]{2,1,0:T(8,128)(2,1)S(1)}, bf16[5,8,4096]{2,1,0:T(8,128)(2,1)S(1)}) custom-call(s32[1]{0:T(128)S(6)} %copy.14.ablock_ref, s32[1,2]{1,0:T(1,128)S(1)} %copy-done, bf16[128,8,4096]{2,1,0:T(8,128)(2,1)} %fields.13, bf16[16,8,4096]{2,1,0:T(8,128)(2,1)} %occupied.13, ...), custom_call_target="tpu_custom_call" | custom-call | flops 100000000 | bytes 1048576 | tf_op jit(solution)/shard_map/block_scatter/pallas_call | solution.py:453
  17.0 2.4 %collective-permute-done.2.crossed.crossed_a = bf16[5,8,4224]{2,1,0:T(8,128)(2,1)S(1)} collective-permute-done((bf16[5,8,4224]{2,1,0:T(8,128)(2,1)S(1)}, bf16[5,8,4224]{2,1,0:T(8,128)(2,1)S(1)}, u32[]{:S(2)}, u32[]{:S(2)}) %collective-permute-start.2) | collective-permute-done | bytes 337952 | tf_op jit(solution)/shard_map/block_scatter/ppermute | solution.py:530
  19.4 2.8 %collective-permute-start.7 = (bf16[5,8,4096]{2,1,0:T(8,128)(2,1)S(1)}, bf16[5,8,4096]{2,1,0:T(8,128)(2,1)S(1)}, u32[]{:S(2)}, u32[]{:S(2)}) collective-permute-start(bf16[5,8,4096]{2,1,0:T(8,128)(2,1)S(1)} %get-tuple-element.48), channel_id=1, source_target_pairs={{0,12},{1,13},{2,14},{3,15},{4,0},{5,1},{6,2},{7,3},{8,4},{9,5},{1... | collective-permute-start | bytes 983048 | tf_op jit(solution)/shard_map/block_scatter/ppermute | solution.py:530
  22.2 1.6 %block_scatter.10 = (bf16[5,8,4224]{2,1,0:T(8,128)(2,1)S(1)}, bf16[5,8,4224]{2,1,0:T(8,128)(2,1)S(1)}) custom-call(s32[1]{0:T(128)S(6)} %copy.14.ablock_ref, s32[1,2]{1,0:T(1,128)S(1)} %copy-done, bf16[128,8,4096]{2,1,0:T(8,128)(2,1)} %fields.13, bf16[16,8,4096]{2,1,0:T(8,128)(2,1)} %occupied.13, bf16[13,8,4224]{2,1,0:T(8,128)(2,1)S(1)} %block_scatter.6.sent_a, ...), custom_call_target="tpu_custom_call" | custom-call | flops 10000000000 | bytes 1048576 | tf_op jit(solution)/shard_map/block_scatter/pallas_call | solution.py:453
  23.8 1.9 %collective-permute-start.8 = (bf16[5,8,4224]{2,1,0:T(8,128)(2,1)S(1)}, bf16[5,8,4224]{2,1,0:T(8,128)(2,1)S(1)}, u32[]{:S(2)}, u32[]{:S(2)}) collective-permute-start(bf16[5,8,4224]{2,1,0:T(8,128)(2,1)S(1)} %get-tuple-element.53), channel_id=1, source_target_pairs={{0,8},{1,9},{2,10},{3,11},{4,12},{5,13},{6,14},{7,15},{8,0},{9,1},... | collective-permute-start | bytes 1013768 | tf_op jit(solution)/shard_map/block_scatter/ppermute | solution.py:530
  26.3 2.4 %collective-permute-done.6.second.below_b = bf16[5,8,4096]{2,1,0:T(8,128)(2,1)S(1)} collective-permute-done((bf16[5,8,4096]{2,1,0:T(8,128)(2,1)S(1)}, bf16[5,8,4096]{2,1,0:T(8,128)(2,1)S(1)}, u32[]{:S(2)}, u32[]{:S(2)}) %collective-permute-start.6) | collective-permute-done | bytes 327712 | tf_op jit(solution)/shard_map/block_scatter/ppermute | solution.py:530
  28.8 8.3 %collective-permute-done.8.far = bf16[5,8,4224]{2,1,0:T(8,128)(2,1)S(1)} collective-permute-done((bf16[5,8,4224]{2,1,0:T(8,128)(2,1)S(1)}, bf16[5,8,4224]{2,1,0:T(8,128)(2,1)S(1)}, u32[]{:S(2)}, u32[]{:S(2)}) %collective-permute-start.8) | collective-permute-done | bytes 337952 | tf_op jit(solution)/shard_map/block_scatter/ppermute | solution.py:530
  37.1 4.0 %transform.4 = (bf16[8,192,256]{2,1,0:T(8,128)(2,1)}, bf16[16,8,128]{2,1,0:T(8,128)(2,1)S(1)}, bf16[1,8,4096]{2,1,0:T(8,128)(2,1)S(1)}, bf16[1,8,4096]{2,1,0:T(8,128)(2,1)S(1)}, bf16[1,8,4096]{2,1,0:T(8,128)(2,1)S(1)}) custom-call(s32[1]{0:T(128)S(6)} %copy.14.ablock_ref, s32[1,2]{1,0:T(1,128)S(1)} %copy-done, bf16[128,8,4096]{2,1,0:T(8,128)(2,1)} %fields.13, ...), custom_call_target="tpu_custom_call" | custom-call | flops 20000000000 | bytes 1048576 | tf_op jit(solution)/shard_map/transform/pallas_call | solution.py:453
  41.1 5.1 %all-to-all-start = ((bf16[8,192,256]{2,1,0:T(8,128)(2,1)}), bf16[8,192,256]{2,1,0:T(8,128)(2,1)S(1)}, u32[]{:S(2)}, u32[]{:S(2)}) async-start(bf16[8,192,256]{2,1,0:T(8,128)(2,1)} %get-tuple-element.62), calls=%async_computation | async-start | bytes 1572864 | tf_op jit(solution)/shard_map/transform/all_to_all | solution.py:623
  46.6 8.9 %all-to-all-done.y_hbm.refs_7_ = bf16[8,192,256]{2,1,0:T(8,128)(2,1)S(1)} async-done(((bf16[8,192,256]{2,1,0:T(8,128)(2,1)}), bf16[8,192,256]{2,1,0:T(8,128)(2,1)S(1)}, u32[]{:S(2)}, u32[]{:S(2)}) %all-to-all-start) | async-done | bytes 786464 | tf_op jit(solution)/shard_map/transform/all_to_all | solution.py:623
  55.6 3.6 %transform.6 = bf16[512,256]{1,0:T(8,128)(2,1)} custom-call(bf16[8,192,256]{2,1,0:T(8,128)(2,1)S(1)} %all-to-all-done.y_hbm.refs_7_, f32[512,128]{1,0:T(8,128)S(1)} %transform.5.weight_ref, bf16[256,256]{1,0:T(8,128)(2,1)} %constant.22.clone.turn_hbm, bf16[512,1024]{1,0:T(8,128)(2,1)} %constant.20.clone.kx_hbm, bf16[512,1024]{1,0:T(8,128)(2,1)} %constant.21.clone.kxt_hbm), custom_call_target="tpu_custom_call" | custom-call | flops 10000000000 | bytes 1048576 | tf_op jit(solution)/shard_map/transform/pallas_call | solution.py:453
  59.1 6.4 %all-to-all-start.1 = ((bf16[8,64,256]{2,1,0:T(8,128)(2,1)}), bf16[8,64,256]{2,1,0:T(8,128)(2,1)S(1)}, u32[]{:S(2)}, u32[]{:S(2)}) async-start(bf16[8,64,256]{2,1,0:T(8,128)(2,1)} %bitcast), calls=%async_computation.1 | async-start | bytes 524288 | tf_op jit(solution)/shard_map/transform/all_to_all | solution.py:645
  66.9 3.3 %collective-permute-done.10.far = bf16[1,8,4096]{2,1,0:T(8,128)(2,1)S(1)} collective-permute-done((bf16[1,8,4096]{2,1,0:T(8,128)(2,1)S(1)}, bf16[1,8,4096]{2,1,0:T(8,128)(2,1)S(1)}, u32[]{:S(2)}, u32[]{:S(2)}) %collective-permute-start.10) | collective-permute-done | bytes 65568 | tf_op jit(solution)/shard_map/transform/ppermute | solution.py:530
  71.7 3.1 %transform.7 = bf16[4,8,4096]{2,1,0:T(8,128)(2,1)S(1)} custom-call(s32[1]{0:T(128)S(6)} %copy.14.ablock_ref, s32[1,2]{1,0:T(1,128)S(1)} %copy-done, bf16[128,8,4096]{2,1,0:T(8,128)(2,1)} %fields.13, bf16[16,8,4096]{2,1,0:T(8,128)(2,1)} %occupied.13, bf16[1,8,4096]{2,1,0:T(8,128)(2,1)S(1)} %get-tuple-element.59.second, ...), custom_call_target="tpu_custom_call" | custom-call | flops 100000000 | bytes 1048576 | tf_op jit(solution)/shard_map/transform/pallas_call | solution.py:453
  74.8 1.5 %collective-permute-start.12 = (bf16[32,4096]{1,0:T(8,128)(2,1)S(1)}, bf16[32,4096]{1,0:T(8,128)(2,1)S(1)}, u32[]{:S(2)}, u32[]{:S(2)}) collective-permute-start(bf16[32,4096]{1,0:T(8,128)(2,1)S(1)} %bitcast.5), channel_id=1, source_target_pairs={{0,8},{1,9},{2,10},{3,11},{4,12},{5,13},{6,14},{7,15},{8,0},{9,1},... | collective-permute-start | bytes 786440 | tf_op jit(solution)/shard_map/block_gather/ppermute | solution.py:530
  76.3 1.5 %collective-permute-start.13 = (bf16[32,4096]{1,0:T(8,128)(2,1)S(1)}, bf16[32,4096]{1,0:T(8,128)(2,1)S(1)}, u32[]{:S(2)}, u32[]{:S(2)}) collective-permute-start(bf16[32,4096]{1,0:T(8,128)(2,1)S(1)} %bitcast.6), channel_id=1, source_target_pairs={{0,2},{1,3},{2,0},{3,1},{4,6},{5,7},{6,4},{7,5},{8,10},{9,11},{10,... | collective-permute-start | bytes 786440 | tf_op jit(solution)/shard_map/block_gather/ppermute | solution.py:530
  79.0 1.5 %collective-permute-start.21 = (bf16[32,4096]{1,0:T(8,128)(2,1)S(1)}, bf16[32,4096]{1,0:T(8,128)(2,1)S(1)}, u32[]{:S(2)}, u32[]{:S(2)}) collective-permute-start(bf16[32,4096]{1,0:T(8,128)(2,1)S(1)} %bitcast.8), channel_id=1, source_target_pairs={{0,12},{1,13},{2,14},{3,15},{4,0},{5,1},{6,2},{7,3},{8,4},{9,5},{1... | collective-permute-start | bytes 786440 | tf_op jit(solution)/shard_map/block_gather/ppermute | solution.py:530
  80.5 3.7 %collective-permute-start.17 = (bf16[32,4096]{1,0:T(8,128)(2,1)S(1)}, bf16[32,4096]{1,0:T(8,128)(2,1)S(1)}, u32[]{:S(2)}, u32[]{:S(2)}) collective-permute-start(bf16[32,4096]{1,0:T(8,128)(2,1)S(1)} %bitcast.9), channel_id=1, source_target_pairs={{0,1},{1,0},{2,3},{3,2},{4,5},{5,4},{6,7},{7,6},{8,9},{9,8},{10,11... | collective-permute-start | bytes 786440 | tf_op jit(solution)/shard_map/block_gather/ppermute | solution.py:530
  84.2 3.4 %block_gather.3.u_ref = bf16[1024,4096]{1,0:T(8,128)(2,1)S(1)} custom-call(bf16[1024,4096]{1,0:T(8,128)(2,1)} %bitcast.13), custom_call_target="tpu_custom_call" | custom-call | flops 100000000 | bytes 1048576 | tf_op jit(solution)/shard_map/block_gather/pallas_call | solution.py:453
  88.6 2.2 %collective-permute-start.20 = (bf16[32,4096]{1,0:T(8,128)(2,1)S(1)}, bf16[32,4096]{1,0:T(8,128)(2,1)S(1)}, u32[]{:S(2)}, u32[]{:S(2)}) collective-permute-start(bf16[32,4096]{1,0:T(8,128)(2,1)S(1)} %collective-permute-done.19.refs_4_), channel_id=1, source_target_pairs={{0,1},{1,0},{2,3},{3,2},{4,5},{5,4},{6,7},{7,6},{8,9},{9,8},{10,11... | collective-permute-start | bytes 786440 | tf_op jit(solution)/shard_map/block_gather/ppermute | solution.py:530
  90.8 1.6 %collective-permute-start.14 = (bf16[32,4096]{1,0:T(8,128)(2,1)S(1)}, bf16[32,4096]{1,0:T(8,128)(2,1)S(1)}, u32[]{:S(2)}, u32[]{:S(2)}) collective-permute-start(bf16[32,4096]{1,0:T(8,128)(2,1)S(1)} %collective-permute-done.12.refs_2_), channel_id=1, source_target_pairs={{0,2},{1,3},{2,0},{3,1},{4,6},{5,7},{6,4},{7,5},{8,10},{9,11},{10,... | collective-permute-start | bytes 786440 | tf_op jit(solution)/shard_map/block_gather/ppermute | solution.py:530
  93.0 2.0 %collective-permute-start.16 = (bf16[32,4096]{1,0:T(8,128)(2,1)S(1)}, bf16[32,4096]{1,0:T(8,128)(2,1)S(1)}, u32[]{:S(2)}, u32[]{:S(2)}) collective-permute-start(bf16[32,4096]{1,0:T(8,128)(2,1)S(1)} %collective-permute-done.13.refs_8_), channel_id=1, source_target_pairs={{0,12},{1,13},{2,14},{3,15},{4,0},{5,1},{6,2},{7,3},{8,4},{9,5},{1... | collective-permute-start | bytes 786440 | tf_op jit(solution)/shard_map/block_gather/ppermute | solution.py:530
  95.0 5.6 %block_gather.4.refs_6_ = f32[128,128]{1,0:T(8,128)S(1)} custom-call(bf16[1024,4096]{1,0:T(8,128)(2,1)S(1)} %block_gather.3.u_ref, bf16[32,4096]{1,0:T(8,128)(2,1)S(1)} %bitcast.10, bf16[32,4096]{1,0:T(8,128)(2,1)S(1)} %collective-permute-done.17.refs_1_, bf16[32,4096]{1,0:T(8,128)(2,1)S(1)} %collective-permute-done.12.refs_2_, ...), custom_call_target="tpu_custom_call" | custom-call | flops 2684354560 | bytes 8388608 | tf_op jit(solution)/shard_map/block_gather/pallas_call | solution.py:511
  100.7 1.6 %collective-permute-start.24 = (bf16[32,4096]{1,0:T(8,128)(2,1)S(1)}, bf16[32,4096]{1,0:T(8,128)(2,1)S(1)}, u32[]{:S(2)}, u32[]{:S(2)}) collective-permute-start(bf16[32,4096]{1,0:T(8,128)(2,1)S(1)} %collective-permute-done.14.refs_0_), channel_id=1, source_target_pairs={{0,1},{1,0},{2,3},{3,2},{4,5},{5,4},{6,7},{7,6},{8,9},{9,8},{10,11... | collective-permute-start | bytes 786440 | tf_op jit(solution)/shard_map/block_gather/ppermute | solution.py:530
  104.2 4.1 %block_gather.5 = bf16[1024,128]{1,0:T(8,128)(2,1)S(1)} custom-call(bf16[1024,4096]{1,0:T(8,128)(2,1)S(1)} %block_gather.3.u_ref, bf16[32,4096]{1,0:T(8,128)(2,1)S(1)} %collective-permute-done.14.refs_0_, bf16[32,4096]{1,0:T(8,128)(2,1)S(1)} %collective-permute-done.24.refs_1_, bf16[32,4096]{1,0:T(8,128)(2,1)S(1)} %collective-permute-done.15.refs_2_, ...), custom_call_target="tpu_custom_call" | custom-call | flops 1610612736 | bytes 8388608 | tf_op jit(solution)/shard_map/block_gather/pallas_call | solution.py:511
  108.3 18.8 %all_to_all.21 = bf16[128,8,128]{2,1,0:T(8,128)(2,1)S(1)} all-to-all(bf16[128,8,128]{2,1,0:T(8,128)(2,1)S(1)} %bitcast.12), channel_id=1, replica_groups=mesh['grid'=8,'band'=16] {'grid','band'}, dimensions={0} | all-to-all | bytes 524288 | tf_op jit(solution)/shard_map/ladder/all_to_all | solution.py:683
  (44 shorter events, 12.8 us)
Async XLA Ops:
  0.0 4.1 %copy-start = (s32[1,2]{1,0:T(1,128)S(1)}, s32[1,2]{1,0:T(1,128)}, u32[]{:S(2)}) copy-start(s32[1,2]{1,0:T(1,128)} %pairs_ref.11) | copy-start | bytes 28
  2.6 3.6 %collective-permute-start = (bf16[13,8,4224]{2,1,0:T(8,128)(2,1)S(1)}, bf16[13,8,4224]{2,1,0:T(8,128)(2,1)S(1)}, u32[]{:S(2)}, u32[]{:S(2)}) collective-permute-start(bf16[13,8,4224]{2,1,0:T(8,128)(2,1)S(1)} %block_scatter.6.sent_a), channel_id=1, source_target_pairs={{0,1},{1,0},{2,3},{3,2},{4,5},{5,4},{6,7},{7,6},{8,9},{9,8},{10,11... | collective-permute-start | bytes 2635784 | tf_op jit(solution)/shard_map/block_scatter/ppermute | solution.py:530
  7.9 6.1 %collective-permute-start.1 = (bf16[21,8,4096]{2,1,0:T(8,128)(2,1)S(1)}, bf16[21,8,4096]{2,1,0:T(8,128)(2,1)S(1)}, u32[]{:S(2)}, u32[]{:S(2)}) collective-permute-start(bf16[21,8,4096]{2,1,0:T(8,128)(2,1)S(1)} %get-tuple-element.43), channel_id=1, source_target_pairs={{0,1},{1,0},{2,3},{3,2},{4,5},{5,4},{6,7},{7,6},{8,9},{9,8},{10,11... | collective-permute-start | bytes 4128776 | tf_op jit(solution)/shard_map/block_scatter/ppermute | solution.py:530
  8.4 11.0 %collective-permute-start.2 = (bf16[5,8,4224]{2,1,0:T(8,128)(2,1)S(1)}, bf16[5,8,4224]{2,1,0:T(8,128)(2,1)S(1)}, u32[]{:S(2)}, u32[]{:S(2)}) collective-permute-start(bf16[5,8,4224]{2,1,0:T(8,128)(2,1)S(1)} %get-tuple-element.44), channel_id=1, source_target_pairs={{0,2},{1,3},{2,0},{3,1},{4,6},{5,7},{6,4},{7,5},{8,10},{9,11},{10,... | collective-permute-start | bytes 1013768 | tf_op jit(solution)/shard_map/block_scatter/ppermute | solution.py:530
  11.2 11.0 %collective-permute-start.3 = (bf16[5,8,4224]{2,1,0:T(8,128)(2,1)S(1)}, bf16[5,8,4224]{2,1,0:T(8,128)(2,1)S(1)}, u32[]{:S(2)}, u32[]{:S(2)}) collective-permute-start(bf16[5,8,4224]{2,1,0:T(8,128)(2,1)S(1)} %get-tuple-element.45), channel_id=1, source_target_pairs={{0,4},{1,5},{2,6},{3,7},{4,8},{5,9},{6,10},{7,11},{8,12},{9,13},{1... | collective-permute-start | bytes 1013768 | tf_op jit(solution)/shard_map/block_scatter/ppermute | solution.py:530
  12.5 9.7 %collective-permute-start.4 = (bf16[5,8,4224]{2,1,0:T(8,128)(2,1)S(1)}, bf16[5,8,4224]{2,1,0:T(8,128)(2,1)S(1)}, u32[]{:S(2)}, u32[]{:S(2)}) collective-permute-start(bf16[5,8,4224]{2,1,0:T(8,128)(2,1)S(1)} %get-tuple-element.46), channel_id=1, source_target_pairs={{0,12},{1,13},{2,14},{3,15},{4,0},{5,1},{6,2},{7,3},{8,4},{9,5},{1... | collective-permute-start | bytes 1013768 | tf_op jit(solution)/shard_map/block_scatter/ppermute | solution.py:530
  15.6 10.7 %collective-permute-start.5 = (bf16[5,8,4096]{2,1,0:T(8,128)(2,1)S(1)}, bf16[5,8,4096]{2,1,0:T(8,128)(2,1)S(1)}, u32[]{:S(2)}, u32[]{:S(2)}) collective-permute-start(bf16[5,8,4096]{2,1,0:T(8,128)(2,1)S(1)} %get-tuple-element.49), channel_id=1, source_target_pairs={{0,2},{1,3},{2,0},{3,1},{4,6},{5,7},{6,4},{7,5},{8,10},{9,11},{10,... | collective-permute-start | bytes 983048 | tf_op jit(solution)/shard_map/block_scatter/ppermute | solution.py:530
  15.9 12.8 %collective-permute-start.6 = (bf16[5,8,4096]{2,1,0:T(8,128)(2,1)S(1)}, bf16[5,8,4096]{2,1,0:T(8,128)(2,1)S(1)}, u32[]{:S(2)}, u32[]{:S(2)}) collective-permute-start(bf16[5,8,4096]{2,1,0:T(8,128)(2,1)S(1)} %get-tuple-element.47), channel_id=1, source_target_pairs={{0,4},{1,5},{2,6},{3,7},{4,8},{5,9},{6,10},{7,11},{8,12},{9,13},{1... | collective-permute-start | bytes 983048 | tf_op jit(solution)/shard_map/block_scatter/ppermute | solution.py:530
  19.4 9.4 %collective-permute-start.7 = (bf16[5,8,4096]{2,1,0:T(8,128)(2,1)S(1)}, bf16[5,8,4096]{2,1,0:T(8,128)(2,1)S(1)}, u32[]{:S(2)}, u32[]{:S(2)}) collective-permute-start(bf16[5,8,4096]{2,1,0:T(8,128)(2,1)S(1)} %get-tuple-element.48), channel_id=1, source_target_pairs={{0,12},{1,13},{2,14},{3,15},{4,0},{5,1},{6,2},{7,3},{8,4},{9,5},{1... | collective-permute-start | bytes 983048 | tf_op jit(solution)/shard_map/block_scatter/ppermute | solution.py:530
  23.8 13.3 %collective-permute-start.8 = (bf16[5,8,4224]{2,1,0:T(8,128)(2,1)S(1)}, bf16[5,8,4224]{2,1,0:T(8,128)(2,1)S(1)}, u32[]{:S(2)}, u32[]{:S(2)}) collective-permute-start(bf16[5,8,4224]{2,1,0:T(8,128)(2,1)S(1)} %get-tuple-element.53), channel_id=1, source_target_pairs={{0,8},{1,9},{2,10},{3,11},{4,12},{5,13},{6,14},{7,15},{8,0},{9,1},... | collective-permute-start | bytes 1013768 | tf_op jit(solution)/shard_map/block_scatter/ppermute | solution.py:530
  25.6 11.5 %collective-permute-start.9 = (bf16[5,8,4224]{2,1,0:T(8,128)(2,1)S(1)}, bf16[5,8,4224]{2,1,0:T(8,128)(2,1)S(1)}, u32[]{:S(2)}, u32[]{:S(2)}) collective-permute-start(bf16[5,8,4224]{2,1,0:T(8,128)(2,1)S(1)} %get-tuple-element.54), channel_id=1, source_target_pairs={{0,2},{1,3},{2,0},{3,1},{4,6},{5,7},{6,4},{7,5},{8,10},{9,11},{10,... | collective-permute-start | bytes 1013768 | tf_op jit(solution)/shard_map/block_scatter/ppermute | solution.py:530
  41.1 14.5 %all-to-all-start = ((bf16[8,192,256]{2,1,0:T(8,128)(2,1)}), bf16[8,192,256]{2,1,0:T(8,128)(2,1)S(1)}, u32[]{:S(2)}, u32[]{:S(2)}) async-start(bf16[8,192,256]{2,1,0:T(8,128)(2,1)} %get-tuple-element.62), calls=%async_computation | async-start | bytes 1572864 | tf_op jit(solution)/shard_map/transform/all_to_all | solution.py:623
  59.1 12.6 %all-to-all-start.1 = ((bf16[8,64,256]{2,1,0:T(8,128)(2,1)}), bf16[8,64,256]{2,1,0:T(8,128)(2,1)S(1)}, u32[]{:S(2)}, u32[]{:S(2)}) async-start(bf16[8,64,256]{2,1,0:T(8,128)(2,1)} %bitcast), calls=%async_computation.1 | async-start | bytes 524288 | tf_op jit(solution)/shard_map/transform/all_to_all | solution.py:645
  65.5 4.6 %collective-permute-start.10 = (bf16[1,8,4096]{2,1,0:T(8,128)(2,1)S(1)}, bf16[1,8,4096]{2,1,0:T(8,128)(2,1)S(1)}, u32[]{:S(2)}, u32[]{:S(2)}) collective-permute-start(bf16[1,8,4096]{2,1,0:T(8,128)(2,1)S(1)} %get-tuple-element.60), channel_id=1, source_target_pairs={{0,8},{1,9},{2,10},{3,11},{4,12},{5,13},{6,14},{7,15},{8,0},{9,1},... | collective-permute-start | bytes 196616 | tf_op jit(solution)/shard_map/transform/ppermute | solution.py:530
  65.5 5.7 %collective-permute-start.11 = (bf16[1,8,4096]{2,1,0:T(8,128)(2,1)S(1)}, bf16[1,8,4096]{2,1,0:T(8,128)(2,1)S(1)}, u32[]{:S(2)}, u32[]{:S(2)}) collective-permute-start(bf16[1,8,4096]{2,1,0:T(8,128)(2,1)S(1)} %get-tuple-element.61), channel_id=1, source_target_pairs={{0,2},{1,3},{2,0},{3,1},{4,6},{5,7},{6,4},{7,5},{8,10},{9,11},{10,... | collective-permute-start | bytes 196616 | tf_op jit(solution)/shard_map/transform/ppermute | solution.py:530
  74.8 12.8 %collective-permute-start.12 = (bf16[32,4096]{1,0:T(8,128)(2,1)S(1)}, bf16[32,4096]{1,0:T(8,128)(2,1)S(1)}, u32[]{:S(2)}, u32[]{:S(2)}) collective-permute-start(bf16[32,4096]{1,0:T(8,128)(2,1)S(1)} %bitcast.5), channel_id=1, source_target_pairs={{0,8},{1,9},{2,10},{3,11},{4,12},{5,13},{6,14},{7,15},{8,0},{9,1},... | collective-permute-start | bytes 786440 | tf_op jit(solution)/shard_map/block_gather/ppermute | solution.py:530
  76.3 11.3 %collective-permute-start.13 = (bf16[32,4096]{1,0:T(8,128)(2,1)S(1)}, bf16[32,4096]{1,0:T(8,128)(2,1)S(1)}, u32[]{:S(2)}, u32[]{:S(2)}) collective-permute-start(bf16[32,4096]{1,0:T(8,128)(2,1)S(1)} %bitcast.6), channel_id=1, source_target_pairs={{0,2},{1,3},{2,0},{3,1},{4,6},{5,7},{6,4},{7,5},{8,10},{9,11},{10,... | collective-permute-start | bytes 786440 | tf_op jit(solution)/shard_map/block_gather/ppermute | solution.py:530
  77.8 10.8 %collective-permute-start.19 = (bf16[32,4096]{1,0:T(8,128)(2,1)S(1)}, bf16[32,4096]{1,0:T(8,128)(2,1)S(1)}, u32[]{:S(2)}, u32[]{:S(2)}) collective-permute-start(bf16[32,4096]{1,0:T(8,128)(2,1)S(1)} %bitcast.7), channel_id=1, source_target_pairs={{0,4},{1,5},{2,6},{3,7},{4,8},{5,9},{6,10},{7,11},{8,12},{9,13},{1... | collective-permute-start | bytes 786440 | tf_op jit(solution)/shard_map/block_gather/ppermute | solution.py:530
  79.0 11.8 %collective-permute-start.21 = (bf16[32,4096]{1,0:T(8,128)(2,1)S(1)}, bf16[32,4096]{1,0:T(8,128)(2,1)S(1)}, u32[]{:S(2)}, u32[]{:S(2)}) collective-permute-start(bf16[32,4096]{1,0:T(8,128)(2,1)S(1)} %bitcast.8), channel_id=1, source_target_pairs={{0,12},{1,13},{2,14},{3,15},{4,0},{5,1},{6,2},{7,3},{8,4},{9,5},{1... | collective-permute-start | bytes 786440 | tf_op jit(solution)/shard_map/block_gather/ppermute | solution.py:530
  80.5 10.3 %collective-permute-start.17 = (bf16[32,4096]{1,0:T(8,128)(2,1)S(1)}, bf16[32,4096]{1,0:T(8,128)(2,1)S(1)}, u32[]{:S(2)}, u32[]{:S(2)}) collective-permute-start(bf16[32,4096]{1,0:T(8,128)(2,1)S(1)} %bitcast.9), channel_id=1, source_target_pairs={{0,1},{1,0},{2,3},{3,2},{4,5},{5,4},{6,7},{7,6},{8,9},{9,8},{10,11... | collective-permute-start | bytes 786440 | tf_op jit(solution)/shard_map/block_gather/ppermute | solution.py:530
  87.6 4.7 %collective-permute-start.18 = (bf16[32,4096]{1,0:T(8,128)(2,1)S(1)}, bf16[32,4096]{1,0:T(8,128)(2,1)S(1)}, u32[]{:S(2)}, u32[]{:S(2)}) collective-permute-start(bf16[32,4096]{1,0:T(8,128)(2,1)S(1)} %collective-permute-done.12.refs_2_), channel_id=1, source_target_pairs={{0,1},{1,0},{2,3},{3,2},{4,5},{5,4},{6,7},{7,6},{8,9},{9,8},{10,11... | collective-permute-start | bytes 786440 | tf_op jit(solution)/shard_map/block_gather/ppermute | solution.py:530
  88.0 5.0 %collective-permute-start.23 = (bf16[32,4096]{1,0:T(8,128)(2,1)S(1)}, bf16[32,4096]{1,0:T(8,128)(2,1)S(1)}, u32[]{:S(2)}, u32[]{:S(2)}) collective-permute-start(bf16[32,4096]{1,0:T(8,128)(2,1)S(1)} %collective-permute-done.13.refs_8_), channel_id=1, source_target_pairs={{0,1},{1,0},{2,3},{3,2},{4,5},{5,4},{6,7},{7,6},{8,9},{9,8},{10,11... | collective-permute-start | bytes 786440 | tf_op jit(solution)/shard_map/block_gather/ppermute | solution.py:530
  88.6 6.5 %collective-permute-start.20 = (bf16[32,4096]{1,0:T(8,128)(2,1)S(1)}, bf16[32,4096]{1,0:T(8,128)(2,1)S(1)}, u32[]{:S(2)}, u32[]{:S(2)}) collective-permute-start(bf16[32,4096]{1,0:T(8,128)(2,1)S(1)} %collective-permute-done.19.refs_4_), channel_id=1, source_target_pairs={{0,1},{1,0},{2,3},{3,2},{4,5},{5,4},{6,7},{7,6},{8,9},{9,8},{10,11... | collective-permute-start | bytes 786440 | tf_op jit(solution)/shard_map/block_gather/ppermute | solution.py:530
  90.8 4.3 %collective-permute-start.22 = (bf16[32,4096]{1,0:T(8,128)(2,1)S(1)}, bf16[32,4096]{1,0:T(8,128)(2,1)S(1)}, u32[]{:S(2)}, u32[]{:S(2)}) collective-permute-start(bf16[32,4096]{1,0:T(8,128)(2,1)S(1)} %collective-permute-done.21.refs_6_), channel_id=1, source_target_pairs={{0,1},{1,0},{2,3},{3,2},{4,5},{5,4},{6,7},{7,6},{8,9},{9,8},{10,11... | collective-permute-start | bytes 786440 | tf_op jit(solution)/shard_map/block_gather/ppermute | solution.py:530
  90.8 9.8 %collective-permute-start.14 = (bf16[32,4096]{1,0:T(8,128)(2,1)S(1)}, bf16[32,4096]{1,0:T(8,128)(2,1)S(1)}, u32[]{:S(2)}, u32[]{:S(2)}) collective-permute-start(bf16[32,4096]{1,0:T(8,128)(2,1)S(1)} %collective-permute-done.12.refs_2_), channel_id=1, source_target_pairs={{0,2},{1,3},{2,0},{3,1},{4,6},{5,7},{6,4},{7,5},{8,10},{9,11},{10,... | collective-permute-start | bytes 786440 | tf_op jit(solution)/shard_map/block_gather/ppermute | solution.py:530
  92.4 8.3 %collective-permute-start.15 = (bf16[32,4096]{1,0:T(8,128)(2,1)S(1)}, bf16[32,4096]{1,0:T(8,128)(2,1)S(1)}, u32[]{:S(2)}, u32[]{:S(2)}) collective-permute-start(bf16[32,4096]{1,0:T(8,128)(2,1)S(1)} %collective-permute-done.13.refs_8_), channel_id=1, source_target_pairs={{0,4},{1,5},{2,6},{3,7},{4,8},{5,9},{6,10},{7,11},{8,12},{9,13},{1... | collective-permute-start | bytes 786440 | tf_op jit(solution)/shard_map/block_gather/ppermute | solution.py:530
  93.0 7.7 %collective-permute-start.16 = (bf16[32,4096]{1,0:T(8,128)(2,1)S(1)}, bf16[32,4096]{1,0:T(8,128)(2,1)S(1)}, u32[]{:S(2)}, u32[]{:S(2)}) collective-permute-start(bf16[32,4096]{1,0:T(8,128)(2,1)S(1)} %collective-permute-done.13.refs_8_), channel_id=1, source_target_pairs={{0,12},{1,13},{2,14},{3,15},{4,0},{5,1},{6,2},{7,3},{8,4},{9,5},{1... | collective-permute-start | bytes 786440 | tf_op jit(solution)/shard_map/block_gather/ppermute | solution.py:530
  100.7 2.7 %collective-permute-start.24 = (bf16[32,4096]{1,0:T(8,128)(2,1)S(1)}, bf16[32,4096]{1,0:T(8,128)(2,1)S(1)}, u32[]{:S(2)}, u32[]{:S(2)}) collective-permute-start(bf16[32,4096]{1,0:T(8,128)(2,1)S(1)} %collective-permute-done.14.refs_0_), channel_id=1, source_target_pairs={{0,1},{1,0},{2,3},{3,2},{4,5},{5,4},{6,7},{7,6},{8,9},{9,8},{10,11... | collective-permute-start | bytes 786440 | tf_op jit(solution)/shard_map/block_gather/ppermute | solution.py:530
  102.3 1.5 %collective-permute-start.25 = (bf16[32,4096]{1,0:T(8,128)(2,1)S(1)}, bf16[32,4096]{1,0:T(8,128)(2,1)S(1)}, u32[]{:S(2)}, u32[]{:S(2)}) collective-permute-start(bf16[32,4096]{1,0:T(8,128)(2,1)S(1)} %collective-permute-done.15.refs_2_), channel_id=1, source_target_pairs={{0,1},{1,0},{2,3},{3,2},{4,5},{5,4},{6,7},{7,6},{8,9},{9,8},{10,11... | collective-permute-start | bytes 786440 | tf_op jit(solution)/shard_map/block_gather/ppermute | solution.py:530
  102.3 1.9 %collective-permute-start.26 = (bf16[32,4096]{1,0:T(8,128)(2,1)S(1)}, bf16[32,4096]{1,0:T(8,128)(2,1)S(1)}, u32[]{:S(2)}, u32[]{:S(2)}) collective-permute-start(bf16[32,4096]{1,0:T(8,128)(2,1)S(1)} %collective-permute-done.16.refs_4_), channel_id=1, source_target_pairs={{0,1},{1,0},{2,3},{3,2},{4,5},{5,4},{6,7},{7,6},{8,9},{9,8},{10,11... | collective-permute-start | bytes 786440 | tf_op jit(solution)/shard_map/block_gather/ppermute | solution.py:530
